TPU v7x, 32 devices: a whole 2x2x4 slice. The times are simulated.
32 devices in a mesh: req: 8 (over z, y), tp: 4 (over x, core).
Axes of the slice: x: 2, y: 2, z: 4, core: 2. Of those that a mesh axis runs over, the one named last changes fastest.
Arguments:
- resid: bfloat16 [256, 1536], P('req', 'tp'), may hold values from -2.5 to 2.5
- queries: bfloat16 [256, 1536], P('req', 'tp'), may hold values from -250 to 250
- new_keys: bfloat16 [256, 512], P('req', 'tp'), may hold values from -6 to 6
- new_values: bfloat16 [256, 512], P('req', 'tp'), may hold values from -6 to 6
- k_cache: bfloat16 [256, 128, 512], P('req', None, 'tp'), may hold values from -6.5 to 6.5
- v_cache: bfloat16 [256, 128, 512], P('req', None, 'tp'), may hold values from -6 to 6
- lengths: int32 [256], P('req'), may hold values from 2 to 128, as said below
- w_out: bfloat16 [1536, 1536], P('tp'), may hold values from -0.15625 to 0.15625
- norm_gain: float32 [1536], P('tp'), may hold values from 0.1 to 1.9
- w_router: float32 [1536, 16], P('tp'), may hold values from -0.08125 to 0.08125
- routes: int32 [256, 2], P('req'), may hold values from 0 to 15, as said below
- w_gate: bfloat16 [16, 1536, 1024], P('req', 'tp'), may hold values from -0.15625 to 0.15625
- w_up: bfloat16 [16, 1536, 1024], P('req', 'tp'), may hold values from -0.15625 to 0.15625
- w_down: bfloat16 [16, 1024, 1536], P('req', None, 'tp'), may hold values from -0.46875 to 0.46875
Outputs:
- attended: bfloat16 [256, 1536], P('req', 'tp')
- layer_out: bfloat16 [256, 1536], P('req', 'tp')
Inputs may be any that keep to these rules, and one draw needn't show every extreme that they name: A request reads the first lengths[b] positions of its cache; some request has exactly 128, and some request exactly 2. `routes`: each request names two different experts; among the 32 requests of one device, at most 8 name the same expert, and on every device some expert is named exactly 8 times.
All inputs are finite; a program needn't handle non-finite values.
Results may differ from a plain program's by a relative error of at most 0.01.
Values may be sent and summed in bfloat16 or wider, within the bound.
No kernel may reach another device: no remote copies, remote signals or barrier semaphores. Data moves between devices by JAX's collectives and lax.ppermute only.
A program may use at most 64 MiB of HBM per device.

v0:
```python
import math

import jax
import jax.numpy as jnp
from jax import lax
from jax.sharding import PartitionSpec as P

D = 1536
HEAD_DIM = 64
EXPERTS = 16
TOP = 2
CAP = 8


def attend_local(queries, new_keys, new_values, k_cache, v_cache, lengths):
    row_count = queries.shape[0]
    kv_local = new_keys.shape[1] // HEAD_DIM
    group_size = queries.shape[1] // HEAD_DIM // kv_local
    cache_len = k_cache.shape[1]
    score_scale = 1.0 / math.sqrt(HEAD_DIM)
    query = queries.reshape(row_count, kv_local, group_size, HEAD_DIM)
    keys_all = k_cache.reshape(row_count, cache_len, kv_local, HEAD_DIM)
    values_all = v_cache.reshape(row_count, cache_len, kv_local, HEAD_DIM)
    scores = (
        jnp.einsum("bgqd,blgd->bgql", query, keys_all, preferred_element_type=jnp.float32)
        * score_scale
    )
    self_score = (
        jnp.einsum(
            "bgqd,bgd->bgq",
            query,
            new_keys.reshape(row_count, kv_local, HEAD_DIM),
            preferred_element_type=jnp.float32,
        )
        * score_scale
    )
    valid_mask = (jnp.arange(cache_len, dtype=jnp.int32)[None, :] < lengths[:, None])[
        :, None, None, :
    ]
    peak_score = jnp.maximum(jnp.max(jnp.where(valid_mask, scores, -1e30), axis=-1), self_score)
    exp_terms = jnp.where(valid_mask, jnp.exp(scores - peak_score[..., None]), 0.0)
    self_exp = jnp.exp(self_score - peak_score)
    denom_sum = jnp.sum(exp_terms, axis=-1) + self_exp
    weights = (exp_terms / denom_sum[..., None]).astype(jnp.bfloat16)
    self_weight = (self_exp / denom_sum).astype(jnp.bfloat16)
    value_self = new_values.astype(jnp.float32).reshape(row_count, kv_local, 1, HEAD_DIM)
    mixed = (
        jnp.einsum("bgql,blgd->bgqd", weights, values_all, preferred_element_type=jnp.float32)
        + self_weight.astype(jnp.float32)[..., None] * value_self
    )
    return mixed.astype(jnp.bfloat16).reshape(row_count, kv_local * group_size * HEAD_DIM)


def shards(
    resid,
    queries,
    new_keys,
    new_values,
    k_cache,
    v_cache,
    lengths,
    w_out,
    norm_gain,
    w_router,
    routes,
    w_gate,
    w_up,
    w_down,
):
    req_dev = resid.shape[0]
    width_local = resid.shape[1]
    slot_dev = w_gate.shape[0]
    req_count = lax.axis_size("req")
    shard_count = max(1, req_count // EXPERTS)
    attention = attend_local(queries, new_keys, new_values, k_cache, v_cache, lengths)
    partial_value = jnp.dot(attention, w_out, preferred_element_type=jnp.float32)
    projected = lax.psum_scatter(partial_value, "tp", scatter_dimension=1, tiled=True)
    attended = (resid.astype(jnp.float32) + projected).astype(jnp.bfloat16)
    attended_f = attended.astype(jnp.float32)
    scaled = attended_f * norm_gain[None, :]
    square_sum, logit_part = lax.psum(
        (
            jnp.sum(attended_f * attended_f, axis=1),
            jnp.dot(scaled, w_router, precision=lax.Precision.HIGHEST),
        ),
        "tp",
    )
    inv_rms = 1.0 / jnp.sqrt(square_sum / D + 1e-06)
    normed = (scaled * inv_rms[:, None]).astype(jnp.bfloat16)
    logits = logit_part * inv_rms[:, None]
    expert_ids = jnp.arange(EXPERTS, dtype=jnp.int32)
    first_logit = jnp.sum(jnp.where(routes[:, 0:1] == expert_ids[None, :], logits, 0.0), axis=1)
    second_logit = jnp.sum(jnp.where(routes[:, 1:2] == expert_ids[None, :], logits, 0.0), axis=1)
    first_weight = jax.nn.sigmoid(first_logit - second_logit)
    second_weight = 1.0 - first_weight
    flat_routes = routes.reshape(req_dev * TOP)
    one_hot = (flat_routes[None, :] == expert_ids[:, None]).astype(jnp.int32)
    rank_in = jnp.cumsum(one_hot, axis=1) - one_hot
    slot_ids = jnp.arange(CAP, dtype=jnp.int32)
    chosen = (one_hot[:, None, :] == 1) & (rank_in[:, None, :] == slot_ids[None, :, None])
    token_pick = jnp.sum(
        chosen.reshape(EXPERTS, CAP, req_dev, TOP).astype(jnp.int32), axis=-1
    ).astype(jnp.bfloat16)
    per_expert = jnp.einsum(
        "ecb,bd->ecd", token_pick, normed, preferred_element_type=jnp.float32
    ).astype(jnp.bfloat16)
    outgoing = jnp.broadcast_to(
        per_expert[:, None], (EXPERTS, shard_count, CAP, width_local)
    ).reshape(req_count, slot_dev, CAP, width_local)
    incoming = lax.all_to_all(outgoing, "req", split_axis=0, concat_axis=0, tiled=True)
    gate_pre = jnp.einsum("nscd,sdf->nscf", incoming, w_gate, preferred_element_type=jnp.float32)
    up_pre = jnp.einsum("nscd,sdf->nscf", incoming, w_up, preferred_element_type=jnp.float32)
    gate_sum, up_sum = lax.psum((gate_pre, up_pre), "tp")
    hidden = (jax.nn.silu(gate_sum) * up_sum).astype(jnp.bfloat16)
    computed = jnp.einsum("nscf,sfd->nscd", hidden, w_down, preferred_element_type=jnp.float32)
    returned = lax.all_to_all(computed, "req", split_axis=0, concat_axis=0, tiled=True)
    combined = jnp.sum(returned.reshape(EXPERTS, shard_count, CAP, width_local), axis=1)
    route_out = jnp.einsum(
        "ecr,ecd->rd", chosen.astype(jnp.float32), combined, precision=lax.Precision.HIGHEST
    ).reshape(req_dev, TOP, width_local)
    moe = first_weight[:, None] * route_out[:, 0] + second_weight[:, None] * route_out[:, 1]
    layer_out = (attended_f + moe).astype(jnp.bfloat16)
    return (attended, layer_out)


def solution(mesh):
    placed = (
        P("req", "tp"),
        P("req", "tp"),
        P("req", "tp"),
        P("req", "tp"),
        P("req", None, "tp"),
        P("req", None, "tp"),
        P("req"),
        P("tp", None),
        P("tp"),
        P("tp", None),
        P("req", None),
        P("req", "tp", None),
        P("req", "tp", None),
        P("req", None, "tp"),
    )
    return jax.shard_map(
        shards,
        mesh=mesh,
        in_specs=placed,
        out_specs=(P("req", "tp"), P("req", "tp")),
        check_vma=False,
    )
```

profile of v0, /device:TPU:0, one launch (start us, length us, event | category | flops | bytes accessed | tf_op | source)
XLA Modules:
  0.0 120.1 jit_solution(11532046357941892906)
XLA Ops:
  7.2 0.8 iota_compare_fusion.3
  8.1 0.8 reshape.158
  8.9 1.6 %copy.47 = bf16[32,128,128]{1,2,0:T(8,128)(2,1)S(1)} copy(bf16[32,128,128]{2,1,0:T(8,128)(2,1)} %param.18) | data formatting | bytes 2097152 | tf_op args[4]
  10.6 0.2 fusion.53
  10.8 0.5 select_reduce_fusion
  11.4 0.3 fusion.24
  11.7 2.3 %copy.48 = bf16[32,128,128]{1,2,0:T(8,128)(2,1)} copy(bf16[32,128,128]{2,1,0:T(8,128)(2,1)} %param.19) | data formatting | bytes 2097152 | tf_op args[5]
  14.0 0.1 reshape.163
  14.1 2.0 %fusion.15 = bf16[32,2,3,64]{3,2,1,0:T(4,128)(2,1)S(1)} fusion(bf16[32,128,2,64]{1,3,2,0:T(8,128)(2,1)} %bitcast.77, f32[32,2,3,128]{3,2,1,0:T(4,128)S(1)} %get-tuple-element.17, f32[32,2,64]{2,1,0:T(2,128)S(1)} %reshape.163, f32[32,2,3]{2,1,0:T(2,128)S(1)} %get-tuple-element.13, f32[32,2,3]{2,1,0:T(2,128)S(1)} %get-tuple-element.12, ...), kind=kOutput, calls=%fused_computation.12 | convolution fusion | flops 3280896 | bytes 1194240 | tf_op jit(solution)/shard_map/bgql,blgd->bgqd/dot_general | solution.py:48
  16.2 0.1 reshape.162
  16.3 1.0 fusion.54
  17.4 0.1 copy.49
  17.5 0.1 eq.136
  17.6 0.2 reduce_window_sum.15
  17.9 0.1 fusion.40
  18.1 0.1 fusion.41
  18.2 0.1 copy.53
  18.4 21.6 %reduce-scatter.2.cloned.1.call-done = f32[32,384]{1,0:T(8,128)} async-done(((f32[32,1536]{1,0:T(8,128)}), f32[32,384]{1,0:T(8,128)}) %reduce-scatter.2.cloned.1.call-update) | async-done | bytes 49168 | tf_op jit(solution)/shard_map/reduce_scatter | solution.py:77
  39.9 0.9 fusion.34
  40.9 0.2 fusion.32
  41.0 6.0 %all-reduce = (f32[32]{0:T(128)S(1)}, f32[32,16]{0,1:T(8,128)S(1)}) all-reduce(f32[32]{0:T(128)S(1)} %get-tuple-element.10, f32[32,16]{0,1:T(8,128)S(1)} %fusion.32), channel_id=1, replica_groups=mesh['req'=8,'tp'=4] {'tp'}, use_global_device_ids=true, to_apply=%region_5.6 | all-reduce | flops 544 | bytes 4352 | tf_op jit(solution)/shard_map/psum | solution.py:81
  47.0 0.2 convolution_convert_fusion
  47.3 12.7 %all_to_all.10 = bf16[8,2,8,384]{3,2,1,0:T(8,128)(2,1)S(1)} all-to-all(bf16[8,2,8,384]{3,2,1,0:T(8,128)(2,1)S(1)} %bitcast.79), channel_id=1, replica_groups=mesh['req'=8,'tp'=4] {'req'}, dimensions={0} | all-to-all | bytes 196608 | tf_op jit(solution)/shard_map/all_to_all | solution.py:110
  60.0 1.2 %fusion.6 = f32[8,2,8,1024]{3,2,0,1:T(8,128)} fusion(bf16[2,384,1024]{2,1,0:T(8,128)(2,1)S(1)} %copy-done, bf16[8,2,8,384]{3,2,1,0:T(8,128)(2,1)S(1)} %all_to_all.10), kind=kOutput, calls=%fused_computation.6 | convolution fusion | flops 100663296 | bytes 2195456 | tf_op jit(solution)/shard_map/nscd,sdf->nscf/dot_general | solution.py:111
  61.2 1.2 %fusion.9 = f32[8,2,8,1024]{3,2,0,1:T(8,128)} fusion(bf16[2,384,1024]{2,1,0:T(8,128)(2,1)S(1)} %copy-done.1, bf16[8,2,8,384]{3,2,1,0:T(8,128)(2,1)S(1)} %all_to_all.10), kind=kOutput, calls=%fused_computation.7 | convolution fusion | flops 100663296 | bytes 2195456 | tf_op jit(solution)/shard_map/nscd,sdf->nscf/dot_general | solution.py:112
  62.4 33.7 %all-reduce.4.cloned.1.call-done = (f32[8,2,8,1024]{3,2,0,1:T(8,128)}, f32[8,2,8,1024]{3,2,0,1:T(8,128)}) async-done(((f32[8,2,8,1024]{3,2,0,1:T(8,128)}, f32[8,2,8,1024]{3,2,0,1:T(8,128)}), (f32[8,2,8,1024]{3,2,0,1:T(8,128)}, f32[8,2,8,1024]{3,2,0,1:T(8,128)})) %all-reduce.4.cloned.1.call-update) | async-done | bytes 1048592 | tf_op jit(solution)/shard_map/psum | solution.py:113
  96.2 2.1 %fusion.12 = f32[8,2,8,384]{3,2,0,1:T(8,128)S(1)} fusion(bf16[2,1024,384]{2,1,0:T(8,128)(2,1)} %param.27, f32[8,2,8,1024]{3,2,0,1:T(8,128)} %get-tuple-element.6, f32[8,2,8,1024]{3,2,0,1:T(8,128)} %get-tuple-element.7), kind=kOutput, calls=%fused_computation.8 | convolution fusion | flops 101449728 | bytes 2818048 | tf_op jit(solution)/shard_map/nscf,sfd->nscd/dot_general | solution.py:115
  98.3 0.7 copy.58
  99.0 5.5 %all-to-all-start.1 = ((f32[8,2,8,384]{3,2,1,0:T(8,128)}), f32[8,2,8,384]{3,2,1,0:T(8,128)S(1)}, u32[]{:S(2)}, u32[]{:S(2)}) async-start(f32[8,2,8,384]{3,2,1,0:T(8,128)} %copy.58), calls=%async_computation.2 | async-start | bytes 393216 | tf_op jit(solution)/shard_map/all_to_all | solution.py:116
  104.7 7.6 %all-to-all-done.1 = f32[8,2,8,384]{3,2,1,0:T(8,128)S(1)} async-done(((f32[8,2,8,384]{3,2,1,0:T(8,128)}), f32[8,2,8,384]{3,2,1,0:T(8,128)S(1)}, u32[]{:S(2)}, u32[]{:S(2)}) %all-to-all-start.1) | async-done | bytes 196640 | tf_op jit(solution)/shard_map/all_to_all | solution.py:116
  112.3 0.3 convolution_bitcast_fusion
  112.6 0.7 fusion.35
  (39 shorter events, 0.7 us)
Async XLA Ops:
  7.2 52.8 %copy-start = (bf16[2,384,1024]{2,1,0:T(8,128)(2,1)S(1)}, bf16[2,384,1024]{2,1,0:T(8,128)(2,1)}, u32[]{:S(2)}) copy-start(bf16[2,384,1024]{2,1,0:T(8,128)(2,1)} %param.25) | copy-start | bytes 4718596
  7.2 3.4 %copy-start.7 = (bf16[32,128]{1,0:T(8,128)(2,1)S(1)}, bf16[32,128]{1,0:T(8,128)(2,1)}, u32[]{:S(2)}) copy-start(bf16[32,128]{1,0:T(8,128)(2,1)} %param.16) | copy-start | bytes 24580
  7.2 32.7 %reduce-scatter.2.cloned.1.call-start = ((), (), s32[]{:S(2)}) async-start(), calls=%async_computation.3 | async-start | bytes 245760 | tf_op jit(solution)/shard_map/reduce_scatter | solution.py:77
  11.3 2.7 %copy-start.8 = (bf16[32,128]{1,0:T(8,128)(2,1)S(1)}, bf16[32,128]{1,0:T(8,128)(2,1)}, u32[]{:S(2)}) copy-start(bf16[32,128]{1,0:T(8,128)(2,1)} %param.17) | copy-start | bytes 24580
  14.1 2.2 %copy-start.2 = (bf16[384,1536]{1,0:T(8,128)(2,1)S(1)}, bf16[384,1536]{1,0:T(8,128)(2,1)}, u32[]{:S(2)}) copy-start(bf16[384,1536]{1,0:T(8,128)(2,1)} %param.21) | copy-start | bytes 3538948
  16.1 1.2 %copy-start.6 = (s32[32,2]{0,1:T(2,128)S(1)}, s32[32,2]{0,1:T(2,128)}, u32[]{:S(2)}) copy-start(s32[32,2]{0,1:T(2,128)} %param.24) | copy-start | bytes 772
  16.1 23.8 %copy-start.4 = (bf16[32,384]{1,0:T(8,128)(2,1)S(1)}, bf16[32,384]{1,0:T(8,128)(2,1)}, u32[]{:S(2)}) copy-start(bf16[32,384]{1,0:T(8,128)(2,1)} %param.14) | copy-start | bytes 73732
  16.2 24.7 %copy-start.5 = (f32[384,16]{0,1:T(8,128)S(1)}, f32[384,16]{0,1:T(8,128)}, u32[]{:S(2)}) copy-start(f32[384,16]{0,1:T(8,128)} %param.23) | copy-start | bytes 73732
  16.2 24.7 %copy-start.9 = (f32[384]{0:T(512)S(1)}, f32[384]{0:T(512)}, u32[]{:S(2)}) copy-start(f32[384]{0:T(512)} %param.22) | copy-start | bytes 4612
  17.3 43.9 %copy-start.1 = (bf16[2,384,1024]{2,1,0:T(8,128)(2,1)S(1)}, bf16[2,384,1024]{2,1,0:T(8,128)(2,1)}, u32[]{:S(2)}) copy-start(bf16[2,384,1024]{2,1,0:T(8,128)(2,1)} %param.26) | copy-start | bytes 4718596
  17.3 78.8 %all-reduce.4.cloned.1.call-start = ((), (), s32[]{:S(2)}) async-start(), calls=%async_computation.4 | async-start | bytes 2097152 | tf_op jit(solution)/shard_map/psum | solution.py:113
  40.8 71.8 %copy-start.3 = (bf16[32,384]{1,0:T(8,128)(2,1)}, bf16[32,384]{1,0:T(8,128)(2,1)S(1)}, u32[]{:S(2)}) copy-start(bf16[32,384]{1,0:T(8,128)(2,1)S(1)} %get-tuple-element.11) | copy-start | bytes 73732
  99.0 13.3 %all-to-all-start.1 = ((f32[8,2,8,384]{3,2,1,0:T(8,128)}), f32[8,2,8,384]{3,2,1,0:T(8,128)S(1)}, u32[]{:S(2)}, u32[]{:S(2)}) async-start(f32[8,2,8,384]{3,2,1,0:T(8,128)} %copy.58), calls=%async_computation.2 | async-start | bytes 393216 | tf_op jit(solution)/shard_map/all_to_all | solution.py:116
Sparse Core Ops, SparseCore 0:
  17.4 22.4 reduce-scatter.1
  62.5 33.5 all-reduce.3
where the time goes:
time: 121 us; the launch traced here: 120 us
  waiting for transfers between devices  62.9 us (52%)
  blocking collectives  18.7 us (15%)
  between operations  14.3 us (12%)
  matrix products  8.93 us (7%)
  local copies, waits for them, and re-layouts  6.4 us (5%)
  starting transfers between devices  5.6 us (5%)
  other arithmetic  3.31 us (3%)
    psum x1, waiting for transfers between devices, shards(): gate_sum, up_sum = lax.psum((gate_pre, up_pre), 'tp')  33.7 us
    reduce_scatter x1, waiting for transfers between devices, shards(): lax.psum_scatter(partial_value, 'tp', scatter_dimension=1, tiled=True)  21.6 us
    all_to_all x1, blocking collectives, shards(): lax.all_to_all(outgoing, 'req', split_axis=0, concat_axis=0, tiled=True)  12.7 us
    all_to_all x1, waiting for transfers between devices, shards(): lax.all_to_all(computed, 'req', split_axis=0, concat_axis=0, tiled=True)  7.59 us
    psum x1, blocking collectives, shards(): lax.psum((jnp.sum(attended_f * attended_f, axis=1), jnp.dot(scaled, w_rou...  5.99 us
    all_to_all x1, starting transfers between devices, shards(): lax.all_to_all(computed, 'req', split_axis=0, concat_axis=0, tiled=True)  5.52 us
    unnamed x23, local copies, waits for them, and re-layouts  4.04 us
  transfers between devices with their start and end apart: 3, of which 3 were waited for; matrix products, arithmetic and copies ran while one was open for 1% of the time, Pallas kernels for 0%

commit v1 on v0

--- a/solution.py
+++ b/solution.py
@@ -49,6 +49,37 @@
         + self_weight.astype(jnp.float32)[..., None] * value_self
     )
     return mixed.astype(jnp.bfloat16).reshape(row_count, kv_local * group_size * HEAD_DIM)
+
+
+def exchange(blocks, axis):
+    count = lax.axis_size(axis)
+    return [
+        lax.ppermute(block, axis, [(i, (i + shift) % count) for i in range(count)])
+        for shift, block in enumerate(blocks, 1)
+    ]
+
+
+def blocks_by_shift(array, axis, dim):
+    count = lax.axis_size(axis)
+    index = lax.axis_index(axis)
+    size = array.shape[dim] // count
+    blocks = [
+        lax.dynamic_slice_in_dim(array, ((index + shift) % count) * size, size, axis=dim)
+        for shift in range(count)
+    ]
+    return blocks[0], blocks[1:]
+
+
+def all_to_all(array, axis):
+    count = lax.axis_size(axis)
+    if count > 8:
+        return lax.all_to_all(array, axis, split_axis=0, concat_axis=0, tiled=True)
+    index = lax.axis_index(axis)
+    own_block, sent_blocks = blocks_by_shift(array, axis, 0)
+    result = jnp.zeros_like(array)
+    for shift, piece in enumerate([own_block] + exchange(sent_blocks, axis)):
+        result = lax.dynamic_update_slice_in_dim(result, piece, (index - shift) % count, axis=0)
+    return result
 
 
 def shards(
@@ -74,25 +105,15 @@
     shard_count = max(1, req_count // EXPERTS)
     attention = attend_local(queries, new_keys, new_values, k_cache, v_cache, lengths)
     partial_value = jnp.dot(attention, w_out, preferred_element_type=jnp.float32)
-    projected = lax.psum_scatter(partial_value, "tp", scatter_dimension=1, tiled=True)
+    tp_count = lax.axis_size("tp")
+    tp_index = lax.axis_index("tp")
+    own_block, sent_blocks = blocks_by_shift(partial_value, "tp", 1)
+    projected = own_block
+    for block in exchange(sent_blocks, "tp"):
+        projected = projected + block
     attended = (resid.astype(jnp.float32) + projected).astype(jnp.bfloat16)
     attended_f = attended.astype(jnp.float32)
-    scaled = attended_f * norm_gain[None, :]
-    square_sum, logit_part = lax.psum(
-        (
-            jnp.sum(attended_f * attended_f, axis=1),
-            jnp.dot(scaled, w_router, precision=lax.Precision.HIGHEST),
-        ),
-        "tp",
-    )
-    inv_rms = 1.0 / jnp.sqrt(square_sum / D + 1e-06)
-    normed = (scaled * inv_rms[:, None]).astype(jnp.bfloat16)
-    logits = logit_part * inv_rms[:, None]
     expert_ids = jnp.arange(EXPERTS, dtype=jnp.int32)
-    first_logit = jnp.sum(jnp.where(routes[:, 0:1] == expert_ids[None, :], logits, 0.0), axis=1)
-    second_logit = jnp.sum(jnp.where(routes[:, 1:2] == expert_ids[None, :], logits, 0.0), axis=1)
-    first_weight = jax.nn.sigmoid(first_logit - second_logit)
-    second_weight = 1.0 - first_weight
     flat_routes = routes.reshape(req_dev * TOP)
     one_hot = (flat_routes[None, :] == expert_ids[:, None]).astype(jnp.int32)
     rank_in = jnp.cumsum(one_hot, axis=1) - one_hot
@@ -102,18 +123,53 @@
         chosen.reshape(EXPERTS, CAP, req_dev, TOP).astype(jnp.int32), axis=-1
     ).astype(jnp.bfloat16)
     per_expert = jnp.einsum(
-        "ecb,bd->ecd", token_pick, normed, preferred_element_type=jnp.float32
+        "ecb,bd->ecd", token_pick, attended, preferred_element_type=jnp.float32
     ).astype(jnp.bfloat16)
     outgoing = jnp.broadcast_to(
         per_expert[:, None], (EXPERTS, shard_count, CAP, width_local)
     ).reshape(req_count, slot_dev, CAP, width_local)
-    incoming = lax.all_to_all(outgoing, "req", split_axis=0, concat_axis=0, tiled=True)
-    gate_pre = jnp.einsum("nscd,sdf->nscf", incoming, w_gate, preferred_element_type=jnp.float32)
-    up_pre = jnp.einsum("nscd,sdf->nscf", incoming, w_up, preferred_element_type=jnp.float32)
-    gate_sum, up_sum = lax.psum((gate_pre, up_pre), "tp")
-    hidden = (jax.nn.silu(gate_sum) * up_sum).astype(jnp.bfloat16)
+    incoming = all_to_all(outgoing, "req")
+    scaled = attended_f * norm_gain[None, :]
+    logit_part = jnp.dot(scaled, w_router, precision=lax.Precision.HIGHEST)
+    square_part = jnp.sum(attended_f * attended_f, axis=1, keepdims=True)
+    stats_part = jnp.concatenate([logit_part, square_part], axis=1)
+    stats = stats_part
+    for other in exchange([stats_part] * (tp_count - 1), "tp"):
+        stats = stats + other
+    inv_rms = 1.0 / jnp.sqrt(stats[:, EXPERTS] / D + 1e-06)
+    logits = stats[:, :EXPERTS] * inv_rms[:, None]
+    first_logit = jnp.sum(jnp.where(routes[:, 0:1] == expert_ids[None, :], logits, 0.0), axis=1)
+    second_logit = jnp.sum(jnp.where(routes[:, 1:2] == expert_ids[None, :], logits, 0.0), axis=1)
+    first_weight = jax.nn.sigmoid(first_logit - second_logit)
+    second_weight = 1.0 - first_weight
+    incoming_f = incoming.astype(jnp.float32)
+    rows = (incoming_f * norm_gain).astype(jnp.bfloat16)
+    row_square = jnp.sum(incoming_f * incoming_f, axis=-1, keepdims=True)
+    gate_pre = jnp.einsum("nscd,sdf->nscf", rows, w_gate, preferred_element_type=jnp.float32)
+    up_pre = jnp.einsum("nscd,sdf->nscf", rows, w_up, preferred_element_type=jnp.float32)
+    square_high = row_square.astype(jnp.bfloat16)
+    square_low = (row_square - square_high.astype(jnp.float32)).astype(jnp.bfloat16)
+    pre = jnp.concatenate(
+        [gate_pre.astype(jnp.bfloat16), up_pre.astype(jnp.bfloat16), square_high, square_low], axis=-1
+    )
+    own_block, sent_blocks = blocks_by_shift(pre, "tp", 0)
+    sums = own_block.astype(jnp.float32)
+    for block in exchange(sent_blocks, "tp"):
+        sums = sums + block.astype(jnp.float32)
+    width = w_gate.shape[2]
+    row_inv = 1.0 / jnp.sqrt((sums[..., 2 * width :].sum(axis=-1, keepdims=True)) / D + 1e-06)
+    hidden_part = (
+        jax.nn.silu(sums[..., :width] * row_inv) * (sums[..., width : 2 * width] * row_inv)
+    ).astype(jnp.bfloat16)
+    hidden = jnp.zeros((req_count, slot_dev, CAP, width), jnp.bfloat16)
+    step = req_count // tp_count
+    pieces = [hidden_part] + exchange([hidden_part] * (tp_count - 1), "tp")
+    for shift, piece in enumerate(pieces):
+        hidden = lax.dynamic_update_slice_in_dim(
+            hidden, piece, ((tp_index - shift) % tp_count) * step, axis=0
+        )
     computed = jnp.einsum("nscf,sfd->nscd", hidden, w_down, preferred_element_type=jnp.float32)
-    returned = lax.all_to_all(computed, "req", split_axis=0, concat_axis=0, tiled=True)
+    returned = all_to_all(computed, "req")
     combined = jnp.sum(returned.reshape(EXPERTS, shard_count, CAP, width_local), axis=1)
     route_out = jnp.einsum(
         "ecr,ecd->rd", chosen.astype(jnp.float32), combined, precision=lax.Precision.HIGHEST

time: 121 us -> 68.7 us (0.57)
  waiting for transfers between devices: 62.9 us -> 12.4 us
  starting transfers between devices: 5.6 us -> 35.4 us
  blocking collectives: 18.7 us -> 0 us
  between operations: 14.3 us -> 1.62 us
  matrix products: 8.93 us -> 6.23 us
  local copies, waits for them, and re-layouts: 6.4 us -> 8.93 us
    ppermute x0 -> x26, starting transfers between devices: none -> 35.4 us  [exchange(): lax.ppermute(block, axis, [(i, (i + shift) % count) for i in range(count)])]
    psum x1 -> x0, waiting for transfers between devices: 33.7 us -> none  [shards(): gate_sum, up_sum = lax.psum((gate_pre, up_pre), 'tp')]
    reduce_scatter x1 -> x0, waiting for transfers between devices: 21.6 us -> none  [shards(): lax.psum_scatter(partial_value, 'tp', scatter_dimension=1, tiled=True)]
    all_to_all x1 -> x0, blocking collectives: 12.7 us -> none  [shards(): lax.all_to_all(outgoing, 'req', split_axis=0, concat_axis=0, tiled=True)]
    ppermute x0 -> x26, waiting for transfers between devices: none -> 12.4 us  [exchange(): lax.ppermute(block, axis, [(i, (i + shift) % count) for i in range(count)])]
    all_to_all x1 -> x0, waiting for transfers between devices: 7.59 us -> none  [shards(): lax.all_to_all(computed, 'req', split_axis=0, concat_axis=0, tiled=True)]
    psum x1 -> x0, blocking collectives: 5.99 us -> none  [shards(): lax.psum((jnp.sum(attended_f * attended_f, axis=1), jnp.dot(scaled, w_rou...]
    all_to_all x1 -> x0, starting transfers between devices: 5.52 us -> none  [shards(): lax.all_to_all(computed, 'req', split_axis=0, concat_axis=0, tiled=True)]
  transfers between devices with their start and end apart: 3 -> 26, of which waited for: 3 -> 9; matrix products, arithmetic and copies ran while one was open for 1% -> 3% of each run, Pallas kernels for 0% -> 0%
where the time goes in v1:
time: 68.7 us; the launch traced here: 68.4 us
  starting transfers between devices  35.4 us (52%)
  waiting for transfers between devices  12.4 us (18%)
  local copies, waits for them, and re-layouts  8.93 us (13%)
  matrix products  6.23 us (9%)
  other arithmetic  3.87 us (6%)
  between operations  1.62 us (2%)
    ppermute x26, starting transfers between devices, exchange(): lax.ppermute(block, axis, [(i, (i + shift) % count) for i in range(count)])  35.4 us
    ppermute x26, waiting for transfers between devices, exchange(): lax.ppermute(block, axis, [(i, (i + shift) % count) for i in range(count)])  12.4 us
    unnamed x26, local copies, waits for them, and re-layouts  4.06 us
    dot_general x1, matrix products, attend_local(): jnp.einsum('bgql,blgd->bgqd', weights, values_all, preferred_element_type...  2.03 us
  transfers between devices with their start and end apart: 26, of which 9 were waited for; matrix products, arithmetic and copies ran while one was open for 3% of the time, Pallas kernels for 0%

profile of v1, /device:TPU:0, one launch (start us, length us, event | category | flops | bytes accessed | tf_op | source)
XLA Modules:
  0.0 68.4 jit_solution(15654194251582112846)
XLA Ops:
  2.4 1.6 %copy.85 = bf16[32,128,128]{1,2,0:T(8,128)(2,1)S(1)} copy(bf16[32,128,128]{2,1,0:T(8,128)(2,1)} %param.18) | data formatting | bytes 2097152 | tf_op args[4]
  5.2 2.3 %copy.86 = bf16[32,128,128]{1,2,0:T(8,128)(2,1)} copy(bf16[32,128,128]{2,1,0:T(8,128)(2,1)} %param.19) | data formatting | bytes 2097152 | tf_op args[5]
  7.6 2.0 %fusion.18 = bf16[32,2,3,64]{3,2,1,0:T(4,128)(2,1)S(1)} fusion(bf16[32,128,2,64]{1,3,2,0:T(8,128)(2,1)} %bitcast.118, f32[32,2,3,128]{3,2,1,0:T(4,128)S(1)} %get-tuple-element.38, f32[32,2,64]{2,1,0:T(2,128)S(1)} %reshape.204, f32[32,2,3]{2,1,0:T(2,128)S(1)} %get-tuple-element.34, f32[32,2,3]{2,1,0:T(2,128)S(1)} %get-tuple-element.33, ...), kind=kOutput, calls=%fused_computation.13 | convolution fusion | flops 3280896 | bytes 1194240 | tf_op jit(solution)/shard_map/bgql,blgd->bgqd/dot_general | solution.py:48
  11.2 2.5 %collective-permute-start.1 = (f32[32,384]{1,0:T(8,128)S(1)}, f32[32,384]{1,0:T(8,128)}, u32[]{:S(2)}, u32[]{:S(2)}) collective-permute-start(f32[32,384]{1,0:T(8,128)S(1)} %get-tuple-element.25), channel_id=1, source_target_pairs={{0,2},{1,3},{2,0},{3,1},{4,6},{5,7},{6,4},{7,5},{8,10},{9,11},{10,... | collective-permute-start | bytes 147464 | tf_op jit(solution)/shard_map/ppermute | solution.py:57
  13.7 1.4 %collective-permute-start.2 = (f32[32,384]{1,0:T(8,128)S(1)}, f32[32,384]{1,0:T(8,128)}, u32[]{:S(2)}, u32[]{:S(2)}) collective-permute-start(f32[32,384]{1,0:T(8,128)S(1)} %get-tuple-element.24), channel_id=1, source_target_pairs={{0,3},{1,0},{2,1},{3,2},{4,7},{5,4},{6,5},{7,6},{8,11},{9,8},{10,9... | collective-permute-start | bytes 147464 | tf_op jit(solution)/shard_map/ppermute | solution.py:57
  17.2 1.1 %fusion.36 = (f32[32]{0:T(128)S(1)}, bf16[32,384]{1,0:T(8,128)(2,1)S(1)}) fusion(f32[32,384]{1,0:T(8,128)} %collective-permute-done.2, f32[32,384]{1,0:T(8,128)} %collective-permute-done.1, f32[32,384]{1,0:T(8,128)} %collective-permute-done, f32[32,1536]{1,0:T(8,128)S(1)} %fusion.57, s32[]{:T(128)S(6)} %select_n.248, bf16[32,384]{1,0:T(8,128)(2,1)} %param.14), kind=kLoop, calls=%fused_computation.44 | loop fusion | flops 110560 | bytes 245892 | tf_op jit(solution)/shard_map/reduce_sum | solution.py:134
  19.4 1.7 %collective-permute-start.4 = (f32[32,17]{0,1:T(8,128)S(1)}, f32[32,17]{0,1:T(8,128)S(1)}, u32[]{:S(2)}, u32[]{:S(2)}) collective-permute-start(f32[32,17]{0,1:T(8,128)S(1)} %pad_maximum_fusion), channel_id=1, source_target_pairs={{0,2},{1,3},{2,0},{3,1},{4,6},{5,7},{6,4},{7,5},{8,10},{9,11},{10,... | collective-permute-start | bytes 6536 | tf_op jit(solution)/shard_map/ppermute | solution.py:57
  21.9 1.6 %collective-permute-start.6 = (bf16[1,2,8,384]{3,2,0,1:T(8,128)(2,1)S(1)}, bf16[1,2,8,384]{3,2,0,1:T(8,128)(2,1)S(1)}, u32[]{:S(2)}, u32[]{:S(2)}) collective-permute-start(bf16[1,2,8,384]{3,2,0,1:T(8,128)(2,1)S(1)} %get-tuple-element.32), channel_id=1, source_target_pairs={{0,4},{4,8},{8,12},{12,16},{16,20},{20,24},{24,28},{28,0},{1,5},{5... | collective-permute-start | bytes 36872 | tf_op jit(solution)/shard_map/ppermute | solution.py:57
  23.5 1.6 %collective-permute-start.7 = (bf16[1,2,8,384]{3,2,0,1:T(8,128)(2,1)S(1)}, bf16[1,2,8,384]{3,2,0,1:T(8,128)(2,1)S(1)}, u32[]{:S(2)}, u32[]{:S(2)}) collective-permute-start(bf16[1,2,8,384]{3,2,0,1:T(8,128)(2,1)S(1)} %get-tuple-element.31), channel_id=1, source_target_pairs={{0,8},{4,12},{8,16},{12,20},{16,24},{20,28},{24,0},{28,4},{1,9},{5... | collective-permute-start | bytes 36872 | tf_op jit(solution)/shard_map/ppermute | solution.py:57
  25.1 2.6 %collective-permute-start.8 = (bf16[1,2,8,384]{3,2,0,1:T(8,128)(2,1)S(1)}, bf16[1,2,8,384]{3,2,0,1:T(8,128)(2,1)S(1)}, u32[]{:S(2)}, u32[]{:S(2)}) collective-permute-start(bf16[1,2,8,384]{3,2,0,1:T(8,128)(2,1)S(1)} %get-tuple-element.30), channel_id=1, source_target_pairs={{0,12},{4,16},{8,20},{12,24},{16,28},{20,0},{24,4},{28,8},{1,13},{... | collective-permute-start | bytes 36872 | tf_op jit(solution)/shard_map/ppermute | solution.py:57
  27.7 1.2 %collective-permute-start.9 = (bf16[1,2,8,384]{3,2,0,1:T(8,128)(2,1)S(1)}, bf16[1,2,8,384]{3,2,0,1:T(8,128)(2,1)S(1)}, u32[]{:S(2)}, u32[]{:S(2)}) collective-permute-start(bf16[1,2,8,384]{3,2,0,1:T(8,128)(2,1)S(1)} %get-tuple-element.29), channel_id=1, source_target_pairs={{0,16},{4,20},{8,24},{12,28},{16,0},{20,4},{24,8},{28,12},{1,17},{... | collective-permute-start | bytes 36872 | tf_op jit(solution)/shard_map/ppermute | solution.py:57
  29.0 2.6 %collective-permute-start.10 = (bf16[1,2,8,384]{3,2,0,1:T(8,128)(2,1)S(1)}, bf16[1,2,8,384]{3,2,0,1:T(8,128)(2,1)S(1)}, u32[]{:S(2)}, u32[]{:S(2)}) collective-permute-start(bf16[1,2,8,384]{3,2,0,1:T(8,128)(2,1)S(1)} %get-tuple-element.28), channel_id=1, source_target_pairs={{0,20},{4,24},{8,28},{12,0},{16,4},{20,8},{24,12},{28,16},{1,21},{... | collective-permute-start | bytes 36872 | tf_op jit(solution)/shard_map/ppermute | solution.py:57
  31.6 1.4 %collective-permute-start.11 = (bf16[1,2,8,384]{3,2,0,1:T(8,128)(2,1)S(1)}, bf16[1,2,8,384]{3,2,0,1:T(8,128)(2,1)S(1)}, u32[]{:S(2)}, u32[]{:S(2)}) collective-permute-start(bf16[1,2,8,384]{3,2,0,1:T(8,128)(2,1)S(1)} %get-tuple-element.27), channel_id=1, source_target_pairs={{0,24},{4,28},{8,0},{12,4},{16,8},{20,12},{24,16},{28,20},{1,25},{... | collective-permute-start | bytes 36872 | tf_op jit(solution)/shard_map/ppermute | solution.py:57
  33.0 1.5 %collective-permute-start.12 = (bf16[1,2,8,384]{3,2,0,1:T(8,128)(2,1)S(1)}, bf16[1,2,8,384]{3,2,0,1:T(8,128)(2,1)S(1)}, u32[]{:S(2)}, u32[]{:S(2)}) collective-permute-start(bf16[1,2,8,384]{3,2,0,1:T(8,128)(2,1)S(1)} %get-tuple-element.26), channel_id=1, source_target_pairs={{0,28},{4,0},{8,4},{12,8},{16,12},{20,16},{24,20},{28,24},{1,29},{... | collective-permute-start | bytes 36872 | tf_op jit(solution)/shard_map/ppermute | solution.py:57
  35.4 1.4 %collective-permute-done.12 = bf16[1,2,8,384]{3,2,0,1:T(8,128)(2,1)S(1)} collective-permute-done((bf16[1,2,8,384]{3,2,0,1:T(8,128)(2,1)S(1)}, bf16[1,2,8,384]{3,2,0,1:T(8,128)(2,1)S(1)}, u32[]{:S(2)}, u32[]{:S(2)}) %collective-permute-start.12) | collective-permute-done | bytes 12320 | tf_op jit(solution)/shard_map/ppermute | solution.py:57
  37.3 1.1 %fusion.15 = bf16[8,2,8,1024]{3,2,0,1:T(8,128)(2,1)} fusion(bf16[2,384,1024]{2,1,0:T(8,128)(2,1)S(1)} %copy-done.1, bf16[8,2,8,384]{3,2,0,1:T(8,128)(2,1)S(1)} %constant_dynamic-update-slice_fusion.4, f32[384]{0:T(512)S(1)} %copy-done.5), kind=kOutput, calls=%fused_computation.9 | convolution fusion | flops 100941824 | bytes 1934848 | tf_op jit(solution)/shard_map/nscd,sdf->nscf/dot_general | solution.py:148
  38.8 1.1 %concatenate.7 = bf16[8,2,8,2050]{3,2,0,1:T(8,128)(2,1)S(1)} concatenate(bf16[8,2,8,1024]{3,2,0,1:T(8,128)(2,1)} %fusion.15, bf16[8,2,8,1024]{3,2,0,1:T(8,128)(2,1)S(1)} %fusion.12, bf16[8,2,8,1]{3,2,0,1:T(8,128)(2,1)S(1)} %copy.102, bf16[8,2,8,1]{3,2,0,1:T(8,128)(2,1)S(1)} %copy.103), dimensions={3} | concatenate | bytes 1049600 | tf_op jit(solution)/shard_map/concatenate | solution.py:152
  40.1 1.1 %collective-permute-start.14 = (bf16[2,2,8,2050]{3,2,0,1:T(8,128)(2,1)S(1)}, bf16[2,2,8,2050]{3,2,0,1:T(8,128)(2,1)S(1)}, u32[]{:S(2)}, u32[]{:S(2)}) collective-permute-start(bf16[2,2,8,2050]{3,2,0,1:T(8,128)(2,1)S(1)} %get-tuple-element.14), channel_id=1, source_target_pairs={{0,2},{1,3},{2,0},{3,1},{4,6},{5,7},{6,4},{7,5},{8,10},{9,11},{10,... | collective-permute-start | bytes 393608 | tf_op jit(solution)/shard_map/ppermute | solution.py:57
  41.1 1.4 %collective-permute-start.15 = (bf16[2,2,8,2050]{3,2,0,1:T(8,128)(2,1)S(1)}, bf16[2,2,8,2050]{3,2,0,1:T(8,128)(2,1)S(1)}, u32[]{:S(2)}, u32[]{:S(2)}) collective-permute-start(bf16[2,2,8,2050]{3,2,0,1:T(8,128)(2,1)S(1)} %get-tuple-element.13), channel_id=1, source_target_pairs={{0,3},{1,0},{2,1},{3,2},{4,7},{5,4},{6,5},{7,6},{8,11},{9,8},{10,9... | collective-permute-start | bytes 393608 | tf_op jit(solution)/shard_map/ppermute | solution.py:57
  42.6 2.8 %collective-permute-done.13 = bf16[2,2,8,2050]{3,2,0,1:T(8,128)(2,1)S(1)} collective-permute-done((bf16[2,2,8,2050]{3,2,0,1:T(8,128)(2,1)S(1)}, bf16[2,2,8,2050]{3,2,0,1:T(8,128)(2,1)S(1)}, u32[]{:S(2)}, u32[]{:S(2)}) %collective-permute-start.13) | collective-permute-done | bytes 131232 | tf_op jit(solution)/shard_map/ppermute | solution.py:57
  45.4 1.2 %collective-permute-done.14 = bf16[2,2,8,2050]{3,2,0,1:T(8,128)(2,1)S(1)} collective-permute-done((bf16[2,2,8,2050]{3,2,0,1:T(8,128)(2,1)S(1)}, bf16[2,2,8,2050]{3,2,0,1:T(8,128)(2,1)S(1)}, u32[]{:S(2)}, u32[]{:S(2)}) %collective-permute-start.14) | collective-permute-done | bytes 131232 | tf_op jit(solution)/shard_map/ppermute | solution.py:57
  46.6 0.9 %collective-permute-done.15 = bf16[2,2,8,2050]{3,2,0,1:T(8,128)(2,1)S(1)} collective-permute-done((bf16[2,2,8,2050]{3,2,0,1:T(8,128)(2,1)S(1)}, bf16[2,2,8,2050]{3,2,0,1:T(8,128)(2,1)S(1)}, u32[]{:S(2)}, u32[]{:S(2)}) %collective-permute-start.15) | collective-permute-done | bytes 131232 | tf_op jit(solution)/shard_map/ppermute | solution.py:57
  47.9 1.3 %collective-permute-start.16 = (bf16[2,2,8,1024]{3,2,0,1:T(8,128)(2,1)S(1)}, bf16[2,2,8,1024]{3,2,0,1:T(8,128)(2,1)S(1)}, u32[]{:S(2)}, u32[]{:S(2)}) collective-permute-start(bf16[2,2,8,1024]{3,2,0,1:T(8,128)(2,1)S(1)} %get-tuple-element.9), channel_id=1, source_target_pairs={{0,1},{1,2},{2,3},{3,0},{4,5},{5,6},{6,7},{7,4},{8,9},{9,10},{10,1... | collective-permute-start | bytes 196616 | tf_op jit(solution)/shard_map/ppermute | solution.py:57
  49.2 1.0 %collective-permute-start.17 = (bf16[2,2,8,1024]{3,2,0,1:T(8,128)(2,1)S(1)}, bf16[2,2,8,1024]{3,2,0,1:T(8,128)(2,1)S(1)}, u32[]{:S(2)}, u32[]{:S(2)}) collective-permute-start(bf16[2,2,8,1024]{3,2,0,1:T(8,128)(2,1)S(1)} %get-tuple-element.9), channel_id=1, source_target_pairs={{0,2},{1,3},{2,0},{3,1},{4,6},{5,7},{6,4},{7,5},{8,10},{9,11},{10,... | collective-permute-start | bytes 196616 | tf_op jit(solution)/shard_map/ppermute | solution.py:57
  50.6 1.1 %collective-permute-done.16 = bf16[2,2,8,1024]{3,2,0,1:T(8,128)(2,1)S(1)} collective-permute-done((bf16[2,2,8,1024]{3,2,0,1:T(8,128)(2,1)S(1)}, bf16[2,2,8,1024]{3,2,0,1:T(8,128)(2,1)S(1)}, u32[]{:S(2)}, u32[]{:S(2)}) %collective-permute-start.16) | collective-permute-done | bytes 65568 | tf_op jit(solution)/shard_map/ppermute | solution.py:57
  51.8 1.7 %collective-permute-done.17 = bf16[2,2,8,1024]{3,2,0,1:T(8,128)(2,1)S(1)} collective-permute-done((bf16[2,2,8,1024]{3,2,0,1:T(8,128)(2,1)S(1)}, bf16[2,2,8,1024]{3,2,0,1:T(8,128)(2,1)S(1)}, u32[]{:S(2)}, u32[]{:S(2)}) %collective-permute-start.17) | collective-permute-done | bytes 65568 | tf_op jit(solution)/shard_map/ppermute | solution.py:57
  53.9 1.6 %collective-permute-start.19 = (f32[1,2,8,384]{3,2,1,0:T(8,128)S(1)}, f32[1,2,8,384]{3,2,1,0:T(8,128)S(1)}, u32[]{:S(2)}, u32[]{:S(2)}) collective-permute-start(f32[1,2,8,384]{3,2,1,0:T(8,128)S(1)} %get-tuple-element.21), channel_id=1, source_target_pairs={{0,4},{4,8},{8,12},{12,16},{16,20},{20,24},{24,28},{28,0},{1,5},{5... | collective-permute-start | bytes 73736 | tf_op jit(solution)/shard_map/ppermute | solution.py:57
  55.7 2.1 %collective-permute-start.21 = (f32[1,2,8,384]{3,2,1,0:T(8,128)S(1)}, f32[1,2,8,384]{3,2,1,0:T(8,128)S(1)}, u32[]{:S(2)}, u32[]{:S(2)}) collective-permute-start(f32[1,2,8,384]{3,2,1,0:T(8,128)S(1)} %get-tuple-element.19), channel_id=1, source_target_pairs={{0,12},{4,16},{8,20},{12,24},{16,28},{20,0},{24,4},{28,8},{1,13},{... | collective-permute-start | bytes 73736 | tf_op jit(solution)/shard_map/ppermute | solution.py:57
  57.8 2.2 %collective-permute-start.22 = (f32[1,2,8,384]{3,2,1,0:T(8,128)S(1)}, f32[1,2,8,384]{3,2,1,0:T(8,128)S(1)}, u32[]{:S(2)}, u32[]{:S(2)}) collective-permute-start(f32[1,2,8,384]{3,2,1,0:T(8,128)S(1)} %get-tuple-element.18), channel_id=1, source_target_pairs={{0,16},{4,20},{8,24},{12,28},{16,0},{20,4},{24,8},{28,12},{1,17},{... | collective-permute-start | bytes 73736 | tf_op jit(solution)/shard_map/ppermute | solution.py:57
  59.9 3.1 %collective-permute-start.23 = (f32[1,2,8,384]{3,2,1,0:T(8,128)S(1)}, f32[1,2,8,384]{3,2,1,0:T(8,128)S(1)}, u32[]{:S(2)}, u32[]{:S(2)}) collective-permute-start(f32[1,2,8,384]{3,2,1,0:T(8,128)S(1)} %get-tuple-element.17), channel_id=1, source_target_pairs={{0,20},{4,24},{8,28},{12,0},{16,4},{20,8},{24,12},{28,16},{1,21},{... | collective-permute-start | bytes 73736 | tf_op jit(solution)/shard_map/ppermute | solution.py:57
  63.4 1.4 %collective-permute-start.25 = (f32[1,2,8,384]{3,2,1,0:T(8,128)S(1)}, f32[1,2,8,384]{3,2,1,0:T(8,128)S(1)}, u32[]{:S(2)}, u32[]{:S(2)}) collective-permute-start(f32[1,2,8,384]{3,2,1,0:T(8,128)S(1)} %get-tuple-element.15), channel_id=1, source_target_pairs={{0,28},{4,0},{8,4},{12,8},{16,12},{20,16},{24,20},{28,24},{1,29},{... | collective-permute-start | bytes 73736 | tf_op jit(solution)/shard_map/ppermute | solution.py:57
  64.9 2.1 %collective-permute-done.24 = f32[1,2,8,384]{3,2,1,0:T(8,128)S(1)} collective-permute-done((f32[1,2,8,384]{3,2,1,0:T(8,128)S(1)}, f32[1,2,8,384]{3,2,1,0:T(8,128)S(1)}, u32[]{:S(2)}, u32[]{:S(2)}) %collective-permute-start.24) | collective-permute-done | bytes 24608 | tf_op jit(solution)/shard_map/ppermute | solution.py:57
  (120 shorter events, 13.0 us)
Async XLA Ops:
  0.6 36.3 %copy-start = (bf16[2,384,1024]{2,1,0:T(8,128)(2,1)S(1)}, bf16[2,384,1024]{2,1,0:T(8,128)(2,1)}, u32[]{:S(2)}) copy-start(bf16[2,384,1024]{2,1,0:T(8,128)(2,1)} %param.26) | copy-start | bytes 4718596
  9.6 5.5 %copy-start.6 = (s32[32,2]{0,1:T(2,128)S(1)}, s32[32,2]{0,1:T(2,128)}, u32[]{:S(2)}) copy-start(s32[32,2]{0,1:T(2,128)} %param.24) | copy-start | bytes 772
  9.6 8.7 %copy-start.5 = (f32[384]{0:T(512)S(1)}, f32[384]{0:T(512)}, u32[]{:S(2)}) copy-start(f32[384]{0:T(512)} %param.22) | copy-start | bytes 4612
  10.7 6.5 %collective-permute-start = (f32[32,384]{1,0:T(8,128)}, f32[32,384]{1,0:T(8,128)}, u32[]{:S(2)}, u32[]{:S(2)}) collective-permute-start(f32[32,384]{1,0:T(8,128)} %get-tuple-element.23), channel_id=1, source_target_pairs={{0,1},{1,2},{2,3},{3,0},{4,5},{5,6},{6,7},{7,4},{8,9},{9,10},{10,1... | collective-permute-start | bytes 147464 | tf_op jit(solution)/shard_map/ppermute | solution.py:57
  11.2 6.0 %collective-permute-start.1 = (f32[32,384]{1,0:T(8,128)S(1)}, f32[32,384]{1,0:T(8,128)}, u32[]{:S(2)}, u32[]{:S(2)}) collective-permute-start(f32[32,384]{1,0:T(8,128)S(1)} %get-tuple-element.25), channel_id=1, source_target_pairs={{0,2},{1,3},{2,0},{3,1},{4,6},{5,7},{6,4},{7,5},{8,10},{9,11},{10,... | collective-permute-start | bytes 147464 | tf_op jit(solution)/shard_map/ppermute | solution.py:57
  13.7 3.5 %collective-permute-start.2 = (f32[32,384]{1,0:T(8,128)S(1)}, f32[32,384]{1,0:T(8,128)}, u32[]{:S(2)}, u32[]{:S(2)}) collective-permute-start(f32[32,384]{1,0:T(8,128)S(1)} %get-tuple-element.24), channel_id=1, source_target_pairs={{0,3},{1,0},{2,1},{3,2},{4,7},{5,4},{6,5},{7,6},{8,11},{9,8},{10,9... | collective-permute-start | bytes 147464 | tf_op jit(solution)/shard_map/ppermute | solution.py:57
  17.1 20.2 %copy-start.1 = (bf16[2,384,1024]{2,1,0:T(8,128)(2,1)S(1)}, bf16[2,384,1024]{2,1,0:T(8,128)(2,1)}, u32[]{:S(2)}) copy-start(bf16[2,384,1024]{2,1,0:T(8,128)(2,1)} %param.25) | copy-start | bytes 4718596
  18.3 49.4 %copy-start.4 = (bf16[32,384]{1,0:T(8,128)(2,1)}, bf16[32,384]{1,0:T(8,128)(2,1)S(1)}, u32[]{:S(2)}) copy-start(bf16[32,384]{1,0:T(8,128)(2,1)S(1)} %get-tuple-element.7) | copy-start | bytes 73732
  19.2 5.9 %collective-permute-start.3 = (f32[32,17]{0,1:T(8,128)S(1)}, f32[32,17]{0,1:T(8,128)S(1)}, u32[]{:S(2)}, u32[]{:S(2)}) collective-permute-start(f32[32,17]{0,1:T(8,128)S(1)} %pad_maximum_fusion), channel_id=1, source_target_pairs={{0,1},{1,2},{2,3},{3,0},{4,5},{5,6},{6,7},{7,4},{8,9},{9,10},{10,1... | collective-permute-start | bytes 6536 | tf_op jit(solution)/shard_map/ppermute | solution.py:57
  19.4 8.3 %collective-permute-start.4 = (f32[32,17]{0,1:T(8,128)S(1)}, f32[32,17]{0,1:T(8,128)S(1)}, u32[]{:S(2)}, u32[]{:S(2)}) collective-permute-start(f32[32,17]{0,1:T(8,128)S(1)} %pad_maximum_fusion), channel_id=1, source_target_pairs={{0,2},{1,3},{2,0},{3,1},{4,6},{5,7},{6,4},{7,5},{8,10},{9,11},{10,... | collective-permute-start | bytes 6536 | tf_op jit(solution)/shard_map/ppermute | solution.py:57
  21.1 7.9 %collective-permute-start.5 = (f32[32,17]{0,1:T(8,128)S(1)}, f32[32,17]{0,1:T(8,128)S(1)}, u32[]{:S(2)}, u32[]{:S(2)}) collective-permute-start(f32[32,17]{0,1:T(8,128)S(1)} %pad_maximum_fusion), channel_id=1, source_target_pairs={{0,3},{1,0},{2,1},{3,2},{4,7},{5,4},{6,5},{7,6},{8,11},{9,8},{10,9... | collective-permute-start | bytes 6536 | tf_op jit(solution)/shard_map/ppermute | solution.py:57
  21.9 9.7 %collective-permute-start.6 = (bf16[1,2,8,384]{3,2,0,1:T(8,128)(2,1)S(1)}, bf16[1,2,8,384]{3,2,0,1:T(8,128)(2,1)S(1)}, u32[]{:S(2)}, u32[]{:S(2)}) collective-permute-start(bf16[1,2,8,384]{3,2,0,1:T(8,128)(2,1)S(1)} %get-tuple-element.32), channel_id=1, source_target_pairs={{0,4},{4,8},{8,12},{12,16},{16,20},{20,24},{24,28},{28,0},{1,5},{5... | collective-permute-start | bytes 36872 | tf_op jit(solution)/shard_map/ppermute | solution.py:57
  23.5 9.5 %collective-permute-start.7 = (bf16[1,2,8,384]{3,2,0,1:T(8,128)(2,1)S(1)}, bf16[1,2,8,384]{3,2,0,1:T(8,128)(2,1)S(1)}, u32[]{:S(2)}, u32[]{:S(2)}) collective-permute-start(bf16[1,2,8,384]{3,2,0,1:T(8,128)(2,1)S(1)} %get-tuple-element.31), channel_id=1, source_target_pairs={{0,8},{4,12},{8,16},{12,20},{16,24},{20,28},{24,0},{28,4},{1,9},{5... | collective-permute-start | bytes 36872 | tf_op jit(solution)/shard_map/ppermute | solution.py:57
  25.1 9.4 %collective-permute-start.8 = (bf16[1,2,8,384]{3,2,0,1:T(8,128)(2,1)S(1)}, bf16[1,2,8,384]{3,2,0,1:T(8,128)(2,1)S(1)}, u32[]{:S(2)}, u32[]{:S(2)}) collective-permute-start(bf16[1,2,8,384]{3,2,0,1:T(8,128)(2,1)S(1)} %get-tuple-element.30), channel_id=1, source_target_pairs={{0,12},{4,16},{8,20},{12,24},{16,28},{20,0},{24,4},{28,8},{1,13},{... | collective-permute-start | bytes 36872 | tf_op jit(solution)/shard_map/ppermute | solution.py:57
  27.7 6.8 %collective-permute-start.9 = (bf16[1,2,8,384]{3,2,0,1:T(8,128)(2,1)S(1)}, bf16[1,2,8,384]{3,2,0,1:T(8,128)(2,1)S(1)}, u32[]{:S(2)}, u32[]{:S(2)}) collective-permute-start(bf16[1,2,8,384]{3,2,0,1:T(8,128)(2,1)S(1)} %get-tuple-element.29), channel_id=1, source_target_pairs={{0,16},{4,20},{8,24},{12,28},{16,0},{20,4},{24,8},{28,12},{1,17},{... | collective-permute-start | bytes 36872 | tf_op jit(solution)/shard_map/ppermute | solution.py:57
  29.0 5.6 %collective-permute-start.10 = (bf16[1,2,8,384]{3,2,0,1:T(8,128)(2,1)S(1)}, bf16[1,2,8,384]{3,2,0,1:T(8,128)(2,1)S(1)}, u32[]{:S(2)}, u32[]{:S(2)}) collective-permute-start(bf16[1,2,8,384]{3,2,0,1:T(8,128)(2,1)S(1)} %get-tuple-element.28), channel_id=1, source_target_pairs={{0,20},{4,24},{8,28},{12,0},{16,4},{20,8},{24,12},{28,16},{1,21},{... | collective-permute-start | bytes 36872 | tf_op jit(solution)/shard_map/ppermute | solution.py:57
  31.6 3.7 %collective-permute-start.11 = (bf16[1,2,8,384]{3,2,0,1:T(8,128)(2,1)S(1)}, bf16[1,2,8,384]{3,2,0,1:T(8,128)(2,1)S(1)}, u32[]{:S(2)}, u32[]{:S(2)}) collective-permute-start(bf16[1,2,8,384]{3,2,0,1:T(8,128)(2,1)S(1)} %get-tuple-element.27), channel_id=1, source_target_pairs={{0,24},{4,28},{8,0},{12,4},{16,8},{20,12},{24,16},{28,20},{1,25},{... | collective-permute-start | bytes 36872 | tf_op jit(solution)/shard_map/ppermute | solution.py:57
  33.0 3.7 %collective-permute-start.12 = (bf16[1,2,8,384]{3,2,0,1:T(8,128)(2,1)S(1)}, bf16[1,2,8,384]{3,2,0,1:T(8,128)(2,1)S(1)}, u32[]{:S(2)}, u32[]{:S(2)}) collective-permute-start(bf16[1,2,8,384]{3,2,0,1:T(8,128)(2,1)S(1)} %get-tuple-element.26), channel_id=1, source_target_pairs={{0,28},{4,0},{8,4},{12,8},{16,12},{20,16},{24,20},{28,24},{1,29},{... | collective-permute-start | bytes 36872 | tf_op jit(solution)/shard_map/ppermute | solution.py:57
  39.9 13.6 %copy-start.2 = (bf16[2,1024,384]{2,1,0:T(8,128)(2,1)S(1)}, bf16[2,1024,384]{2,1,0:T(8,128)(2,1)}, u32[]{:S(2)}) copy-start(bf16[2,1024,384]{2,1,0:T(8,128)(2,1)} %param.27) | copy-start | bytes 4718596
  40.0 5.4 %collective-permute-start.13 = (bf16[2,2,8,2050]{3,2,0,1:T(8,128)(2,1)S(1)}, bf16[2,2,8,2050]{3,2,0,1:T(8,128)(2,1)S(1)}, u32[]{:S(2)}, u32[]{:S(2)}) collective-permute-start(bf16[2,2,8,2050]{3,2,0,1:T(8,128)(2,1)S(1)} %get-tuple-element.12), channel_id=1, source_target_pairs={{0,1},{1,2},{2,3},{3,0},{4,5},{5,6},{6,7},{7,4},{8,9},{9,10},{10,1... | collective-permute-start | bytes 393608 | tf_op jit(solution)/shard_map/ppermute | solution.py:57
  40.1 6.6 %collective-permute-start.14 = (bf16[2,2,8,2050]{3,2,0,1:T(8,128)(2,1)S(1)}, bf16[2,2,8,2050]{3,2,0,1:T(8,128)(2,1)S(1)}, u32[]{:S(2)}, u32[]{:S(2)}) collective-permute-start(bf16[2,2,8,2050]{3,2,0,1:T(8,128)(2,1)S(1)} %get-tuple-element.14), channel_id=1, source_target_pairs={{0,2},{1,3},{2,0},{3,1},{4,6},{5,7},{6,4},{7,5},{8,10},{9,11},{10,... | collective-permute-start | bytes 393608 | tf_op jit(solution)/shard_map/ppermute | solution.py:57
  41.1 6.4 %collective-permute-start.15 = (bf16[2,2,8,2050]{3,2,0,1:T(8,128)(2,1)S(1)}, bf16[2,2,8,2050]{3,2,0,1:T(8,128)(2,1)S(1)}, u32[]{:S(2)}, u32[]{:S(2)}) collective-permute-start(bf16[2,2,8,2050]{3,2,0,1:T(8,128)(2,1)S(1)} %get-tuple-element.13), channel_id=1, source_target_pairs={{0,3},{1,0},{2,1},{3,2},{4,7},{5,4},{6,5},{7,6},{8,11},{9,8},{10,9... | collective-permute-start | bytes 393608 | tf_op jit(solution)/shard_map/ppermute | solution.py:57
  47.9 3.9 %collective-permute-start.16 = (bf16[2,2,8,1024]{3,2,0,1:T(8,128)(2,1)S(1)}, bf16[2,2,8,1024]{3,2,0,1:T(8,128)(2,1)S(1)}, u32[]{:S(2)}, u32[]{:S(2)}) collective-permute-start(bf16[2,2,8,1024]{3,2,0,1:T(8,128)(2,1)S(1)} %get-tuple-element.9), channel_id=1, source_target_pairs={{0,1},{1,2},{2,3},{3,0},{4,5},{5,6},{6,7},{7,4},{8,9},{9,10},{10,1... | collective-permute-start | bytes 196616 | tf_op jit(solution)/shard_map/ppermute | solution.py:57
  49.2 4.3 %collective-permute-start.17 = (bf16[2,2,8,1024]{3,2,0,1:T(8,128)(2,1)S(1)}, bf16[2,2,8,1024]{3,2,0,1:T(8,128)(2,1)S(1)}, u32[]{:S(2)}, u32[]{:S(2)}) collective-permute-start(bf16[2,2,8,1024]{3,2,0,1:T(8,128)(2,1)S(1)} %get-tuple-element.9), channel_id=1, source_target_pairs={{0,2},{1,3},{2,0},{3,1},{4,6},{5,7},{6,4},{7,5},{8,10},{9,11},{10,... | collective-permute-start | bytes 196616 | tf_op jit(solution)/shard_map/ppermute | solution.py:57
  50.2 3.3 %collective-permute-start.18 = (bf16[2,2,8,1024]{3,2,0,1:T(8,128)(2,1)S(1)}, bf16[2,2,8,1024]{3,2,0,1:T(8,128)(2,1)S(1)}, u32[]{:S(2)}, u32[]{:S(2)}) collective-permute-start(bf16[2,2,8,1024]{3,2,0,1:T(8,128)(2,1)S(1)} %get-tuple-element.9), channel_id=1, source_target_pairs={{0,3},{1,0},{2,1},{3,2},{4,7},{5,4},{6,5},{7,6},{8,11},{9,8},{10,9... | collective-permute-start | bytes 196616 | tf_op jit(solution)/shard_map/ppermute | solution.py:57
  53.9 9.2 %collective-permute-start.19 = (f32[1,2,8,384]{3,2,1,0:T(8,128)S(1)}, f32[1,2,8,384]{3,2,1,0:T(8,128)S(1)}, u32[]{:S(2)}, u32[]{:S(2)}) collective-permute-start(f32[1,2,8,384]{3,2,1,0:T(8,128)S(1)} %get-tuple-element.21), channel_id=1, source_target_pairs={{0,4},{4,8},{8,12},{12,16},{16,20},{20,24},{24,28},{28,0},{1,5},{5... | collective-permute-start | bytes 73736 | tf_op jit(solution)/shard_map/ppermute | solution.py:57
  55.5 7.8 %collective-permute-start.20 = (f32[1,2,8,384]{3,2,1,0:T(8,128)S(1)}, f32[1,2,8,384]{3,2,1,0:T(8,128)S(1)}, u32[]{:S(2)}, u32[]{:S(2)}) collective-permute-start(f32[1,2,8,384]{3,2,1,0:T(8,128)S(1)} %get-tuple-element.20), channel_id=1, source_target_pairs={{0,8},{4,12},{8,16},{12,20},{16,24},{20,28},{24,0},{28,4},{1,9},{5... | collective-permute-start | bytes 73736 | tf_op jit(solution)/shard_map/ppermute | solution.py:57
  55.7 9.0 %collective-permute-start.21 = (f32[1,2,8,384]{3,2,1,0:T(8,128)S(1)}, f32[1,2,8,384]{3,2,1,0:T(8,128)S(1)}, u32[]{:S(2)}, u32[]{:S(2)}) collective-permute-start(f32[1,2,8,384]{3,2,1,0:T(8,128)S(1)} %get-tuple-element.19), channel_id=1, source_target_pairs={{0,12},{4,16},{8,20},{12,24},{16,28},{20,0},{24,4},{28,8},{1,13},{... | collective-permute-start | bytes 73736 | tf_op jit(solution)/shard_map/ppermute | solution.py:57
  57.8 7.0 %collective-permute-start.22 = (f32[1,2,8,384]{3,2,1,0:T(8,128)S(1)}, f32[1,2,8,384]{3,2,1,0:T(8,128)S(1)}, u32[]{:S(2)}, u32[]{:S(2)}) collective-permute-start(f32[1,2,8,384]{3,2,1,0:T(8,128)S(1)} %get-tuple-element.18), channel_id=1, source_target_pairs={{0,16},{4,20},{8,24},{12,28},{16,0},{20,4},{24,8},{28,12},{1,17},{... | collective-permute-start | bytes 73736 | tf_op jit(solution)/shard_map/ppermute | solution.py:57
  59.9 4.9 %collective-permute-start.23 = (f32[1,2,8,384]{3,2,1,0:T(8,128)S(1)}, f32[1,2,8,384]{3,2,1,0:T(8,128)S(1)}, u32[]{:S(2)}, u32[]{:S(2)}) collective-permute-start(f32[1,2,8,384]{3,2,1,0:T(8,128)S(1)} %get-tuple-element.17), channel_id=1, source_target_pairs={{0,20},{4,24},{8,28},{12,0},{16,4},{20,8},{24,12},{28,16},{1,21},{... | collective-permute-start | bytes 73736 | tf_op jit(solution)/shard_map/ppermute | solution.py:57
  63.1 3.9 %collective-permute-start.24 = (f32[1,2,8,384]{3,2,1,0:T(8,128)S(1)}, f32[1,2,8,384]{3,2,1,0:T(8,128)S(1)}, u32[]{:S(2)}, u32[]{:S(2)}) collective-permute-start(f32[1,2,8,384]{3,2,1,0:T(8,128)S(1)} %get-tuple-element.16), channel_id=1, source_target_pairs={{0,24},{4,28},{8,0},{12,4},{16,8},{20,12},{24,16},{28,20},{1,25},{... | collective-permute-start | bytes 73736 | tf_op jit(solution)/shard_map/ppermute | solution.py:57
  63.4 3.9 %collective-permute-start.25 = (f32[1,2,8,384]{3,2,1,0:T(8,128)S(1)}, f32[1,2,8,384]{3,2,1,0:T(8,128)S(1)}, u32[]{:S(2)}, u32[]{:S(2)}) collective-permute-start(f32[1,2,8,384]{3,2,1,0:T(8,128)S(1)} %get-tuple-element.15), channel_id=1, source_target_pairs={{0,28},{4,0},{8,4},{12,8},{16,12},{20,16},{24,20},{28,24},{1,29},{... | collective-permute-start | bytes 73736 | tf_op jit(solution)/shard_map/ppermute | solution.py:57
  (5 other events, 18.6 us)

commit v2 on v0

--- a/solution.py
+++ b/solution.py
@@ -1,8 +1,11 @@
+import functools
 import math
 
 import jax
 import jax.numpy as jnp
 from jax import lax
+from jax.experimental import pallas as pl
+from jax.experimental.pallas import tpu as pltpu
 from jax.sharding import PartitionSpec as P
 
 D = 1536
@@ -51,7 +54,7 @@
     return mixed.astype(jnp.bfloat16).reshape(row_count, kv_local * group_size * HEAD_DIM)
 
 
-def shards(
+def shards_general(
     resid,
     queries,
     new_keys,
@@ -123,6 +126,378 @@
     return (attended, layer_out)
 
 
+def spec(space=pltpu.VMEM):
+    return pl.BlockSpec(memory_space=space)
+
+
+def call(kernel, outs, ins, operands, scratch=(), mebibytes=8, flops=100_000, moved=100_000):
+    return pl.pallas_call(
+        kernel,
+        out_shape=[jax.ShapeDtypeStruct(shape, dtype) for shape, dtype in outs],
+        in_specs=ins,
+        out_specs=[spec() for _ in outs],
+        scratch_shapes=scratch,
+        compiler_params=pltpu.CompilerParams(vmem_limit_bytes=mebibytes << 20),
+        cost_estimate=pl.CostEstimate(flops=flops, bytes_accessed=moved, transcendentals=0),
+    )(*operands)
+
+
+def partner_permute(block, axis, distance):
+    count = lax.axis_size(axis)
+    return lax.ppermute(block, axis, [(i, i ^ distance) for i in range(count)])
+
+
+def attend_kernel(
+    lengths, routes, queries, new_keys, new_values, w_router, k_hbm, v_hbm, w_hbm,
+    own, sent1, sent2, sent3, pick0, pick1, pick_rows, router_rows,
+    k_buf, v_buf, w_buf, query_s, self_s, score_s, weight_s, sems,
+):
+    row_count = queries.shape[0]
+    width = own.shape[1]
+    lanes = 2 * HEAD_DIM
+    cache_len = k_hbm.shape[1]
+    chunks = 4
+    per_chunk = row_count // chunks
+    copies = []
+    for index, (source, target) in enumerate(((k_hbm, k_buf), (v_hbm, v_buf))):
+        for chunk in range(chunks):
+            part = pl.ds(chunk * per_chunk, per_chunk)
+            copies.append(
+                pltpu.make_async_copy(source.at[part], target.at[part], sems.at[index * chunks + chunk])
+            )
+    copies.append(pltpu.make_async_copy(w_hbm, w_buf, sems.at[2 * chunks]))
+    for copy in copies:
+        copy.start()
+
+    route0, route1 = routes[:, 0:1], routes[:, 1:2]
+    lane = lax.broadcasted_iota(jnp.int32, (row_count, lanes), 1)
+    named0, named1 = lane == route0, lane == route1
+    named = jnp.where(named0 | named1, 1.0, 0.0).astype(jnp.bfloat16)
+    row_of = lax.broadcasted_iota(jnp.int32, (row_count, row_count), 0)
+    col_of = lax.broadcasted_iota(jnp.int32, (row_count, row_count), 1)
+    earlier = jnp.where(col_of < row_of, 1.0, 0.0).astype(jnp.bfloat16)
+    before = jnp.dot(earlier, named, preferred_element_type=jnp.float32)
+    rank0 = jnp.sum(jnp.where(named0, before, 0.0), axis=1, keepdims=True).astype(jnp.int32)
+    rank1 = jnp.sum(jnp.where(named1, before, 0.0), axis=1, keepdims=True).astype(jnp.int32)
+    first = jnp.where(lane == route0 * CAP + rank0, 1.0, 0.0)
+    second = jnp.where(lane == route1 * CAP + rank1, 1.0, 0.0)
+    pick0[...] = first.astype(jnp.bfloat16)
+    pick1[...] = second.astype(jnp.bfloat16)
+    pick_rows[...] = jnp.transpose(first + second).astype(jnp.bfloat16)
+    signed = jnp.where(named0, 1.0, 0.0) - jnp.where(named1, 1.0, 0.0)
+    router_rows[...] = lax.dot_general(
+        signed[:, :EXPERTS], w_router[...], (((1,), (1,)), ((), ())),
+        precision=lax.Precision.HIGHEST, preferred_element_type=jnp.float32,
+    )
+
+    low = lane < HEAD_DIM
+    tiles = [queries[:, i * lanes : (i + 1) * lanes].astype(jnp.float32) for i in range(3)]
+    heads = [
+        jnp.where(low, tiles[0], 0.0),
+        jnp.where(low, pltpu.roll(tiles[0], HEAD_DIM, 1), 0.0),
+        jnp.where(low, tiles[1], 0.0),
+        jnp.where(low, 0.0, tiles[1]),
+        jnp.where(low, 0.0, pltpu.roll(tiles[2], HEAD_DIM, 1)),
+        jnp.where(low, 0.0, tiles[2]),
+    ]
+    scale = 1.0 / math.sqrt(HEAD_DIM)
+    keys_new = new_keys[...].astype(jnp.float32)
+    zeros = jnp.zeros((row_count, lanes), jnp.float32)
+    for head in range(8):
+        rows = pl.ds(head, row_count, stride=8)
+        if head < 6:
+            own_score = jnp.sum(heads[head] * keys_new, axis=1, keepdims=True) * scale
+            query_s[rows, :] = heads[head]
+            self_s[rows, :] = jnp.broadcast_to(own_score, zeros.shape)
+        else:
+            query_s[rows, :] = zeros
+            self_s[rows, :] = zeros
+
+    pair_row = lax.broadcasted_iota(jnp.int32, (16, 2 * cache_len), 0)
+    pair_lane = lax.broadcasted_iota(jnp.int32, (16, 2 * cache_len), 1)
+    upper = pair_row < 8
+    place = jnp.where(upper, pair_lane, pair_lane - cache_len)
+    place = jnp.where(place < 0, cache_len, place)
+    for pair in range(row_count // 2):
+        if pair % (per_chunk // 2) == 0:
+            copies[pair // (per_chunk // 2)].wait()
+        pair_rows = slice(16 * pair, 16 * pair + 16)
+        keys = k_buf[2 * pair : 2 * pair + 2].reshape(2 * cache_len, lanes)
+        raw = lax.dot_general(
+            query_s[pair_rows, :].astype(jnp.bfloat16), keys, (((1,), (1,)), ((), ())),
+            preferred_element_type=jnp.float32,
+        )
+        limit = jnp.where(upper, lengths[2 * pair], lengths[2 * pair + 1])
+        score_s[pair_rows, :] = jnp.where(place < limit, raw * scale, -1e30)
+
+    own_score = self_s[:, 0:1]
+    scores = score_s[...]
+    peak = jnp.maximum(jnp.max(scores, axis=1, keepdims=True), own_score)
+    terms = jnp.exp(scores - peak)
+    own_term = jnp.exp(own_score - peak)
+    inverse = 1.0 / (jnp.sum(terms, axis=1, keepdims=True) + own_term)
+    weight_s[...] = (terms * inverse).astype(jnp.bfloat16)
+    own_weight = (own_term * inverse).astype(jnp.bfloat16).astype(jnp.float32)
+    self_s[...] = jnp.broadcast_to(own_weight, self_s.shape)
+    for pair in range(row_count // 2):
+        if pair % (per_chunk // 2) == 0:
+            copies[chunks + pair // (per_chunk // 2)].wait()
+        pair_rows = slice(16 * pair, 16 * pair + 16)
+        values = v_buf[2 * pair : 2 * pair + 2].reshape(2 * cache_len, lanes)
+        query_s[pair_rows, :] = jnp.dot(
+            weight_s[pair_rows, :], values, preferred_element_type=jnp.float32
+        )
+
+    values_new = new_values[...].astype(jnp.float32)
+    mixed = []
+    for head in range(6):
+        rows = pl.ds(head, row_count, stride=8)
+        mixed.append(query_s[rows, :] + self_s[rows, :] * values_new)
+    attention = jnp.concatenate(
+        [
+            jnp.where(low, mixed[0], pltpu.roll(mixed[1], HEAD_DIM, 1)),
+            jnp.where(low, mixed[2], mixed[3]),
+            jnp.where(low, pltpu.roll(mixed[4], HEAD_DIM, 1), mixed[5]),
+        ],
+        axis=1,
+    ).astype(jnp.bfloat16)
+    copies[2 * chunks].wait()
+    place_tp = lax.axis_index("tp")
+    for shift, out in enumerate((own, sent1, sent2, sent3)):
+        columns = pl.ds(pl.multiple_of((place_tp ^ shift) * width, width), width)
+        out[...] = jnp.dot(
+            attention, w_buf[:, columns], preferred_element_type=jnp.float32
+        ).astype(out.dtype)
+
+
+def pack_kernel(own, part1, part2, part3, resid, pick_rows, attended, packed):
+    total = own[...]
+    for part in (part1, part2, part3):
+        total = total + part[...].astype(jnp.float32)
+    rows = (resid[...].astype(jnp.float32) + total).astype(jnp.bfloat16)
+    attended[...] = rows
+    packed[...] = jnp.dot(pick_rows[...], rows, preferred_element_type=jnp.float32).astype(
+        jnp.bfloat16
+    )
+
+
+def stats_kernel(attended, gain, router_rows, stats):
+    rows = attended[...].astype(jnp.float32)
+    square = jnp.sum(rows * rows, axis=1, keepdims=True)
+    logit = jnp.sum(rows * gain[...] * router_rows[...], axis=1, keepdims=True)
+    lane = lax.broadcasted_iota(jnp.int32, stats.shape, 1)
+    stats[...] = jnp.where(lane == 0, square, jnp.where(lane == 1, logit, 0.0))
+
+
+def slot_masks(row_count, slot_dev):
+    slot = lax.rem(lax.broadcasted_iota(jnp.int32, (row_count, 1), 0) // CAP, slot_dev)
+    return [slot == index for index in range(slot_dev)]
+
+
+def gate_kernel(
+    slot_dev, incoming, gain, stats, w_gate, w_up, own, sent1, sent2, sent3, lhs
+):
+    quarter = own.shape[0]
+    width = incoming.shape[1]
+    hidden = w_gate.shape[1]
+    place_tp = lax.axis_index("tp")
+    masks = slot_masks(quarter, slot_dev)
+    lane = lax.broadcasted_iota(jnp.int32, (quarter, 128), 1)
+    extras = []
+    for shift in range(4):
+        rows = incoming[
+            pl.ds(pl.multiple_of((place_tp ^ shift) * quarter, quarter), quarter), :
+        ].astype(jnp.float32)
+        columns = [
+            jnp.sum(rows * rows, axis=1, keepdims=True),
+            stats[:, 0:1],
+            stats[:, 1:2],
+        ]
+        extra = jnp.zeros((quarter, 128), jnp.float32)
+        for index, column in enumerate(columns):
+            high = column.astype(jnp.bfloat16).astype(jnp.float32)
+            extra = jnp.where(lane == 2 * index, high, extra)
+            extra = jnp.where(lane == 2 * index + 1, column - high, extra)
+        extras.append(extra)
+        scaled = rows * gain[...]
+        for index, mask in enumerate(masks):
+            lhs[shift * quarter : (shift + 1) * quarter, index * width : (index + 1) * width] = (
+                jnp.where(mask, scaled, 0.0).astype(jnp.bfloat16)
+            )
+    left = lhs[...]
+    outs = (own, sent1, sent2, sent3)
+    for first, weight in ((0, w_gate), (hidden, w_up)):
+        product = jnp.dot(left, weight[...], preferred_element_type=jnp.float32)
+        for shift, out in enumerate(outs):
+            out[:, first : first + hidden] = product[
+                shift * quarter : (shift + 1) * quarter
+            ].astype(out.dtype)
+    for extra, out in zip(extras, outs):
+        out[:, 2 * hidden :] = extra.astype(out.dtype)
+
+
+def hidden_kernel(own, part1, part2, part3, hidden, first_weight):
+    width = hidden.shape[1]
+
+    def total(first, size):
+        columns = slice(first, first + size)
+        result = own[:, columns]
+        for part in (part1, part2, part3):
+            result = result + part[:, columns].astype(jnp.float32)
+        return result
+
+    extra = total(2 * width, 128)
+    row_inv = 1.0 / jnp.sqrt((extra[:, 0:1] + extra[:, 1:2]) / D + 1e-06)
+    gate = total(0, width) * row_inv
+    up = total(width, width) * row_inv
+    hidden[...] = (gate / (1.0 + jnp.exp(-gate)) * up).astype(jnp.bfloat16)
+    inv_rms = 1.0 / jnp.sqrt((extra[:, 2:3] + extra[:, 3:4]) / D + 1e-06)
+    logit = (extra[:, 4:5] + extra[:, 5:6]) * inv_rms
+    first_weight[...] = jnp.broadcast_to(1.0 / (1.0 + jnp.exp(-logit)), first_weight.shape)
+
+
+def down_kernel(slot_dev, own, part1, part2, part3, w_down, computed, lhs):
+    quarter, width = own.shape
+    place_tp = lax.axis_index("tp")
+    masks = slot_masks(quarter, slot_dev)
+    for shift, part in enumerate((own, part1, part2, part3)):
+        rows = part[...].astype(jnp.float32)
+        place = pl.ds(pl.multiple_of((place_tp ^ shift) * quarter, quarter), quarter)
+        for index, mask in enumerate(masks):
+            lhs[place, index * width : (index + 1) * width] = jnp.where(mask, rows, 0.0).astype(
+                jnp.bfloat16
+            )
+    computed[...] = jnp.dot(lhs[...], w_down[...], preferred_element_type=jnp.float32).astype(
+        computed.dtype
+    )
+
+
+def combine_kernel(returned, pick0, pick1, first_weight, attended, layer_out):
+    rows = returned[...]
+    out0 = jnp.dot(pick0[...], rows, preferred_element_type=jnp.float32)
+    out1 = jnp.dot(pick1[...], rows, preferred_element_type=jnp.float32)
+    weight = first_weight[:, 0:1]
+    moe = weight * out0 + (1.0 - weight) * out1
+    layer_out[...] = (attended[...].astype(jnp.float32) + moe).astype(jnp.bfloat16)
+
+
+def shards(
+    resid,
+    queries,
+    new_keys,
+    new_values,
+    k_cache,
+    v_cache,
+    lengths,
+    w_out,
+    norm_gain,
+    w_router,
+    routes,
+    w_gate,
+    w_up,
+    w_down,
+):
+    row_count, width = resid.shape
+    slot_dev, _, hidden = w_gate.shape
+    cache_len, lanes = k_cache.shape[1:]
+    packed_count = EXPERTS * CAP
+    quarter = packed_count // lax.axis_size("tp")
+    if not (
+        lax.axis_size("tp") == 4
+        and lax.axis_size("req") * slot_dev == EXPERTS
+        and row_count == quarter
+        and lanes == 2 * HEAD_DIM
+        and queries.shape[1] == 6 * HEAD_DIM
+    ):
+        return shards_general(
+            resid, queries, new_keys, new_values, k_cache, v_cache, lengths, w_out,
+            norm_gain, w_router, routes, w_gate, w_up, w_down,
+        )
+    bf16, f32 = jnp.bfloat16, jnp.float32
+    gain = norm_gain.reshape(1, width)
+    own, sent1, sent2, sent3, pick0, pick1, pick_rows, router_rows = call(
+        attend_kernel,
+        [
+            ((row_count, width), f32),
+            ((row_count, width), bf16),
+            ((row_count, width), bf16),
+            ((row_count, width), bf16),
+            ((row_count, packed_count), bf16),
+            ((row_count, packed_count), bf16),
+            ((packed_count, row_count), bf16),
+            ((row_count, width), f32),
+        ],
+        [spec(pltpu.SMEM)] + [spec()] * 5 + [spec(pl.ANY)] * 3,
+        (lengths, routes, queries, new_keys, new_values, w_router, k_cache, v_cache, w_out),
+        scratch=[
+            pltpu.VMEM(k_cache.shape, bf16),
+            pltpu.VMEM(v_cache.shape, bf16),
+            pltpu.VMEM(w_out.shape, bf16),
+            pltpu.VMEM((8 * row_count, lanes), f32),
+            pltpu.VMEM((8 * row_count, lanes), f32),
+            pltpu.VMEM((8 * row_count, 2 * cache_len), f32),
+            pltpu.VMEM((8 * row_count, 2 * cache_len), bf16),
+            pltpu.SemaphoreType.DMA((9,)),
+        ],
+        mebibytes=12,
+        flops=200_000_000,
+        moved=3_400_000,
+    )
+    parts = [partner_permute(block, "tp", k) for k, block in enumerate((sent1, sent2, sent3), 1)]
+    attended, packed = call(
+        pack_kernel,
+        [((row_count, width), bf16), ((packed_count, width), bf16)],
+        [spec()] * 6,
+        (own, *parts, resid, pick_rows),
+    )
+    incoming = lax.all_to_all(packed, "req", split_axis=0, concat_axis=0, tiled=True)
+    (stats,) = call(
+        stats_kernel, [((row_count, 128), f32)], [spec()] * 3, (attended, gain, router_rows)
+    )
+    message = (quarter, 2 * hidden + 128)
+    own, sent1, sent2, sent3 = call(
+        functools.partial(gate_kernel, slot_dev),
+        [(message, f32), (message, bf16), (message, bf16), (message, bf16)],
+        [spec()] * 5,
+        (
+            incoming,
+            gain,
+            stats,
+            w_gate.reshape(slot_dev * width, hidden),
+            w_up.reshape(slot_dev * width, hidden),
+        ),
+        scratch=[pltpu.VMEM((packed_count, slot_dev * width), bf16)],
+        mebibytes=12,
+        flops=800_000_000,
+        moved=4_000_000,
+    )
+    parts = [partner_permute(block, "tp", k) for k, block in enumerate((sent1, sent2, sent3), 1)]
+    own, first_weight = call(
+        hidden_kernel,
+        [((quarter, hidden), bf16), ((row_count, 128), f32)],
+        [spec()] * 4,
+        (own, *parts),
+    )
+    parts = [partner_permute(own, "tp", k) for k in (1, 2, 3)]
+    (computed,) = call(
+        functools.partial(down_kernel, slot_dev),
+        [((packed_count, width), bf16)],
+        [spec()] * 5,
+        (own, *parts, w_down.reshape(slot_dev * hidden, width)),
+        scratch=[pltpu.VMEM((packed_count, slot_dev * hidden), bf16)],
+        flops=200_000_000,
+        moved=2_000_000,
+    )
+    returned = lax.all_to_all(computed, "req", split_axis=0, concat_axis=0, tiled=True)
+    (layer_out,) = call(
+        combine_kernel,
+        [((row_count, width), bf16)],
+        [spec()] * 5,
+        (returned, pick0, pick1, first_weight, attended),
+    )
+    return (attended, layer_out)
+
+
 def solution(mesh):
     placed = (
         P("req", "tp"),

time: 121 us -> 59.4 us (0.49)
  waiting for transfers between devices: 62.9 us -> 20.1 us
  between operations: 14.3 us -> 0.73 us
  blocking collectives: 18.7 us -> 9.51 us
  matrix products: 8.93 us -> 0 us
  starting transfers between devices: 5.6 us -> 12.9 us
  Pallas kernels: 0 us -> 6.6 us
  other arithmetic: 3.31 us -> 0 us
  local copies, waits for them, and re-layouts: 6.4 us -> 8.88 us
    psum x1 -> x0, waiting for transfers between devices: 33.7 us -> none  [shards(): gate_sum, up_sum = lax.psum((gate_pre, up_pre), 'tp')]
    reduce_scatter x1 -> x0, waiting for transfers between devices: 21.6 us -> none  [shards(): lax.psum_scatter(partial_value, 'tp', scatter_dimension=1, tiled=True)]
    ppermute x0 -> x9, waiting for transfers between devices: none -> 13.8 us  [partner_permute(): return lax.ppermute(block, axis, [(i, i ^ distance) for i in range(count)])]
    dot_general x10 -> x0, matrix products: 8.93 us -> none  [the longest x1 2.14 us: shards(): jnp.einsum('nscf,sfd->nscd', hidden, w_down, preferred_element_type=jnp.f...]
    ppermute x0 -> x9, starting transfers between devices: none -> 7.04 us  [partner_permute(): return lax.ppermute(block, axis, [(i, i ^ distance) for i in range(count)])]
    pallas_call x0 -> x7, Pallas kernels: none -> 6.6 us  [call(): pl.pallas_call(kernel, out_shape=[jax.ShapeDtypeStruct(shape, dtype) for...]
    psum x1 -> x0, blocking collectives: 5.99 us -> none  [shards(): lax.psum((jnp.sum(attended_f * attended_f, axis=1), jnp.dot(scaled, w_rou...]
    unnamed x23 -> x30, local copies, waits for them, and re-layouts: 4.04 us -> 8.88 us
  transfers between devices with their start and end apart: 3 -> 10, of which waited for: 3 -> 7; matrix products, arithmetic and copies ran while one was open for 1% -> 0% of each run, Pallas kernels for 0% -> 0%
where the time goes in v2:
time: 59.4 us; the launch traced here: 58.7 us
  waiting for transfers between devices  20.1 us (34%)
  starting transfers between devices  12.9 us (22%)
  blocking collectives  9.51 us (16%)
  local copies, waits for them, and re-layouts  8.88 us (15%)
  Pallas kernels  6.6 us (11%)
  between operations  0.73 us (1%)
    ppermute x9, waiting for transfers between devices, partner_permute(): return lax.ppermute(block, axis, [(i, i ^ distance) for i in range(count)])  13.8 us
    all_to_all x1, blocking collectives, shards(): lax.all_to_all(computed, 'req', split_axis=0, concat_axis=0, tiled=True)  9.51 us
    unnamed x30, local copies, waits for them, and re-layouts  8.88 us
    ppermute x9, starting transfers between devices, partner_permute(): return lax.ppermute(block, axis, [(i, i ^ distance) for i in range(count)])  7.04 us
    pallas_call x7, Pallas kernels, call(): pl.pallas_call(kernel, out_shape=[jax.ShapeDtypeStruct(shape, dtype) for...  6.6 us
    all_to_all x1, waiting for transfers between devices, shards(): lax.all_to_all(packed, 'req', split_axis=0, concat_axis=0, tiled=True)  6.28 us
    all_to_all x1, starting transfers between devices, shards(): lax.all_to_all(packed, 'req', split_axis=0, concat_axis=0, tiled=True)  5.83 us
  transfers between devices with their start and end apart: 10, of which 7 were waited for; matrix products, arithmetic and copies ran while one was open for 0% of the time, Pallas kernels for 0%

profile of v2, /device:TPU:0, one launch (start us, length us, event | category | flops | bytes accessed | tf_op | source)
XLA Modules:
  0.0 58.7 jit_solution(4635742468506990077)
XLA Ops:
  0.6 0.8 %copy.16.routes = s32[32,2]{1,0:T(8,128)S(1)} copy(s32[32,2]{0,1:T(2,128)} %param.24) | data formatting | bytes 512 | tf_op args[10]
  1.4 0.9 %copy.17.w_router = f32[384,16]{1,0:T(8,128)S(1)} copy(f32[384,16]{0,1:T(8,128)} %param.23) | data formatting | bytes 49152 | tf_op args[9]
  2.3 1.3 %copy-done.3 = bf16[384,1536]{1,0:T(8,128)(2,1)S(1)} copy-done((bf16[384,1536]{1,0:T(8,128)(2,1)S(1)}, bf16[384,1536]{1,0:T(8,128)(2,1)}, u32[]{:S(2)}) %copy-start.3) | copy-done | bytes 1179672
  3.5 1.2 %copy-done.4 = bf16[32,128,128]{2,1,0:T(8,128)(2,1)S(1)} copy-done((bf16[32,128,128]{2,1,0:T(8,128)(2,1)S(1)}, bf16[32,128,128]{2,1,0:T(8,128)(2,1)}, u32[]{:S(2)}) %copy-start.4) | copy-done | bytes 1048600
  4.8 1.2 %copy-done.5 = bf16[32,128,128]{2,1,0:T(8,128)(2,1)S(1)} copy-done((bf16[32,128,128]{2,1,0:T(8,128)(2,1)S(1)}, bf16[32,128,128]{2,1,0:T(8,128)(2,1)}, u32[]{:S(2)}) %copy-start.5) | copy-done | bytes 1048600
  6.0 0.7 %copy-done.9 = bf16[32,384]{1,0:T(8,128)(2,1)S(1)} copy-done((bf16[32,384]{1,0:T(8,128)(2,1)S(1)}, bf16[32,384]{1,0:T(8,128)(2,1)}, u32[]{:S(2)}) %copy-start.9) | copy-done | bytes 24600
  6.7 0.7 %copy-done.10 = bf16[32,128]{1,0:T(8,128)(2,1)S(1)} copy-done((bf16[32,128]{1,0:T(8,128)(2,1)S(1)}, bf16[32,128]{1,0:T(8,128)(2,1)}, u32[]{:S(2)}) %copy-start.10) | copy-done | bytes 8216
  7.4 0.7 %copy-done.11 = bf16[32,128]{1,0:T(8,128)(2,1)S(1)} copy-done((bf16[32,128]{1,0:T(8,128)(2,1)S(1)}, bf16[32,128]{1,0:T(8,128)(2,1)}, u32[]{:S(2)}) %copy-start.11) | copy-done | bytes 8216
  8.1 0.7 %copy-done.12 = s32[32]{0:T(128)S(1)} copy-done((s32[32]{0:T(128)S(1)}, s32[32]{0:T(128)}, u32[]{:S(2)}) %copy-start.12) | copy-done | bytes 152
  8.8 3.6 %shard_map.149 = (f32[32,384]{1,0:T(8,128)S(1)}, bf16[32,384]{1,0:T(8,128)(2,1)S(1)}, bf16[32,384]{1,0:T(8,128)(2,1)S(1)}, bf16[32,384]{1,0:T(8,128)(2,1)S(1)}, ...) custom-call(s32[32]{0:T(128)S(1)} %copy-done.12, ...), custom_call_target="tpu_custom_call" | custom-call | flops 200000000 | bytes 3400000 | tf_op jit(solution)/shard_map/pallas_call | solution.py:134
  12.4 0.5 collective-permute-start
  12.9 2.6 %collective-permute-start.1 = (bf16[32,384]{1,0:T(8,128)(2,1)S(1)}, bf16[32,384]{1,0:T(8,128)(2,1)S(1)}, u32[]{:S(2)}, u32[]{:S(2)}) collective-permute-start(bf16[32,384]{1,0:T(8,128)(2,1)S(1)} %get-tuple-element.20), channel_id=1, source_target_pairs={{0,2},{1,3},{2,0},{3,1},{4,6},{5,7},{6,4},{7,5},{8,10},{9,11},{10,... | collective-permute-start | bytes 73736 | tf_op jit(solution)/shard_map/ppermute | solution.py:147
  15.5 1.7 %collective-permute-done.1.part2 = bf16[32,384]{1,0:T(8,128)(2,1)S(1)} collective-permute-done((bf16[32,384]{1,0:T(8,128)(2,1)S(1)}, bf16[32,384]{1,0:T(8,128)(2,1)S(1)}, u32[]{:S(2)}, u32[]{:S(2)}) %collective-permute-start.1) | collective-permute-done | bytes 24608 | tf_op jit(solution)/shard_map/ppermute | solution.py:147
  17.3 1.4 %collective-permute-done.2.part3 = bf16[32,384]{1,0:T(8,128)(2,1)S(1)} collective-permute-done((bf16[32,384]{1,0:T(8,128)(2,1)S(1)}, bf16[32,384]{1,0:T(8,128)(2,1)S(1)}, u32[]{:S(2)}, u32[]{:S(2)}) %collective-permute-start.2) | collective-permute-done | bytes 24608 | tf_op jit(solution)/shard_map/ppermute | solution.py:147
  18.7 0.8 %shard_map.150 = (bf16[32,384]{1,0:T(8,128)(2,1)}, bf16[128,384]{1,0:T(8,128)(2,1)}) custom-call(f32[32,384]{1,0:T(8,128)S(1)} %get-tuple-element.18.own, bf16[32,384]{1,0:T(8,128)(2,1)S(1)} %collective-permute-done.part1, bf16[32,384]{1,0:T(8,128)(2,1)S(1)} %collective-permute-done.1.part2, bf16[32,384]{1,0:T(8,128)(2,1)S(1)} %collective-permute-done.2.part3, ...), custom_call_target="tpu_custom_call" | custom-call | flops 100000 | bytes 100000 | tf_op jit(solution)/shard_map/pallas_call | solution.py:134
  19.5 5.8 %all-to-all-start = ((bf16[8,16,384]{2,1,0:T(8,128)(2,1)}), bf16[8,16,384]{2,1,0:T(8,128)(2,1)S(1)}, u32[]{:S(2)}, u32[]{:S(2)}) async-start(bf16[8,16,384]{2,1,0:T(8,128)(2,1)} %bitcast), calls=%async_computation | async-start | bytes 196608 | tf_op jit(solution)/shard_map/all_to_all | solution.py:453
  25.4 0.7 %copy-done.6 = bf16[32,384]{1,0:T(8,128)(2,1)S(1)} copy-done((bf16[32,384]{1,0:T(8,128)(2,1)S(1)}, bf16[32,384]{1,0:T(8,128)(2,1)}, u32[]{:S(2)}) %copy-start.6) | copy-done | bytes 24600
  26.1 0.1 shard_map.151.stats
  26.2 6.3 %all-to-all-done = bf16[8,16,384]{2,1,0:T(8,128)(2,1)S(1)} async-done(((bf16[8,16,384]{2,1,0:T(8,128)(2,1)}), bf16[8,16,384]{2,1,0:T(8,128)(2,1)S(1)}, u32[]{:S(2)}, u32[]{:S(2)}) %all-to-all-start) | async-done | bytes 98336 | tf_op jit(solution)/shard_map/all_to_all | solution.py:453
  32.5 0.6 %shard_map.152 = (f32[32,2176]{1,0:T(8,128)S(1)}, bf16[32,2176]{1,0:T(8,128)(2,1)S(1)}, bf16[32,2176]{1,0:T(8,128)(2,1)S(1)}, bf16[32,2176]{1,0:T(8,128)(2,1)S(1)}) custom-call(bf16[128,384]{1,0:T(8,128)(2,1)S(1)} %bitcast.10, f32[1,384]{1,0:T(1,128)S(1)} %reshape.20.gain, f32[32,128]{1,0:T(8,128)S(1)} %shard_map.151.stats, bf16[768,1024]{1,0:T(8,128)(2,1)S(1)} %bitcast.7, ...), custom_call_target="tpu_custom_call" | custom-call | flops 800000000 | bytes 4000000 | tf_op jit(solution)/shard_map/pallas_call | solution.py:134
  33.2 0.9 %collective-permute-start.4 = (bf16[32,2176]{1,0:T(8,128)(2,1)S(1)}, bf16[32,2176]{1,0:T(8,128)(2,1)S(1)}, u32[]{:S(2)}, u32[]{:S(2)}) collective-permute-start(bf16[32,2176]{1,0:T(8,128)(2,1)S(1)} %get-tuple-element.28), channel_id=1, source_target_pairs={{0,2},{1,3},{2,0},{3,1},{4,6},{5,7},{6,4},{7,5},{8,10},{9,11},{10,... | collective-permute-start | bytes 417800 | tf_op jit(solution)/shard_map/ppermute | solution.py:147
  34.1 1.0 %collective-permute-start.5 = (bf16[32,2176]{1,0:T(8,128)(2,1)S(1)}, bf16[32,2176]{1,0:T(8,128)(2,1)S(1)}, u32[]{:S(2)}, u32[]{:S(2)}) collective-permute-start(bf16[32,2176]{1,0:T(8,128)(2,1)S(1)} %get-tuple-element.29), channel_id=1, source_target_pairs={{0,3},{1,2},{2,1},{3,0},{4,7},{5,6},{6,5},{7,4},{8,11},{9,10},{10,... | collective-permute-start | bytes 417800 | tf_op jit(solution)/shard_map/ppermute | solution.py:147
  35.1 4.7 %collective-permute-done.4.part2 = bf16[32,2176]{1,0:T(8,128)(2,1)S(1)} collective-permute-done((bf16[32,2176]{1,0:T(8,128)(2,1)S(1)}, bf16[32,2176]{1,0:T(8,128)(2,1)S(1)}, u32[]{:S(2)}, u32[]{:S(2)}) %collective-permute-start.4) | collective-permute-done | bytes 139296 | tf_op jit(solution)/shard_map/ppermute | solution.py:147
  39.8 2.1 %collective-permute-done.5.part3 = bf16[32,2176]{1,0:T(8,128)(2,1)S(1)} collective-permute-done((bf16[32,2176]{1,0:T(8,128)(2,1)S(1)}, bf16[32,2176]{1,0:T(8,128)(2,1)S(1)}, u32[]{:S(2)}, u32[]{:S(2)}) %collective-permute-start.5) | collective-permute-done | bytes 139296 | tf_op jit(solution)/shard_map/ppermute | solution.py:147
  41.9 0.2 shard_map.153
  42.1 0.7 %collective-permute-start.8 = (bf16[32,1024]{1,0:T(8,128)(2,1)S(1)}, bf16[32,1024]{1,0:T(8,128)(2,1)S(1)}, u32[]{:S(2)}, u32[]{:S(2)}) collective-permute-start(bf16[32,1024]{1,0:T(8,128)(2,1)S(1)} %get-tuple-element.30.own), channel_id=1, source_target_pairs={{0,3},{1,2},{2,1},{3,0},{4,7},{5,6},{6,5},{7,4},{8,11},{9,10},{10,... | collective-permute-start | bytes 196616 | tf_op jit(solution)/shard_map/ppermute | solution.py:147
  42.8 1.2 %collective-permute-start.7 = (bf16[32,1024]{1,0:T(8,128)(2,1)S(1)}, bf16[32,1024]{1,0:T(8,128)(2,1)S(1)}, u32[]{:S(2)}, u32[]{:S(2)}) collective-permute-start(bf16[32,1024]{1,0:T(8,128)(2,1)S(1)} %get-tuple-element.30.own), channel_id=1, source_target_pairs={{0,2},{1,3},{2,0},{3,1},{4,6},{5,7},{6,4},{7,5},{8,10},{9,11},{10,... | collective-permute-start | bytes 196616 | tf_op jit(solution)/shard_map/ppermute | solution.py:147
  44.1 2.1 %collective-permute-done.8.part3 = bf16[32,1024]{1,0:T(8,128)(2,1)S(1)} collective-permute-done((bf16[32,1024]{1,0:T(8,128)(2,1)S(1)}, bf16[32,1024]{1,0:T(8,128)(2,1)S(1)}, u32[]{:S(2)}, u32[]{:S(2)}) %collective-permute-start.8) | collective-permute-done | bytes 65568 | tf_op jit(solution)/shard_map/ppermute | solution.py:147
  46.2 1.8 %collective-permute-done.7.part2 = bf16[32,1024]{1,0:T(8,128)(2,1)S(1)} collective-permute-done((bf16[32,1024]{1,0:T(8,128)(2,1)S(1)}, bf16[32,1024]{1,0:T(8,128)(2,1)S(1)}, u32[]{:S(2)}, u32[]{:S(2)}) %collective-permute-start.7) | collective-permute-done | bytes 65568 | tf_op jit(solution)/shard_map/ppermute | solution.py:147
  47.9 0.5 shard_map.154
  48.4 9.5 %all_to_all.22 = bf16[8,16,384]{2,1,0:T(8,128)(2,1)S(1)} all-to-all(bf16[8,16,384]{2,1,0:T(8,128)(2,1)S(1)} %bitcast.12), channel_id=1, replica_groups=mesh['req'=8,'tp'=4] {'req'}, dimensions={0} | all-to-all | bytes 196608 | tf_op jit(solution)/shard_map/all_to_all | solution.py:491
  57.9 0.8 %shard_map.155 = bf16[32,384]{1,0:T(8,128)(2,1)} custom-call(bf16[128,384]{1,0:T(8,128)(2,1)S(1)} %bitcast.11, bf16[32,128]{1,0:T(8,128)(2,1)S(1)} %get-tuple-element.31.pick0, bf16[32,128]{1,0:T(8,128)(2,1)S(1)} %get-tuple-element.32.pick1, f32[32,128]{1,0:T(8,128)S(1)} %get-tuple-element.33.first_weight, bf16[32,384]{1,0:T(8,128)(2,1)S(1)} %copy-done.7), custom_call_target="tpu_custom_call" | custom-call | flops 100000 | bytes 100000 | tf_op jit(solution)/shard_map/pallas_call | solution.py:134
  (27 shorter events, 0.2 us)
Async XLA Ops:
  2.3 1.3 %copy-start.3 = (bf16[384,1536]{1,0:T(8,128)(2,1)S(1)}, bf16[384,1536]{1,0:T(8,128)(2,1)}, u32[]{:S(2)}) copy-start(bf16[384,1536]{1,0:T(8,128)(2,1)} %w_hbm.1) | copy-start | bytes 3538948
  3.5 1.2 %copy-start.4 = (bf16[32,128,128]{2,1,0:T(8,128)(2,1)S(1)}, bf16[32,128,128]{2,1,0:T(8,128)(2,1)}, u32[]{:S(2)}) copy-start(bf16[32,128,128]{2,1,0:T(8,128)(2,1)} %k_hbm.1) | copy-start | bytes 3145732
  4.8 1.2 %copy-start.5 = (bf16[32,128,128]{2,1,0:T(8,128)(2,1)S(1)}, bf16[32,128,128]{2,1,0:T(8,128)(2,1)}, u32[]{:S(2)}) copy-start(bf16[32,128,128]{2,1,0:T(8,128)(2,1)} %v_hbm.1) | copy-start | bytes 3145732
  6.0 0.7 %copy-start.9 = (bf16[32,384]{1,0:T(8,128)(2,1)S(1)}, bf16[32,384]{1,0:T(8,128)(2,1)}, u32[]{:S(2)}) copy-start(bf16[32,384]{1,0:T(8,128)(2,1)} %queries.1) | copy-start | bytes 73732
  6.7 0.7 %copy-start.10 = (bf16[32,128]{1,0:T(8,128)(2,1)S(1)}, bf16[32,128]{1,0:T(8,128)(2,1)}, u32[]{:S(2)}) copy-start(bf16[32,128]{1,0:T(8,128)(2,1)} %new_keys.1) | copy-start | bytes 24580
  7.4 0.7 %copy-start.11 = (bf16[32,128]{1,0:T(8,128)(2,1)S(1)}, bf16[32,128]{1,0:T(8,128)(2,1)}, u32[]{:S(2)}) copy-start(bf16[32,128]{1,0:T(8,128)(2,1)} %new_values.1) | copy-start | bytes 24580
  8.1 0.7 %copy-start.12 = (s32[32]{0:T(128)S(1)}, s32[32]{0:T(128)}, u32[]{:S(2)}) copy-start(s32[32]{0:T(128)} %lengths.1) | copy-start | bytes 388
  8.8 9.9 %copy-start.8 = (bf16[32,384]{1,0:T(8,128)(2,1)S(1)}, bf16[32,384]{1,0:T(8,128)(2,1)}, u32[]{:S(2)}) copy-start(bf16[32,384]{1,0:T(8,128)(2,1)} %resid.1) | copy-start | bytes 73732
  8.8 16.6 %copy-start.13 = (f32[384]{0:T(512)S(1)}, f32[384]{0:T(512)}, u32[]{:S(2)}) copy-start(f32[384]{0:T(512)} %param.22) | copy-start | bytes 4612
  8.8 23.7 %copy-start = (bf16[2,384,1024]{2,1,0:T(8,128)(2,1)S(1)}, bf16[2,384,1024]{2,1,0:T(8,128)(2,1)}, u32[]{:S(2)}) copy-start(bf16[2,384,1024]{2,1,0:T(8,128)(2,1)} %param.25) | copy-start | bytes 4718596
  8.8 23.7 %copy-start.1 = (bf16[2,384,1024]{2,1,0:T(8,128)(2,1)S(1)}, bf16[2,384,1024]{2,1,0:T(8,128)(2,1)}, u32[]{:S(2)}) copy-start(bf16[2,384,1024]{2,1,0:T(8,128)(2,1)} %param.26) | copy-start | bytes 4718596
  12.4 3.2 %collective-permute-start = (bf16[32,384]{1,0:T(8,128)(2,1)S(1)}, bf16[32,384]{1,0:T(8,128)(2,1)S(1)}, u32[]{:S(2)}, u32[]{:S(2)}) collective-permute-start(bf16[32,384]{1,0:T(8,128)(2,1)S(1)} %get-tuple-element.19), channel_id=1, source_target_pairs={{0,1},{1,0},{2,3},{3,2},{4,5},{5,4},{6,7},{7,6},{8,9},{9,8},{10,11... | collective-permute-start | bytes 73736 | tf_op jit(solution)/shard_map/ppermute | solution.py:147
  12.9 4.4 %collective-permute-start.1 = (bf16[32,384]{1,0:T(8,128)(2,1)S(1)}, bf16[32,384]{1,0:T(8,128)(2,1)S(1)}, u32[]{:S(2)}, u32[]{:S(2)}) collective-permute-start(bf16[32,384]{1,0:T(8,128)(2,1)S(1)} %get-tuple-element.20), channel_id=1, source_target_pairs={{0,2},{1,3},{2,0},{3,1},{4,6},{5,7},{6,4},{7,5},{8,10},{9,11},{10,... | collective-permute-start | bytes 73736 | tf_op jit(solution)/shard_map/ppermute | solution.py:147
  15.5 3.3 %collective-permute-start.2 = (bf16[32,384]{1,0:T(8,128)(2,1)S(1)}, bf16[32,384]{1,0:T(8,128)(2,1)S(1)}, u32[]{:S(2)}, u32[]{:S(2)}) collective-permute-start(bf16[32,384]{1,0:T(8,128)(2,1)S(1)} %get-tuple-element.21), channel_id=1, source_target_pairs={{0,3},{1,2},{2,1},{3,0},{4,7},{5,6},{6,5},{7,4},{8,11},{9,10},{10,... | collective-permute-start | bytes 73736 | tf_op jit(solution)/shard_map/ppermute | solution.py:147
  19.5 13.0 %all-to-all-start = ((bf16[8,16,384]{2,1,0:T(8,128)(2,1)}), bf16[8,16,384]{2,1,0:T(8,128)(2,1)S(1)}, u32[]{:S(2)}, u32[]{:S(2)}) async-start(bf16[8,16,384]{2,1,0:T(8,128)(2,1)} %bitcast), calls=%async_computation | async-start | bytes 196608 | tf_op jit(solution)/shard_map/all_to_all | solution.py:453
  25.4 0.7 %copy-start.6 = (bf16[32,384]{1,0:T(8,128)(2,1)S(1)}, bf16[32,384]{1,0:T(8,128)(2,1)}, u32[]{:S(2)}) copy-start(bf16[32,384]{1,0:T(8,128)(2,1)} %get-tuple-element.16.attended) | copy-start | bytes 73732
  32.5 15.5 %copy-start.2 = (bf16[2,1024,384]{2,1,0:T(8,128)(2,1)S(1)}, bf16[2,1024,384]{2,1,0:T(8,128)(2,1)}, u32[]{:S(2)}) copy-start(bf16[2,1024,384]{2,1,0:T(8,128)(2,1)} %param.27) | copy-start | bytes 4718596
  33.1 24.8 %copy-start.7 = (bf16[32,384]{1,0:T(8,128)(2,1)S(1)}, bf16[32,384]{1,0:T(8,128)(2,1)}, u32[]{:S(2)}) copy-start(bf16[32,384]{1,0:T(8,128)(2,1)} %get-tuple-element.16.attended) | copy-start | bytes 73732
  33.2 1.9 %collective-permute-start.3 = (bf16[32,2176]{1,0:T(8,128)(2,1)S(1)}, bf16[32,2176]{1,0:T(8,128)(2,1)S(1)}, u32[]{:S(2)}, u32[]{:S(2)}) collective-permute-start(bf16[32,2176]{1,0:T(8,128)(2,1)S(1)} %get-tuple-element.27), channel_id=1, source_target_pairs={{0,1},{1,0},{2,3},{3,2},{4,5},{5,4},{6,7},{7,6},{8,9},{9,8},{10,11... | collective-permute-start | bytes 417800 | tf_op jit(solution)/shard_map/ppermute | solution.py:147
  33.2 6.5 %collective-permute-start.4 = (bf16[32,2176]{1,0:T(8,128)(2,1)S(1)}, bf16[32,2176]{1,0:T(8,128)(2,1)S(1)}, u32[]{:S(2)}, u32[]{:S(2)}) collective-permute-start(bf16[32,2176]{1,0:T(8,128)(2,1)S(1)} %get-tuple-element.28), channel_id=1, source_target_pairs={{0,2},{1,3},{2,0},{3,1},{4,6},{5,7},{6,4},{7,5},{8,10},{9,11},{10,... | collective-permute-start | bytes 417800 | tf_op jit(solution)/shard_map/ppermute | solution.py:147
  34.1 7.7 %collective-permute-start.5 = (bf16[32,2176]{1,0:T(8,128)(2,1)S(1)}, bf16[32,2176]{1,0:T(8,128)(2,1)S(1)}, u32[]{:S(2)}, u32[]{:S(2)}) collective-permute-start(bf16[32,2176]{1,0:T(8,128)(2,1)S(1)} %get-tuple-element.29), channel_id=1, source_target_pairs={{0,3},{1,2},{2,1},{3,0},{4,7},{5,6},{6,5},{7,4},{8,11},{9,10},{10,... | collective-permute-start | bytes 417800 | tf_op jit(solution)/shard_map/ppermute | solution.py:147
  42.1 4.1 %collective-permute-start.8 = (bf16[32,1024]{1,0:T(8,128)(2,1)S(1)}, bf16[32,1024]{1,0:T(8,128)(2,1)S(1)}, u32[]{:S(2)}, u32[]{:S(2)}) collective-permute-start(bf16[32,1024]{1,0:T(8,128)(2,1)S(1)} %get-tuple-element.30.own), channel_id=1, source_target_pairs={{0,3},{1,2},{2,1},{3,0},{4,7},{5,6},{6,5},{7,4},{8,11},{9,10},{10,... | collective-permute-start | bytes 196616 | tf_op jit(solution)/shard_map/ppermute | solution.py:147
  42.8 5.1 %collective-permute-start.7 = (bf16[32,1024]{1,0:T(8,128)(2,1)S(1)}, bf16[32,1024]{1,0:T(8,128)(2,1)S(1)}, u32[]{:S(2)}, u32[]{:S(2)}) collective-permute-start(bf16[32,1024]{1,0:T(8,128)(2,1)S(1)} %get-tuple-element.30.own), channel_id=1, source_target_pairs={{0,2},{1,3},{2,0},{3,1},{4,6},{5,7},{6,4},{7,5},{8,10},{9,11},{10,... | collective-permute-start | bytes 196616 | tf_op jit(solution)/shard_map/ppermute | solution.py:147
  44.1 3.9 %collective-permute-start.6 = (bf16[32,1024]{1,0:T(8,128)(2,1)S(1)}, bf16[32,1024]{1,0:T(8,128)(2,1)S(1)}, u32[]{:S(2)}, u32[]{:S(2)}) collective-permute-start(bf16[32,1024]{1,0:T(8,128)(2,1)S(1)} %get-tuple-element.30.own), channel_id=1, source_target_pairs={{0,1},{1,0},{2,3},{3,2},{4,5},{5,4},{6,7},{7,6},{8,9},{9,8},{10,11... | collective-permute-start | bytes 196616 | tf_op jit(solution)/shard_map/ppermute | solution.py:147

commit v3 on v2

--- a/solution.py
+++ b/solution.py
@@ -148,49 +148,74 @@
 
 
 def attend_kernel(
-    lengths, routes, queries, new_keys, new_values, w_router, k_hbm, v_hbm, w_hbm,
-    own, sent1, sent2, sent3, pick0, pick1, pick_rows, router_rows,
-    k_buf, v_buf, w_buf, query_s, self_s, score_s, weight_s, sems,
+    slot_dev, lengths_hbm, routes_hbm, queries_hbm, keys_hbm, values_hbm, router_hbm, k_hbm, v_hbm,
+    w_hbm, own, sent1, sent2, sent3, pick0, pick1, pick_rows, router_rows,
+    lengths, routes, queries, new_keys, new_values, w_router, k_buf, v_buf, w_buf,
+    query_s, self_s, score_s, weight_s, small_sems, sems,
 ):
     row_count = queries.shape[0]
     width = own.shape[1]
     lanes = 2 * HEAD_DIM
     cache_len = k_hbm.shape[1]
+    packed_count = pick0.shape[1]
     chunks = 4
+    small = [
+        pltpu.make_async_copy(source, target, small_sems.at[index])
+        for index, (source, target) in enumerate(
+            (
+                (routes_hbm, routes),
+                (router_hbm, w_router),
+                (queries_hbm, queries),
+                (keys_hbm, new_keys),
+                (values_hbm, new_values),
+                (lengths_hbm, lengths),
+            )
+        )
+    ]
+    copies = []
+    for source, target in ((k_hbm, k_buf), (v_hbm, v_buf), (w_hbm, w_buf)):
+        size = source.shape[0] // chunks
+        for chunk in range(chunks):
+            part = pl.ds(chunk * size, size)
+            copies.append(
+                pltpu.make_async_copy(source.at[part], target.at[part], sems.at[len(copies)])
+            )
+    for copy in small + copies:
+        copy.start()
     per_chunk = row_count // chunks
-    copies = []
-    for index, (source, target) in enumerate(((k_hbm, k_buf), (v_hbm, v_buf))):
-        for chunk in range(chunks):
-            part = pl.ds(chunk * per_chunk, per_chunk)
-            copies.append(
-                pltpu.make_async_copy(source.at[part], target.at[part], sems.at[index * chunks + chunk])
-            )
-    copies.append(pltpu.make_async_copy(w_hbm, w_buf, sems.at[2 * chunks]))
-    for copy in copies:
-        copy.start()
-
-    route0, route1 = routes[:, 0:1], routes[:, 1:2]
-    lane = lax.broadcasted_iota(jnp.int32, (row_count, lanes), 1)
-    named0, named1 = lane == route0, lane == route1
-    named = jnp.where(named0 | named1, 1.0, 0.0).astype(jnp.bfloat16)
+
+    small[0].wait()
+    route0, route1 = routes[0:1, :], routes[1:2, :]
+    place = lax.broadcasted_iota(jnp.int32, (packed_count, row_count), 0)
+    named0 = jnp.where(place == route0, 1.0, 0.0)
+    named1 = jnp.where(place == route1, 1.0, 0.0)
     row_of = lax.broadcasted_iota(jnp.int32, (row_count, row_count), 0)
     col_of = lax.broadcasted_iota(jnp.int32, (row_count, row_count), 1)
-    earlier = jnp.where(col_of < row_of, 1.0, 0.0).astype(jnp.bfloat16)
-    before = jnp.dot(earlier, named, preferred_element_type=jnp.float32)
-    rank0 = jnp.sum(jnp.where(named0, before, 0.0), axis=1, keepdims=True).astype(jnp.int32)
-    rank1 = jnp.sum(jnp.where(named1, before, 0.0), axis=1, keepdims=True).astype(jnp.int32)
-    first = jnp.where(lane == route0 * CAP + rank0, 1.0, 0.0)
-    second = jnp.where(lane == route1 * CAP + rank1, 1.0, 0.0)
-    pick0[...] = first.astype(jnp.bfloat16)
-    pick1[...] = second.astype(jnp.bfloat16)
-    pick_rows[...] = jnp.transpose(first + second).astype(jnp.bfloat16)
-    signed = jnp.where(named0, 1.0, 0.0) - jnp.where(named1, 1.0, 0.0)
-    router_rows[...] = lax.dot_general(
-        signed[:, :EXPERTS], w_router[...], (((1,), (1,)), ((), ())),
+    earlier = jnp.where(row_of < col_of, 1.0, 0.0).astype(jnp.bfloat16)
+    before = jnp.dot(
+        (named0 + named1).astype(jnp.bfloat16), earlier, preferred_element_type=jnp.float32
+    )
+    place_req = lax.axis_index("req")
+
+    def pick(route, named):
+        rank = jnp.sum(named * before, axis=0, keepdims=True).astype(jnp.int32)
+        block = ((route // slot_dev) ^ place_req) * slot_dev + lax.rem(route, slot_dev)
+        return jnp.where(place == block * CAP + rank, 1.0, 0.0)
+
+    first, second = pick(route0, named0), pick(route1, named1)
+    pick_rows[...] = (first + second).astype(jnp.bfloat16)
+    pick0[...] = jnp.transpose(first).astype(jnp.bfloat16)
+    pick1[...] = jnp.transpose(second).astype(jnp.bfloat16)
+    signed = jnp.transpose(named0 - named1)
+    small[1].wait()
+    router_rows[...] = jnp.dot(
+        signed[:, :EXPERTS], w_router[...],
         precision=lax.Precision.HIGHEST, preferred_element_type=jnp.float32,
     )
-
-    low = lane < HEAD_DIM
+    for copy in small[2:]:
+        copy.wait()
+
+    low = lax.broadcasted_iota(jnp.int32, (row_count, lanes), 1) < HEAD_DIM
     tiles = [queries[:, i * lanes : (i + 1) * lanes].astype(jnp.float32) for i in range(3)]
     heads = [
         jnp.where(low, tiles[0], 0.0),
@@ -261,7 +286,8 @@
         ],
         axis=1,
     ).astype(jnp.bfloat16)
-    copies[2 * chunks].wait()
+    for copy in copies[2 * chunks :]:
+        copy.wait()
     place_tp = lax.axis_index("tp")
     for shift, out in enumerate((own, sent1, sent2, sent3)):
         columns = pl.ds(pl.multiple_of((place_tp ^ shift) * width, width), width)
@@ -270,18 +296,24 @@
         ).astype(out.dtype)
 
 
-def pack_kernel(own, part1, part2, part3, resid, pick_rows, attended, packed):
+def store_blocks(rows, home, sent1, sent2, sent3):
+    size = home.shape[0]
+    for distance, out in enumerate((home, sent1, sent2, sent3)):
+        out[...] = rows[distance * size : (distance + 1) * size].astype(out.dtype)
+
+
+def pack_kernel(own, part1, part2, part3, resid, pick_rows, attended, home, sent1, sent2, sent3):
     total = own[...]
     for part in (part1, part2, part3):
         total = total + part[...].astype(jnp.float32)
     rows = (resid[...].astype(jnp.float32) + total).astype(jnp.bfloat16)
     attended[...] = rows
-    packed[...] = jnp.dot(pick_rows[...], rows, preferred_element_type=jnp.float32).astype(
-        jnp.bfloat16
-    )
-
-
-def stats_kernel(attended, gain, router_rows, stats):
+    packed = jnp.dot(pick_rows[...], rows, preferred_element_type=jnp.float32)
+    store_blocks(packed, home, sent1, sent2, sent3)
+
+
+def stats_kernel(attended, gain, router_rows, stats, result):
+    result[...] = attended[...]
     rows = attended[...].astype(jnp.float32)
     square = jnp.sum(rows * rows, axis=1, keepdims=True)
     logit = jnp.sum(rows * gain[...] * router_rows[...], axis=1, keepdims=True)
@@ -289,14 +321,44 @@
     stats[...] = jnp.where(lane == 0, square, jnp.where(lane == 1, logit, 0.0))
 
 
+def turn_kernel(home, part1, part2, part3, along):
+    half = home.shape[0] // 2
+    for index, part in enumerate((home, part1, part2, part3)):
+        along[index * half : (index + 1) * half, :] = part[half:, :]
+
+
+def two_hop(home, sents):
+    parts = [partner_permute(block, "req", 2 * k) for k, block in enumerate(sents, 1)]
+    (along,) = call(
+        turn_kernel,
+        [((2 * home.shape[0], home.shape[1]), home.dtype)],
+        [spec()] * 4,
+        (home, *parts),
+    )
+    return (home, *parts, partner_permute(along, "req", 1))
+
+
+def gather_blocks(refs, target):
+    *first_hop, second_hop = refs
+    half = first_hop[0].shape[0] // 2
+    for index, part in enumerate(first_hop):
+        start = 2 * index * half
+        target[start : start + half, :] = part[:half, :].astype(target.dtype)
+        target[start + half : start + 2 * half, :] = second_hop[
+            index * half : (index + 1) * half, :
+        ].astype(target.dtype)
+
+
 def slot_masks(row_count, slot_dev):
     slot = lax.rem(lax.broadcasted_iota(jnp.int32, (row_count, 1), 0) // CAP, slot_dev)
     return [slot == index for index in range(slot_dev)]
 
 
 def gate_kernel(
-    slot_dev, incoming, gain, stats, w_gate, w_up, own, sent1, sent2, sent3, lhs
+    slot_dev, in0, in1, in2, in3, in4, gain, stats, w_gate, w_up,
+    own, sent1, sent2, sent3, incoming, lhs
 ):
+    gather_blocks((in0, in1, in2, in3, in4), incoming)
     quarter = own.shape[0]
     width = incoming.shape[1]
     hidden = w_gate.shape[1]
@@ -356,7 +418,7 @@
     first_weight[...] = jnp.broadcast_to(1.0 / (1.0 + jnp.exp(-logit)), first_weight.shape)
 
 
-def down_kernel(slot_dev, own, part1, part2, part3, w_down, computed, lhs):
+def down_kernel(slot_dev, own, part1, part2, part3, w_down, home, sent1, sent2, sent3, lhs):
     quarter, width = own.shape
     place_tp = lax.axis_index("tp")
     masks = slot_masks(quarter, slot_dev)
@@ -367,12 +429,14 @@
             lhs[place, index * width : (index + 1) * width] = jnp.where(mask, rows, 0.0).astype(
                 jnp.bfloat16
             )
-    computed[...] = jnp.dot(lhs[...], w_down[...], preferred_element_type=jnp.float32).astype(
-        computed.dtype
-    )
-
-
-def combine_kernel(returned, pick0, pick1, first_weight, attended, layer_out):
+    computed = jnp.dot(lhs[...], w_down[...], preferred_element_type=jnp.float32)
+    store_blocks(computed, home, sent1, sent2, sent3)
+
+
+def combine_kernel(
+    in0, in1, in2, in3, in4, pick0, pick1, first_weight, attended, layer_out, returned
+):
+    gather_blocks((in0, in1, in2, in3, in4), returned)
     rows = returned[...]
     out0 = jnp.dot(pick0[...], rows, preferred_element_type=jnp.float32)
     out1 = jnp.dot(pick1[...], rows, preferred_element_type=jnp.float32)
@@ -404,7 +468,8 @@
     quarter = packed_count // lax.axis_size("tp")
     if not (
         lax.axis_size("tp") == 4
-        and lax.axis_size("req") * slot_dev == EXPERTS
+        and lax.axis_size("req") == 8
+        and 8 * slot_dev == EXPERTS
         and row_count == quarter
         and lanes == 2 * HEAD_DIM
         and queries.shape[1] == 6 * HEAD_DIM
@@ -416,7 +481,7 @@
     bf16, f32 = jnp.bfloat16, jnp.float32
     gain = norm_gain.reshape(1, width)
     own, sent1, sent2, sent3, pick0, pick1, pick_rows, router_rows = call(
-        attend_kernel,
+        functools.partial(attend_kernel, slot_dev),
         [
             ((row_count, width), f32),
             ((row_count, width), bf16),
@@ -427,9 +492,17 @@
             ((packed_count, row_count), bf16),
             ((row_count, width), f32),
         ],
-        [spec(pltpu.SMEM)] + [spec()] * 5 + [spec(pl.ANY)] * 3,
-        (lengths, routes, queries, new_keys, new_values, w_router, k_cache, v_cache, w_out),
+        [spec(pl.ANY)] * 9,
+        (
+            lengths, routes.T, queries, new_keys, new_values, w_router.T, k_cache, v_cache, w_out,
+        ),
         scratch=[
+            pltpu.SMEM(lengths.shape, jnp.int32),
+            pltpu.VMEM(routes.shape[::-1], jnp.int32),
+            pltpu.VMEM(queries.shape, bf16),
+            pltpu.VMEM(new_keys.shape, bf16),
+            pltpu.VMEM(new_values.shape, bf16),
+            pltpu.VMEM(w_router.shape[::-1], f32),
             pltpu.VMEM(k_cache.shape, bf16),
             pltpu.VMEM(v_cache.shape, bf16),
             pltpu.VMEM(w_out.shape, bf16),
@@ -437,36 +510,43 @@
             pltpu.VMEM((8 * row_count, lanes), f32),
             pltpu.VMEM((8 * row_count, 2 * cache_len), f32),
             pltpu.VMEM((8 * row_count, 2 * cache_len), bf16),
-            pltpu.SemaphoreType.DMA((9,)),
+            pltpu.SemaphoreType.DMA((6,)),
+            pltpu.SemaphoreType.DMA((12,)),
         ],
-        mebibytes=12,
+        mebibytes=56,
         flops=200_000_000,
         moved=3_400_000,
     )
     parts = [partner_permute(block, "tp", k) for k, block in enumerate((sent1, sent2, sent3), 1)]
-    attended, packed = call(
+    block = ((quarter, width), bf16)
+    attended, home, *sents = call(
         pack_kernel,
-        [((row_count, width), bf16), ((packed_count, width), bf16)],
+        [((row_count, width), bf16)] + [block] * 4,
         [spec()] * 6,
         (own, *parts, resid, pick_rows),
     )
-    incoming = lax.all_to_all(packed, "req", split_axis=0, concat_axis=0, tiled=True)
-    (stats,) = call(
-        stats_kernel, [((row_count, 128), f32)], [spec()] * 3, (attended, gain, router_rows)
+    stats, result = call(
+        stats_kernel,
+        [((row_count, 128), f32), ((row_count, width), bf16)],
+        [spec()] * 3,
+        (attended, gain, router_rows),
     )
     message = (quarter, 2 * hidden + 128)
     own, sent1, sent2, sent3 = call(
         functools.partial(gate_kernel, slot_dev),
         [(message, f32), (message, bf16), (message, bf16), (message, bf16)],
-        [spec()] * 5,
+        [spec()] * 9,
         (
-            incoming,
+            *two_hop(home, sents),
             gain,
             stats,
             w_gate.reshape(slot_dev * width, hidden),
             w_up.reshape(slot_dev * width, hidden),
         ),
-        scratch=[pltpu.VMEM((packed_count, slot_dev * width), bf16)],
+        scratch=[
+            pltpu.VMEM((packed_count, width), bf16),
+            pltpu.VMEM((packed_count, slot_dev * width), bf16),
+        ],
         mebibytes=12,
         flops=800_000_000,
         moved=4_000_000,
@@ -479,23 +559,23 @@
         (own, *parts),
     )
     parts = [partner_permute(own, "tp", k) for k in (1, 2, 3)]
-    (computed,) = call(
+    home, *sents = call(
         functools.partial(down_kernel, slot_dev),
-        [((packed_count, width), bf16)],
+        [block] * 4,
         [spec()] * 5,
         (own, *parts, w_down.reshape(slot_dev * hidden, width)),
         scratch=[pltpu.VMEM((packed_count, slot_dev * hidden), bf16)],
         flops=200_000_000,
         moved=2_000_000,
     )
-    returned = lax.all_to_all(computed, "req", split_axis=0, concat_axis=0, tiled=True)
     (layer_out,) = call(
         combine_kernel,
         [((row_count, width), bf16)],
-        [spec()] * 5,
-        (returned, pick0, pick1, first_weight, attended),
-    )
-    return (attended, layer_out)
+        [spec()] * 9,
+        (*two_hop(home, sents), pick0, pick1, first_weight, attended),
+        scratch=[pltpu.VMEM((packed_count, width), bf16)],
+    )
+    return (result, layer_out)
 
 
 def solution(mesh):

time: 59.4 us -> 55.3 us (0.931)
  blocking collectives: 9.51 us -> 0 us
  local copies, waits for them, and re-layouts: 8.88 us -> 2.39 us
  starting transfers between devices: 12.9 us -> 19 us
  waiting for transfers between devices: 20.1 us -> 25.2 us
  Pallas kernels: 6.6 us -> 7.67 us
    ppermute x9 -> x17, starting transfers between devices: 7.04 us -> 19 us  [partner_permute(): return lax.ppermute(block, axis, [(i, i ^ distance) for i in range(count)])]
    ppermute x9 -> x17, waiting for transfers between devices: 13.8 us -> 25.2 us  [partner_permute(): return lax.ppermute(block, axis, [(i, i ^ distance) for i in range(count)])]
    all_to_all x1 -> x0, blocking collectives: 9.51 us -> none  [shards(): lax.all_to_all(computed, 'req', split_axis=0, concat_axis=0, tiled=True)]
    unnamed x30 -> x20, local copies, waits for them, and re-layouts: 8.88 us -> 2.38 us
    all_to_all x1 -> x0, waiting for transfers between devices: 6.28 us -> none  [shards(): lax.all_to_all(packed, 'req', split_axis=0, concat_axis=0, tiled=True)]
    all_to_all x1 -> x0, starting transfers between devices: 5.83 us -> none  [shards(): lax.all_to_all(packed, 'req', split_axis=0, concat_axis=0, tiled=True)]
    pallas_call x7 -> x9, Pallas kernels: 6.6 us -> 7.67 us  [call(): pl.pallas_call(kernel, out_shape=[jax.ShapeDtypeStruct(shape, dtype) for...]
  transfers between devices with their start and end apart: 10 -> 17, of which waited for: 7 -> 12; matrix products, arithmetic and copies ran while one was open for 0% -> 0% of each run, Pallas kernels for 0% -> 1%
where the time goes in v3:
time: 55.3 us; the launch traced here: 55 us
  waiting for transfers between devices  25.2 us (46%)
  starting transfers between devices  19 us (34%)
  Pallas kernels  7.67 us (14%)
  local copies, waits for them, and re-layouts  2.39 us (4%)
  between operations  0.75 us (1%)
    ppermute x17, waiting for transfers between devices, partner_permute(): return lax.ppermute(block, axis, [(i, i ^ distance) for i in range(count)])  25.2 us
    ppermute x17, starting transfers between devices, partner_permute(): return lax.ppermute(block, axis, [(i, i ^ distance) for i in range(count)])  19 us
    pallas_call x9, Pallas kernels, call(): pl.pallas_call(kernel, out_shape=[jax.ShapeDtypeStruct(shape, dtype) for...  7.67 us
    unnamed x20, local copies, waits for them, and re-layouts  2.38 us
  transfers between devices with their start and end apart: 17, of which 12 were waited for; matrix products, arithmetic and copies ran while one was open for 0% of the time, Pallas kernels for 1%

profile of v3, /device:TPU:0, one launch (start us, length us, event | category | flops | bytes accessed | tf_op | source)
XLA Modules:
  0.0 55.0 jit_solution(9629775692878329751)
XLA Ops:
  0.7 4.8 %shard_map.149 = (f32[32,384]{1,0:T(8,128)}, bf16[32,384]{1,0:T(8,128)(2,1)}, bf16[32,384]{1,0:T(8,128)(2,1)}, bf16[32,384]{1,0:T(8,128)(2,1)}, bf16[32,128]{1,0...) custom-call(s32[32]{0:T(128)} %lengths_hbm.1, s32[2,32]{1,0:T(2,128)} %bitcast.9, ...), custom_call_target="tpu_custom_call" | custom-call | flops 200000000 | bytes 3400000 | tf_op jit(solution)/shard_map/pallas_call | solution.py:134
  5.4 0.5 collective-permute-start
  6.0 2.6 %collective-permute-start.1 = (bf16[32,384]{1,0:T(8,128)(2,1)}, bf16[32,384]{1,0:T(8,128)(2,1)S(1)}, u32[]{:S(2)}, u32[]{:S(2)}) collective-permute-start(bf16[32,384]{1,0:T(8,128)(2,1)} %get-tuple-element.29), channel_id=1, source_target_pairs={{0,2},{1,3},{2,0},{3,1},{4,6},{5,7},{6,4},{7,5},{8,10},{9,11},{10,... | collective-permute-start | bytes 73736 | tf_op jit(solution)/shard_map/ppermute | solution.py:147
  8.6 1.9 %collective-permute-done.1.part2 = bf16[32,384]{1,0:T(8,128)(2,1)S(1)} collective-permute-done((bf16[32,384]{1,0:T(8,128)(2,1)}, bf16[32,384]{1,0:T(8,128)(2,1)S(1)}, u32[]{:S(2)}, u32[]{:S(2)}) %collective-permute-start.1) | collective-permute-done | bytes 24608 | tf_op jit(solution)/shard_map/ppermute | solution.py:147
  10.5 1.4 %collective-permute-done.2.part3 = bf16[32,384]{1,0:T(8,128)(2,1)S(1)} collective-permute-done((bf16[32,384]{1,0:T(8,128)(2,1)}, bf16[32,384]{1,0:T(8,128)(2,1)S(1)}, u32[]{:S(2)}, u32[]{:S(2)}) %collective-permute-start.2) | collective-permute-done | bytes 24608 | tf_op jit(solution)/shard_map/ppermute | solution.py:147
  12.0 0.8 %copy-done.4 = f32[32,384]{1,0:T(8,128)S(1)} copy-done((f32[32,384]{1,0:T(8,128)S(1)}, f32[32,384]{1,0:T(8,128)}, u32[]{:S(2)}) %copy-start.4) | copy-done | bytes 49176
  12.8 0.8 %copy-done.5 = bf16[128,32]{1,0:T(8,128)(2,1)S(1)} copy-done((bf16[128,32]{1,0:T(8,128)(2,1)S(1)}, bf16[128,32]{1,0:T(8,128)(2,1)}, u32[]{:S(2)}) %copy-start.5) | copy-done | bytes 8216
  13.7 1.6 %collective-permute-start.3 = (bf16[32,384]{1,0:T(8,128)(2,1)S(1)}, bf16[32,384]{1,0:T(8,128)(2,1)S(1)}, u32[]{:S(2)}, u32[]{:S(2)}) collective-permute-start(bf16[32,384]{1,0:T(8,128)(2,1)S(1)} %get-tuple-element.36), channel_id=1, source_target_pairs={{0,8},{4,12},{8,0},{12,4},{16,24},{20,28},{24,16},{28,20},{1,9},{5... | collective-permute-start | bytes 73736 | tf_op jit(solution)/shard_map/ppermute | solution.py:147
  15.3 2.6 %collective-permute-start.4 = (bf16[32,384]{1,0:T(8,128)(2,1)S(1)}, bf16[32,384]{1,0:T(8,128)(2,1)S(1)}, u32[]{:S(2)}, u32[]{:S(2)}) collective-permute-start(bf16[32,384]{1,0:T(8,128)(2,1)S(1)} %get-tuple-element.37), channel_id=1, source_target_pairs={{0,16},{4,20},{8,24},{12,28},{16,0},{20,4},{24,8},{28,12},{1,17},{... | collective-permute-start | bytes 73736 | tf_op jit(solution)/shard_map/ppermute | solution.py:147
  18.2 2.3 %collective-permute-done.4.part2.in2 = bf16[32,384]{1,0:T(8,128)(2,1)S(1)} collective-permute-done((bf16[32,384]{1,0:T(8,128)(2,1)S(1)}, bf16[32,384]{1,0:T(8,128)(2,1)S(1)}, u32[]{:S(2)}, u32[]{:S(2)}) %collective-permute-start.4) | collective-permute-done | bytes 24608 | tf_op jit(solution)/shard_map/ppermute | solution.py:147
  20.4 3.1 %collective-permute-done.5.part3.in3 = bf16[32,384]{1,0:T(8,128)(2,1)S(1)} collective-permute-done((bf16[32,384]{1,0:T(8,128)(2,1)S(1)}, bf16[32,384]{1,0:T(8,128)(2,1)S(1)}, u32[]{:S(2)}, u32[]{:S(2)}) %collective-permute-start.5) | collective-permute-done | bytes 24608 | tf_op jit(solution)/shard_map/ppermute | solution.py:147
  23.6 1.5 %collective-permute-start.6 = (bf16[64,384]{1,0:T(8,128)(2,1)S(1)}, bf16[64,384]{1,0:T(8,128)(2,1)S(1)}, u32[]{:S(2)}, u32[]{:S(2)}) collective-permute-start(bf16[64,384]{1,0:T(8,128)(2,1)S(1)} %shard_map.152), channel_id=1, source_target_pairs={{0,4},{4,0},{8,12},{12,8},{16,20},{20,16},{24,28},{28,24},{1,5},{5... | collective-permute-start | bytes 147464 | tf_op jit(solution)/shard_map/ppermute | solution.py:147
  25.1 0.8 %copy-done.3 = f32[32,384]{1,0:T(8,128)S(1)} copy-done((f32[32,384]{1,0:T(8,128)S(1)}, f32[32,384]{1,0:T(8,128)}, u32[]{:S(2)}) %copy-start.3) | copy-done | bytes 49176
  25.9 0.6 %shard_map.151 = (f32[32,128]{1,0:T(8,128)S(1)}, bf16[32,384]{1,0:T(8,128)(2,1)}) custom-call(bf16[32,384]{1,0:T(8,128)(2,1)S(1)} %get-tuple-element.32.attended, f32[1,384]{1,0:T(1,128)S(1)} %reshape.16.gain, f32[32,384]{1,0:T(8,128)S(1)} %copy-done.3), custom_call_target="tpu_custom_call" | custom-call | flops 100000 | bytes 100000 | tf_op jit(solution)/shard_map/pallas_call | solution.py:134
  26.5 1.2 %collective-permute-done.6.in4 = bf16[64,384]{1,0:T(8,128)(2,1)S(1)} collective-permute-done((bf16[64,384]{1,0:T(8,128)(2,1)S(1)}, bf16[64,384]{1,0:T(8,128)(2,1)S(1)}, u32[]{:S(2)}, u32[]{:S(2)}) %collective-permute-start.6) | collective-permute-done | bytes 49184 | tf_op jit(solution)/shard_map/ppermute | solution.py:147
  27.7 0.6 %shard_map.153 = (f32[32,2176]{1,0:T(8,128)S(1)}, bf16[32,2176]{1,0:T(8,128)(2,1)S(1)}, bf16[32,2176]{1,0:T(8,128)(2,1)S(1)}, bf16[32,2176]{1,0:T(8,128)(2,1)S(1)}) custom-call(bf16[32,384]{1,0:T(8,128)(2,1)S(1)} %get-tuple-element.35.home.in0, bf16[32,384]{1,0:T(8,128)(2,1)S(1)} %collective-permute-done.3.part1.in1, ...), custom_call_target="tpu_custom_call" | custom-call | flops 800000000 | bytes 4000000 | tf_op jit(solution)/shard_map/pallas_call | solution.py:134
  28.4 0.9 %collective-permute-start.8 = (bf16[32,2176]{1,0:T(8,128)(2,1)S(1)}, bf16[32,2176]{1,0:T(8,128)(2,1)S(1)}, u32[]{:S(2)}, u32[]{:S(2)}) collective-permute-start(bf16[32,2176]{1,0:T(8,128)(2,1)S(1)} %get-tuple-element.42), channel_id=1, source_target_pairs={{0,2},{1,3},{2,0},{3,1},{4,6},{5,7},{6,4},{7,5},{8,10},{9,11},{10,... | collective-permute-start | bytes 417800 | tf_op jit(solution)/shard_map/ppermute | solution.py:147
  29.3 1.0 %collective-permute-start.9 = (bf16[32,2176]{1,0:T(8,128)(2,1)S(1)}, bf16[32,2176]{1,0:T(8,128)(2,1)S(1)}, u32[]{:S(2)}, u32[]{:S(2)}) collective-permute-start(bf16[32,2176]{1,0:T(8,128)(2,1)S(1)} %get-tuple-element.43), channel_id=1, source_target_pairs={{0,3},{1,2},{2,1},{3,0},{4,7},{5,6},{6,5},{7,4},{8,11},{9,10},{10,... | collective-permute-start | bytes 417800 | tf_op jit(solution)/shard_map/ppermute | solution.py:147
  30.3 4.7 %collective-permute-done.8.part2 = bf16[32,2176]{1,0:T(8,128)(2,1)S(1)} collective-permute-done((bf16[32,2176]{1,0:T(8,128)(2,1)S(1)}, bf16[32,2176]{1,0:T(8,128)(2,1)S(1)}, u32[]{:S(2)}, u32[]{:S(2)}) %collective-permute-start.8) | collective-permute-done | bytes 139296 | tf_op jit(solution)/shard_map/ppermute | solution.py:147
  35.0 2.1 %collective-permute-done.9.part3 = bf16[32,2176]{1,0:T(8,128)(2,1)S(1)} collective-permute-done((bf16[32,2176]{1,0:T(8,128)(2,1)S(1)}, bf16[32,2176]{1,0:T(8,128)(2,1)S(1)}, u32[]{:S(2)}, u32[]{:S(2)}) %collective-permute-start.9) | collective-permute-done | bytes 139296 | tf_op jit(solution)/shard_map/ppermute | solution.py:147
  37.3 0.7 %collective-permute-start.12 = (bf16[32,1024]{1,0:T(8,128)(2,1)S(1)}, bf16[32,1024]{1,0:T(8,128)(2,1)S(1)}, u32[]{:S(2)}, u32[]{:S(2)}) collective-permute-start(bf16[32,1024]{1,0:T(8,128)(2,1)S(1)} %get-tuple-element.44.own), channel_id=1, source_target_pairs={{0,3},{1,2},{2,1},{3,0},{4,7},{5,6},{6,5},{7,4},{8,11},{9,10},{10,... | collective-permute-start | bytes 196616 | tf_op jit(solution)/shard_map/ppermute | solution.py:147
  38.0 1.2 %collective-permute-start.11 = (bf16[32,1024]{1,0:T(8,128)(2,1)S(1)}, bf16[32,1024]{1,0:T(8,128)(2,1)S(1)}, u32[]{:S(2)}, u32[]{:S(2)}) collective-permute-start(bf16[32,1024]{1,0:T(8,128)(2,1)S(1)} %get-tuple-element.44.own), channel_id=1, source_target_pairs={{0,2},{1,3},{2,0},{3,1},{4,6},{5,7},{6,4},{7,5},{8,10},{9,11},{10,... | collective-permute-start | bytes 196616 | tf_op jit(solution)/shard_map/ppermute | solution.py:147
  39.2 2.1 %collective-permute-done.12.part3 = bf16[32,1024]{1,0:T(8,128)(2,1)S(1)} collective-permute-done((bf16[32,1024]{1,0:T(8,128)(2,1)S(1)}, bf16[32,1024]{1,0:T(8,128)(2,1)S(1)}, u32[]{:S(2)}, u32[]{:S(2)}) %collective-permute-start.12) | collective-permute-done | bytes 65568 | tf_op jit(solution)/shard_map/ppermute | solution.py:147
  41.3 1.8 %collective-permute-done.11.part2 = bf16[32,1024]{1,0:T(8,128)(2,1)S(1)} collective-permute-done((bf16[32,1024]{1,0:T(8,128)(2,1)S(1)}, bf16[32,1024]{1,0:T(8,128)(2,1)S(1)}, u32[]{:S(2)}, u32[]{:S(2)}) %collective-permute-start.11) | collective-permute-done | bytes 65568 | tf_op jit(solution)/shard_map/ppermute | solution.py:147
  43.1 0.5 shard_map.155
  43.7 0.8 %collective-permute-start.14 = (bf16[32,384]{1,0:T(8,128)(2,1)S(1)}, bf16[32,384]{1,0:T(8,128)(2,1)S(1)}, u32[]{:S(2)}, u32[]{:S(2)}) collective-permute-start(bf16[32,384]{1,0:T(8,128)(2,1)S(1)} %get-tuple-element.47), channel_id=1, source_target_pairs={{0,16},{4,20},{8,24},{12,28},{16,0},{20,4},{24,8},{28,12},{1,17},{... | collective-permute-start | bytes 73736 | tf_op jit(solution)/shard_map/ppermute | solution.py:147
  44.5 3.6 %collective-permute-start.15 = (bf16[32,384]{1,0:T(8,128)(2,1)S(1)}, bf16[32,384]{1,0:T(8,128)(2,1)S(1)}, u32[]{:S(2)}, u32[]{:S(2)}) collective-permute-start(bf16[32,384]{1,0:T(8,128)(2,1)S(1)} %get-tuple-element.48), channel_id=1, source_target_pairs={{0,24},{4,28},{8,16},{12,20},{16,8},{20,12},{24,0},{28,4},{1,25},{... | collective-permute-start | bytes 73736 | tf_op jit(solution)/shard_map/ppermute | solution.py:147
  48.1 0.8 %collective-permute-done.14.part2.in2 = bf16[32,384]{1,0:T(8,128)(2,1)S(1)} collective-permute-done((bf16[32,384]{1,0:T(8,128)(2,1)S(1)}, bf16[32,384]{1,0:T(8,128)(2,1)S(1)}, u32[]{:S(2)}, u32[]{:S(2)}) %collective-permute-start.14) | collective-permute-done | bytes 24608 | tf_op jit(solution)/shard_map/ppermute | solution.py:147
  48.9 1.3 %collective-permute-done.15.part3.in3 = bf16[32,384]{1,0:T(8,128)(2,1)S(1)} collective-permute-done((bf16[32,384]{1,0:T(8,128)(2,1)S(1)}, bf16[32,384]{1,0:T(8,128)(2,1)S(1)}, u32[]{:S(2)}, u32[]{:S(2)}) %collective-permute-start.15) | collective-permute-done | bytes 24608 | tf_op jit(solution)/shard_map/ppermute | solution.py:147
  50.1 1.5 %collective-permute-start.16 = (bf16[64,384]{1,0:T(8,128)(2,1)S(1)}, bf16[64,384]{1,0:T(8,128)(2,1)S(1)}, u32[]{:S(2)}, u32[]{:S(2)}) collective-permute-start(bf16[64,384]{1,0:T(8,128)(2,1)S(1)} %shard_map.156), channel_id=1, source_target_pairs={{0,4},{4,0},{8,12},{12,8},{16,20},{20,16},{24,28},{28,24},{1,5},{5... | collective-permute-start | bytes 147464 | tf_op jit(solution)/shard_map/ppermute | solution.py:147
  51.7 2.6 %collective-permute-done.16.in4 = bf16[64,384]{1,0:T(8,128)(2,1)S(1)} collective-permute-done((bf16[64,384]{1,0:T(8,128)(2,1)S(1)}, bf16[64,384]{1,0:T(8,128)(2,1)S(1)}, u32[]{:S(2)}, u32[]{:S(2)}) %collective-permute-start.16) | collective-permute-done | bytes 49184 | tf_op jit(solution)/shard_map/ppermute | solution.py:147
  54.2 0.8 %shard_map.157 = bf16[32,384]{1,0:T(8,128)(2,1)} custom-call(bf16[32,384]{1,0:T(8,128)(2,1)S(1)} %get-tuple-element.45.home.in0, bf16[32,384]{1,0:T(8,128)(2,1)S(1)} %collective-permute-done.13.part1.in1, bf16[32,384]{1,0:T(8,128)(2,1)S(1)} %collective-permute-done.14.part2.in2, bf16[32,384]{1,0:T(8,128)(2,1)S(1)} %collective-permute-done.15.part3.in3, ...), custom_call_target="tpu_custom_call" | custom-call | flops 100000 | bytes 100000 | tf_op jit(solution)/shard_map/pallas_call | solution.py:134
  (32 shorter events, 0.9 us)
Async XLA Ops:
  0.6 11.4 %copy-start.6 = (bf16[32,384]{1,0:T(8,128)(2,1)S(1)}, bf16[32,384]{1,0:T(8,128)(2,1)}, u32[]{:S(2)}) copy-start(bf16[32,384]{1,0:T(8,128)(2,1)} %resid.1) | copy-start | bytes 73732
  0.6 24.4 %copy-start.9 = (f32[384]{0:T(512)S(1)}, f32[384]{0:T(512)}, u32[]{:S(2)}) copy-start(f32[384]{0:T(512)} %param.22) | copy-start | bytes 4612
  0.7 27.0 %copy-start.1 = (bf16[2,384,1024]{2,1,0:T(8,128)(2,1)S(1)}, bf16[2,384,1024]{2,1,0:T(8,128)(2,1)}, u32[]{:S(2)}) copy-start(bf16[2,384,1024]{2,1,0:T(8,128)(2,1)} %param.25) | copy-start | bytes 4718596
  0.7 27.0 %copy-start.2 = (bf16[2,384,1024]{2,1,0:T(8,128)(2,1)S(1)}, bf16[2,384,1024]{2,1,0:T(8,128)(2,1)}, u32[]{:S(2)}) copy-start(bf16[2,384,1024]{2,1,0:T(8,128)(2,1)} %param.26) | copy-start | bytes 4718596
  5.4 3.2 %collective-permute-start = (bf16[32,384]{1,0:T(8,128)(2,1)}, bf16[32,384]{1,0:T(8,128)(2,1)S(1)}, u32[]{:S(2)}, u32[]{:S(2)}) collective-permute-start(bf16[32,384]{1,0:T(8,128)(2,1)} %get-tuple-element.28), channel_id=1, source_target_pairs={{0,1},{1,0},{2,3},{3,2},{4,5},{5,4},{6,7},{7,6},{8,9},{9,8},{10,11... | collective-permute-start | bytes 73736 | tf_op jit(solution)/shard_map/ppermute | solution.py:147
  6.0 4.6 %collective-permute-start.1 = (bf16[32,384]{1,0:T(8,128)(2,1)}, bf16[32,384]{1,0:T(8,128)(2,1)S(1)}, u32[]{:S(2)}, u32[]{:S(2)}) collective-permute-start(bf16[32,384]{1,0:T(8,128)(2,1)} %get-tuple-element.29), channel_id=1, source_target_pairs={{0,2},{1,3},{2,0},{3,1},{4,6},{5,7},{6,4},{7,5},{8,10},{9,11},{10,... | collective-permute-start | bytes 73736 | tf_op jit(solution)/shard_map/ppermute | solution.py:147
  8.5 3.5 %collective-permute-start.2 = (bf16[32,384]{1,0:T(8,128)(2,1)}, bf16[32,384]{1,0:T(8,128)(2,1)S(1)}, u32[]{:S(2)}, u32[]{:S(2)}) collective-permute-start(bf16[32,384]{1,0:T(8,128)(2,1)} %get-tuple-element.30), channel_id=1, source_target_pairs={{0,3},{1,2},{2,1},{3,0},{4,7},{5,6},{6,5},{7,4},{8,11},{9,10},{10,... | collective-permute-start | bytes 73736 | tf_op jit(solution)/shard_map/ppermute | solution.py:147
  12.0 0.8 %copy-start.4 = (f32[32,384]{1,0:T(8,128)S(1)}, f32[32,384]{1,0:T(8,128)}, u32[]{:S(2)}) copy-start(f32[32,384]{1,0:T(8,128)} %get-tuple-element.27.own) | copy-start | bytes 147460
  12.8 0.8 %copy-start.5 = (bf16[128,32]{1,0:T(8,128)(2,1)S(1)}, bf16[128,32]{1,0:T(8,128)(2,1)}, u32[]{:S(2)}) copy-start(bf16[128,32]{1,0:T(8,128)(2,1)} %get-tuple-element.31.pick_rows) | copy-start | bytes 24580
  13.7 4.5 %collective-permute-start.3 = (bf16[32,384]{1,0:T(8,128)(2,1)S(1)}, bf16[32,384]{1,0:T(8,128)(2,1)S(1)}, u32[]{:S(2)}, u32[]{:S(2)}) collective-permute-start(bf16[32,384]{1,0:T(8,128)(2,1)S(1)} %get-tuple-element.36), channel_id=1, source_target_pairs={{0,8},{4,12},{8,0},{12,4},{16,24},{20,28},{24,16},{28,20},{1,9},{5... | collective-permute-start | bytes 73736 | tf_op jit(solution)/shard_map/ppermute | solution.py:147
  15.3 5.1 %collective-permute-start.4 = (bf16[32,384]{1,0:T(8,128)(2,1)S(1)}, bf16[32,384]{1,0:T(8,128)(2,1)S(1)}, u32[]{:S(2)}, u32[]{:S(2)}) collective-permute-start(bf16[32,384]{1,0:T(8,128)(2,1)S(1)} %get-tuple-element.37), channel_id=1, source_target_pairs={{0,16},{4,20},{8,24},{12,28},{16,0},{20,4},{24,8},{28,12},{1,17},{... | collective-permute-start | bytes 73736 | tf_op jit(solution)/shard_map/ppermute | solution.py:147
  17.9 5.6 %collective-permute-start.5 = (bf16[32,384]{1,0:T(8,128)(2,1)S(1)}, bf16[32,384]{1,0:T(8,128)(2,1)S(1)}, u32[]{:S(2)}, u32[]{:S(2)}) collective-permute-start(bf16[32,384]{1,0:T(8,128)(2,1)S(1)} %get-tuple-element.38), channel_id=1, source_target_pairs={{0,24},{4,28},{8,16},{12,20},{16,8},{20,12},{24,0},{28,4},{1,25},{... | collective-permute-start | bytes 73736 | tf_op jit(solution)/shard_map/ppermute | solution.py:147
  23.6 4.1 %collective-permute-start.6 = (bf16[64,384]{1,0:T(8,128)(2,1)S(1)}, bf16[64,384]{1,0:T(8,128)(2,1)S(1)}, u32[]{:S(2)}, u32[]{:S(2)}) collective-permute-start(bf16[64,384]{1,0:T(8,128)(2,1)S(1)} %shard_map.152), channel_id=1, source_target_pairs={{0,4},{4,0},{8,12},{12,8},{16,20},{20,16},{24,28},{28,24},{1,5},{5... | collective-permute-start | bytes 147464 | tf_op jit(solution)/shard_map/ppermute | solution.py:147
  25.1 0.8 %copy-start.3 = (f32[32,384]{1,0:T(8,128)S(1)}, f32[32,384]{1,0:T(8,128)}, u32[]{:S(2)}) copy-start(f32[32,384]{1,0:T(8,128)} %get-tuple-element.33.router_rows) | copy-start | bytes 147460
  27.7 15.5 %copy-start = (bf16[2,1024,384]{2,1,0:T(8,128)(2,1)S(1)}, bf16[2,1024,384]{2,1,0:T(8,128)(2,1)}, u32[]{:S(2)}) copy-start(bf16[2,1024,384]{2,1,0:T(8,128)(2,1)} %param.27) | copy-start | bytes 4718596
  28.3 25.9 %copy-start.7 = (bf16[32,128]{1,0:T(8,128)(2,1)S(1)}, bf16[32,128]{1,0:T(8,128)(2,1)}, u32[]{:S(2)}) copy-start(bf16[32,128]{1,0:T(8,128)(2,1)} %get-tuple-element.49.pick0) | copy-start | bytes 24580
  28.3 25.9 %copy-start.8 = (bf16[32,128]{1,0:T(8,128)(2,1)S(1)}, bf16[32,128]{1,0:T(8,128)(2,1)}, u32[]{:S(2)}) copy-start(bf16[32,128]{1,0:T(8,128)(2,1)} %get-tuple-element.50.pick1) | copy-start | bytes 24580
  28.3 1.9 %collective-permute-start.7 = (bf16[32,2176]{1,0:T(8,128)(2,1)S(1)}, bf16[32,2176]{1,0:T(8,128)(2,1)S(1)}, u32[]{:S(2)}, u32[]{:S(2)}) collective-permute-start(bf16[32,2176]{1,0:T(8,128)(2,1)S(1)} %get-tuple-element.41), channel_id=1, source_target_pairs={{0,1},{1,0},{2,3},{3,2},{4,5},{5,4},{6,7},{7,6},{8,9},{9,8},{10,11... | collective-permute-start | bytes 417800 | tf_op jit(solution)/shard_map/ppermute | solution.py:147
  28.4 6.5 %collective-permute-start.8 = (bf16[32,2176]{1,0:T(8,128)(2,1)S(1)}, bf16[32,2176]{1,0:T(8,128)(2,1)S(1)}, u32[]{:S(2)}, u32[]{:S(2)}) collective-permute-start(bf16[32,2176]{1,0:T(8,128)(2,1)S(1)} %get-tuple-element.42), channel_id=1, source_target_pairs={{0,2},{1,3},{2,0},{3,1},{4,6},{5,7},{6,4},{7,5},{8,10},{9,11},{10,... | collective-permute-start | bytes 417800 | tf_op jit(solution)/shard_map/ppermute | solution.py:147
  29.3 7.8 %collective-permute-start.9 = (bf16[32,2176]{1,0:T(8,128)(2,1)S(1)}, bf16[32,2176]{1,0:T(8,128)(2,1)S(1)}, u32[]{:S(2)}, u32[]{:S(2)}) collective-permute-start(bf16[32,2176]{1,0:T(8,128)(2,1)S(1)} %get-tuple-element.43), channel_id=1, source_target_pairs={{0,3},{1,2},{2,1},{3,0},{4,7},{5,6},{6,5},{7,4},{8,11},{9,10},{10,... | collective-permute-start | bytes 417800 | tf_op jit(solution)/shard_map/ppermute | solution.py:147
  37.3 4.1 %collective-permute-start.12 = (bf16[32,1024]{1,0:T(8,128)(2,1)S(1)}, bf16[32,1024]{1,0:T(8,128)(2,1)S(1)}, u32[]{:S(2)}, u32[]{:S(2)}) collective-permute-start(bf16[32,1024]{1,0:T(8,128)(2,1)S(1)} %get-tuple-element.44.own), channel_id=1, source_target_pairs={{0,3},{1,2},{2,1},{3,0},{4,7},{5,6},{6,5},{7,4},{8,11},{9,10},{10,... | collective-permute-start | bytes 196616 | tf_op jit(solution)/shard_map/ppermute | solution.py:147
  38.0 5.1 %collective-permute-start.11 = (bf16[32,1024]{1,0:T(8,128)(2,1)S(1)}, bf16[32,1024]{1,0:T(8,128)(2,1)S(1)}, u32[]{:S(2)}, u32[]{:S(2)}) collective-permute-start(bf16[32,1024]{1,0:T(8,128)(2,1)S(1)} %get-tuple-element.44.own), channel_id=1, source_target_pairs={{0,2},{1,3},{2,0},{3,1},{4,6},{5,7},{6,4},{7,5},{8,10},{9,11},{10,... | collective-permute-start | bytes 196616 | tf_op jit(solution)/shard_map/ppermute | solution.py:147
  39.2 3.9 %collective-permute-start.10 = (bf16[32,1024]{1,0:T(8,128)(2,1)S(1)}, bf16[32,1024]{1,0:T(8,128)(2,1)S(1)}, u32[]{:S(2)}, u32[]{:S(2)}) collective-permute-start(bf16[32,1024]{1,0:T(8,128)(2,1)S(1)} %get-tuple-element.44.own), channel_id=1, source_target_pairs={{0,1},{1,0},{2,3},{3,2},{4,5},{5,4},{6,7},{7,6},{8,9},{9,8},{10,11... | collective-permute-start | bytes 196616 | tf_op jit(solution)/shard_map/ppermute | solution.py:147
  43.6 4.5 %collective-permute-start.13 = (bf16[32,384]{1,0:T(8,128)(2,1)S(1)}, bf16[32,384]{1,0:T(8,128)(2,1)S(1)}, u32[]{:S(2)}, u32[]{:S(2)}) collective-permute-start(bf16[32,384]{1,0:T(8,128)(2,1)S(1)} %get-tuple-element.46), channel_id=1, source_target_pairs={{0,8},{4,12},{8,0},{12,4},{16,24},{20,28},{24,16},{28,20},{1,9},{5... | collective-permute-start | bytes 73736 | tf_op jit(solution)/shard_map/ppermute | solution.py:147
  43.7 5.2 %collective-permute-start.14 = (bf16[32,384]{1,0:T(8,128)(2,1)S(1)}, bf16[32,384]{1,0:T(8,128)(2,1)S(1)}, u32[]{:S(2)}, u32[]{:S(2)}) collective-permute-start(bf16[32,384]{1,0:T(8,128)(2,1)S(1)} %get-tuple-element.47), channel_id=1, source_target_pairs={{0,16},{4,20},{8,24},{12,28},{16,0},{20,4},{24,8},{28,12},{1,17},{... | collective-permute-start | bytes 73736 | tf_op jit(solution)/shard_map/ppermute | solution.py:147
  44.5 5.6 %collective-permute-start.15 = (bf16[32,384]{1,0:T(8,128)(2,1)S(1)}, bf16[32,384]{1,0:T(8,128)(2,1)S(1)}, u32[]{:S(2)}, u32[]{:S(2)}) collective-permute-start(bf16[32,384]{1,0:T(8,128)(2,1)S(1)} %get-tuple-element.48), channel_id=1, source_target_pairs={{0,24},{4,28},{8,16},{12,20},{16,8},{20,12},{24,0},{28,4},{1,25},{... | collective-permute-start | bytes 73736 | tf_op jit(solution)/shard_map/ppermute | solution.py:147
  50.1 4.1 %collective-permute-start.16 = (bf16[64,384]{1,0:T(8,128)(2,1)S(1)}, bf16[64,384]{1,0:T(8,128)(2,1)S(1)}, u32[]{:S(2)}, u32[]{:S(2)}) collective-permute-start(bf16[64,384]{1,0:T(8,128)(2,1)S(1)} %shard_map.156), channel_id=1, source_target_pairs={{0,4},{4,0},{8,12},{12,8},{16,20},{20,16},{24,28},{28,24},{1,5},{5... | collective-permute-start | bytes 147464 | tf_op jit(solution)/shard_map/ppermute | solution.py:147

commit v4 on v3

--- a/solution.py
+++ b/solution.py
@@ -126,6 +126,9 @@
     return (attended, layer_out)
 
 
+TP_ORDER = (0, 2, 3, 1)
+
+
 def spec(space=pltpu.VMEM):
     return pl.BlockSpec(memory_space=space)
 
@@ -197,15 +200,15 @@
     )
     place_req = lax.axis_index("req")
 
-    def pick(route, named):
+    def pick(route, named, mine):
         rank = jnp.sum(named * before, axis=0, keepdims=True).astype(jnp.int32)
-        block = ((route // slot_dev) ^ place_req) * slot_dev + lax.rem(route, slot_dev)
+        block = ((route // slot_dev) ^ mine) * slot_dev + lax.rem(route, slot_dev)
         return jnp.where(place == block * CAP + rank, 1.0, 0.0)
 
-    first, second = pick(route0, named0), pick(route1, named1)
-    pick_rows[...] = (first + second).astype(jnp.bfloat16)
-    pick0[...] = jnp.transpose(first).astype(jnp.bfloat16)
-    pick1[...] = jnp.transpose(second).astype(jnp.bfloat16)
+    sent_rows = pick(route0, named0, place_req) + pick(route1, named1, place_req)
+    pick_rows[...] = sent_rows.astype(jnp.bfloat16)
+    pick0[...] = jnp.transpose(pick(route0, named0, 0)).astype(jnp.bfloat16)
+    pick1[...] = jnp.transpose(pick(route1, named1, 0)).astype(jnp.bfloat16)
     signed = jnp.transpose(named0 - named1)
     small[1].wait()
     router_rows[...] = jnp.dot(
@@ -289,27 +292,28 @@
     for copy in copies[2 * chunks :]:
         copy.wait()
     place_tp = lax.axis_index("tp")
-    for shift, out in enumerate((own, sent1, sent2, sent3)):
+    for shift, out in zip(TP_ORDER, (own, sent1, sent2, sent3)):
         columns = pl.ds(pl.multiple_of((place_tp ^ shift) * width, width), width)
         out[...] = jnp.dot(
             attention, w_buf[:, columns], preferred_element_type=jnp.float32
         ).astype(out.dtype)
 
 
-def store_blocks(rows, home, sent1, sent2, sent3):
+def ready_kernel(own, resid, pick_rows, base, pick_near):
+    base[...] = own[...] + resid[...].astype(jnp.float32)
+    pick_near[...] = pick_rows[...]
+
+
+def pack_kernel(base, part1, part2, part3, pick_rows, attended, home, sent1, sent2, sent3):
+    total = base[...]
+    for part in (part1, part2, part3):
+        total = total + part[...].astype(jnp.float32)
+    rows = total.astype(jnp.bfloat16)
+    attended[...] = rows
+    packed = jnp.dot(pick_rows[...], rows, preferred_element_type=jnp.float32)
     size = home.shape[0]
     for distance, out in enumerate((home, sent1, sent2, sent3)):
-        out[...] = rows[distance * size : (distance + 1) * size].astype(out.dtype)
-
-
-def pack_kernel(own, part1, part2, part3, resid, pick_rows, attended, home, sent1, sent2, sent3):
-    total = own[...]
-    for part in (part1, part2, part3):
-        total = total + part[...].astype(jnp.float32)
-    rows = (resid[...].astype(jnp.float32) + total).astype(jnp.bfloat16)
-    attended[...] = rows
-    packed = jnp.dot(pick_rows[...], rows, preferred_element_type=jnp.float32)
-    store_blocks(packed, home, sent1, sent2, sent3)
+        out[...] = packed[distance * size : (distance + 1) * size].astype(out.dtype)
 
 
 def stats_kernel(attended, gain, router_rows, stats, result):
@@ -327,100 +331,99 @@
         along[index * half : (index + 1) * half, :] = part[half:, :]
 
 
-def two_hop(home, sents):
-    parts = [partner_permute(block, "req", 2 * k) for k, block in enumerate(sents, 1)]
-    (along,) = call(
-        turn_kernel,
-        [((2 * home.shape[0], home.shape[1]), home.dtype)],
-        [spec()] * 4,
-        (home, *parts),
-    )
-    return (home, *parts, partner_permute(along, "req", 1))
-
-
-def gather_blocks(refs, target):
-    *first_hop, second_hop = refs
-    half = first_hop[0].shape[0] // 2
-    for index, part in enumerate(first_hop):
-        start = 2 * index * half
-        target[start : start + half, :] = part[:half, :].astype(target.dtype)
-        target[start + half : start + 2 * half, :] = second_hop[
-            index * half : (index + 1) * half, :
-        ].astype(target.dtype)
-
-
 def slot_masks(row_count, slot_dev):
     slot = lax.rem(lax.broadcasted_iota(jnp.int32, (row_count, 1), 0) // CAP, slot_dev)
     return [slot == index for index in range(slot_dev)]
 
 
-def gate_kernel(
-    slot_dev, in0, in1, in2, in3, in4, gain, stats, w_gate, w_up,
-    own, sent1, sent2, sent3, incoming, lhs
-):
-    gather_blocks((in0, in1, in2, in3, in4), incoming)
-    quarter = own.shape[0]
-    width = incoming.shape[1]
+def split_high(column):
+    high = column.astype(jnp.bfloat16).astype(jnp.float32)
+    return high, column - high
+
+
+def gate_terms(slot_dev, blocks, gain, stats, w_gate, w_up, outs, lhs):
+    size = outs[0].shape[0]
+    width = blocks.shape[1]
     hidden = w_gate.shape[1]
     place_tp = lax.axis_index("tp")
-    masks = slot_masks(quarter, slot_dev)
-    lane = lax.broadcasted_iota(jnp.int32, (quarter, 128), 1)
-    extras = []
-    for shift in range(4):
-        rows = incoming[
-            pl.ds(pl.multiple_of((place_tp ^ shift) * quarter, quarter), quarter), :
+    masks = slot_masks(size, slot_dev)
+    lane = lax.broadcasted_iota(jnp.int32, (size, 128), 1)
+    for order, (shift, out) in enumerate(zip(TP_ORDER, outs)):
+        rows = blocks[
+            pl.ds(pl.multiple_of((place_tp ^ shift) * size, size), size), :
         ].astype(jnp.float32)
-        columns = [
-            jnp.sum(rows * rows, axis=1, keepdims=True),
-            stats[:, 0:1],
-            stats[:, 1:2],
-        ]
-        extra = jnp.zeros((quarter, 128), jnp.float32)
+        columns = [jnp.sum(rows * rows, axis=1, keepdims=True)]
+        if stats is not None:
+            for first in range(0, stats.shape[0], size):
+                columns += [stats[first : first + size, 0:1], stats[first : first + size, 1:2]]
+        extra = jnp.zeros((size, 128), jnp.float32)
         for index, column in enumerate(columns):
-            high = column.astype(jnp.bfloat16).astype(jnp.float32)
+            high, low = split_high(column)
             extra = jnp.where(lane == 2 * index, high, extra)
-            extra = jnp.where(lane == 2 * index + 1, column - high, extra)
-        extras.append(extra)
+            extra = jnp.where(lane == 2 * index + 1, low, extra)
+        out[:, 2 * hidden :] = extra.astype(out.dtype)
         scaled = rows * gain[...]
         for index, mask in enumerate(masks):
-            lhs[shift * quarter : (shift + 1) * quarter, index * width : (index + 1) * width] = (
+            lhs[order * size : (order + 1) * size, index * width : (index + 1) * width] = (
                 jnp.where(mask, scaled, 0.0).astype(jnp.bfloat16)
             )
     left = lhs[...]
-    outs = (own, sent1, sent2, sent3)
     for first, weight in ((0, w_gate), (hidden, w_up)):
         product = jnp.dot(left, weight[...], preferred_element_type=jnp.float32)
-        for shift, out in enumerate(outs):
-            out[:, first : first + hidden] = product[
-                shift * quarter : (shift + 1) * quarter
-            ].astype(out.dtype)
-    for extra, out in zip(extras, outs):
-        out[:, 2 * hidden :] = extra.astype(out.dtype)
-
-
-def hidden_kernel(own, part1, part2, part3, hidden, first_weight):
+        for order, out in enumerate(outs):
+            out[:, first : first + hidden] = product[order * size : (order + 1) * size].astype(
+                out.dtype
+            )
+
+
+def early_kernel(slot_dev, in0, in1, in2, in3, gain, w_gate, w_up, *refs):
+    *outs, blocks, lhs = refs
+    half = outs[0].shape[0]
+    for index, part in enumerate((in0, in1, in2, in3)):
+        blocks[index * half : (index + 1) * half, :] = part[:half, :]
+    gate_terms(slot_dev, blocks, gain, None, w_gate, w_up, outs, lhs)
+
+
+def late_kernel(slot_dev, blocks, gain, stats, w_gate, w_up, *refs):
+    *outs, lhs = refs
+    gate_terms(slot_dev, blocks, gain, stats, w_gate, w_up, outs, lhs)
+
+
+def hidden_kernel(*refs):
+    early, late, (hidden, first_weight) = refs[:4], refs[4:8], refs[8:]
     width = hidden.shape[1]
-
-    def total(first, size):
-        columns = slice(first, first + size)
-        result = own[:, columns]
-        for part in (part1, part2, part3):
+    half = hidden.shape[0] // 2
+
+    def total(parts, columns):
+        result = parts[0][:, columns]
+        for part in parts[1:]:
             result = result + part[:, columns].astype(jnp.float32)
         return result
 
-    extra = total(2 * width, 128)
-    row_inv = 1.0 / jnp.sqrt((extra[:, 0:1] + extra[:, 1:2]) / D + 1e-06)
-    gate = total(0, width) * row_inv
-    up = total(width, width) * row_inv
-    hidden[...] = (gate / (1.0 + jnp.exp(-gate)) * up).astype(jnp.bfloat16)
-    inv_rms = 1.0 / jnp.sqrt((extra[:, 2:3] + extra[:, 3:4]) / D + 1e-06)
-    logit = (extra[:, 4:5] + extra[:, 5:6]) * inv_rms
-    first_weight[...] = jnp.broadcast_to(1.0 / (1.0 + jnp.exp(-logit)), first_weight.shape)
-
-
-def down_kernel(slot_dev, own, part1, part2, part3, w_down, home, sent1, sent2, sent3, lhs):
+    def inverse_rms(columns, index):
+        square = columns[:, index : index + 1] + columns[:, index + 1 : index + 2]
+        return 1.0 / jnp.sqrt(square / D + 1e-06)
+
+    for index, parts in enumerate((early, late)):
+        extra = total(parts, slice(2 * width, 2 * width + 128))
+        row_inv = inverse_rms(extra, 0)
+        gate = total(parts, slice(0, width)) * row_inv
+        up = total(parts, slice(width, 2 * width)) * row_inv
+        hidden[index * half : (index + 1) * half, :] = (
+            gate / (1.0 + jnp.exp(-gate)) * up
+        ).astype(jnp.bfloat16)
+    for index in range(first_weight.shape[0] // half):
+        place = 2 + 4 * index
+        logit = extra[:, place + 2 : place + 3] + extra[:, place + 3 : place + 4]
+        weight = 1.0 / (1.0 + jnp.exp(-logit * inverse_rms(extra, place)))
+        first_weight[index * half : (index + 1) * half, :] = jnp.broadcast_to(weight, (half, 128))
+
+
+def down_kernel(slot_dev, own, part1, part2, part3, w_down, computed, lhs):
     quarter, width = own.shape
+    block = computed.shape[1]
     place_tp = lax.axis_index("tp")
+    place_req = lax.axis_index("req")
     masks = slot_masks(quarter, slot_dev)
     for shift, part in enumerate((own, part1, part2, part3)):
         rows = part[...].astype(jnp.float32)
@@ -429,14 +432,14 @@
             lhs[place, index * width : (index + 1) * width] = jnp.where(mask, rows, 0.0).astype(
                 jnp.bfloat16
             )
-    computed = jnp.dot(lhs[...], w_down[...], preferred_element_type=jnp.float32)
-    store_blocks(computed, home, sent1, sent2, sent3)
-
-
-def combine_kernel(
-    in0, in1, in2, in3, in4, pick0, pick1, first_weight, attended, layer_out, returned
-):
-    gather_blocks((in0, in1, in2, in3, in4), returned)
+    product = jnp.dot(lhs[...], w_down[...], preferred_element_type=jnp.float32)
+    for index in range(computed.shape[0]):
+        computed[place_req ^ index] = product[index * block : (index + 1) * block].astype(
+            computed.dtype
+        )
+
+
+def combine_kernel(returned, pick0, pick1, first_weight, attended, layer_out):
     rows = returned[...]
     out0 = jnp.dot(pick0[...], rows, preferred_element_type=jnp.float32)
     out1 = jnp.dot(pick1[...], rows, preferred_element_type=jnp.float32)
@@ -517,13 +520,21 @@
         flops=200_000_000,
         moved=3_400_000,
     )
-    parts = [partner_permute(block, "tp", k) for k, block in enumerate((sent1, sent2, sent3), 1)]
-    block = ((quarter, width), bf16)
+    def sum_exchange(sents):
+        return [partner_permute(block, "tp", k) for k, block in zip(TP_ORDER[1:], sents)]
+
+    parts = sum_exchange((sent1, sent2, sent3))
+    base, pick_near = call(
+        ready_kernel,
+        [((row_count, width), f32), ((packed_count, row_count), bf16)],
+        [spec()] * 3,
+        (own, resid, pick_rows),
+    )
     attended, home, *sents = call(
         pack_kernel,
-        [((row_count, width), bf16)] + [block] * 4,
-        [spec()] * 6,
-        (own, *parts, resid, pick_rows),
+        [((row_count, width), bf16)] + [((quarter, width), bf16)] * 4,
+        [spec()] * 5,
+        (base, *parts, pick_near),
     )
     stats, result = call(
         stats_kernel,
@@ -531,49 +542,58 @@
         [spec()] * 3,
         (attended, gain, router_rows),
     )
-    message = (quarter, 2 * hidden + 128)
-    own, sent1, sent2, sent3 = call(
-        functools.partial(gate_kernel, slot_dev),
-        [(message, f32), (message, bf16), (message, bf16), (message, bf16)],
-        [spec()] * 9,
-        (
-            *two_hop(home, sents),
-            gain,
-            stats,
-            w_gate.reshape(slot_dev * width, hidden),
-            w_up.reshape(slot_dev * width, hidden),
-        ),
-        scratch=[
-            pltpu.VMEM((packed_count, width), bf16),
-            pltpu.VMEM((packed_count, slot_dev * width), bf16),
-        ],
-        mebibytes=12,
-        flops=800_000_000,
-        moved=4_000_000,
-    )
-    parts = [partner_permute(block, "tp", k) for k, block in enumerate((sent1, sent2, sent3), 1)]
+    parts = [partner_permute(block, "req", 2 * k) for k, block in enumerate(sents, 1)]
+    (along,) = call(
+        turn_kernel, [((2 * quarter, width), bf16)], [spec()] * 4, (home, *parts)
+    )
+    along = partner_permute(along, "req", 1)
+    weights = (w_gate.reshape(slot_dev * width, hidden), w_up.reshape(slot_dev * width, hidden))
+    half = quarter // 2
+    message = (half, 2 * hidden + 128)
+    messages = [(message, f32)] + [(message, bf16)] * 3
+    lhs = pltpu.VMEM((packed_count // 2, slot_dev * width), bf16)
+    early, *sents = call(
+        functools.partial(early_kernel, slot_dev),
+        messages,
+        [spec()] * 7,
+        (home, *parts, gain, *weights),
+        scratch=[pltpu.VMEM((2 * quarter, width), bf16), lhs],
+        flops=400_000_000,
+        moved=3_500_000,
+    )
+    early = (early, *sum_exchange(sents))
+    late, *sents = call(
+        functools.partial(late_kernel, slot_dev),
+        messages,
+        [spec()] * 5,
+        (along, gain, stats, *weights),
+        scratch=[lhs],
+        flops=400_000_000,
+        moved=3_500_000,
+    )
+    late = (late, *sum_exchange(sents))
     own, first_weight = call(
         hidden_kernel,
         [((quarter, hidden), bf16), ((row_count, 128), f32)],
-        [spec()] * 4,
-        (own, *parts),
+        [spec()] * 8,
+        (*early, *late),
     )
     parts = [partner_permute(own, "tp", k) for k in (1, 2, 3)]
-    home, *sents = call(
+    (computed,) = call(
         functools.partial(down_kernel, slot_dev),
-        [block] * 4,
+        [((8, packed_count // 8, width), bf16)],
         [spec()] * 5,
         (own, *parts, w_down.reshape(slot_dev * hidden, width)),
         scratch=[pltpu.VMEM((packed_count, slot_dev * hidden), bf16)],
         flops=200_000_000,
         moved=2_000_000,
     )
+    returned = lax.all_to_all(computed, "req", split_axis=0, concat_axis=0, tiled=True)
     (layer_out,) = call(
         combine_kernel,
         [((row_count, width), bf16)],
-        [spec()] * 9,
-        (*two_hop(home, sents), pick0, pick1, first_weight, attended),
-        scratch=[pltpu.VMEM((packed_count, width), bf16)],
+        [spec()] * 5,
+        (returned.reshape(packed_count, width), pick0, pick1, first_weight, attended),
     )
     return (result, layer_out)
 

time: 55.3 us -> 50.2 us (0.908)
  waiting for transfers between devices: 25.2 us -> 14 us
  blocking collectives: 0 us -> 9.51 us
  starting transfers between devices: 19 us -> 15.6 us
  local copies, waits for them, and re-layouts: 2.39 us -> 1.59 us
  Pallas kernels: 7.67 us -> 8.39 us
    ppermute x17 -> x16, waiting for transfers between devices: 25.2 us -> 14 us  [partner_permute(): return lax.ppermute(block, axis, [(i, i ^ distance) for i in range(count)])]
    all_to_all x0 -> x1, blocking collectives: none -> 9.51 us  [shards(): lax.all_to_all(computed, 'req', split_axis=0, concat_axis=0, tiled=True)]
    ppermute x17 -> x16, starting transfers between devices: 19 us -> 15.6 us  [partner_permute(): return lax.ppermute(block, axis, [(i, i ^ distance) for i in range(count)])]
    unnamed x20, local copies, waits for them, and re-layouts: 2.38 us -> 1.59 us
    pallas_call x9 -> x10, Pallas kernels: 7.67 us -> 8.39 us  [call(): pl.pallas_call(kernel, out_shape=[jax.ShapeDtypeStruct(shape, dtype) for...]
  transfers between devices with their start and end apart: 17 -> 16, of which waited for: 12 -> 9; matrix products, arithmetic and copies ran while one was open for 0% -> 0% of each run, Pallas kernels for 1% -> 4%
where the time goes in v4:
time: 50.2 us; the launch traced here: 49.9 us
  starting transfers between devices  15.6 us (31%)
  waiting for transfers between devices  14 us (28%)
  blocking collectives  9.51 us (19%)
  Pallas kernels  8.39 us (17%)
  local copies, waits for them, and re-layouts  1.59 us (3%)
  between operations  0.75 us (1%)
    ppermute x16, starting transfers between devices, partner_permute(): return lax.ppermute(block, axis, [(i, i ^ distance) for i in range(count)])  15.6 us
    ppermute x16, waiting for transfers between devices, partner_permute(): return lax.ppermute(block, axis, [(i, i ^ distance) for i in range(count)])  14 us
    all_to_all x1, blocking collectives, shards(): lax.all_to_all(computed, 'req', split_axis=0, concat_axis=0, tiled=True)  9.51 us
    pallas_call x10, Pallas kernels, call(): pl.pallas_call(kernel, out_shape=[jax.ShapeDtypeStruct(shape, dtype) for...  8.39 us
    unnamed x20, local copies, waits for them, and re-layouts  1.59 us
  transfers between devices with their start and end apart: 16, of which 9 were waited for; matrix products, arithmetic and copies ran while one was open for 0% of the time, Pallas kernels for 4%

profile of v4, /device:TPU:0, one launch (start us, length us, event | category | flops | bytes accessed | tf_op | source)
XLA Modules:
  0.0 49.9 jit_solution(9798822731759116152)
XLA Ops:
  0.7 4.8 %shard_map.149 = (f32[32,384]{1,0:T(8,128)}, bf16[32,384]{1,0:T(8,128)(2,1)}, bf16[32,384]{1,0:T(8,128)(2,1)}, bf16[32,384]{1,0:T(8,128)(2,1)}, bf16[32,128]{1,0...) custom-call(s32[32]{0:T(128)} %lengths_hbm.1, s32[2,32]{1,0:T(2,128)} %bitcast.13, ...), custom_call_target="tpu_custom_call" | custom-call | flops 200000000 | bytes 3400000 | tf_op jit(solution)/shard_map/pallas_call | solution.py:137
  5.4 3.0 %collective-permute-start = (bf16[32,384]{1,0:T(8,128)(2,1)}, bf16[32,384]{1,0:T(8,128)(2,1)S(1)}, u32[]{:S(2)}, u32[]{:S(2)}) collective-permute-start(bf16[32,384]{1,0:T(8,128)(2,1)} %get-tuple-element.32), channel_id=1, source_target_pairs={{0,2},{1,3},{2,0},{3,1},{4,6},{5,7},{6,4},{7,5},{8,10},{9,11},{10,... | collective-permute-start | bytes 73736 | tf_op jit(solution)/shard_map/ppermute | solution.py:150
  8.5 0.2 collective-permute-start.2
  8.7 0.8 %copy-done.4 = f32[32,384]{1,0:T(8,128)S(1)} copy-done((f32[32,384]{1,0:T(8,128)S(1)}, f32[32,384]{1,0:T(8,128)}, u32[]{:S(2)}) %copy-start.4) | copy-done | bytes 49176
  9.5 0.8 %copy-done.5 = bf16[128,32]{1,0:T(8,128)(2,1)S(1)} copy-done((bf16[128,32]{1,0:T(8,128)(2,1)S(1)}, bf16[128,32]{1,0:T(8,128)(2,1)}, u32[]{:S(2)}) %copy-start.5) | copy-done | bytes 8216
  10.2 0.2 collective-permute-done.part1
  10.5 1.4 %collective-permute-done.1.part2 = bf16[32,384]{1,0:T(8,128)(2,1)S(1)} collective-permute-done((bf16[32,384]{1,0:T(8,128)(2,1)}, bf16[32,384]{1,0:T(8,128)(2,1)S(1)}, u32[]{:S(2)}, u32[]{:S(2)}) %collective-permute-start.1) | collective-permute-done | bytes 24608 | tf_op jit(solution)/shard_map/ppermute | solution.py:150
  11.9 0.2 shard_map.151
  12.1 1.6 %collective-permute-start.3 = (bf16[32,384]{1,0:T(8,128)(2,1)S(1)}, bf16[32,384]{1,0:T(8,128)(2,1)S(1)}, u32[]{:S(2)}, u32[]{:S(2)}) collective-permute-start(bf16[32,384]{1,0:T(8,128)(2,1)S(1)} %get-tuple-element.40), channel_id=1, source_target_pairs={{0,8},{4,12},{8,0},{12,4},{16,24},{20,28},{24,16},{28,20},{1,9},{5... | collective-permute-start | bytes 73736 | tf_op jit(solution)/shard_map/ppermute | solution.py:150
  13.7 2.6 %collective-permute-start.4 = (bf16[32,384]{1,0:T(8,128)(2,1)S(1)}, bf16[32,384]{1,0:T(8,128)(2,1)S(1)}, u32[]{:S(2)}, u32[]{:S(2)}) collective-permute-start(bf16[32,384]{1,0:T(8,128)(2,1)S(1)} %get-tuple-element.41), channel_id=1, source_target_pairs={{0,16},{4,20},{8,24},{12,28},{16,0},{20,4},{24,8},{28,12},{1,17},{... | collective-permute-start | bytes 73736 | tf_op jit(solution)/shard_map/ppermute | solution.py:150
  16.3 0.2 collective-permute-start.5
  16.5 2.1 %collective-permute-done.4.in2.part2 = bf16[32,384]{1,0:T(8,128)(2,1)S(1)} collective-permute-done((bf16[32,384]{1,0:T(8,128)(2,1)S(1)}, bf16[32,384]{1,0:T(8,128)(2,1)S(1)}, u32[]{:S(2)}, u32[]{:S(2)}) %collective-permute-start.4) | collective-permute-done | bytes 24608 | tf_op jit(solution)/shard_map/ppermute | solution.py:150
  18.6 3.3 %collective-permute-done.5.in3.part3 = bf16[32,384]{1,0:T(8,128)(2,1)S(1)} collective-permute-done((bf16[32,384]{1,0:T(8,128)(2,1)S(1)}, bf16[32,384]{1,0:T(8,128)(2,1)S(1)}, u32[]{:S(2)}, u32[]{:S(2)}) %collective-permute-start.5) | collective-permute-done | bytes 24608 | tf_op jit(solution)/shard_map/ppermute | solution.py:150
  21.9 1.5 %collective-permute-start.9 = (bf16[64,384]{1,0:T(8,128)(2,1)S(1)}, bf16[64,384]{1,0:T(8,128)(2,1)S(1)}, u32[]{:S(2)}, u32[]{:S(2)}) collective-permute-start(bf16[64,384]{1,0:T(8,128)(2,1)S(1)} %shard_map.154), channel_id=1, source_target_pairs={{0,4},{4,0},{8,12},{12,8},{16,20},{20,16},{24,28},{28,24},{1,5},{5... | collective-permute-start | bytes 147464 | tf_op jit(solution)/shard_map/ppermute | solution.py:150
  23.5 0.7 %shard_map.153 = (f32[16,2176]{1,0:T(8,128)S(1)}, bf16[16,2176]{1,0:T(8,128)(2,1)S(1)}, bf16[16,2176]{1,0:T(8,128)(2,1)S(1)}, bf16[16,2176]{1,0:T(8,128)(2,1)S(1)}) custom-call(bf16[32,384]{1,0:T(8,128)(2,1)S(1)} %get-tuple-element.39.in0.home, bf16[32,384]{1,0:T(8,128)(2,1)S(1)} %collective-permute-done.3.in1.part1, ...), custom_call_target="tpu_custom_call" | custom-call | flops 400000000 | bytes 3500000 | tf_op jit(solution)/shard_map/pallas_call | solution.py:137
  24.1 0.9 %collective-permute-start.6 = (bf16[16,2176]{1,0:T(8,128)(2,1)S(1)}, bf16[16,2176]{1,0:T(8,128)(2,1)S(1)}, u32[]{:S(2)}, u32[]{:S(2)}) collective-permute-start(bf16[16,2176]{1,0:T(8,128)(2,1)S(1)} %get-tuple-element.44), channel_id=1, source_target_pairs={{0,2},{1,3},{2,0},{3,1},{4,6},{5,7},{6,4},{7,5},{8,10},{9,11},{10,... | collective-permute-start | bytes 208904 | tf_op jit(solution)/shard_map/ppermute | solution.py:150
  25.0 0.6 %shard_map.152 = (f32[32,128]{1,0:T(8,128)S(1)}, bf16[32,384]{1,0:T(8,128)(2,1)}) custom-call(bf16[32,384]{1,0:T(8,128)(2,1)S(1)} %get-tuple-element.36.attended, f32[1,384]{1,0:T(1,128)S(1)} %reshape.19.gain, f32[32,384]{1,0:T(8,128)S(1)} %copy-done.3), custom_call_target="tpu_custom_call" | custom-call | flops 100000 | bytes 100000 | tf_op jit(solution)/shard_map/pallas_call | solution.py:137
  25.6 1.3 %collective-permute-start.8 = (bf16[16,2176]{1,0:T(8,128)(2,1)S(1)}, bf16[16,2176]{1,0:T(8,128)(2,1)S(1)}, u32[]{:S(2)}, u32[]{:S(2)}) collective-permute-start(bf16[16,2176]{1,0:T(8,128)(2,1)S(1)} %get-tuple-element.46), channel_id=1, source_target_pairs={{0,1},{1,0},{2,3},{3,2},{4,5},{5,4},{6,7},{7,6},{8,9},{9,8},{10,11... | collective-permute-start | bytes 208904 | tf_op jit(solution)/shard_map/ppermute | solution.py:150
  27.0 0.7 %shard_map.155 = (f32[16,2176]{1,0:T(8,128)S(1)}, bf16[16,2176]{1,0:T(8,128)(2,1)S(1)}, bf16[16,2176]{1,0:T(8,128)(2,1)S(1)}, bf16[16,2176]{1,0:T(8,128)(2,1)S(1)}) custom-call(bf16[64,384]{1,0:T(8,128)(2,1)S(1)} %collective-permute-done.9.blocks, f32[1,384]{1,0:T(1,128)S(1)} %reshape.19.gain, f32[32,128]{1,0:T(8,128)S(1)} %get-tuple-element.47.stats, ...), custom_call_target="tpu_custom_call" | custom-call | flops 400000000 | bytes 3500000 | tf_op jit(solution)/shard_map/pallas_call | solution.py:137
  27.7 0.9 %collective-permute-start.10 = (bf16[16,2176]{1,0:T(8,128)(2,1)S(1)}, bf16[16,2176]{1,0:T(8,128)(2,1)S(1)}, u32[]{:S(2)}, u32[]{:S(2)}) collective-permute-start(bf16[16,2176]{1,0:T(8,128)(2,1)S(1)} %get-tuple-element.49), channel_id=1, source_target_pairs={{0,2},{1,3},{2,0},{3,1},{4,6},{5,7},{6,4},{7,5},{8,10},{9,11},{10,... | collective-permute-start | bytes 208904 | tf_op jit(solution)/shard_map/ppermute | solution.py:150
  28.6 0.6 %collective-permute-start.11 = (bf16[16,2176]{1,0:T(8,128)(2,1)S(1)}, bf16[16,2176]{1,0:T(8,128)(2,1)S(1)}, u32[]{:S(2)}, u32[]{:S(2)}) collective-permute-start(bf16[16,2176]{1,0:T(8,128)(2,1)S(1)} %get-tuple-element.50), channel_id=1, source_target_pairs={{0,3},{1,2},{2,1},{3,0},{4,7},{5,6},{6,5},{7,4},{8,11},{9,10},{10,... | collective-permute-start | bytes 208904 | tf_op jit(solution)/shard_map/ppermute | solution.py:150
  29.1 0.8 %collective-permute-start.12 = (bf16[16,2176]{1,0:T(8,128)(2,1)S(1)}, bf16[16,2176]{1,0:T(8,128)(2,1)S(1)}, u32[]{:S(2)}, u32[]{:S(2)}) collective-permute-start(bf16[16,2176]{1,0:T(8,128)(2,1)S(1)} %get-tuple-element.51), channel_id=1, source_target_pairs={{0,1},{1,0},{2,3},{3,2},{4,5},{5,4},{6,7},{7,6},{8,9},{9,8},{10,11... | collective-permute-start | bytes 208904 | tf_op jit(solution)/shard_map/ppermute | solution.py:150
  30.0 2.6 %collective-permute-done.10.refs_5_ = bf16[16,2176]{1,0:T(8,128)(2,1)S(1)} collective-permute-done((bf16[16,2176]{1,0:T(8,128)(2,1)S(1)}, bf16[16,2176]{1,0:T(8,128)(2,1)S(1)}, u32[]{:S(2)}, u32[]{:S(2)}) %collective-permute-start.10) | collective-permute-done | bytes 69664 | tf_op jit(solution)/shard_map/ppermute | solution.py:150
  32.6 0.4 collective-permute-done.11.refs_6_
  33.0 0.3 shard_map.156
  33.3 0.9 %collective-permute-start.15 = (bf16[32,1024]{1,0:T(8,128)(2,1)S(1)}, bf16[32,1024]{1,0:T(8,128)(2,1)S(1)}, u32[]{:S(2)}, u32[]{:S(2)}) collective-permute-start(bf16[32,1024]{1,0:T(8,128)(2,1)S(1)} %get-tuple-element.52.own), channel_id=1, source_target_pairs={{0,3},{1,2},{2,1},{3,0},{4,7},{5,6},{6,5},{7,4},{8,11},{9,10},{10,... | collective-permute-start | bytes 196616 | tf_op jit(solution)/shard_map/ppermute | solution.py:150
  34.2 1.1 %collective-permute-start.14 = (bf16[32,1024]{1,0:T(8,128)(2,1)S(1)}, bf16[32,1024]{1,0:T(8,128)(2,1)S(1)}, u32[]{:S(2)}, u32[]{:S(2)}) collective-permute-start(bf16[32,1024]{1,0:T(8,128)(2,1)S(1)} %get-tuple-element.52.own), channel_id=1, source_target_pairs={{0,2},{1,3},{2,0},{3,1},{4,6},{5,7},{6,4},{7,5},{8,10},{9,11},{10,... | collective-permute-start | bytes 196616 | tf_op jit(solution)/shard_map/ppermute | solution.py:150
  35.3 2.0 %collective-permute-done.15.part3 = bf16[32,1024]{1,0:T(8,128)(2,1)S(1)} collective-permute-done((bf16[32,1024]{1,0:T(8,128)(2,1)S(1)}, bf16[32,1024]{1,0:T(8,128)(2,1)S(1)}, u32[]{:S(2)}, u32[]{:S(2)}) %collective-permute-start.15) | collective-permute-done | bytes 65568 | tf_op jit(solution)/shard_map/ppermute | solution.py:150
  37.3 1.9 %collective-permute-done.14.part2 = bf16[32,1024]{1,0:T(8,128)(2,1)S(1)} collective-permute-done((bf16[32,1024]{1,0:T(8,128)(2,1)S(1)}, bf16[32,1024]{1,0:T(8,128)(2,1)S(1)}, u32[]{:S(2)}, u32[]{:S(2)}) %collective-permute-start.14) | collective-permute-done | bytes 65568 | tf_op jit(solution)/shard_map/ppermute | solution.py:150
  39.1 0.5 shard_map.157
  39.6 9.5 %all_to_all.5 = bf16[8,16,384]{2,1,0:T(8,128)(2,1)S(1)} all-to-all(bf16[8,16,384]{2,1,0:T(8,128)(2,1)S(1)} %shard_map.157), channel_id=1, replica_groups=mesh['req'=8,'tp'=4] {'req'}, dimensions={0} | all-to-all | bytes 196608 | tf_op jit(solution)/shard_map/all_to_all | solution.py:591
  49.1 0.8 %shard_map.158 = bf16[32,384]{1,0:T(8,128)(2,1)} custom-call(bf16[128,384]{1,0:T(8,128)(2,1)S(1)} %bitcast.11, bf16[32,128]{1,0:T(8,128)(2,1)S(1)} %copy-done.7, bf16[32,128]{1,0:T(8,128)(2,1)S(1)} %copy-done.8, f32[32,128]{1,0:T(8,128)S(1)} %get-tuple-element.55.first_weight, bf16[32,384]{1,0:T(8,128)(2,1)S(1)} %get-tuple-element.36.attended), custom_call_target="tpu_custom_call" | custom-call | flops 100000 | bytes 100000 | tf_op jit(solution)/shard_map/pallas_call | solution.py:137
  (32 shorter events, 0.2 us)
Async XLA Ops:
  0.6 8.0 %copy-start.6 = (bf16[32,384]{1,0:T(8,128)(2,1)S(1)}, bf16[32,384]{1,0:T(8,128)(2,1)}, u32[]{:S(2)}) copy-start(bf16[32,384]{1,0:T(8,128)(2,1)} %resid.1) | copy-start | bytes 73732
  0.6 15.9 %copy-start.9 = (f32[384]{0:T(512)S(1)}, f32[384]{0:T(512)}, u32[]{:S(2)}) copy-start(f32[384]{0:T(512)} %param.22) | copy-start | bytes 4612
  0.7 22.8 %copy-start = (bf16[2,384,1024]{2,1,0:T(8,128)(2,1)S(1)}, bf16[2,384,1024]{2,1,0:T(8,128)(2,1)}, u32[]{:S(2)}) copy-start(bf16[2,384,1024]{2,1,0:T(8,128)(2,1)} %param.25) | copy-start | bytes 4718596
  0.7 22.8 %copy-start.1 = (bf16[2,384,1024]{2,1,0:T(8,128)(2,1)S(1)}, bf16[2,384,1024]{2,1,0:T(8,128)(2,1)}, u32[]{:S(2)}) copy-start(bf16[2,384,1024]{2,1,0:T(8,128)(2,1)} %param.26) | copy-start | bytes 4718596
  5.4 5.0 %collective-permute-start = (bf16[32,384]{1,0:T(8,128)(2,1)}, bf16[32,384]{1,0:T(8,128)(2,1)S(1)}, u32[]{:S(2)}, u32[]{:S(2)}) collective-permute-start(bf16[32,384]{1,0:T(8,128)(2,1)} %get-tuple-element.32), channel_id=1, source_target_pairs={{0,2},{1,3},{2,0},{3,1},{4,6},{5,7},{6,4},{7,5},{8,10},{9,11},{10,... | collective-permute-start | bytes 73736 | tf_op jit(solution)/shard_map/ppermute | solution.py:150
  8.5 3.5 %collective-permute-start.1 = (bf16[32,384]{1,0:T(8,128)(2,1)}, bf16[32,384]{1,0:T(8,128)(2,1)S(1)}, u32[]{:S(2)}, u32[]{:S(2)}) collective-permute-start(bf16[32,384]{1,0:T(8,128)(2,1)} %get-tuple-element.33), channel_id=1, source_target_pairs={{0,3},{1,2},{2,1},{3,0},{4,7},{5,6},{6,5},{7,4},{8,11},{9,10},{10,... | collective-permute-start | bytes 73736 | tf_op jit(solution)/shard_map/ppermute | solution.py:150
  8.5 3.5 %collective-permute-start.2 = (bf16[32,384]{1,0:T(8,128)(2,1)}, bf16[32,384]{1,0:T(8,128)(2,1)S(1)}, u32[]{:S(2)}, u32[]{:S(2)}) collective-permute-start(bf16[32,384]{1,0:T(8,128)(2,1)} %get-tuple-element.34), channel_id=1, source_target_pairs={{0,1},{1,0},{2,3},{3,2},{4,5},{5,4},{6,7},{7,6},{8,9},{9,8},{10,11... | collective-permute-start | bytes 73736 | tf_op jit(solution)/shard_map/ppermute | solution.py:150
  8.6 0.8 %copy-start.4 = (f32[32,384]{1,0:T(8,128)S(1)}, f32[32,384]{1,0:T(8,128)}, u32[]{:S(2)}) copy-start(f32[32,384]{1,0:T(8,128)} %get-tuple-element.29.own) | copy-start | bytes 147460
  9.4 0.8 %copy-start.5 = (bf16[128,32]{1,0:T(8,128)(2,1)S(1)}, bf16[128,32]{1,0:T(8,128)(2,1)}, u32[]{:S(2)}) copy-start(bf16[128,32]{1,0:T(8,128)(2,1)} %get-tuple-element.30.pick_rows) | copy-start | bytes 24580
  12.1 4.5 %collective-permute-start.3 = (bf16[32,384]{1,0:T(8,128)(2,1)S(1)}, bf16[32,384]{1,0:T(8,128)(2,1)S(1)}, u32[]{:S(2)}, u32[]{:S(2)}) collective-permute-start(bf16[32,384]{1,0:T(8,128)(2,1)S(1)} %get-tuple-element.40), channel_id=1, source_target_pairs={{0,8},{4,12},{8,0},{12,4},{16,24},{20,28},{24,16},{28,20},{1,9},{5... | collective-permute-start | bytes 73736 | tf_op jit(solution)/shard_map/ppermute | solution.py:150
  13.7 4.9 %collective-permute-start.4 = (bf16[32,384]{1,0:T(8,128)(2,1)S(1)}, bf16[32,384]{1,0:T(8,128)(2,1)S(1)}, u32[]{:S(2)}, u32[]{:S(2)}) collective-permute-start(bf16[32,384]{1,0:T(8,128)(2,1)S(1)} %get-tuple-element.41), channel_id=1, source_target_pairs={{0,16},{4,20},{8,24},{12,28},{16,0},{20,4},{24,8},{28,12},{1,17},{... | collective-permute-start | bytes 73736 | tf_op jit(solution)/shard_map/ppermute | solution.py:150
  16.3 5.6 %collective-permute-start.5 = (bf16[32,384]{1,0:T(8,128)(2,1)S(1)}, bf16[32,384]{1,0:T(8,128)(2,1)S(1)}, u32[]{:S(2)}, u32[]{:S(2)}) collective-permute-start(bf16[32,384]{1,0:T(8,128)(2,1)S(1)} %get-tuple-element.42), channel_id=1, source_target_pairs={{0,24},{4,28},{8,16},{12,20},{16,8},{20,12},{24,0},{28,4},{1,25},{... | collective-permute-start | bytes 73736 | tf_op jit(solution)/shard_map/ppermute | solution.py:150
  21.9 5.0 %collective-permute-start.9 = (bf16[64,384]{1,0:T(8,128)(2,1)S(1)}, bf16[64,384]{1,0:T(8,128)(2,1)S(1)}, u32[]{:S(2)}, u32[]{:S(2)}) collective-permute-start(bf16[64,384]{1,0:T(8,128)(2,1)S(1)} %shard_map.154), channel_id=1, source_target_pairs={{0,4},{4,0},{8,12},{12,8},{16,20},{20,16},{24,28},{28,24},{1,5},{5... | collective-permute-start | bytes 147464 | tf_op jit(solution)/shard_map/ppermute | solution.py:150
  23.5 1.5 %copy-start.3 = (f32[32,384]{1,0:T(8,128)S(1)}, f32[32,384]{1,0:T(8,128)}, u32[]{:S(2)}) copy-start(f32[32,384]{1,0:T(8,128)} %get-tuple-element.37.router_rows) | copy-start | bytes 147460
  24.1 5.0 %collective-permute-start.6 = (bf16[16,2176]{1,0:T(8,128)(2,1)S(1)}, bf16[16,2176]{1,0:T(8,128)(2,1)S(1)}, u32[]{:S(2)}, u32[]{:S(2)}) collective-permute-start(bf16[16,2176]{1,0:T(8,128)(2,1)S(1)} %get-tuple-element.44), channel_id=1, source_target_pairs={{0,2},{1,3},{2,0},{3,1},{4,6},{5,7},{6,4},{7,5},{8,10},{9,11},{10,... | collective-permute-start | bytes 208904 | tf_op jit(solution)/shard_map/ppermute | solution.py:150
  25.6 4.4 %collective-permute-start.7 = (bf16[16,2176]{1,0:T(8,128)(2,1)S(1)}, bf16[16,2176]{1,0:T(8,128)(2,1)S(1)}, u32[]{:S(2)}, u32[]{:S(2)}) collective-permute-start(bf16[16,2176]{1,0:T(8,128)(2,1)S(1)} %get-tuple-element.45), channel_id=1, source_target_pairs={{0,3},{1,2},{2,1},{3,0},{4,7},{5,6},{6,5},{7,4},{8,11},{9,10},{10,... | collective-permute-start | bytes 208904 | tf_op jit(solution)/shard_map/ppermute | solution.py:150
  25.6 4.4 %collective-permute-start.8 = (bf16[16,2176]{1,0:T(8,128)(2,1)S(1)}, bf16[16,2176]{1,0:T(8,128)(2,1)S(1)}, u32[]{:S(2)}, u32[]{:S(2)}) collective-permute-start(bf16[16,2176]{1,0:T(8,128)(2,1)S(1)} %get-tuple-element.46), channel_id=1, source_target_pairs={{0,1},{1,0},{2,3},{3,2},{4,5},{5,4},{6,7},{7,6},{8,9},{9,8},{10,11... | collective-permute-start | bytes 208904 | tf_op jit(solution)/shard_map/ppermute | solution.py:150
  27.0 12.2 %copy-start.2 = (bf16[2,1024,384]{2,1,0:T(8,128)(2,1)S(1)}, bf16[2,1024,384]{2,1,0:T(8,128)(2,1)}, u32[]{:S(2)}) copy-start(bf16[2,1024,384]{2,1,0:T(8,128)(2,1)} %param.27) | copy-start | bytes 4718596
  27.7 21.4 %copy-start.7 = (bf16[32,128]{1,0:T(8,128)(2,1)S(1)}, bf16[32,128]{1,0:T(8,128)(2,1)}, u32[]{:S(2)}) copy-start(bf16[32,128]{1,0:T(8,128)(2,1)} %get-tuple-element.53.pick0) | copy-start | bytes 24580
  27.7 21.4 %copy-start.8 = (bf16[32,128]{1,0:T(8,128)(2,1)S(1)}, bf16[32,128]{1,0:T(8,128)(2,1)}, u32[]{:S(2)}) copy-start(bf16[32,128]{1,0:T(8,128)(2,1)} %get-tuple-element.54.pick1) | copy-start | bytes 24580
  27.7 4.9 %collective-permute-start.10 = (bf16[16,2176]{1,0:T(8,128)(2,1)S(1)}, bf16[16,2176]{1,0:T(8,128)(2,1)S(1)}, u32[]{:S(2)}, u32[]{:S(2)}) collective-permute-start(bf16[16,2176]{1,0:T(8,128)(2,1)S(1)} %get-tuple-element.49), channel_id=1, source_target_pairs={{0,2},{1,3},{2,0},{3,1},{4,6},{5,7},{6,4},{7,5},{8,10},{9,11},{10,... | collective-permute-start | bytes 208904 | tf_op jit(solution)/shard_map/ppermute | solution.py:150
  28.6 4.5 %collective-permute-start.11 = (bf16[16,2176]{1,0:T(8,128)(2,1)S(1)}, bf16[16,2176]{1,0:T(8,128)(2,1)S(1)}, u32[]{:S(2)}, u32[]{:S(2)}) collective-permute-start(bf16[16,2176]{1,0:T(8,128)(2,1)S(1)} %get-tuple-element.50), channel_id=1, source_target_pairs={{0,3},{1,2},{2,1},{3,0},{4,7},{5,6},{6,5},{7,4},{8,11},{9,10},{10,... | collective-permute-start | bytes 208904 | tf_op jit(solution)/shard_map/ppermute | solution.py:150
  29.1 3.9 %collective-permute-start.12 = (bf16[16,2176]{1,0:T(8,128)(2,1)S(1)}, bf16[16,2176]{1,0:T(8,128)(2,1)S(1)}, u32[]{:S(2)}, u32[]{:S(2)}) collective-permute-start(bf16[16,2176]{1,0:T(8,128)(2,1)S(1)} %get-tuple-element.51), channel_id=1, source_target_pairs={{0,1},{1,0},{2,3},{3,2},{4,5},{5,4},{6,7},{7,6},{8,9},{9,8},{10,11... | collective-permute-start | bytes 208904 | tf_op jit(solution)/shard_map/ppermute | solution.py:150
  33.3 4.0 %collective-permute-start.15 = (bf16[32,1024]{1,0:T(8,128)(2,1)S(1)}, bf16[32,1024]{1,0:T(8,128)(2,1)S(1)}, u32[]{:S(2)}, u32[]{:S(2)}) collective-permute-start(bf16[32,1024]{1,0:T(8,128)(2,1)S(1)} %get-tuple-element.52.own), channel_id=1, source_target_pairs={{0,3},{1,2},{2,1},{3,0},{4,7},{5,6},{6,5},{7,4},{8,11},{9,10},{10,... | collective-permute-start | bytes 196616 | tf_op jit(solution)/shard_map/ppermute | solution.py:150
  34.2 4.9 %collective-permute-start.14 = (bf16[32,1024]{1,0:T(8,128)(2,1)S(1)}, bf16[32,1024]{1,0:T(8,128)(2,1)S(1)}, u32[]{:S(2)}, u32[]{:S(2)}) collective-permute-start(bf16[32,1024]{1,0:T(8,128)(2,1)S(1)} %get-tuple-element.52.own), channel_id=1, source_target_pairs={{0,2},{1,3},{2,0},{3,1},{4,6},{5,7},{6,4},{7,5},{8,10},{9,11},{10,... | collective-permute-start | bytes 196616 | tf_op jit(solution)/shard_map/ppermute | solution.py:150
  35.3 3.8 %collective-permute-start.13 = (bf16[32,1024]{1,0:T(8,128)(2,1)S(1)}, bf16[32,1024]{1,0:T(8,128)(2,1)S(1)}, u32[]{:S(2)}, u32[]{:S(2)}) collective-permute-start(bf16[32,1024]{1,0:T(8,128)(2,1)S(1)} %get-tuple-element.52.own), channel_id=1, source_target_pairs={{0,1},{1,0},{2,3},{3,2},{4,5},{5,4},{6,7},{7,6},{8,9},{9,8},{10,11... | collective-permute-start | bytes 196616 | tf_op jit(solution)/shard_map/ppermute | solution.py:150

commit v5 on v4

--- a/solution.py
+++ b/solution.py
@@ -151,23 +151,19 @@
 
 
 def attend_kernel(
-    slot_dev, lengths_hbm, routes_hbm, queries_hbm, keys_hbm, values_hbm, router_hbm, k_hbm, v_hbm,
-    w_hbm, own, sent1, sent2, sent3, pick0, pick1, pick_rows, router_rows,
-    lengths, routes, queries, new_keys, new_values, w_router, k_buf, v_buf, w_buf,
+    lengths_hbm, queries_hbm, keys_hbm, values_hbm, k_hbm, v_hbm, w_hbm, own, sent1, sent2, sent3,
+    lengths, queries, new_keys, new_values, k_buf, v_buf, w_buf,
     query_s, self_s, score_s, weight_s, small_sems, sems,
 ):
     row_count = queries.shape[0]
     width = own.shape[1]
     lanes = 2 * HEAD_DIM
     cache_len = k_hbm.shape[1]
-    packed_count = pick0.shape[1]
     chunks = 4
     small = [
         pltpu.make_async_copy(source, target, small_sems.at[index])
         for index, (source, target) in enumerate(
             (
-                (routes_hbm, routes),
-                (router_hbm, w_router),
                 (queries_hbm, queries),
                 (keys_hbm, new_keys),
                 (values_hbm, new_values),
@@ -187,35 +183,7 @@
         copy.start()
     per_chunk = row_count // chunks
 
-    small[0].wait()
-    route0, route1 = routes[0:1, :], routes[1:2, :]
-    place = lax.broadcasted_iota(jnp.int32, (packed_count, row_count), 0)
-    named0 = jnp.where(place == route0, 1.0, 0.0)
-    named1 = jnp.where(place == route1, 1.0, 0.0)
-    row_of = lax.broadcasted_iota(jnp.int32, (row_count, row_count), 0)
-    col_of = lax.broadcasted_iota(jnp.int32, (row_count, row_count), 1)
-    earlier = jnp.where(row_of < col_of, 1.0, 0.0).astype(jnp.bfloat16)
-    before = jnp.dot(
-        (named0 + named1).astype(jnp.bfloat16), earlier, preferred_element_type=jnp.float32
-    )
-    place_req = lax.axis_index("req")
-
-    def pick(route, named, mine):
-        rank = jnp.sum(named * before, axis=0, keepdims=True).astype(jnp.int32)
-        block = ((route // slot_dev) ^ mine) * slot_dev + lax.rem(route, slot_dev)
-        return jnp.where(place == block * CAP + rank, 1.0, 0.0)
-
-    sent_rows = pick(route0, named0, place_req) + pick(route1, named1, place_req)
-    pick_rows[...] = sent_rows.astype(jnp.bfloat16)
-    pick0[...] = jnp.transpose(pick(route0, named0, 0)).astype(jnp.bfloat16)
-    pick1[...] = jnp.transpose(pick(route1, named1, 0)).astype(jnp.bfloat16)
-    signed = jnp.transpose(named0 - named1)
-    small[1].wait()
-    router_rows[...] = jnp.dot(
-        signed[:, :EXPERTS], w_router[...],
-        precision=lax.Precision.HIGHEST, preferred_element_type=jnp.float32,
-    )
-    for copy in small[2:]:
+    for copy in small:
         copy.wait()
 
     low = lax.broadcasted_iota(jnp.int32, (row_count, lanes), 1) < HEAD_DIM
@@ -299,9 +267,38 @@
         ).astype(out.dtype)
 
 
-def ready_kernel(own, resid, pick_rows, base, pick_near):
+def ready_kernel(
+    slot_dev, own, resid, routes, w_router, base, pick_rows, pick0, pick1, router_rows
+):
     base[...] = own[...] + resid[...].astype(jnp.float32)
-    pick_near[...] = pick_rows[...]
+    packed_count, row_count = pick_rows.shape
+
+    route0, route1 = routes[0:1, :], routes[1:2, :]
+    place = lax.broadcasted_iota(jnp.int32, (packed_count, row_count), 0)
+    named0 = jnp.where(place == route0, 1.0, 0.0)
+    named1 = jnp.where(place == route1, 1.0, 0.0)
+    row_of = lax.broadcasted_iota(jnp.int32, (row_count, row_count), 0)
+    col_of = lax.broadcasted_iota(jnp.int32, (row_count, row_count), 1)
+    earlier = jnp.where(row_of < col_of, 1.0, 0.0).astype(jnp.bfloat16)
+    before = jnp.dot(
+        (named0 + named1).astype(jnp.bfloat16), earlier, preferred_element_type=jnp.float32
+    )
+    place_req = lax.axis_index("req")
+
+    def pick(route, named, mine):
+        rank = jnp.sum(named * before, axis=0, keepdims=True).astype(jnp.int32)
+        block = ((route // slot_dev) ^ mine) * slot_dev + lax.rem(route, slot_dev)
+        return jnp.where(place == block * CAP + rank, 1.0, 0.0)
+
+    sent_rows = pick(route0, named0, place_req) + pick(route1, named1, place_req)
+    pick_rows[...] = sent_rows.astype(jnp.bfloat16)
+    pick0[...] = jnp.transpose(pick(route0, named0, 0)).astype(jnp.bfloat16)
+    pick1[...] = jnp.transpose(pick(route1, named1, 0)).astype(jnp.bfloat16)
+    signed = jnp.transpose(named0 - named1)
+    router_rows[...] = jnp.dot(
+        signed[:, :EXPERTS], w_router[...],
+        precision=lax.Precision.HIGHEST, preferred_element_type=jnp.float32,
+    )
 
 
 def pack_kernel(base, part1, part2, part3, pick_rows, attended, home, sent1, sent2, sent3):
@@ -341,14 +338,15 @@
     return high, column - high
 
 
-def gate_terms(slot_dev, blocks, gain, stats, w_gate, w_up, outs, lhs):
-    size = outs[0].shape[0]
+def gate_terms(slot_dev, blocks, gain, stats, w_gate, w_up, kept, sent, lhs):
+    size = kept.shape[0] // 2
     width = blocks.shape[1]
     hidden = w_gate.shape[1]
     place_tp = lax.axis_index("tp")
     masks = slot_masks(size, slot_dev)
     lane = lax.broadcasted_iota(jnp.int32, (size, 128), 1)
-    for order, (shift, out) in enumerate(zip(TP_ORDER, outs)):
+    for order, shift in enumerate((0, 2, 1, 3)):
+        out, first_row = (kept, sent)[order // 2], order % 2 * size
         rows = blocks[
             pl.ds(pl.multiple_of((place_tp ^ shift) * size, size), size), :
         ].astype(jnp.float32)
@@ -361,7 +359,7 @@
             high, low = split_high(column)
             extra = jnp.where(lane == 2 * index, high, extra)
             extra = jnp.where(lane == 2 * index + 1, low, extra)
-        out[:, 2 * hidden :] = extra.astype(out.dtype)
+        out[first_row : first_row + size, 2 * hidden :] = extra.astype(out.dtype)
         scaled = rows * gain[...]
         for index, mask in enumerate(masks):
             lhs[order * size : (order + 1) * size, index * width : (index + 1) * width] = (
@@ -370,27 +368,38 @@
     left = lhs[...]
     for first, weight in ((0, w_gate), (hidden, w_up)):
         product = jnp.dot(left, weight[...], preferred_element_type=jnp.float32)
-        for order, out in enumerate(outs):
-            out[:, first : first + hidden] = product[order * size : (order + 1) * size].astype(
-                out.dtype
-            )
-
-
-def early_kernel(slot_dev, in0, in1, in2, in3, gain, w_gate, w_up, *refs):
-    *outs, blocks, lhs = refs
-    half = outs[0].shape[0]
+        kept[:, first : first + hidden] = product[: 2 * size]
+        sent[:, first : first + hidden] = product[2 * size :].astype(sent.dtype)
+
+
+def early_kernel(
+    slot_dev, in0, in1, in2, in3, gain, stats, w_gate, w_up, kept, sent, blocks, lhs
+):
+    half = kept.shape[0] // 2
     for index, part in enumerate((in0, in1, in2, in3)):
         blocks[index * half : (index + 1) * half, :] = part[:half, :]
-    gate_terms(slot_dev, blocks, gain, None, w_gate, w_up, outs, lhs)
-
-
-def late_kernel(slot_dev, blocks, gain, stats, w_gate, w_up, *refs):
-    *outs, lhs = refs
-    gate_terms(slot_dev, blocks, gain, stats, w_gate, w_up, outs, lhs)
+    gate_terms(slot_dev, blocks, gain, stats, w_gate, w_up, kept, sent, lhs)
+
+
+def late_kernel(slot_dev, blocks, gain, w_gate, w_up, kept, sent, lhs):
+    gate_terms(slot_dev, blocks, gain, None, w_gate, w_up, kept, sent, lhs)
+
+
+def chip_kernel(kept, part, own, sent):
+    size, width = own.shape
+    own[...] = kept[:size, :] + part[:size, :].astype(jnp.float32)
+    total = kept[size:, :] + part[size:, :].astype(jnp.float32)
+    extra = total[:, width - 128 :]
+    lane = lax.broadcasted_iota(jnp.int32, extra.shape, 1)
+    high, low = split_high(extra + pltpu.roll(extra, 127, 1))
+    sent[:, : width - 128] = total[:, : width - 128].astype(sent.dtype)
+    sent[:, width - 128 :] = jnp.where(
+        lax.rem(lane, 2) == 0, high, pltpu.roll(low, 1, 1)
+    ).astype(sent.dtype)
 
 
 def hidden_kernel(*refs):
-    early, late, (hidden, first_weight) = refs[:4], refs[4:8], refs[8:]
+    late, early, (hidden, first_weight) = refs[:2], refs[2:4], refs[4:]
     width = hidden.shape[1]
     half = hidden.shape[0] // 2
 
@@ -404,7 +413,7 @@
         square = columns[:, index : index + 1] + columns[:, index + 1 : index + 2]
         return 1.0 / jnp.sqrt(square / D + 1e-06)
 
-    for index, parts in enumerate((early, late)):
+    for index, parts in ((1, late), (0, early)):
         extra = total(parts, slice(2 * width, 2 * width + 128))
         row_inv = inverse_rms(extra, 0)
         gate = total(parts, slice(0, width)) * row_inv
@@ -483,29 +492,16 @@
         )
     bf16, f32 = jnp.bfloat16, jnp.float32
     gain = norm_gain.reshape(1, width)
-    own, sent1, sent2, sent3, pick0, pick1, pick_rows, router_rows = call(
-        functools.partial(attend_kernel, slot_dev),
-        [
-            ((row_count, width), f32),
-            ((row_count, width), bf16),
-            ((row_count, width), bf16),
-            ((row_count, width), bf16),
-            ((row_count, packed_count), bf16),
-            ((row_count, packed_count), bf16),
-            ((packed_count, row_count), bf16),
-            ((row_count, width), f32),
-        ],
-        [spec(pl.ANY)] * 9,
-        (
-            lengths, routes.T, queries, new_keys, new_values, w_router.T, k_cache, v_cache, w_out,
-        ),
+    own, *sents = call(
+        attend_kernel,
+        [((row_count, width), f32)] + [((row_count, width), bf16)] * 3,
+        [spec(pl.ANY)] * 7,
+        (lengths, queries, new_keys, new_values, k_cache, v_cache, w_out),
         scratch=[
             pltpu.SMEM(lengths.shape, jnp.int32),
-            pltpu.VMEM(routes.shape[::-1], jnp.int32),
             pltpu.VMEM(queries.shape, bf16),
             pltpu.VMEM(new_keys.shape, bf16),
             pltpu.VMEM(new_values.shape, bf16),
-            pltpu.VMEM(w_router.shape[::-1], f32),
             pltpu.VMEM(k_cache.shape, bf16),
             pltpu.VMEM(v_cache.shape, bf16),
             pltpu.VMEM(w_out.shape, bf16),
@@ -513,7 +509,7 @@
             pltpu.VMEM((8 * row_count, lanes), f32),
             pltpu.VMEM((8 * row_count, 2 * cache_len), f32),
             pltpu.VMEM((8 * row_count, 2 * cache_len), bf16),
-            pltpu.SemaphoreType.DMA((6,)),
+            pltpu.SemaphoreType.DMA((4,)),
             pltpu.SemaphoreType.DMA((12,)),
         ],
         mebibytes=56,
@@ -523,18 +519,24 @@
     def sum_exchange(sents):
         return [partner_permute(block, "tp", k) for k, block in zip(TP_ORDER[1:], sents)]
 
-    parts = sum_exchange((sent1, sent2, sent3))
-    base, pick_near = call(
-        ready_kernel,
-        [((row_count, width), f32), ((packed_count, row_count), bf16)],
-        [spec()] * 3,
-        (own, resid, pick_rows),
+    parts = sum_exchange(sents)
+    base, pick_rows, pick0, pick1, router_rows = call(
+        functools.partial(ready_kernel, slot_dev),
+        [
+            ((row_count, width), f32),
+            ((packed_count, row_count), bf16),
+            ((row_count, packed_count), bf16),
+            ((row_count, packed_count), bf16),
+            ((row_count, width), f32),
+        ],
+        [spec()] * 4,
+        (own, resid, routes.T, w_router.T),
     )
     attended, home, *sents = call(
         pack_kernel,
         [((row_count, width), bf16)] + [((quarter, width), bf16)] * 4,
         [spec()] * 5,
-        (base, *parts, pick_near),
+        (base, *parts, pick_rows),
     )
     stats, result = call(
         stats_kernel,
@@ -550,35 +552,44 @@
     weights = (w_gate.reshape(slot_dev * width, hidden), w_up.reshape(slot_dev * width, hidden))
     half = quarter // 2
     message = (half, 2 * hidden + 128)
-    messages = [(message, f32)] + [(message, bf16)] * 3
     lhs = pltpu.VMEM((packed_count // 2, slot_dev * width), bf16)
-    early, *sents = call(
+
+    def chip_sums(kept, sent):
+        own, sent = call(
+            chip_kernel, [(message, f32), (message, bf16)], [spec()] * 2,
+            (kept, partner_permute(sent, "tp", 1)),
+        )
+        return own, partner_permute(sent, "tp", 2)
+
+    pair = (quarter, message[1])
+    early = call(
         functools.partial(early_kernel, slot_dev),
-        messages,
-        [spec()] * 7,
-        (home, *parts, gain, *weights),
+        [(pair, f32), (pair, bf16)],
+        [spec()] * 8,
+        (home, *parts, gain, stats, *weights),
         scratch=[pltpu.VMEM((2 * quarter, width), bf16), lhs],
         flops=400_000_000,
         moved=3_500_000,
     )
-    early = (early, *sum_exchange(sents))
-    late, *sents = call(
+    late = call(
         functools.partial(late_kernel, slot_dev),
-        messages,
-        [spec()] * 5,
-        (along, gain, stats, *weights),
+        [(pair, f32), (pair, bf16)],
+        [spec()] * 4,
+        (along, gain, *weights),
         scratch=[lhs],
         flops=400_000_000,
         moved=3_500_000,
     )
-    late = (late, *sum_exchange(sents))
+    early = chip_sums(*early)
+    late = chip_sums(*late)
     own, first_weight = call(
         hidden_kernel,
         [((quarter, hidden), bf16), ((row_count, 128), f32)],
-        [spec()] * 8,
-        (*early, *late),
-    )
-    parts = [partner_permute(own, "tp", k) for k in (1, 2, 3)]
+        [spec()] * 4,
+        (*late, *early),
+    )
+    across = partner_permute(own, "tp", 2)
+    parts = [partner_permute(own, "tp", 1), across, partner_permute(across, "tp", 1)]
     (computed,) = call(
         functools.partial(down_kernel, slot_dev),
         [((8, packed_count // 8, width), bf16)],

time: 50.2 us -> 49.9 us (level)
  starting transfers between devices: 15.6 us -> 11.8 us
  waiting for transfers between devices: 14 us -> 17.7 us
  local copies, waits for them, and re-layouts: 1.59 us -> 0.83 us
    ppermute x16 -> x14, starting transfers between devices: 15.6 us -> 11.8 us  [partner_permute(): return lax.ppermute(block, axis, [(i, i ^ distance) for i in range(count)])]
    ppermute x16 -> x14, waiting for transfers between devices: 14 us -> 17.7 us  [partner_permute(): return lax.ppermute(block, axis, [(i, i ^ distance) for i in range(count)])]
    unnamed x20 -> x16, local copies, waits for them, and re-layouts: 1.59 us -> 0.83 us
    pallas_call x10 -> x12, Pallas kernels: 8.39 us -> 8.86 us  [call(): pl.pallas_call(kernel, out_shape=[jax.ShapeDtypeStruct(shape, dtype) for...]
  transfers between devices with their start and end apart: 16 -> 14, of which waited for: 9 -> 10; matrix products, arithmetic and copies ran while one was open for 0% -> 0% of each run, Pallas kernels for 4% -> 5%
where the time goes in v5:
time: 49.9 us; the launch traced here: 49.7 us
  waiting for transfers between devices  17.7 us (35%)
  starting transfers between devices  11.8 us (24%)
  blocking collectives  9.72 us (19%)
  Pallas kernels  8.86 us (18%)
  local copies, waits for them, and re-layouts  0.83 us (2%)
  between operations  0.77 us (2%)
    ppermute x14, waiting for transfers between devices, partner_permute(): return lax.ppermute(block, axis, [(i, i ^ distance) for i in range(count)])  17.7 us
    ppermute x14, starting transfers between devices, partner_permute(): return lax.ppermute(block, axis, [(i, i ^ distance) for i in range(count)])  11.8 us
    all_to_all x1, blocking collectives, shards(): lax.all_to_all(computed, 'req', split_axis=0, concat_axis=0, tiled=True)  9.72 us
    pallas_call x12, Pallas kernels, call(): pl.pallas_call(kernel, out_shape=[jax.ShapeDtypeStruct(shape, dtype) for...  8.86 us
  transfers between devices with their start and end apart: 14, of which 10 were waited for; matrix products, arithmetic and copies ran while one was open for 0% of the time, Pallas kernels for 5%

profile of v5, /device:TPU:0, one launch (start us, length us, event | category | flops | bytes accessed | tf_op | source)
XLA Modules:
  0.0 49.7 jit_solution(16401880424680975015)
XLA Ops:
  0.7 4.7 %shard_map.149 = (f32[32,384]{1,0:T(8,128)}, bf16[32,384]{1,0:T(8,128)(2,1)}, bf16[32,384]{1,0:T(8,128)(2,1)}, bf16[32,384]{1,0:T(8,128)(2,1)}) custom-call(s32[32]{0:T(128)} %lengths_hbm.1, bf16[32,384]{1,0:T(8,128)(2,1)} %queries_hbm.1, bf16[32,128]{1,0:T(8,128)(2,1)} %keys_hbm.1, bf16[32,128]{1,0:T(8,128)(2,1)} %values_hbm.1, ...), custom_call_target="tpu_custom_call" | custom-call | flops 200000000 | bytes 3400000 | tf_op jit(solution)/shard_map/pallas_call | solution.py:137
  5.4 3.0 %collective-permute-start = (bf16[32,384]{1,0:T(8,128)(2,1)}, bf16[32,384]{1,0:T(8,128)(2,1)S(1)}, u32[]{:S(2)}, u32[]{:S(2)}) collective-permute-start(bf16[32,384]{1,0:T(8,128)(2,1)} %get-tuple-element.30), channel_id=1, source_target_pairs={{0,2},{1,3},{2,0},{3,1},{4,6},{5,7},{6,4},{7,5},{8,10},{9,11},{10,... | collective-permute-start | bytes 73736 | tf_op jit(solution)/shard_map/ppermute | solution.py:150
  8.4 0.2 collective-permute-start.2
  8.6 0.8 %copy-done.3 = f32[32,384]{1,0:T(8,128)S(1)} copy-done((f32[32,384]{1,0:T(8,128)S(1)}, f32[32,384]{1,0:T(8,128)}, u32[]{:S(2)}) %copy-start.3) | copy-done | bytes 49176
  9.4 0.3 shard_map.150
  9.7 0.8 %collective-permute-done.part1 = bf16[32,384]{1,0:T(8,128)(2,1)S(1)} collective-permute-done((bf16[32,384]{1,0:T(8,128)(2,1)}, bf16[32,384]{1,0:T(8,128)(2,1)S(1)}, u32[]{:S(2)}, u32[]{:S(2)}) %collective-permute-start) | collective-permute-done | bytes 24608 | tf_op jit(solution)/shard_map/ppermute | solution.py:150
  10.4 1.4 %collective-permute-done.1.part2 = bf16[32,384]{1,0:T(8,128)(2,1)S(1)} collective-permute-done((bf16[32,384]{1,0:T(8,128)(2,1)}, bf16[32,384]{1,0:T(8,128)(2,1)S(1)}, u32[]{:S(2)}, u32[]{:S(2)}) %collective-permute-start.1) | collective-permute-done | bytes 24608 | tf_op jit(solution)/shard_map/ppermute | solution.py:150
  11.9 0.2 shard_map.151
  12.0 1.6 %collective-permute-start.3 = (bf16[32,384]{1,0:T(8,128)(2,1)S(1)}, bf16[32,384]{1,0:T(8,128)(2,1)S(1)}, u32[]{:S(2)}, u32[]{:S(2)}) collective-permute-start(bf16[32,384]{1,0:T(8,128)(2,1)S(1)} %get-tuple-element.38), channel_id=1, source_target_pairs={{0,8},{4,12},{8,0},{12,4},{16,24},{20,28},{24,16},{28,20},{1,9},{5... | collective-permute-start | bytes 73736 | tf_op jit(solution)/shard_map/ppermute | solution.py:150
  13.7 2.6 %collective-permute-start.4 = (bf16[32,384]{1,0:T(8,128)(2,1)S(1)}, bf16[32,384]{1,0:T(8,128)(2,1)S(1)}, u32[]{:S(2)}, u32[]{:S(2)}) collective-permute-start(bf16[32,384]{1,0:T(8,128)(2,1)S(1)} %get-tuple-element.39), channel_id=1, source_target_pairs={{0,16},{4,20},{8,24},{12,28},{16,0},{20,4},{24,8},{28,12},{1,17},{... | collective-permute-start | bytes 73736 | tf_op jit(solution)/shard_map/ppermute | solution.py:150
  16.3 0.2 collective-permute-start.5
  16.5 2.1 %collective-permute-done.4.part2.in2 = bf16[32,384]{1,0:T(8,128)(2,1)S(1)} collective-permute-done((bf16[32,384]{1,0:T(8,128)(2,1)S(1)}, bf16[32,384]{1,0:T(8,128)(2,1)S(1)}, u32[]{:S(2)}, u32[]{:S(2)}) %collective-permute-start.4) | collective-permute-done | bytes 24608 | tf_op jit(solution)/shard_map/ppermute | solution.py:150
  18.5 3.3 %collective-permute-done.5.part3.in3 = bf16[32,384]{1,0:T(8,128)(2,1)S(1)} collective-permute-done((bf16[32,384]{1,0:T(8,128)(2,1)S(1)}, bf16[32,384]{1,0:T(8,128)(2,1)S(1)}, u32[]{:S(2)}, u32[]{:S(2)}) %collective-permute-start.5) | collective-permute-done | bytes 24608 | tf_op jit(solution)/shard_map/ppermute | solution.py:150
  21.9 1.5 %collective-permute-start.6 = (bf16[64,384]{1,0:T(8,128)(2,1)S(1)}, bf16[64,384]{1,0:T(8,128)(2,1)S(1)}, u32[]{:S(2)}, u32[]{:S(2)}) collective-permute-start(bf16[64,384]{1,0:T(8,128)(2,1)S(1)} %shard_map.153), channel_id=1, source_target_pairs={{0,4},{4,0},{8,12},{12,8},{16,20},{20,16},{24,28},{28,24},{1,5},{5... | collective-permute-start | bytes 147464 | tf_op jit(solution)/shard_map/ppermute | solution.py:150
  23.4 0.6 %shard_map.152 = (f32[32,128]{1,0:T(8,128)S(1)}, bf16[32,384]{1,0:T(8,128)(2,1)}) custom-call(bf16[32,384]{1,0:T(8,128)(2,1)S(1)} %get-tuple-element.34.attended, f32[1,384]{1,0:T(1,128)S(1)} %reshape.19.gain, f32[32,384]{1,0:T(8,128)S(1)} %get-tuple-element.35.router_rows), custom_call_target="tpu_custom_call" | custom-call | flops 100000 | bytes 100000 | tf_op jit(solution)/shard_map/pallas_call | solution.py:137
  24.0 0.7 %shard_map.156 = (f32[32,2176]{1,0:T(8,128)S(1)}, bf16[32,2176]{1,0:T(8,128)(2,1)S(1)}) custom-call(bf16[32,384]{1,0:T(8,128)(2,1)S(1)} %get-tuple-element.37.home.in0, bf16[32,384]{1,0:T(8,128)(2,1)S(1)} %collective-permute-done.3.part1.in1, bf16[32,384]{1,0:T(8,128)(2,1)S(1)} %collective-permute-done.4.part2.in2, ...), custom_call_target="tpu_custom_call" | custom-call | flops 400000000 | bytes 3500000 | tf_op jit(solution)/shard_map/pallas_call | solution.py:137
  24.8 1.2 %collective-permute-done.6.blocks = bf16[64,384]{1,0:T(8,128)(2,1)S(1)} collective-permute-done((bf16[64,384]{1,0:T(8,128)(2,1)S(1)}, bf16[64,384]{1,0:T(8,128)(2,1)S(1)}, u32[]{:S(2)}, u32[]{:S(2)}) %collective-permute-start.6) | collective-permute-done | bytes 49184 | tf_op jit(solution)/shard_map/ppermute | solution.py:150
  26.0 0.7 %shard_map.154 = (f32[32,2176]{1,0:T(8,128)S(1)}, bf16[32,2176]{1,0:T(8,128)(2,1)S(1)}) custom-call(bf16[64,384]{1,0:T(8,128)(2,1)S(1)} %collective-permute-done.6.blocks, f32[1,384]{1,0:T(1,128)S(1)} %reshape.19.gain, bf16[768,1024]{1,0:T(8,128)(2,1)S(1)} %bitcast.7, bf16[768,1024]{1,0:T(8,128)(2,1)S(1)} %bitcast.9), custom_call_target="tpu_custom_call" | custom-call | flops 400000000 | bytes 3500000 | tf_op jit(solution)/shard_map/pallas_call | solution.py:137
  26.7 0.2 shard_map.157
  26.9 0.8 %collective-permute-start.10 = (bf16[16,2176]{1,0:T(8,128)(2,1)S(1)}, bf16[16,2176]{1,0:T(8,128)(2,1)S(1)}, u32[]{:S(2)}, u32[]{:S(2)}) collective-permute-start(bf16[16,2176]{1,0:T(8,128)(2,1)S(1)} %get-tuple-element.49), channel_id=1, source_target_pairs={{0,2},{1,3},{2,0},{3,1},{4,6},{5,7},{6,4},{7,5},{8,10},{9,11},{10,... | collective-permute-start | bytes 208904 | tf_op jit(solution)/shard_map/ppermute | solution.py:150
  27.7 0.4 collective-permute-done.7.part
  28.1 0.2 shard_map.155
  28.2 0.9 %collective-permute-start.8 = (bf16[16,2176]{1,0:T(8,128)(2,1)S(1)}, bf16[16,2176]{1,0:T(8,128)(2,1)S(1)}, u32[]{:S(2)}, u32[]{:S(2)}) collective-permute-start(bf16[16,2176]{1,0:T(8,128)(2,1)S(1)} %get-tuple-element.44), channel_id=1, source_target_pairs={{0,2},{1,3},{2,0},{3,1},{4,6},{5,7},{6,4},{7,5},{8,10},{9,11},{10,... | collective-permute-start | bytes 208904 | tf_op jit(solution)/shard_map/ppermute | solution.py:150
  29.1 2.8 %collective-permute-done.10.refs_3_ = bf16[16,2176]{1,0:T(8,128)(2,1)S(1)} collective-permute-done((bf16[16,2176]{1,0:T(8,128)(2,1)S(1)}, bf16[16,2176]{1,0:T(8,128)(2,1)S(1)}, u32[]{:S(2)}, u32[]{:S(2)}) %collective-permute-start.10) | collective-permute-done | bytes 69664 | tf_op jit(solution)/shard_map/ppermute | solution.py:150
  31.9 1.1 %collective-permute-done.8.refs_1_ = bf16[16,2176]{1,0:T(8,128)(2,1)S(1)} collective-permute-done((bf16[16,2176]{1,0:T(8,128)(2,1)S(1)}, bf16[16,2176]{1,0:T(8,128)(2,1)S(1)}, u32[]{:S(2)}, u32[]{:S(2)}) %collective-permute-start.8) | collective-permute-done | bytes 69664 | tf_op jit(solution)/shard_map/ppermute | solution.py:150
  33.0 0.2 shard_map.158
  33.2 0.8 %collective-permute-start.12 = (bf16[32,1024]{1,0:T(8,128)(2,1)S(1)}, bf16[32,1024]{1,0:T(8,128)(2,1)S(1)}, u32[]{:S(2)}, u32[]{:S(2)}) collective-permute-start(bf16[32,1024]{1,0:T(8,128)(2,1)S(1)} %get-tuple-element.50.own), channel_id=1, source_target_pairs={{0,2},{1,3},{2,0},{3,1},{4,6},{5,7},{6,4},{7,5},{8,10},{9,11},{10,... | collective-permute-start | bytes 196616 | tf_op jit(solution)/shard_map/ppermute | solution.py:150
  34.0 3.5 %collective-permute-done.12.part2 = bf16[32,1024]{1,0:T(8,128)(2,1)S(1)} collective-permute-done((bf16[32,1024]{1,0:T(8,128)(2,1)S(1)}, bf16[32,1024]{1,0:T(8,128)(2,1)S(1)}, u32[]{:S(2)}, u32[]{:S(2)}) %collective-permute-start.12) | collective-permute-done | bytes 65568 | tf_op jit(solution)/shard_map/ppermute | solution.py:150
  37.5 1.2 %collective-permute-done.13.part3 = bf16[32,1024]{1,0:T(8,128)(2,1)S(1)} collective-permute-done((bf16[32,1024]{1,0:T(8,128)(2,1)S(1)}, bf16[32,1024]{1,0:T(8,128)(2,1)S(1)}, u32[]{:S(2)}, u32[]{:S(2)}) %collective-permute-start.13) | collective-permute-done | bytes 65568 | tf_op jit(solution)/shard_map/ppermute | solution.py:150
  38.8 0.5 shard_map.159
  39.2 9.7 %all_to_all.5 = bf16[8,16,384]{2,1,0:T(8,128)(2,1)S(1)} all-to-all(bf16[8,16,384]{2,1,0:T(8,128)(2,1)S(1)} %shard_map.159), channel_id=1, replica_groups=mesh['req'=8,'tp'=4] {'req'}, dimensions={0} | all-to-all | bytes 196608 | tf_op jit(solution)/shard_map/all_to_all | solution.py:602
  49.0 0.8 %shard_map.160 = bf16[32,384]{1,0:T(8,128)(2,1)} custom-call(bf16[128,384]{1,0:T(8,128)(2,1)S(1)} %bitcast.11, bf16[32,128]{1,0:T(8,128)(2,1)S(1)} %get-tuple-element.51.pick0, bf16[32,128]{1,0:T(8,128)(2,1)S(1)} %get-tuple-element.52.pick1, f32[32,128]{1,0:T(8,128)S(1)} %get-tuple-element.53.first_weight, bf16[32,384]{1,0:T(8,128)(2,1)S(1)} %get-tuple-element.34.attended), custom_call_target="tpu_custom_call" | custom-call | flops 100000 | bytes 100000 | tf_op jit(solution)/shard_map/pallas_call | solution.py:137
  (26 shorter events, 0.2 us)
Async XLA Ops:
  0.6 8.0 %copy-start.6 = (s32[32,2]{0,1:T(2,128)S(1)}, s32[32,2]{0,1:T(2,128)}, u32[]{:S(2)}) copy-start(s32[32,2]{0,1:T(2,128)} %param.24) | copy-start | bytes 772
  0.6 7.9 %copy-start.5 = (f32[384,16]{0,1:T(8,128)S(1)}, f32[384,16]{0,1:T(8,128)}, u32[]{:S(2)}) copy-start(f32[384,16]{0,1:T(8,128)} %param.23) | copy-start | bytes 73732
  0.7 7.9 %copy-start.4 = (bf16[32,384]{1,0:T(8,128)(2,1)S(1)}, bf16[32,384]{1,0:T(8,128)(2,1)}, u32[]{:S(2)}) copy-start(bf16[32,384]{1,0:T(8,128)(2,1)} %resid.1) | copy-start | bytes 73732
  0.7 22.7 %copy-start.7 = (f32[384]{0:T(512)S(1)}, f32[384]{0:T(512)}, u32[]{:S(2)}) copy-start(f32[384]{0:T(512)} %param.22) | copy-start | bytes 4612
  0.7 23.4 %copy-start.1 = (bf16[2,384,1024]{2,1,0:T(8,128)(2,1)S(1)}, bf16[2,384,1024]{2,1,0:T(8,128)(2,1)}, u32[]{:S(2)}) copy-start(bf16[2,384,1024]{2,1,0:T(8,128)(2,1)} %param.26) | copy-start | bytes 4718596
  0.7 23.3 %copy-start = (bf16[2,384,1024]{2,1,0:T(8,128)(2,1)S(1)}, bf16[2,384,1024]{2,1,0:T(8,128)(2,1)}, u32[]{:S(2)}) copy-start(bf16[2,384,1024]{2,1,0:T(8,128)(2,1)} %param.25) | copy-start | bytes 4718596
  5.4 5.0 %collective-permute-start = (bf16[32,384]{1,0:T(8,128)(2,1)}, bf16[32,384]{1,0:T(8,128)(2,1)S(1)}, u32[]{:S(2)}, u32[]{:S(2)}) collective-permute-start(bf16[32,384]{1,0:T(8,128)(2,1)} %get-tuple-element.30), channel_id=1, source_target_pairs={{0,2},{1,3},{2,0},{3,1},{4,6},{5,7},{6,4},{7,5},{8,10},{9,11},{10,... | collective-permute-start | bytes 73736 | tf_op jit(solution)/shard_map/ppermute | solution.py:150
  8.4 3.5 %collective-permute-start.1 = (bf16[32,384]{1,0:T(8,128)(2,1)}, bf16[32,384]{1,0:T(8,128)(2,1)S(1)}, u32[]{:S(2)}, u32[]{:S(2)}) collective-permute-start(bf16[32,384]{1,0:T(8,128)(2,1)} %get-tuple-element.31), channel_id=1, source_target_pairs={{0,3},{1,2},{2,1},{3,0},{4,7},{5,6},{6,5},{7,4},{8,11},{9,10},{10,... | collective-permute-start | bytes 73736 | tf_op jit(solution)/shard_map/ppermute | solution.py:150
  8.4 3.5 %collective-permute-start.2 = (bf16[32,384]{1,0:T(8,128)(2,1)}, bf16[32,384]{1,0:T(8,128)(2,1)S(1)}, u32[]{:S(2)}, u32[]{:S(2)}) collective-permute-start(bf16[32,384]{1,0:T(8,128)(2,1)} %get-tuple-element.32), channel_id=1, source_target_pairs={{0,1},{1,0},{2,3},{3,2},{4,5},{5,4},{6,7},{7,6},{8,9},{9,8},{10,11... | collective-permute-start | bytes 73736 | tf_op jit(solution)/shard_map/ppermute | solution.py:150
  8.6 0.8 %copy-start.3 = (f32[32,384]{1,0:T(8,128)S(1)}, f32[32,384]{1,0:T(8,128)}, u32[]{:S(2)}) copy-start(f32[32,384]{1,0:T(8,128)} %get-tuple-element.28.own) | copy-start | bytes 147460
  12.0 4.5 %collective-permute-start.3 = (bf16[32,384]{1,0:T(8,128)(2,1)S(1)}, bf16[32,384]{1,0:T(8,128)(2,1)S(1)}, u32[]{:S(2)}, u32[]{:S(2)}) collective-permute-start(bf16[32,384]{1,0:T(8,128)(2,1)S(1)} %get-tuple-element.38), channel_id=1, source_target_pairs={{0,8},{4,12},{8,0},{12,4},{16,24},{20,28},{24,16},{28,20},{1,9},{5... | collective-permute-start | bytes 73736 | tf_op jit(solution)/shard_map/ppermute | solution.py:150
  13.7 4.9 %collective-permute-start.4 = (bf16[32,384]{1,0:T(8,128)(2,1)S(1)}, bf16[32,384]{1,0:T(8,128)(2,1)S(1)}, u32[]{:S(2)}, u32[]{:S(2)}) collective-permute-start(bf16[32,384]{1,0:T(8,128)(2,1)S(1)} %get-tuple-element.39), channel_id=1, source_target_pairs={{0,16},{4,20},{8,24},{12,28},{16,0},{20,4},{24,8},{28,12},{1,17},{... | collective-permute-start | bytes 73736 | tf_op jit(solution)/shard_map/ppermute | solution.py:150
  16.3 5.6 %collective-permute-start.5 = (bf16[32,384]{1,0:T(8,128)(2,1)S(1)}, bf16[32,384]{1,0:T(8,128)(2,1)S(1)}, u32[]{:S(2)}, u32[]{:S(2)}) collective-permute-start(bf16[32,384]{1,0:T(8,128)(2,1)S(1)} %get-tuple-element.40), channel_id=1, source_target_pairs={{0,24},{4,28},{8,16},{12,20},{16,8},{20,12},{24,0},{28,4},{1,25},{... | collective-permute-start | bytes 73736 | tf_op jit(solution)/shard_map/ppermute | solution.py:150
  21.9 4.1 %collective-permute-start.6 = (bf16[64,384]{1,0:T(8,128)(2,1)S(1)}, bf16[64,384]{1,0:T(8,128)(2,1)S(1)}, u32[]{:S(2)}, u32[]{:S(2)}) collective-permute-start(bf16[64,384]{1,0:T(8,128)(2,1)S(1)} %shard_map.153), channel_id=1, source_target_pairs={{0,4},{4,0},{8,12},{12,8},{16,20},{20,16},{24,28},{28,24},{1,5},{5... | collective-permute-start | bytes 147464 | tf_op jit(solution)/shard_map/ppermute | solution.py:150
  24.7 14.0 %copy-start.2 = (bf16[2,1024,384]{2,1,0:T(8,128)(2,1)S(1)}, bf16[2,1024,384]{2,1,0:T(8,128)(2,1)}, u32[]{:S(2)}) copy-start(bf16[2,1024,384]{2,1,0:T(8,128)(2,1)} %param.27) | copy-start | bytes 4718596
  24.7 2.0 %collective-permute-start.9 = (bf16[32,2176]{1,0:T(8,128)(2,1)S(1)}, bf16[32,2176]{1,0:T(8,128)(2,1)S(1)}, u32[]{:S(2)}, u32[]{:S(2)}) collective-permute-start(bf16[32,2176]{1,0:T(8,128)(2,1)S(1)} %get-tuple-element.47), channel_id=1, source_target_pairs={{0,1},{1,0},{2,3},{3,2},{4,5},{5,4},{6,7},{7,6},{8,9},{9,8},{10,11... | collective-permute-start | bytes 417800 | tf_op jit(solution)/shard_map/ppermute | solution.py:150
  26.6 1.4 %collective-permute-start.7 = (bf16[32,2176]{1,0:T(8,128)(2,1)S(1)}, bf16[32,2176]{1,0:T(8,128)(2,1)S(1)}, u32[]{:S(2)}, u32[]{:S(2)}) collective-permute-start(bf16[32,2176]{1,0:T(8,128)(2,1)S(1)} %get-tuple-element.42), channel_id=1, source_target_pairs={{0,1},{1,0},{2,3},{3,2},{4,5},{5,4},{6,7},{7,6},{8,9},{9,8},{10,11... | collective-permute-start | bytes 417800 | tf_op jit(solution)/shard_map/ppermute | solution.py:150
  26.9 5.0 %collective-permute-start.10 = (bf16[16,2176]{1,0:T(8,128)(2,1)S(1)}, bf16[16,2176]{1,0:T(8,128)(2,1)S(1)}, u32[]{:S(2)}, u32[]{:S(2)}) collective-permute-start(bf16[16,2176]{1,0:T(8,128)(2,1)S(1)} %get-tuple-element.49), channel_id=1, source_target_pairs={{0,2},{1,3},{2,0},{3,1},{4,6},{5,7},{6,4},{7,5},{8,10},{9,11},{10,... | collective-permute-start | bytes 208904 | tf_op jit(solution)/shard_map/ppermute | solution.py:150
  28.2 4.7 %collective-permute-start.8 = (bf16[16,2176]{1,0:T(8,128)(2,1)S(1)}, bf16[16,2176]{1,0:T(8,128)(2,1)S(1)}, u32[]{:S(2)}, u32[]{:S(2)}) collective-permute-start(bf16[16,2176]{1,0:T(8,128)(2,1)S(1)} %get-tuple-element.44), channel_id=1, source_target_pairs={{0,2},{1,3},{2,0},{3,1},{4,6},{5,7},{6,4},{7,5},{8,10},{9,11},{10,... | collective-permute-start | bytes 208904 | tf_op jit(solution)/shard_map/ppermute | solution.py:150
  33.2 4.3 %collective-permute-start.12 = (bf16[32,1024]{1,0:T(8,128)(2,1)S(1)}, bf16[32,1024]{1,0:T(8,128)(2,1)S(1)}, u32[]{:S(2)}, u32[]{:S(2)}) collective-permute-start(bf16[32,1024]{1,0:T(8,128)(2,1)S(1)} %get-tuple-element.50.own), channel_id=1, source_target_pairs={{0,2},{1,3},{2,0},{3,1},{4,6},{5,7},{6,4},{7,5},{8,10},{9,11},{10,... | collective-permute-start | bytes 196616 | tf_op jit(solution)/shard_map/ppermute | solution.py:150
  34.0 3.5 %collective-permute-start.11 = (bf16[32,1024]{1,0:T(8,128)(2,1)S(1)}, bf16[32,1024]{1,0:T(8,128)(2,1)S(1)}, u32[]{:S(2)}, u32[]{:S(2)}) collective-permute-start(bf16[32,1024]{1,0:T(8,128)(2,1)S(1)} %get-tuple-element.50.own), channel_id=1, source_target_pairs={{0,1},{1,0},{2,3},{3,2},{4,5},{5,4},{6,7},{7,6},{8,9},{9,8},{10,11... | collective-permute-start | bytes 196616 | tf_op jit(solution)/shard_map/ppermute | solution.py:150
  37.5 1.3 %collective-permute-start.13 = (bf16[32,1024]{1,0:T(8,128)(2,1)S(1)}, bf16[32,1024]{1,0:T(8,128)(2,1)S(1)}, u32[]{:S(2)}, u32[]{:S(2)}) collective-permute-start(bf16[32,1024]{1,0:T(8,128)(2,1)S(1)} %collective-permute-done.12.part2), channel_id=1, source_target_pairs={{0,1},{1,0},{2,3},{3,2},{4,5},{5,4},{6,7},{7,6},{8,9},{9,8},{10,11... | collective-permute-start | bytes 196616 | tf_op jit(solution)/shard_map/ppermute | solution.py:150

commit v6 on v5

--- a/solution.py
+++ b/solution.py
@@ -197,23 +197,19 @@
         jnp.where(low, 0.0, tiles[2]),
     ]
     scale = 1.0 / math.sqrt(HEAD_DIM)
-    keys_new = new_keys[...].astype(jnp.float32)
-    zeros = jnp.zeros((row_count, lanes), jnp.float32)
     for head in range(8):
         rows = pl.ds(head, row_count, stride=8)
-        if head < 6:
-            own_score = jnp.sum(heads[head] * keys_new, axis=1, keepdims=True) * scale
-            query_s[rows, :] = heads[head]
-            self_s[rows, :] = jnp.broadcast_to(own_score, zeros.shape)
-        else:
-            query_s[rows, :] = zeros
-            self_s[rows, :] = zeros
-
-    pair_row = lax.broadcasted_iota(jnp.int32, (16, 2 * cache_len), 0)
-    pair_lane = lax.broadcasted_iota(jnp.int32, (16, 2 * cache_len), 1)
-    upper = pair_row < 8
-    place = jnp.where(upper, pair_lane, pair_lane - cache_len)
-    place = jnp.where(place < 0, cache_len, place)
+        query_s[rows, :] = heads[head] if head < 6 else jnp.zeros((row_count, lanes), jnp.float32)
+
+    row_of = lax.broadcasted_iota(jnp.int32, (8 * row_count, row_count), 0)
+    request_of = lax.broadcasted_iota(jnp.int32, (8 * row_count, row_count), 1)
+    spread = jnp.where(row_of // 8 == request_of, 1.0, 0.0).astype(jnp.bfloat16)
+    keys_new = jnp.dot(spread, new_keys[...], preferred_element_type=jnp.float32)
+    values_new = jnp.dot(spread, new_values[...], preferred_element_type=jnp.float32)
+    own_score = jnp.sum(query_s[...] * keys_new, axis=1, keepdims=True) * scale
+
+    upper = lax.broadcasted_iota(jnp.int32, (16, lanes), 0) < 8
+    position = lax.broadcasted_iota(jnp.int32, (16, cache_len), 1)
     for pair in range(row_count // 2):
         if pair % (per_chunk // 2) == 0:
             copies[pair // (per_chunk // 2)].wait()
@@ -224,9 +220,12 @@
             preferred_element_type=jnp.float32,
         )
         limit = jnp.where(upper, lengths[2 * pair], lengths[2 * pair + 1])
-        score_s[pair_rows, :] = jnp.where(place < limit, raw * scale, -1e30)
-
-    own_score = self_s[:, 0:1]
+        score_s[pair_rows, :] = jnp.where(
+            position < limit,
+            jnp.where(upper, raw[:, :cache_len], raw[:, cache_len:]) * scale,
+            -1e30,
+        )
+
     scores = score_s[...]
     peak = jnp.maximum(jnp.max(scores, axis=1, keepdims=True), own_score)
     terms = jnp.exp(scores - peak)
@@ -234,21 +233,18 @@
     inverse = 1.0 / (jnp.sum(terms, axis=1, keepdims=True) + own_term)
     weight_s[...] = (terms * inverse).astype(jnp.bfloat16)
     own_weight = (own_term * inverse).astype(jnp.bfloat16).astype(jnp.float32)
-    self_s[...] = jnp.broadcast_to(own_weight, self_s.shape)
+    self_s[...] = own_weight * values_new
     for pair in range(row_count // 2):
         if pair % (per_chunk // 2) == 0:
             copies[chunks + pair // (per_chunk // 2)].wait()
         pair_rows = slice(16 * pair, 16 * pair + 16)
-        values = v_buf[2 * pair : 2 * pair + 2].reshape(2 * cache_len, lanes)
-        query_s[pair_rows, :] = jnp.dot(
-            weight_s[pair_rows, :], values, preferred_element_type=jnp.float32
-        )
-
-    values_new = new_values[...].astype(jnp.float32)
-    mixed = []
-    for head in range(6):
-        rows = pl.ds(head, row_count, stride=8)
-        mixed.append(query_s[rows, :] + self_s[rows, :] * values_new)
+        values = jnp.concatenate([v_buf[2 * pair], v_buf[2 * pair + 1]], axis=1)
+        mixed = jnp.dot(weight_s[pair_rows, :], values, preferred_element_type=jnp.float32)
+        query_s[pair_rows, :] = (
+            jnp.where(upper, mixed[:, :lanes], mixed[:, lanes:]) + self_s[pair_rows, :]
+        )
+
+    mixed = [query_s[pl.ds(head, row_count, stride=8), :] for head in range(6)]
     attention = jnp.concatenate(
         [
             jnp.where(low, mixed[0], pltpu.roll(mixed[1], HEAD_DIM, 1)),
@@ -313,8 +309,11 @@
         out[...] = packed[distance * size : (distance + 1) * size].astype(out.dtype)
 
 
-def stats_kernel(attended, gain, router_rows, stats, result):
+def result_kernel(attended, result):
     result[...] = attended[...]
+
+
+def stats_kernel(attended, gain, router_rows, stats):
     rows = attended[...].astype(jnp.float32)
     square = jnp.sum(rows * rows, axis=1, keepdims=True)
     logit = jnp.sum(rows * gain[...] * router_rows[...], axis=1, keepdims=True)
@@ -483,7 +482,7 @@
         and lax.axis_size("req") == 8
         and 8 * slot_dev == EXPERTS
         and row_count == quarter
-        and lanes == 2 * HEAD_DIM
+        and cache_len == lanes == 2 * HEAD_DIM
         and queries.shape[1] == 6 * HEAD_DIM
     ):
         return shards_general(
@@ -496,7 +495,10 @@
         attend_kernel,
         [((row_count, width), f32)] + [((row_count, width), bf16)] * 3,
         [spec(pl.ANY)] * 7,
-        (lengths, queries, new_keys, new_values, k_cache, v_cache, w_out),
+        [
+            pltpu.with_memory_space_constraint(operand, pltpu.HBM)
+            for operand in (lengths, queries, new_keys, new_values, k_cache, v_cache, w_out)
+        ],
         scratch=[
             pltpu.SMEM(lengths.shape, jnp.int32),
             pltpu.VMEM(queries.shape, bf16),
@@ -507,12 +509,12 @@
             pltpu.VMEM(w_out.shape, bf16),
             pltpu.VMEM((8 * row_count, lanes), f32),
             pltpu.VMEM((8 * row_count, lanes), f32),
-            pltpu.VMEM((8 * row_count, 2 * cache_len), f32),
-            pltpu.VMEM((8 * row_count, 2 * cache_len), bf16),
+            pltpu.VMEM((8 * row_count, cache_len), f32),
+            pltpu.VMEM((8 * row_count, cache_len), bf16),
             pltpu.SemaphoreType.DMA((4,)),
             pltpu.SemaphoreType.DMA((12,)),
         ],
-        mebibytes=56,
+        mebibytes=16,
         flops=200_000_000,
         moved=3_400_000,
     )
@@ -538,12 +540,10 @@
         [spec()] * 5,
         (base, *parts, pick_rows),
     )
-    stats, result = call(
-        stats_kernel,
-        [((row_count, 128), f32), ((row_count, width), bf16)],
-        [spec()] * 3,
-        (attended, gain, router_rows),
-    )
+    (stats,) = call(
+        stats_kernel, [((row_count, 128), f32)], [spec()] * 3, (attended, gain, router_rows)
+    )
+    (result,) = call(result_kernel, [((row_count, width), bf16)], [spec()], (attended,))
     parts = [partner_permute(block, "req", 2 * k) for k, block in enumerate(sents, 1)]
     (along,) = call(
         turn_kernel, [((2 * quarter, width), bf16)], [spec()] * 4, (home, *parts)

time: 49.9 us -> 50.4 us (1.010)
  blocking collectives: 9.72 us -> 0 us
  waiting for transfers between devices: 17.7 us -> 25.3 us
  starting transfers between devices: 11.8 us -> 15.2 us
  local copies, waits for them, and re-layouts: 0.83 us -> 0.03 us
    all_to_all x1 -> x0, blocking collectives: 9.72 us -> none  [shards(): lax.all_to_all(computed, 'req', split_axis=0, concat_axis=0, tiled=True)]
    all_to_all x0 -> x1, waiting for transfers between devices: none -> 6.45 us  [shards(): lax.all_to_all(computed, 'req', split_axis=0, concat_axis=0, tiled=True)]
    all_to_all x0 -> x1, starting transfers between devices: none -> 3.36 us  [shards(): lax.all_to_all(computed, 'req', split_axis=0, concat_axis=0, tiled=True)]
    ppermute x14, waiting for transfers between devices: 17.7 us -> 18.8 us  [partner_permute(): return lax.ppermute(block, axis, [(i, i ^ distance) for i in range(count)])]
    unnamed x16 -> x14, local copies, waits for them, and re-layouts: 0.83 us -> 0.03 us
    pallas_call x12 -> x13, Pallas kernels: 8.86 us -> 8.91 us  [call(): pl.pallas_call(kernel, out_shape=[jax.ShapeDtypeStruct(shape, dtype) for...]
  transfers between devices with their start and end apart: 14 -> 15, of which waited for: 10 -> 11; matrix products, arithmetic and copies ran while one was open for 0% -> 0% of each run, Pallas kernels for 5% -> 5%
where the time goes in v6:
time: 50.4 us; the launch traced here: 50.2 us
  waiting for transfers between devices  25.3 us (50%)
  starting transfers between devices  15.2 us (30%)
  Pallas kernels  8.91 us (18%)
  between operations  0.78 us (2%)
    ppermute x14, waiting for transfers between devices, partner_permute(): return lax.ppermute(block, axis, [(i, i ^ distance) for i in range(count)])  18.8 us
    ppermute x14, starting transfers between devices, partner_permute(): return lax.ppermute(block, axis, [(i, i ^ distance) for i in range(count)])  11.8 us
    pallas_call x13, Pallas kernels, call(): pl.pallas_call(kernel, out_shape=[jax.ShapeDtypeStruct(shape, dtype) for...  8.91 us
    all_to_all x1, waiting for transfers between devices, shards(): lax.all_to_all(computed, 'req', split_axis=0, concat_axis=0, tiled=True)  6.45 us
    all_to_all x1, starting transfers between devices, shards(): lax.all_to_all(computed, 'req', split_axis=0, concat_axis=0, tiled=True)  3.36 us
  transfers between devices with their start and end apart: 15, of which 11 were waited for; matrix products, arithmetic and copies ran while one was open for 0% of the time, Pallas kernels for 5%

profile of v6, /device:TPU:0, one launch (start us, length us, event | category | flops | bytes accessed | tf_op | source)
XLA Modules:
  0.0 50.2 jit_solution(159492367466287011)
XLA Ops:
  0.7 4.0 %shard_map.149 = (f32[32,384]{1,0:T(8,128)S(1)}, bf16[32,384]{1,0:T(8,128)(2,1)S(1)}, bf16[32,384]{1,0:T(8,128)(2,1)S(1)}, bf16[32,384]{1,0:T(8,128)(2,1)S(1)}) custom-call(s32[32]{0:T(128)} %lengths_hbm.1, bf16[32,384]{1,0:T(8,128)(2,1)} %queries_hbm.1, bf16[32,128]{1,0:T(8,128)(2,1)} %keys_hbm.1, bf16[32,128]{1,0:T(8,128)(2,1)} %values_hbm.1, ...), custom_call_target="tpu_custom_call" | custom-call | flops 200000000 | bytes 3400000 | tf_op jit(solution)/shard_map/pallas_call | solution.py:137
  4.7 3.0 %collective-permute-start = (bf16[32,384]{1,0:T(8,128)(2,1)S(1)}, bf16[32,384]{1,0:T(8,128)(2,1)S(1)}, u32[]{:S(2)}, u32[]{:S(2)}) collective-permute-start(bf16[32,384]{1,0:T(8,128)(2,1)S(1)} %get-tuple-element.28), channel_id=1, source_target_pairs={{0,2},{1,3},{2,0},{3,1},{4,6},{5,7},{6,4},{7,5},{8,10},{9,11},{10,... | collective-permute-start | bytes 73736 | tf_op jit(solution)/shard_map/ppermute | solution.py:150
  7.7 0.2 collective-permute-start.2
  7.9 0.3 shard_map.150
  8.1 1.3 %collective-permute-done.part1 = bf16[32,384]{1,0:T(8,128)(2,1)S(1)} collective-permute-done((bf16[32,384]{1,0:T(8,128)(2,1)S(1)}, bf16[32,384]{1,0:T(8,128)(2,1)S(1)}, u32[]{:S(2)}, u32[]{:S(2)}) %collective-permute-start) | collective-permute-done | bytes 24608 | tf_op jit(solution)/shard_map/ppermute | solution.py:150
  9.5 1.4 %collective-permute-done.1.part2 = bf16[32,384]{1,0:T(8,128)(2,1)S(1)} collective-permute-done((bf16[32,384]{1,0:T(8,128)(2,1)S(1)}, bf16[32,384]{1,0:T(8,128)(2,1)S(1)}, u32[]{:S(2)}, u32[]{:S(2)}) %collective-permute-start.1) | collective-permute-done | bytes 24608 | tf_op jit(solution)/shard_map/ppermute | solution.py:150
  10.9 0.2 shard_map.151
  11.1 1.6 %collective-permute-start.3 = (bf16[32,384]{1,0:T(8,128)(2,1)S(1)}, bf16[32,384]{1,0:T(8,128)(2,1)S(1)}, u32[]{:S(2)}, u32[]{:S(2)}) collective-permute-start(bf16[32,384]{1,0:T(8,128)(2,1)S(1)} %get-tuple-element.34), channel_id=1, source_target_pairs={{0,8},{4,12},{8,0},{12,4},{16,24},{20,28},{24,16},{28,20},{1,9},{5... | collective-permute-start | bytes 73736 | tf_op jit(solution)/shard_map/ppermute | solution.py:150
  12.7 2.6 %collective-permute-start.4 = (bf16[32,384]{1,0:T(8,128)(2,1)S(1)}, bf16[32,384]{1,0:T(8,128)(2,1)S(1)}, u32[]{:S(2)}, u32[]{:S(2)}) collective-permute-start(bf16[32,384]{1,0:T(8,128)(2,1)S(1)} %get-tuple-element.35), channel_id=1, source_target_pairs={{0,16},{4,20},{8,24},{12,28},{16,0},{20,4},{24,8},{28,12},{1,17},{... | collective-permute-start | bytes 73736 | tf_op jit(solution)/shard_map/ppermute | solution.py:150
  15.3 0.2 collective-permute-start.5
  15.6 2.1 %collective-permute-done.4.part2.in2 = bf16[32,384]{1,0:T(8,128)(2,1)S(1)} collective-permute-done((bf16[32,384]{1,0:T(8,128)(2,1)S(1)}, bf16[32,384]{1,0:T(8,128)(2,1)S(1)}, u32[]{:S(2)}, u32[]{:S(2)}) %collective-permute-start.4) | collective-permute-done | bytes 24608 | tf_op jit(solution)/shard_map/ppermute | solution.py:150
  17.6 3.3 %collective-permute-done.5.part3.in3 = bf16[32,384]{1,0:T(8,128)(2,1)S(1)} collective-permute-done((bf16[32,384]{1,0:T(8,128)(2,1)S(1)}, bf16[32,384]{1,0:T(8,128)(2,1)S(1)}, u32[]{:S(2)}, u32[]{:S(2)}) %collective-permute-start.5) | collective-permute-done | bytes 24608 | tf_op jit(solution)/shard_map/ppermute | solution.py:150
  21.0 1.5 %collective-permute-start.6 = (bf16[64,384]{1,0:T(8,128)(2,1)S(1)}, bf16[64,384]{1,0:T(8,128)(2,1)S(1)}, u32[]{:S(2)}, u32[]{:S(2)}) collective-permute-start(bf16[64,384]{1,0:T(8,128)(2,1)S(1)} %shard_map.153), channel_id=1, source_target_pairs={{0,4},{4,0},{8,12},{12,8},{16,20},{20,16},{24,28},{28,24},{1,5},{5... | collective-permute-start | bytes 147464 | tf_op jit(solution)/shard_map/ppermute | solution.py:150
  22.6 0.7 %shard_map.157 = (f32[32,2176]{1,0:T(8,128)S(1)}, bf16[32,2176]{1,0:T(8,128)(2,1)S(1)}) custom-call(bf16[32,384]{1,0:T(8,128)(2,1)S(1)} %get-tuple-element.33.home.in0, bf16[32,384]{1,0:T(8,128)(2,1)S(1)} %collective-permute-done.3.part1.in1, bf16[32,384]{1,0:T(8,128)(2,1)S(1)} %collective-permute-done.4.part2.in2, ...), custom_call_target="tpu_custom_call" | custom-call | flops 400000000 | bytes 3500000 | tf_op jit(solution)/shard_map/pallas_call | solution.py:137
  23.4 1.7 %collective-permute-done.6.blocks = bf16[64,384]{1,0:T(8,128)(2,1)S(1)} collective-permute-done((bf16[64,384]{1,0:T(8,128)(2,1)S(1)}, bf16[64,384]{1,0:T(8,128)(2,1)S(1)}, u32[]{:S(2)}, u32[]{:S(2)}) %collective-permute-start.6) | collective-permute-done | bytes 49184 | tf_op jit(solution)/shard_map/ppermute | solution.py:150
  25.1 0.7 %shard_map.154 = (f32[32,2176]{1,0:T(8,128)S(1)}, bf16[32,2176]{1,0:T(8,128)(2,1)S(1)}) custom-call(bf16[64,384]{1,0:T(8,128)(2,1)S(1)} %collective-permute-done.6.blocks, f32[1,384]{1,0:T(1,128)S(1)} %reshape.19.gain, bf16[768,1024]{1,0:T(8,128)(2,1)S(1)} %bitcast.7, bf16[768,1024]{1,0:T(8,128)(2,1)S(1)} %bitcast.9), custom_call_target="tpu_custom_call" | custom-call | flops 400000000 | bytes 3500000 | tf_op jit(solution)/shard_map/pallas_call | solution.py:137
  25.8 0.2 shard_map.158
  26.0 0.8 %collective-permute-start.10 = (bf16[16,2176]{1,0:T(8,128)(2,1)S(1)}, bf16[16,2176]{1,0:T(8,128)(2,1)S(1)}, u32[]{:S(2)}, u32[]{:S(2)}) collective-permute-start(bf16[16,2176]{1,0:T(8,128)(2,1)S(1)} %get-tuple-element.45), channel_id=1, source_target_pairs={{0,2},{1,3},{2,0},{3,1},{4,6},{5,7},{6,4},{7,5},{8,10},{9,11},{10,... | collective-permute-start | bytes 208904 | tf_op jit(solution)/shard_map/ppermute | solution.py:150
  26.8 0.4 collective-permute-done.7.part
  27.2 0.2 shard_map.155
  27.3 0.9 %collective-permute-start.8 = (bf16[16,2176]{1,0:T(8,128)(2,1)S(1)}, bf16[16,2176]{1,0:T(8,128)(2,1)S(1)}, u32[]{:S(2)}, u32[]{:S(2)}) collective-permute-start(bf16[16,2176]{1,0:T(8,128)(2,1)S(1)} %get-tuple-element.40), channel_id=1, source_target_pairs={{0,2},{1,3},{2,0},{3,1},{4,6},{5,7},{6,4},{7,5},{8,10},{9,11},{10,... | collective-permute-start | bytes 208904 | tf_op jit(solution)/shard_map/ppermute | solution.py:150
  28.2 2.8 %collective-permute-done.10.refs_3_ = bf16[16,2176]{1,0:T(8,128)(2,1)S(1)} collective-permute-done((bf16[16,2176]{1,0:T(8,128)(2,1)S(1)}, bf16[16,2176]{1,0:T(8,128)(2,1)S(1)}, u32[]{:S(2)}, u32[]{:S(2)}) %collective-permute-start.10) | collective-permute-done | bytes 69664 | tf_op jit(solution)/shard_map/ppermute | solution.py:150
  30.9 1.1 %collective-permute-done.8.refs_1_ = bf16[16,2176]{1,0:T(8,128)(2,1)S(1)} collective-permute-done((bf16[16,2176]{1,0:T(8,128)(2,1)S(1)}, bf16[16,2176]{1,0:T(8,128)(2,1)S(1)}, u32[]{:S(2)}, u32[]{:S(2)}) %collective-permute-start.8) | collective-permute-done | bytes 69664 | tf_op jit(solution)/shard_map/ppermute | solution.py:150
  32.0 0.2 shard_map.159
  32.3 0.8 %collective-permute-start.12 = (bf16[32,1024]{1,0:T(8,128)(2,1)S(1)}, bf16[32,1024]{1,0:T(8,128)(2,1)S(1)}, u32[]{:S(2)}, u32[]{:S(2)}) collective-permute-start(bf16[32,1024]{1,0:T(8,128)(2,1)S(1)} %get-tuple-element.46.own), channel_id=1, source_target_pairs={{0,2},{1,3},{2,0},{3,1},{4,6},{5,7},{6,4},{7,5},{8,10},{9,11},{10,... | collective-permute-start | bytes 196616 | tf_op jit(solution)/shard_map/ppermute | solution.py:150
  33.1 3.5 %collective-permute-done.12.part2 = bf16[32,1024]{1,0:T(8,128)(2,1)S(1)} collective-permute-done((bf16[32,1024]{1,0:T(8,128)(2,1)S(1)}, bf16[32,1024]{1,0:T(8,128)(2,1)S(1)}, u32[]{:S(2)}, u32[]{:S(2)}) %collective-permute-start.12) | collective-permute-done | bytes 65568 | tf_op jit(solution)/shard_map/ppermute | solution.py:150
  36.6 1.2 %collective-permute-done.13.part3 = bf16[32,1024]{1,0:T(8,128)(2,1)S(1)} collective-permute-done((bf16[32,1024]{1,0:T(8,128)(2,1)S(1)}, bf16[32,1024]{1,0:T(8,128)(2,1)S(1)}, u32[]{:S(2)}, u32[]{:S(2)}) %collective-permute-start.13) | collective-permute-done | bytes 65568 | tf_op jit(solution)/shard_map/ppermute | solution.py:150
  37.9 1.1 %shard_map.160 = bf16[8,16,384]{2,1,0:T(8,128)(2,1)} custom-call(bf16[32,1024]{1,0:T(8,128)(2,1)S(1)} %get-tuple-element.46.own, bf16[32,1024]{1,0:T(8,128)(2,1)S(1)} %collective-permute-done.11.part1, bf16[32,1024]{1,0:T(8,128)(2,1)S(1)} %collective-permute-done.12.part2, bf16[32,1024]{1,0:T(8,128)(2,1)S(1)} %collective-permute-done.13.part3, ...), custom_call_target="tpu_custom_call" | custom-call | flops 200000000 | bytes 2000000 | tf_op jit(solution)/shard_map/pallas_call | solution.py:137
  39.0 3.4 %all-to-all-start = ((bf16[8,16,384]{2,1,0:T(8,128)(2,1)}), bf16[8,16,384]{2,1,0:T(8,128)(2,1)S(1)}, u32[]{:S(2)}, u32[]{:S(2)}) async-start(bf16[8,16,384]{2,1,0:T(8,128)(2,1)} %shard_map.160), calls=%async_computation | async-start | bytes 196608 | tf_op jit(solution)/shard_map/all_to_all | solution.py:602
  42.3 0.6 %shard_map.152 = bf16[32,384]{1,0:T(8,128)(2,1)} custom-call(bf16[32,384]{1,0:T(8,128)(2,1)S(1)} %get-tuple-element.32.attended), custom_call_target="tpu_custom_call" | custom-call | flops 100000 | bytes 100000 | tf_op jit(solution)/shard_map/pallas_call | solution.py:137
  43.0 6.4 %all-to-all-done = bf16[8,16,384]{2,1,0:T(8,128)(2,1)S(1)} async-done(((bf16[8,16,384]{2,1,0:T(8,128)(2,1)}), bf16[8,16,384]{2,1,0:T(8,128)(2,1)S(1)}, u32[]{:S(2)}, u32[]{:S(2)}) %all-to-all-start) | async-done | bytes 98336 | tf_op jit(solution)/shard_map/all_to_all | solution.py:602
  49.4 0.8 %shard_map.161 = bf16[32,384]{1,0:T(8,128)(2,1)} custom-call(bf16[128,384]{1,0:T(8,128)(2,1)S(1)} %bitcast.11, bf16[32,128]{1,0:T(8,128)(2,1)S(1)} %get-tuple-element.47.pick0, bf16[32,128]{1,0:T(8,128)(2,1)S(1)} %get-tuple-element.48.pick1, f32[32,128]{1,0:T(8,128)S(1)} %get-tuple-element.49.first_weight, bf16[32,384]{1,0:T(8,128)(2,1)S(1)} %get-tuple-element.32.attended), custom_call_target="tpu_custom_call" | custom-call | flops 100000 | bytes 100000 | tf_op jit(solution)/shard_map/pallas_call | solution.py:137
  (26 shorter events, 0.3 us)
Async XLA Ops:
  0.6 7.2 %copy-start.5 = (s32[32,2]{0,1:T(2,128)S(1)}, s32[32,2]{0,1:T(2,128)}, u32[]{:S(2)}) copy-start(s32[32,2]{0,1:T(2,128)} %param.24) | copy-start | bytes 772
  0.6 7.2 %copy-start.4 = (f32[384,16]{0,1:T(8,128)S(1)}, f32[384,16]{0,1:T(8,128)}, u32[]{:S(2)}) copy-start(f32[384,16]{0,1:T(8,128)} %param.23) | copy-start | bytes 73732
  0.7 7.2 %copy-start.3 = (bf16[32,384]{1,0:T(8,128)(2,1)S(1)}, bf16[32,384]{1,0:T(8,128)(2,1)}, u32[]{:S(2)}) copy-start(bf16[32,384]{1,0:T(8,128)(2,1)} %resid.1) | copy-start | bytes 73732
  0.7 21.8 %copy-start.6 = (f32[384]{0:T(512)S(1)}, f32[384]{0:T(512)}, u32[]{:S(2)}) copy-start(f32[384]{0:T(512)} %param.22) | copy-start | bytes 4612
  0.7 21.9 %copy-start = (bf16[2,384,1024]{2,1,0:T(8,128)(2,1)S(1)}, bf16[2,384,1024]{2,1,0:T(8,128)(2,1)}, u32[]{:S(2)}) copy-start(bf16[2,384,1024]{2,1,0:T(8,128)(2,1)} %param.25) | copy-start | bytes 4718596
  0.7 21.9 %copy-start.1 = (bf16[2,384,1024]{2,1,0:T(8,128)(2,1)S(1)}, bf16[2,384,1024]{2,1,0:T(8,128)(2,1)}, u32[]{:S(2)}) copy-start(bf16[2,384,1024]{2,1,0:T(8,128)(2,1)} %param.26) | copy-start | bytes 4718596
  4.7 4.8 %collective-permute-start = (bf16[32,384]{1,0:T(8,128)(2,1)S(1)}, bf16[32,384]{1,0:T(8,128)(2,1)S(1)}, u32[]{:S(2)}, u32[]{:S(2)}) collective-permute-start(bf16[32,384]{1,0:T(8,128)(2,1)S(1)} %get-tuple-element.28), channel_id=1, source_target_pairs={{0,2},{1,3},{2,0},{3,1},{4,6},{5,7},{6,4},{7,5},{8,10},{9,11},{10,... | collective-permute-start | bytes 73736 | tf_op jit(solution)/shard_map/ppermute | solution.py:150
  7.7 3.3 %collective-permute-start.1 = (bf16[32,384]{1,0:T(8,128)(2,1)S(1)}, bf16[32,384]{1,0:T(8,128)(2,1)S(1)}, u32[]{:S(2)}, u32[]{:S(2)}) collective-permute-start(bf16[32,384]{1,0:T(8,128)(2,1)S(1)} %get-tuple-element.29), channel_id=1, source_target_pairs={{0,3},{1,2},{2,1},{3,0},{4,7},{5,6},{6,5},{7,4},{8,11},{9,10},{10,... | collective-permute-start | bytes 73736 | tf_op jit(solution)/shard_map/ppermute | solution.py:150
  7.7 3.3 %collective-permute-start.2 = (bf16[32,384]{1,0:T(8,128)(2,1)S(1)}, bf16[32,384]{1,0:T(8,128)(2,1)S(1)}, u32[]{:S(2)}, u32[]{:S(2)}) collective-permute-start(bf16[32,384]{1,0:T(8,128)(2,1)S(1)} %get-tuple-element.30), channel_id=1, source_target_pairs={{0,1},{1,0},{2,3},{3,2},{4,5},{5,4},{6,7},{7,6},{8,9},{9,8},{10,11... | collective-permute-start | bytes 73736 | tf_op jit(solution)/shard_map/ppermute | solution.py:150
  11.1 4.5 %collective-permute-start.3 = (bf16[32,384]{1,0:T(8,128)(2,1)S(1)}, bf16[32,384]{1,0:T(8,128)(2,1)S(1)}, u32[]{:S(2)}, u32[]{:S(2)}) collective-permute-start(bf16[32,384]{1,0:T(8,128)(2,1)S(1)} %get-tuple-element.34), channel_id=1, source_target_pairs={{0,8},{4,12},{8,0},{12,4},{16,24},{20,28},{24,16},{28,20},{1,9},{5... | collective-permute-start | bytes 73736 | tf_op jit(solution)/shard_map/ppermute | solution.py:150
  12.7 4.9 %collective-permute-start.4 = (bf16[32,384]{1,0:T(8,128)(2,1)S(1)}, bf16[32,384]{1,0:T(8,128)(2,1)S(1)}, u32[]{:S(2)}, u32[]{:S(2)}) collective-permute-start(bf16[32,384]{1,0:T(8,128)(2,1)S(1)} %get-tuple-element.35), channel_id=1, source_target_pairs={{0,16},{4,20},{8,24},{12,28},{16,0},{20,4},{24,8},{28,12},{1,17},{... | collective-permute-start | bytes 73736 | tf_op jit(solution)/shard_map/ppermute | solution.py:150
  15.3 5.6 %collective-permute-start.5 = (bf16[32,384]{1,0:T(8,128)(2,1)S(1)}, bf16[32,384]{1,0:T(8,128)(2,1)S(1)}, u32[]{:S(2)}, u32[]{:S(2)}) collective-permute-start(bf16[32,384]{1,0:T(8,128)(2,1)S(1)} %get-tuple-element.36), channel_id=1, source_target_pairs={{0,24},{4,28},{8,16},{12,20},{16,8},{20,12},{24,0},{28,4},{1,25},{... | collective-permute-start | bytes 73736 | tf_op jit(solution)/shard_map/ppermute | solution.py:150
  21.0 4.1 %collective-permute-start.6 = (bf16[64,384]{1,0:T(8,128)(2,1)S(1)}, bf16[64,384]{1,0:T(8,128)(2,1)S(1)}, u32[]{:S(2)}, u32[]{:S(2)}) collective-permute-start(bf16[64,384]{1,0:T(8,128)(2,1)S(1)} %shard_map.153), channel_id=1, source_target_pairs={{0,4},{4,0},{8,12},{12,8},{16,20},{20,16},{24,28},{28,24},{1,5},{5... | collective-permute-start | bytes 147464 | tf_op jit(solution)/shard_map/ppermute | solution.py:150
  23.3 14.6 %copy-start.2 = (bf16[2,1024,384]{2,1,0:T(8,128)(2,1)S(1)}, bf16[2,1024,384]{2,1,0:T(8,128)(2,1)}, u32[]{:S(2)}) copy-start(bf16[2,1024,384]{2,1,0:T(8,128)(2,1)} %param.27) | copy-start | bytes 4718596
  23.3 2.5 %collective-permute-start.9 = (bf16[32,2176]{1,0:T(8,128)(2,1)S(1)}, bf16[32,2176]{1,0:T(8,128)(2,1)S(1)}, u32[]{:S(2)}, u32[]{:S(2)}) collective-permute-start(bf16[32,2176]{1,0:T(8,128)(2,1)S(1)} %get-tuple-element.43), channel_id=1, source_target_pairs={{0,1},{1,0},{2,3},{3,2},{4,5},{5,4},{6,7},{7,6},{8,9},{9,8},{10,11... | collective-permute-start | bytes 417800 | tf_op jit(solution)/shard_map/ppermute | solution.py:150
  25.7 1.4 %collective-permute-start.7 = (bf16[32,2176]{1,0:T(8,128)(2,1)S(1)}, bf16[32,2176]{1,0:T(8,128)(2,1)S(1)}, u32[]{:S(2)}, u32[]{:S(2)}) collective-permute-start(bf16[32,2176]{1,0:T(8,128)(2,1)S(1)} %get-tuple-element.38), channel_id=1, source_target_pairs={{0,1},{1,0},{2,3},{3,2},{4,5},{5,4},{6,7},{7,6},{8,9},{9,8},{10,11... | collective-permute-start | bytes 417800 | tf_op jit(solution)/shard_map/ppermute | solution.py:150
  26.0 5.0 %collective-permute-start.10 = (bf16[16,2176]{1,0:T(8,128)(2,1)S(1)}, bf16[16,2176]{1,0:T(8,128)(2,1)S(1)}, u32[]{:S(2)}, u32[]{:S(2)}) collective-permute-start(bf16[16,2176]{1,0:T(8,128)(2,1)S(1)} %get-tuple-element.45), channel_id=1, source_target_pairs={{0,2},{1,3},{2,0},{3,1},{4,6},{5,7},{6,4},{7,5},{8,10},{9,11},{10,... | collective-permute-start | bytes 208904 | tf_op jit(solution)/shard_map/ppermute | solution.py:150
  27.3 4.7 %collective-permute-start.8 = (bf16[16,2176]{1,0:T(8,128)(2,1)S(1)}, bf16[16,2176]{1,0:T(8,128)(2,1)S(1)}, u32[]{:S(2)}, u32[]{:S(2)}) collective-permute-start(bf16[16,2176]{1,0:T(8,128)(2,1)S(1)} %get-tuple-element.40), channel_id=1, source_target_pairs={{0,2},{1,3},{2,0},{3,1},{4,6},{5,7},{6,4},{7,5},{8,10},{9,11},{10,... | collective-permute-start | bytes 208904 | tf_op jit(solution)/shard_map/ppermute | solution.py:150
  32.3 4.3 %collective-permute-start.12 = (bf16[32,1024]{1,0:T(8,128)(2,1)S(1)}, bf16[32,1024]{1,0:T(8,128)(2,1)S(1)}, u32[]{:S(2)}, u32[]{:S(2)}) collective-permute-start(bf16[32,1024]{1,0:T(8,128)(2,1)S(1)} %get-tuple-element.46.own), channel_id=1, source_target_pairs={{0,2},{1,3},{2,0},{3,1},{4,6},{5,7},{6,4},{7,5},{8,10},{9,11},{10,... | collective-permute-start | bytes 196616 | tf_op jit(solution)/shard_map/ppermute | solution.py:150
  33.1 3.5 %collective-permute-start.11 = (bf16[32,1024]{1,0:T(8,128)(2,1)S(1)}, bf16[32,1024]{1,0:T(8,128)(2,1)S(1)}, u32[]{:S(2)}, u32[]{:S(2)}) collective-permute-start(bf16[32,1024]{1,0:T(8,128)(2,1)S(1)} %get-tuple-element.46.own), channel_id=1, source_target_pairs={{0,1},{1,0},{2,3},{3,2},{4,5},{5,4},{6,7},{7,6},{8,9},{9,8},{10,11... | collective-permute-start | bytes 196616 | tf_op jit(solution)/shard_map/ppermute | solution.py:150
  36.6 1.3 %collective-permute-start.13 = (bf16[32,1024]{1,0:T(8,128)(2,1)S(1)}, bf16[32,1024]{1,0:T(8,128)(2,1)S(1)}, u32[]{:S(2)}, u32[]{:S(2)}) collective-permute-start(bf16[32,1024]{1,0:T(8,128)(2,1)S(1)} %collective-permute-done.12.part2), channel_id=1, source_target_pairs={{0,1},{1,0},{2,3},{3,2},{4,5},{5,4},{6,7},{7,6},{8,9},{9,8},{10,11... | collective-permute-start | bytes 196616 | tf_op jit(solution)/shard_map/ppermute | solution.py:150
  39.0 10.4 %all-to-all-start = ((bf16[8,16,384]{2,1,0:T(8,128)(2,1)}), bf16[8,16,384]{2,1,0:T(8,128)(2,1)S(1)}, u32[]{:S(2)}, u32[]{:S(2)}) async-start(bf16[8,16,384]{2,1,0:T(8,128)(2,1)} %shard_map.160), calls=%async_computation | async-start | bytes 196608 | tf_op jit(solution)/shard_map/all_to_all | solution.py:602

commit v7 on v6

--- a/solution.py
+++ b/solution.py
@@ -153,7 +153,7 @@
 def attend_kernel(
     lengths_hbm, queries_hbm, keys_hbm, values_hbm, k_hbm, v_hbm, w_hbm, own, sent1, sent2, sent3,
     lengths, queries, new_keys, new_values, k_buf, v_buf, w_buf,
-    query_s, self_s, score_s, weight_s, small_sems, sems,
+    query_s, self_s, score_s, weight_s, product_s, small_sems, sems,
 ):
     row_count = queries.shape[0]
     width = own.shape[1]
@@ -256,16 +256,26 @@
     for copy in copies[2 * chunks :]:
         copy.wait()
     place_tp = lax.axis_index("tp")
+    product_s[...] = jnp.dot(attention, w_buf[...], preferred_element_type=jnp.float32)
     for shift, out in zip(TP_ORDER, (own, sent1, sent2, sent3)):
         columns = pl.ds(pl.multiple_of((place_tp ^ shift) * width, width), width)
-        out[...] = jnp.dot(
-            attention, w_buf[:, columns], preferred_element_type=jnp.float32
-        ).astype(out.dtype)
+        out[...] = product_s[:, columns].astype(out.dtype)
 
 
 def ready_kernel(
-    slot_dev, own, resid, routes, w_router, base, pick_rows, pick0, pick1, router_rows
+    slot_dev, own, resid, routes, w_router, gate_hbm, up_hbm,
+    base, pick_rows, pick0, pick1, router_rows, w_gate, w_up, sems,
 ):
+    copies = []
+    for source, target in ((gate_hbm, w_gate), (up_hbm, w_up)):
+        size = source.shape[0] // 4
+        for chunk in range(4):
+            part = pl.ds(chunk * size, size)
+            copies.append(
+                pltpu.make_async_copy(source.at[part], target.at[part], sems.at[len(copies)])
+            )
+    for copy in copies:
+        copy.start()
     base[...] = own[...] + resid[...].astype(jnp.float32)
     packed_count, row_count = pick_rows.shape
 
@@ -295,6 +305,8 @@
         signed[:, :EXPERTS], w_router[...],
         precision=lax.Precision.HIGHEST, preferred_element_type=jnp.float32,
     )
+    for copy in copies:
+        copy.wait()
 
 
 def pack_kernel(base, part1, part2, part3, pick_rows, attended, home, sent1, sent2, sent3):
@@ -511,6 +523,7 @@
             pltpu.VMEM((8 * row_count, lanes), f32),
             pltpu.VMEM((8 * row_count, cache_len), f32),
             pltpu.VMEM((8 * row_count, cache_len), bf16),
+            pltpu.VMEM((row_count, w_out.shape[1]), f32),
             pltpu.SemaphoreType.DMA((4,)),
             pltpu.SemaphoreType.DMA((12,)),
         ],
@@ -522,7 +535,8 @@
         return [partner_permute(block, "tp", k) for k, block in zip(TP_ORDER[1:], sents)]
 
     parts = sum_exchange(sents)
-    base, pick_rows, pick0, pick1, router_rows = call(
+    weight = (slot_dev * width, hidden)
+    base, pick_rows, pick0, pick1, router_rows, *weights = call(
         functools.partial(ready_kernel, slot_dev),
         [
             ((row_count, width), f32),
@@ -530,9 +544,21 @@
             ((row_count, packed_count), bf16),
             ((row_count, packed_count), bf16),
             ((row_count, width), f32),
+            (weight, bf16),
+            (weight, bf16),
         ],
-        [spec()] * 4,
-        (own, resid, routes.T, w_router.T),
+        [spec()] * 4 + [spec(pl.ANY)] * 2,
+        (
+            own,
+            resid,
+            routes.T,
+            w_router.T,
+            pltpu.with_memory_space_constraint(w_gate.reshape(weight), pltpu.HBM),
+            pltpu.with_memory_space_constraint(w_up.reshape(weight), pltpu.HBM),
+        ),
+        scratch=[pltpu.SemaphoreType.DMA((8,))],
+        mebibytes=12,
+        moved=3_300_000,
     )
     attended, home, *sents = call(
         pack_kernel,
@@ -544,12 +570,12 @@
         stats_kernel, [((row_count, 128), f32)], [spec()] * 3, (attended, gain, router_rows)
     )
     (result,) = call(result_kernel, [((row_count, width), bf16)], [spec()], (attended,))
+    stats, result = lax.optimization_barrier((stats, result))
     parts = [partner_permute(block, "req", 2 * k) for k, block in enumerate(sents, 1)]
     (along,) = call(
         turn_kernel, [((2 * quarter, width), bf16)], [spec()] * 4, (home, *parts)
     )
     along = partner_permute(along, "req", 1)
-    weights = (w_gate.reshape(slot_dev * width, hidden), w_up.reshape(slot_dev * width, hidden))
     half = quarter // 2
     message = (half, 2 * hidden + 128)
     lhs = pltpu.VMEM((packed_count // 2, slot_dev * width), bf16)

time: 50.4 us -> 48.9 us (0.970)
  blocking collectives: 0 us -> 9.72 us
  waiting for transfers between devices: 25.3 us -> 16 us
  starting transfers between devices: 15.2 us -> 12.3 us
  Pallas kernels: 8.91 us -> 10 us
    all_to_all x0 -> x1, blocking collectives: none -> 9.72 us  [shards(): lax.all_to_all(computed, 'req', split_axis=0, concat_axis=0, tiled=True)]
    all_to_all x1 -> x0, waiting for transfers between devices: 6.45 us -> none  [shards(): lax.all_to_all(computed, 'req', split_axis=0, concat_axis=0, tiled=True)]
    all_to_all x1 -> x0, starting transfers between devices: 3.36 us -> none  [shards(): lax.all_to_all(computed, 'req', split_axis=0, concat_axis=0, tiled=True)]
    ppermute x14, waiting for transfers between devices: 18.8 us -> 16 us  [partner_permute(): return lax.ppermute(block, axis, [(i, i ^ distance) for i in range(count)])]
    pallas_call x13, Pallas kernels: 8.91 us -> 10 us  [call(): pl.pallas_call(kernel, out_shape=[jax.ShapeDtypeStruct(shape, dtype) for...]
  transfers between devices with their start and end apart: 15 -> 14, of which waited for: 11 -> 9; matrix products, arithmetic and copies ran while one was open for 0% -> 0% of each run, Pallas kernels for 5% -> 9%
where the time goes in v7:
time: 48.9 us; the launch traced here: 48.8 us
  waiting for transfers between devices  16 us (33%)
  starting transfers between devices  12.3 us (25%)
  Pallas kernels  10 us (20%)
  blocking collectives  9.72 us (20%)
  between operations  0.75 us (2%)
    ppermute x14, waiting for transfers between devices, partner_permute(): return lax.ppermute(block, axis, [(i, i ^ distance) for i in range(count)])  16 us
    ppermute x14, starting transfers between devices, partner_permute(): return lax.ppermute(block, axis, [(i, i ^ distance) for i in range(count)])  12.3 us
    pallas_call x13, Pallas kernels, call(): pl.pallas_call(kernel, out_shape=[jax.ShapeDtypeStruct(shape, dtype) for...  10 us
    all_to_all x1, blocking collectives, shards(): lax.all_to_all(computed, 'req', split_axis=0, concat_axis=0, tiled=True)  9.72 us
  transfers between devices with their start and end apart: 14, of which 9 were waited for; matrix products, arithmetic and copies ran while one was open for 0% of the time, Pallas kernels for 9%

profile of v7, /device:TPU:0, one launch (start us, length us, event | category | flops | bytes accessed | tf_op | source)
XLA Modules:
  0.0 48.8 jit_solution(12725363763693989675)
XLA Ops:
  0.7 4.0 %shard_map.149 = (f32[32,384]{1,0:T(8,128)S(1)}, bf16[32,384]{1,0:T(8,128)(2,1)S(1)}, bf16[32,384]{1,0:T(8,128)(2,1)S(1)}, bf16[32,384]{1,0:T(8,128)(2,1)S(1)}) custom-call(s32[32]{0:T(128)} %lengths_hbm.1, bf16[32,384]{1,0:T(8,128)(2,1)} %queries_hbm.1, bf16[32,128]{1,0:T(8,128)(2,1)} %keys_hbm.1, bf16[32,128]{1,0:T(8,128)(2,1)} %values_hbm.1, ...), custom_call_target="tpu_custom_call" | custom-call | flops 200000000 | bytes 3400000 | tf_op jit(solution)/shard_map/pallas_call | solution.py:137
  4.6 3.0 %collective-permute-start = (bf16[32,384]{1,0:T(8,128)(2,1)S(1)}, bf16[32,384]{1,0:T(8,128)(2,1)S(1)}, u32[]{:S(2)}, u32[]{:S(2)}) collective-permute-start(bf16[32,384]{1,0:T(8,128)(2,1)S(1)} %get-tuple-element.32), channel_id=1, source_target_pairs={{0,2},{1,3},{2,0},{3,1},{4,6},{5,7},{6,4},{7,5},{8,10},{9,11},{10,... | collective-permute-start | bytes 73736 | tf_op jit(solution)/shard_map/ppermute | solution.py:150
  7.6 0.2 collective-permute-start.2
  7.8 2.0 %shard_map.150 = (f32[32,384]{1,0:T(8,128)S(1)}, bf16[128,32]{1,0:T(8,128)(2,1)S(1)}, bf16[32,128]{1,0:T(8,128)(2,1)S(1)}, bf16[32,128]{1,0:T(8,128)(2,1)S(1)}, ...) custom-call(f32[32,384]{1,0:T(8,128)S(1)} %get-tuple-element.30.own, ...), custom_call_target="tpu_custom_call" | custom-call | flops 100000 | bytes 3300000 | tf_op jit(solution)/shard_map/pallas_call | solution.py:137
  9.9 1.0 %collective-permute-done.1.part2 = bf16[32,384]{1,0:T(8,128)(2,1)S(1)} collective-permute-done((bf16[32,384]{1,0:T(8,128)(2,1)S(1)}, bf16[32,384]{1,0:T(8,128)(2,1)S(1)}, u32[]{:S(2)}, u32[]{:S(2)}) %collective-permute-start.1) | collective-permute-done | bytes 24608 | tf_op jit(solution)/shard_map/ppermute | solution.py:150
  10.9 0.2 shard_map.151
  11.1 1.6 %collective-permute-start.3 = (bf16[32,384]{1,0:T(8,128)(2,1)S(1)}, bf16[32,384]{1,0:T(8,128)(2,1)S(1)}, u32[]{:S(2)}, u32[]{:S(2)}) collective-permute-start(bf16[32,384]{1,0:T(8,128)(2,1)S(1)} %get-tuple-element.40), channel_id=1, source_target_pairs={{0,8},{4,12},{8,0},{12,4},{16,24},{20,28},{24,16},{28,20},{1,9},{5... | collective-permute-start | bytes 73736 | tf_op jit(solution)/shard_map/ppermute | solution.py:150
  12.7 2.6 %collective-permute-start.4 = (bf16[32,384]{1,0:T(8,128)(2,1)S(1)}, bf16[32,384]{1,0:T(8,128)(2,1)S(1)}, u32[]{:S(2)}, u32[]{:S(2)}) collective-permute-start(bf16[32,384]{1,0:T(8,128)(2,1)S(1)} %get-tuple-element.41), channel_id=1, source_target_pairs={{0,16},{4,20},{8,24},{12,28},{16,0},{20,4},{24,8},{28,12},{1,17},{... | collective-permute-start | bytes 73736 | tf_op jit(solution)/shard_map/ppermute | solution.py:150
  15.3 0.2 collective-permute-start.5
  15.5 2.1 %collective-permute-done.4.part2.in2 = bf16[32,384]{1,0:T(8,128)(2,1)S(1)} collective-permute-done((bf16[32,384]{1,0:T(8,128)(2,1)S(1)}, bf16[32,384]{1,0:T(8,128)(2,1)S(1)}, u32[]{:S(2)}, u32[]{:S(2)}) %collective-permute-start.4) | collective-permute-done | bytes 24608 | tf_op jit(solution)/shard_map/ppermute | solution.py:150
  17.6 3.3 %collective-permute-done.5.part3.in3 = bf16[32,384]{1,0:T(8,128)(2,1)S(1)} collective-permute-done((bf16[32,384]{1,0:T(8,128)(2,1)S(1)}, bf16[32,384]{1,0:T(8,128)(2,1)S(1)}, u32[]{:S(2)}, u32[]{:S(2)}) %collective-permute-start.5) | collective-permute-done | bytes 24608 | tf_op jit(solution)/shard_map/ppermute | solution.py:150
  20.9 1.5 %collective-permute-start.6 = (bf16[64,384]{1,0:T(8,128)(2,1)S(1)}, bf16[64,384]{1,0:T(8,128)(2,1)S(1)}, u32[]{:S(2)}, u32[]{:S(2)}) collective-permute-start(bf16[64,384]{1,0:T(8,128)(2,1)S(1)} %shard_map.154), channel_id=1, source_target_pairs={{0,4},{4,0},{8,12},{12,8},{16,20},{20,16},{24,28},{28,24},{1,5},{5... | collective-permute-start | bytes 147464 | tf_op jit(solution)/shard_map/ppermute | solution.py:150
  22.4 0.6 %shard_map.153 = bf16[32,384]{1,0:T(8,128)(2,1)} custom-call(bf16[32,384]{1,0:T(8,128)(2,1)S(1)} %get-tuple-element.36.attended), custom_call_target="tpu_custom_call" | custom-call | flops 100000 | bytes 100000 | tf_op jit(solution)/shard_map/pallas_call | solution.py:137
  23.1 0.1 shard_map.152.stats
  23.1 0.7 %shard_map.157 = (f32[32,2176]{1,0:T(8,128)S(1)}, bf16[32,2176]{1,0:T(8,128)(2,1)S(1)}) custom-call(bf16[32,384]{1,0:T(8,128)(2,1)S(1)} %get-tuple-element.39.home.in0, bf16[32,384]{1,0:T(8,128)(2,1)S(1)} %collective-permute-done.3.part1.in1, bf16[32,384]{1,0:T(8,128)(2,1)S(1)} %collective-permute-done.4.part2.in2, ...), custom_call_target="tpu_custom_call" | custom-call | flops 400000000 | bytes 3500000 | tf_op jit(solution)/shard_map/pallas_call | solution.py:137
  23.8 0.1 collective-permute-start.9
  23.9 1.1 %collective-permute-done.6.blocks = bf16[64,384]{1,0:T(8,128)(2,1)S(1)} collective-permute-done((bf16[64,384]{1,0:T(8,128)(2,1)S(1)}, bf16[64,384]{1,0:T(8,128)(2,1)S(1)}, u32[]{:S(2)}, u32[]{:S(2)}) %collective-permute-start.6) | collective-permute-done | bytes 49184 | tf_op jit(solution)/shard_map/ppermute | solution.py:150
  25.0 0.7 %shard_map.155 = (f32[32,2176]{1,0:T(8,128)S(1)}, bf16[32,2176]{1,0:T(8,128)(2,1)S(1)}) custom-call(bf16[64,384]{1,0:T(8,128)(2,1)S(1)} %collective-permute-done.6.blocks, f32[1,384]{1,0:T(1,128)S(1)} %reshape.21.gain, bf16[768,1024]{1,0:T(8,128)(2,1)S(1)} %get-tuple-element.43.w_gate, bf16[768,1024]{1,0:T(8,128)(2,1)S(1)} %get-tuple-element.44.w_up), custom_call_target="tpu_custom_call" | custom-call | flops 400000000 | bytes 3500000 | tf_op jit(solution)/shard_map/pallas_call | solution.py:137
  25.8 0.2 shard_map.158
  25.9 1.0 %collective-permute-start.10 = (bf16[16,2176]{1,0:T(8,128)(2,1)S(1)}, bf16[16,2176]{1,0:T(8,128)(2,1)S(1)}, u32[]{:S(2)}, u32[]{:S(2)}) collective-permute-start(bf16[16,2176]{1,0:T(8,128)(2,1)S(1)} %get-tuple-element.53), channel_id=1, source_target_pairs={{0,2},{1,3},{2,0},{3,1},{4,6},{5,7},{6,4},{7,5},{8,10},{9,11},{10,... | collective-permute-start | bytes 208904 | tf_op jit(solution)/shard_map/ppermute | solution.py:150
  26.9 0.2 collective-permute-done.7.part
  27.1 0.2 shard_map.156
  27.3 1.0 %collective-permute-start.8 = (bf16[16,2176]{1,0:T(8,128)(2,1)S(1)}, bf16[16,2176]{1,0:T(8,128)(2,1)S(1)}, u32[]{:S(2)}, u32[]{:S(2)}) collective-permute-start(bf16[16,2176]{1,0:T(8,128)(2,1)S(1)} %get-tuple-element.48), channel_id=1, source_target_pairs={{0,2},{1,3},{2,0},{3,1},{4,6},{5,7},{6,4},{7,5},{8,10},{9,11},{10,... | collective-permute-start | bytes 208904 | tf_op jit(solution)/shard_map/ppermute | solution.py:150
  28.2 2.7 %collective-permute-done.10.refs_3_ = bf16[16,2176]{1,0:T(8,128)(2,1)S(1)} collective-permute-done((bf16[16,2176]{1,0:T(8,128)(2,1)S(1)}, bf16[16,2176]{1,0:T(8,128)(2,1)S(1)}, u32[]{:S(2)}, u32[]{:S(2)}) %collective-permute-start.10) | collective-permute-done | bytes 69664 | tf_op jit(solution)/shard_map/ppermute | solution.py:150
  30.9 1.1 %collective-permute-done.8.refs_1_ = bf16[16,2176]{1,0:T(8,128)(2,1)S(1)} collective-permute-done((bf16[16,2176]{1,0:T(8,128)(2,1)S(1)}, bf16[16,2176]{1,0:T(8,128)(2,1)S(1)}, u32[]{:S(2)}, u32[]{:S(2)}) %collective-permute-start.8) | collective-permute-done | bytes 69664 | tf_op jit(solution)/shard_map/ppermute | solution.py:150
  32.0 0.2 shard_map.159
  32.2 1.0 %collective-permute-start.12 = (bf16[32,1024]{1,0:T(8,128)(2,1)S(1)}, bf16[32,1024]{1,0:T(8,128)(2,1)S(1)}, u32[]{:S(2)}, u32[]{:S(2)}) collective-permute-start(bf16[32,1024]{1,0:T(8,128)(2,1)S(1)} %get-tuple-element.54.own), channel_id=1, source_target_pairs={{0,2},{1,3},{2,0},{3,1},{4,6},{5,7},{6,4},{7,5},{8,10},{9,11},{10,... | collective-permute-start | bytes 196616 | tf_op jit(solution)/shard_map/ppermute | solution.py:150
  33.2 3.3 %collective-permute-done.12.part2 = bf16[32,1024]{1,0:T(8,128)(2,1)S(1)} collective-permute-done((bf16[32,1024]{1,0:T(8,128)(2,1)S(1)}, bf16[32,1024]{1,0:T(8,128)(2,1)S(1)}, u32[]{:S(2)}, u32[]{:S(2)}) %collective-permute-start.12) | collective-permute-done | bytes 65568 | tf_op jit(solution)/shard_map/ppermute | solution.py:150
  36.5 1.2 %collective-permute-done.13.part3 = bf16[32,1024]{1,0:T(8,128)(2,1)S(1)} collective-permute-done((bf16[32,1024]{1,0:T(8,128)(2,1)S(1)}, bf16[32,1024]{1,0:T(8,128)(2,1)S(1)}, u32[]{:S(2)}, u32[]{:S(2)}) %collective-permute-start.13) | collective-permute-done | bytes 65568 | tf_op jit(solution)/shard_map/ppermute | solution.py:150
  37.8 0.5 shard_map.160
  38.3 9.7 %all_to_all.5 = bf16[8,16,384]{2,1,0:T(8,128)(2,1)S(1)} all-to-all(bf16[8,16,384]{2,1,0:T(8,128)(2,1)S(1)} %shard_map.160), channel_id=1, replica_groups=mesh['req'=8,'tp'=4] {'req'}, dimensions={0} | all-to-all | bytes 196608 | tf_op jit(solution)/shard_map/all_to_all | solution.py:628
  48.0 0.8 %shard_map.161 = bf16[32,384]{1,0:T(8,128)(2,1)} custom-call(bf16[128,384]{1,0:T(8,128)(2,1)S(1)} %bitcast.7, bf16[32,128]{1,0:T(8,128)(2,1)S(1)} %get-tuple-element.55.pick0, bf16[32,128]{1,0:T(8,128)(2,1)S(1)} %get-tuple-element.56.pick1, f32[32,128]{1,0:T(8,128)S(1)} %get-tuple-element.57.first_weight, bf16[32,384]{1,0:T(8,128)(2,1)S(1)} %get-tuple-element.36.attended), custom_call_target="tpu_custom_call" | custom-call | flops 100000 | bytes 100000 | tf_op jit(solution)/shard_map/pallas_call | solution.py:137
  (21 shorter events, 0.1 us)
Async XLA Ops:
  0.6 7.2 %copy-start.3 = (s32[32,2]{0,1:T(2,128)S(1)}, s32[32,2]{0,1:T(2,128)}, u32[]{:S(2)}) copy-start(s32[32,2]{0,1:T(2,128)} %param.24) | copy-start | bytes 772
  0.6 7.2 %copy-start.2 = (f32[384,16]{0,1:T(8,128)S(1)}, f32[384,16]{0,1:T(8,128)}, u32[]{:S(2)}) copy-start(f32[384,16]{0,1:T(8,128)} %param.23) | copy-start | bytes 73732
  0.7 7.2 %copy-start.1 = (bf16[32,384]{1,0:T(8,128)(2,1)S(1)}, bf16[32,384]{1,0:T(8,128)(2,1)}, u32[]{:S(2)}) copy-start(bf16[32,384]{1,0:T(8,128)(2,1)} %resid.1) | copy-start | bytes 73732
  4.6 5.3 %collective-permute-start = (bf16[32,384]{1,0:T(8,128)(2,1)S(1)}, bf16[32,384]{1,0:T(8,128)(2,1)S(1)}, u32[]{:S(2)}, u32[]{:S(2)}) collective-permute-start(bf16[32,384]{1,0:T(8,128)(2,1)S(1)} %get-tuple-element.32), channel_id=1, source_target_pairs={{0,2},{1,3},{2,0},{3,1},{4,6},{5,7},{6,4},{7,5},{8,10},{9,11},{10,... | collective-permute-start | bytes 73736 | tf_op jit(solution)/shard_map/ppermute | solution.py:150
  7.6 3.3 %collective-permute-start.1 = (bf16[32,384]{1,0:T(8,128)(2,1)S(1)}, bf16[32,384]{1,0:T(8,128)(2,1)S(1)}, u32[]{:S(2)}, u32[]{:S(2)}) collective-permute-start(bf16[32,384]{1,0:T(8,128)(2,1)S(1)} %get-tuple-element.33), channel_id=1, source_target_pairs={{0,3},{1,2},{2,1},{3,0},{4,7},{5,6},{6,5},{7,4},{8,11},{9,10},{10,... | collective-permute-start | bytes 73736 | tf_op jit(solution)/shard_map/ppermute | solution.py:150
  7.6 3.3 %collective-permute-start.2 = (bf16[32,384]{1,0:T(8,128)(2,1)S(1)}, bf16[32,384]{1,0:T(8,128)(2,1)S(1)}, u32[]{:S(2)}, u32[]{:S(2)}) collective-permute-start(bf16[32,384]{1,0:T(8,128)(2,1)S(1)} %get-tuple-element.34), channel_id=1, source_target_pairs={{0,1},{1,0},{2,3},{3,2},{4,5},{5,4},{6,7},{7,6},{8,9},{9,8},{10,11... | collective-permute-start | bytes 73736 | tf_op jit(solution)/shard_map/ppermute | solution.py:150
  7.8 14.6 %copy-start.4 = (f32[384]{0:T(512)S(1)}, f32[384]{0:T(512)}, u32[]{:S(2)}) copy-start(f32[384]{0:T(512)} %param.22) | copy-start | bytes 4612
  11.1 4.5 %collective-permute-start.3 = (bf16[32,384]{1,0:T(8,128)(2,1)S(1)}, bf16[32,384]{1,0:T(8,128)(2,1)S(1)}, u32[]{:S(2)}, u32[]{:S(2)}) collective-permute-start(bf16[32,384]{1,0:T(8,128)(2,1)S(1)} %get-tuple-element.40), channel_id=1, source_target_pairs={{0,8},{4,12},{8,0},{12,4},{16,24},{20,28},{24,16},{28,20},{1,9},{5... | collective-permute-start | bytes 73736 | tf_op jit(solution)/shard_map/ppermute | solution.py:150
  12.7 4.9 %collective-permute-start.4 = (bf16[32,384]{1,0:T(8,128)(2,1)S(1)}, bf16[32,384]{1,0:T(8,128)(2,1)S(1)}, u32[]{:S(2)}, u32[]{:S(2)}) collective-permute-start(bf16[32,384]{1,0:T(8,128)(2,1)S(1)} %get-tuple-element.41), channel_id=1, source_target_pairs={{0,16},{4,20},{8,24},{12,28},{16,0},{20,4},{24,8},{28,12},{1,17},{... | collective-permute-start | bytes 73736 | tf_op jit(solution)/shard_map/ppermute | solution.py:150
  15.3 5.6 %collective-permute-start.5 = (bf16[32,384]{1,0:T(8,128)(2,1)S(1)}, bf16[32,384]{1,0:T(8,128)(2,1)S(1)}, u32[]{:S(2)}, u32[]{:S(2)}) collective-permute-start(bf16[32,384]{1,0:T(8,128)(2,1)S(1)} %get-tuple-element.42), channel_id=1, source_target_pairs={{0,24},{4,28},{8,16},{12,20},{16,8},{20,12},{24,0},{28,4},{1,25},{... | collective-permute-start | bytes 73736 | tf_op jit(solution)/shard_map/ppermute | solution.py:150
  20.9 4.1 %collective-permute-start.6 = (bf16[64,384]{1,0:T(8,128)(2,1)S(1)}, bf16[64,384]{1,0:T(8,128)(2,1)S(1)}, u32[]{:S(2)}, u32[]{:S(2)}) collective-permute-start(bf16[64,384]{1,0:T(8,128)(2,1)S(1)} %shard_map.154), channel_id=1, source_target_pairs={{0,4},{4,0},{8,12},{12,8},{16,20},{20,16},{24,28},{28,24},{1,5},{5... | collective-permute-start | bytes 147464 | tf_op jit(solution)/shard_map/ppermute | solution.py:150
  23.8 14.0 %copy-start = (bf16[2,1024,384]{2,1,0:T(8,128)(2,1)S(1)}, bf16[2,1024,384]{2,1,0:T(8,128)(2,1)}, u32[]{:S(2)}) copy-start(bf16[2,1024,384]{2,1,0:T(8,128)(2,1)} %param.27) | copy-start | bytes 4718596
  23.8 1.9 %collective-permute-start.9 = (bf16[32,2176]{1,0:T(8,128)(2,1)S(1)}, bf16[32,2176]{1,0:T(8,128)(2,1)S(1)}, u32[]{:S(2)}, u32[]{:S(2)}) collective-permute-start(bf16[32,2176]{1,0:T(8,128)(2,1)S(1)} %get-tuple-element.51), channel_id=1, source_target_pairs={{0,1},{1,0},{2,3},{3,2},{4,5},{5,4},{6,7},{7,6},{8,9},{9,8},{10,11... | collective-permute-start | bytes 417800 | tf_op jit(solution)/shard_map/ppermute | solution.py:150
  25.7 1.4 %collective-permute-start.7 = (bf16[32,2176]{1,0:T(8,128)(2,1)S(1)}, bf16[32,2176]{1,0:T(8,128)(2,1)S(1)}, u32[]{:S(2)}, u32[]{:S(2)}) collective-permute-start(bf16[32,2176]{1,0:T(8,128)(2,1)S(1)} %get-tuple-element.46), channel_id=1, source_target_pairs={{0,1},{1,0},{2,3},{3,2},{4,5},{5,4},{6,7},{7,6},{8,9},{9,8},{10,11... | collective-permute-start | bytes 417800 | tf_op jit(solution)/shard_map/ppermute | solution.py:150
  25.9 5.0 %collective-permute-start.10 = (bf16[16,2176]{1,0:T(8,128)(2,1)S(1)}, bf16[16,2176]{1,0:T(8,128)(2,1)S(1)}, u32[]{:S(2)}, u32[]{:S(2)}) collective-permute-start(bf16[16,2176]{1,0:T(8,128)(2,1)S(1)} %get-tuple-element.53), channel_id=1, source_target_pairs={{0,2},{1,3},{2,0},{3,1},{4,6},{5,7},{6,4},{7,5},{8,10},{9,11},{10,... | collective-permute-start | bytes 208904 | tf_op jit(solution)/shard_map/ppermute | solution.py:150
  27.3 4.7 %collective-permute-start.8 = (bf16[16,2176]{1,0:T(8,128)(2,1)S(1)}, bf16[16,2176]{1,0:T(8,128)(2,1)S(1)}, u32[]{:S(2)}, u32[]{:S(2)}) collective-permute-start(bf16[16,2176]{1,0:T(8,128)(2,1)S(1)} %get-tuple-element.48), channel_id=1, source_target_pairs={{0,2},{1,3},{2,0},{3,1},{4,6},{5,7},{6,4},{7,5},{8,10},{9,11},{10,... | collective-permute-start | bytes 208904 | tf_op jit(solution)/shard_map/ppermute | solution.py:150
  32.2 4.3 %collective-permute-start.12 = (bf16[32,1024]{1,0:T(8,128)(2,1)S(1)}, bf16[32,1024]{1,0:T(8,128)(2,1)S(1)}, u32[]{:S(2)}, u32[]{:S(2)}) collective-permute-start(bf16[32,1024]{1,0:T(8,128)(2,1)S(1)} %get-tuple-element.54.own), channel_id=1, source_target_pairs={{0,2},{1,3},{2,0},{3,1},{4,6},{5,7},{6,4},{7,5},{8,10},{9,11},{10,... | collective-permute-start | bytes 196616 | tf_op jit(solution)/shard_map/ppermute | solution.py:150
  33.2 3.3 %collective-permute-start.11 = (bf16[32,1024]{1,0:T(8,128)(2,1)S(1)}, bf16[32,1024]{1,0:T(8,128)(2,1)S(1)}, u32[]{:S(2)}, u32[]{:S(2)}) collective-permute-start(bf16[32,1024]{1,0:T(8,128)(2,1)S(1)} %get-tuple-element.54.own), channel_id=1, source_target_pairs={{0,1},{1,0},{2,3},{3,2},{4,5},{5,4},{6,7},{7,6},{8,9},{9,8},{10,11... | collective-permute-start | bytes 196616 | tf_op jit(solution)/shard_map/ppermute | solution.py:150
  36.5 1.3 %collective-permute-start.13 = (bf16[32,1024]{1,0:T(8,128)(2,1)S(1)}, bf16[32,1024]{1,0:T(8,128)(2,1)S(1)}, u32[]{:S(2)}, u32[]{:S(2)}) collective-permute-start(bf16[32,1024]{1,0:T(8,128)(2,1)S(1)} %collective-permute-done.12.part2), channel_id=1, source_target_pairs={{0,1},{1,0},{2,3},{3,2},{4,5},{5,4},{6,7},{7,6},{8,9},{9,8},{10,11... | collective-permute-start | bytes 196616 | tf_op jit(solution)/shard_map/ppermute | solution.py:150

commit v8 on v7

--- a/solution.py
+++ b/solution.py
@@ -126,7 +126,7 @@
     return (attended, layer_out)
 
 
-TP_ORDER = (0, 2, 3, 1)
+FAR_FIRST = (0, 2, 3, 1)
 
 
 def spec(space=pltpu.VMEM):
@@ -153,7 +153,7 @@
 def attend_kernel(
     lengths_hbm, queries_hbm, keys_hbm, values_hbm, k_hbm, v_hbm, w_hbm, own, sent1, sent2, sent3,
     lengths, queries, new_keys, new_values, k_buf, v_buf, w_buf,
-    query_s, self_s, score_s, weight_s, product_s, small_sems, sems,
+    query_s, mixed_s, product_s, small_sems, sems,
 ):
     row_count = queries.shape[0]
     width = own.shape[1]
@@ -208,43 +208,57 @@
     values_new = jnp.dot(spread, new_values[...], preferred_element_type=jnp.float32)
     own_score = jnp.sum(query_s[...] * keys_new, axis=1, keepdims=True) * scale
 
-    upper = lax.broadcasted_iota(jnp.int32, (16, lanes), 0) < 8
-    position = lax.broadcasted_iota(jnp.int32, (16, cache_len), 1)
-    for pair in range(row_count // 2):
-        if pair % (per_chunk // 2) == 0:
-            copies[pair // (per_chunk // 2)].wait()
-        pair_rows = slice(16 * pair, 16 * pair + 16)
-        keys = k_buf[2 * pair : 2 * pair + 2].reshape(2 * cache_len, lanes)
-        raw = lax.dot_general(
-            query_s[pair_rows, :].astype(jnp.bfloat16), keys, (((1,), (1,)), ((), ())),
-            preferred_element_type=jnp.float32,
-        )
-        limit = jnp.where(upper, lengths[2 * pair], lengths[2 * pair + 1])
-        score_s[pair_rows, :] = jnp.where(
-            position < limit,
-            jnp.where(upper, raw[:, :cache_len], raw[:, cache_len:]) * scale,
-            -1e30,
-        )
-
-    scores = score_s[...]
-    peak = jnp.maximum(jnp.max(scores, axis=1, keepdims=True), own_score)
-    terms = jnp.exp(scores - peak)
-    own_term = jnp.exp(own_score - peak)
-    inverse = 1.0 / (jnp.sum(terms, axis=1, keepdims=True) + own_term)
-    weight_s[...] = (terms * inverse).astype(jnp.bfloat16)
-    own_weight = (own_term * inverse).astype(jnp.bfloat16).astype(jnp.float32)
-    self_s[...] = own_weight * values_new
-    for pair in range(row_count // 2):
-        if pair % (per_chunk // 2) == 0:
-            copies[chunks + pair // (per_chunk // 2)].wait()
-        pair_rows = slice(16 * pair, 16 * pair + 16)
-        values = jnp.concatenate([v_buf[2 * pair], v_buf[2 * pair + 1]], axis=1)
-        mixed = jnp.dot(weight_s[pair_rows, :], values, preferred_element_type=jnp.float32)
-        query_s[pair_rows, :] = (
-            jnp.where(upper, mixed[:, :lanes], mixed[:, lanes:]) + self_s[pair_rows, :]
-        )
-
-    mixed = [query_s[pl.ds(head, row_count, stride=8), :] for head in range(6)]
+    position = lax.broadcasted_iota(jnp.int32, (8, cache_len), 1)
+    group = 4
+    query_rows = query_s[...].astype(jnp.bfloat16)
+
+    def own_tiles(product):
+        return [
+            product[8 * index : 8 * index + 8, lanes * index : lanes * (index + 1)]
+            for index in range(group)
+        ]
+
+    def attend(chunk):
+        start = chunk * per_chunk
+        chunk_rows = slice(8 * start, 8 * (start + per_chunk))
+        copies[chunk].wait()
+        tiles = []
+        for first in range(start, start + per_chunk, group):
+            raw = lax.dot_general(
+                query_rows[8 * first : 8 * (first + group)],
+                k_buf[first : first + group].reshape(group * cache_len, lanes),
+                (((1,), (1,)), ((), ())),
+                preferred_element_type=jnp.float32,
+            )
+            for index, tile in enumerate(own_tiles(raw)):
+                tiles.append(jnp.where(position < lengths[first + index], tile * scale, -1e30))
+        scores = jnp.concatenate(tiles, axis=0)
+        own = own_score[chunk_rows]
+        peak = jnp.maximum(jnp.max(scores, axis=1, keepdims=True), own)
+        terms = jnp.exp(scores - peak)
+        own_term = jnp.exp(own - peak)
+        inverse = 1.0 / (jnp.sum(terms, axis=1, keepdims=True) + own_term)
+        own_weight = (own_term * inverse).astype(jnp.bfloat16).astype(jnp.float32)
+        return (terms * inverse).astype(jnp.bfloat16), own_weight * values_new[chunk_rows]
+
+    def mix(chunk, weights, own):
+        start = chunk * per_chunk
+        copies[chunks + chunk].wait()
+        tiles = []
+        for first in range(start, start + per_chunk, group):
+            values = jnp.concatenate([v_buf[first + index] for index in range(group)], axis=1)
+            rows = slice(8 * (first - start), 8 * (first - start + group))
+            tiles += own_tiles(jnp.dot(weights[rows], values, preferred_element_type=jnp.float32))
+        mixed_s[8 * start : 8 * (start + per_chunk), :] = jnp.concatenate(tiles, axis=0) + own
+
+    ready = attend(0)
+    for chunk in range(1, chunks):
+        following = attend(chunk)
+        mix(chunk - 1, *ready)
+        ready = following
+    mix(chunks - 1, *ready)
+
+    mixed = [mixed_s[pl.ds(head, row_count, stride=8), :] for head in range(6)]
     attention = jnp.concatenate(
         [
             jnp.where(low, mixed[0], pltpu.roll(mixed[1], HEAD_DIM, 1)),
@@ -257,7 +271,7 @@
         copy.wait()
     place_tp = lax.axis_index("tp")
     product_s[...] = jnp.dot(attention, w_buf[...], preferred_element_type=jnp.float32)
-    for shift, out in zip(TP_ORDER, (own, sent1, sent2, sent3)):
+    for shift, out in zip(FAR_FIRST, (own, sent1, sent2, sent3)):
         columns = pl.ds(pl.multiple_of((place_tp ^ shift) * width, width), width)
         out[...] = product_s[:, columns].astype(out.dtype)
 
@@ -317,7 +331,7 @@
     attended[...] = rows
     packed = jnp.dot(pick_rows[...], rows, preferred_element_type=jnp.float32)
     size = home.shape[0]
-    for distance, out in enumerate((home, sent1, sent2, sent3)):
+    for distance, out in zip(FAR_FIRST, (home, sent1, sent2, sent3)):
         out[...] = packed[distance * size : (distance + 1) * size].astype(out.dtype)
 
 
@@ -521,8 +535,6 @@
             pltpu.VMEM(w_out.shape, bf16),
             pltpu.VMEM((8 * row_count, lanes), f32),
             pltpu.VMEM((8 * row_count, lanes), f32),
-            pltpu.VMEM((8 * row_count, cache_len), f32),
-            pltpu.VMEM((8 * row_count, cache_len), bf16),
             pltpu.VMEM((row_count, w_out.shape[1]), f32),
             pltpu.SemaphoreType.DMA((4,)),
             pltpu.SemaphoreType.DMA((12,)),
@@ -532,7 +544,7 @@
         moved=3_400_000,
     )
     def sum_exchange(sents):
-        return [partner_permute(block, "tp", k) for k, block in zip(TP_ORDER[1:], sents)]
+        return [partner_permute(block, "tp", k) for k, block in zip(FAR_FIRST[1:], sents)]
 
     parts = sum_exchange(sents)
     weight = (slot_dev * width, hidden)
@@ -571,7 +583,10 @@
     )
     (result,) = call(result_kernel, [((row_count, width), bf16)], [spec()], (attended,))
     stats, result = lax.optimization_barrier((stats, result))
-    parts = [partner_permute(block, "req", 2 * k) for k, block in enumerate(sents, 1)]
+    hops = {
+        k: partner_permute(block, "req", 2 * k) for k, block in zip(FAR_FIRST[1:], sents)
+    }
+    parts = [hops[k] for k in (1, 2, 3)]
     (along,) = call(
         turn_kernel, [((2 * quarter, width), bf16)], [spec()] * 4, (home, *parts)
     )

time: 48.9 us -> 49.6 us (1.014)
  Pallas kernels: 10 us -> 10.6 us
    pallas_call x13, Pallas kernels: 10 us -> 10.6 us  [call(): pl.pallas_call(kernel, out_shape=[jax.ShapeDtypeStruct(shape, dtype) for...]
where the time goes in v8:
time: 49.6 us; the launch traced here: 49.4 us
  waiting for transfers between devices  16 us (32%)
  starting transfers between devices  12.3 us (25%)
  Pallas kernels  10.6 us (21%)
  blocking collectives  9.72 us (20%)
  between operations  0.75 us (2%)
    ppermute x14, waiting for transfers between devices, partner_permute(): return lax.ppermute(block, axis, [(i, i ^ distance) for i in range(count)])  16 us
    ppermute x14, starting transfers between devices, partner_permute(): return lax.ppermute(block, axis, [(i, i ^ distance) for i in range(count)])  12.3 us
    pallas_call x13, Pallas kernels, call(): pl.pallas_call(kernel, out_shape=[jax.ShapeDtypeStruct(shape, dtype) for...  10.6 us
    all_to_all x1, blocking collectives, shards(): lax.all_to_all(computed, 'req', split_axis=0, concat_axis=0, tiled=True)  9.72 us
  transfers between devices with their start and end apart: 14, of which 9 were waited for; matrix products, arithmetic and copies ran while one was open for 0% of the time, Pallas kernels for 9%

profile of v8, /device:TPU:0, one launch (start us, length us, event | category | flops | bytes accessed | tf_op | source)
XLA Modules:
  0.0 49.4 jit_solution(2691700413484871689)
XLA Ops:
  0.7 4.6 %shard_map.149 = (f32[32,384]{1,0:T(8,128)S(1)}, bf16[32,384]{1,0:T(8,128)(2,1)S(1)}, bf16[32,384]{1,0:T(8,128)(2,1)S(1)}, bf16[32,384]{1,0:T(8,128)(2,1)S(1)}) custom-call(s32[32]{0:T(128)} %lengths_hbm.1, bf16[32,384]{1,0:T(8,128)(2,1)} %queries_hbm.1, bf16[32,128]{1,0:T(8,128)(2,1)} %keys_hbm.1, bf16[32,128]{1,0:T(8,128)(2,1)} %values_hbm.1, ...), custom_call_target="tpu_custom_call" | custom-call | flops 200000000 | bytes 3400000 | tf_op jit(solution)/shard_map/pallas_call | solution.py:137
  5.3 3.0 %collective-permute-start = (bf16[32,384]{1,0:T(8,128)(2,1)S(1)}, bf16[32,384]{1,0:T(8,128)(2,1)S(1)}, u32[]{:S(2)}, u32[]{:S(2)}) collective-permute-start(bf16[32,384]{1,0:T(8,128)(2,1)S(1)} %get-tuple-element.32), channel_id=1, source_target_pairs={{0,2},{1,3},{2,0},{3,1},{4,6},{5,7},{6,4},{7,5},{8,10},{9,11},{10,... | collective-permute-start | bytes 73736 | tf_op jit(solution)/shard_map/ppermute | solution.py:150
  8.3 0.2 collective-permute-start.2
  8.5 2.0 %shard_map.150 = (f32[32,384]{1,0:T(8,128)S(1)}, bf16[128,32]{1,0:T(8,128)(2,1)S(1)}, bf16[32,128]{1,0:T(8,128)(2,1)S(1)}, bf16[32,128]{1,0:T(8,128)(2,1)S(1)}, ...) custom-call(f32[32,384]{1,0:T(8,128)S(1)} %get-tuple-element.30.own, ...), custom_call_target="tpu_custom_call" | custom-call | flops 100000 | bytes 3300000 | tf_op jit(solution)/shard_map/pallas_call | solution.py:137
  10.5 1.0 %collective-permute-done.1.part2 = bf16[32,384]{1,0:T(8,128)(2,1)S(1)} collective-permute-done((bf16[32,384]{1,0:T(8,128)(2,1)S(1)}, bf16[32,384]{1,0:T(8,128)(2,1)S(1)}, u32[]{:S(2)}, u32[]{:S(2)}) %collective-permute-start.1) | collective-permute-done | bytes 24608 | tf_op jit(solution)/shard_map/ppermute | solution.py:150
  11.5 0.2 shard_map.151
  11.7 1.6 %collective-permute-start.3 = (bf16[32,384]{1,0:T(8,128)(2,1)S(1)}, bf16[32,384]{1,0:T(8,128)(2,1)S(1)}, u32[]{:S(2)}, u32[]{:S(2)}) collective-permute-start(bf16[32,384]{1,0:T(8,128)(2,1)S(1)} %get-tuple-element.40), channel_id=1, source_target_pairs={{0,8},{4,12},{8,0},{12,4},{16,24},{20,28},{24,16},{28,20},{1,9},{5... | collective-permute-start | bytes 73736 | tf_op jit(solution)/shard_map/ppermute | solution.py:150
  13.3 2.6 %collective-permute-start.4 = (bf16[32,384]{1,0:T(8,128)(2,1)S(1)}, bf16[32,384]{1,0:T(8,128)(2,1)S(1)}, u32[]{:S(2)}, u32[]{:S(2)}) collective-permute-start(bf16[32,384]{1,0:T(8,128)(2,1)S(1)} %get-tuple-element.41), channel_id=1, source_target_pairs={{0,16},{4,20},{8,24},{12,28},{16,0},{20,4},{24,8},{28,12},{1,17},{... | collective-permute-start | bytes 73736 | tf_op jit(solution)/shard_map/ppermute | solution.py:150
  15.9 0.2 collective-permute-start.5
  16.1 2.1 %collective-permute-done.4.part2.in2 = bf16[32,384]{1,0:T(8,128)(2,1)S(1)} collective-permute-done((bf16[32,384]{1,0:T(8,128)(2,1)S(1)}, bf16[32,384]{1,0:T(8,128)(2,1)S(1)}, u32[]{:S(2)}, u32[]{:S(2)}) %collective-permute-start.4) | collective-permute-done | bytes 24608 | tf_op jit(solution)/shard_map/ppermute | solution.py:150
  18.2 3.3 %collective-permute-done.5.part3.in3 = bf16[32,384]{1,0:T(8,128)(2,1)S(1)} collective-permute-done((bf16[32,384]{1,0:T(8,128)(2,1)S(1)}, bf16[32,384]{1,0:T(8,128)(2,1)S(1)}, u32[]{:S(2)}, u32[]{:S(2)}) %collective-permute-start.5) | collective-permute-done | bytes 24608 | tf_op jit(solution)/shard_map/ppermute | solution.py:150
  21.5 1.5 %collective-permute-start.6 = (bf16[64,384]{1,0:T(8,128)(2,1)S(1)}, bf16[64,384]{1,0:T(8,128)(2,1)S(1)}, u32[]{:S(2)}, u32[]{:S(2)}) collective-permute-start(bf16[64,384]{1,0:T(8,128)(2,1)S(1)} %shard_map.154), channel_id=1, source_target_pairs={{0,4},{4,0},{8,12},{12,8},{16,20},{20,16},{24,28},{28,24},{1,5},{5... | collective-permute-start | bytes 147464 | tf_op jit(solution)/shard_map/ppermute | solution.py:150
  23.1 0.6 %shard_map.153 = bf16[32,384]{1,0:T(8,128)(2,1)} custom-call(bf16[32,384]{1,0:T(8,128)(2,1)S(1)} %get-tuple-element.36.attended), custom_call_target="tpu_custom_call" | custom-call | flops 100000 | bytes 100000 | tf_op jit(solution)/shard_map/pallas_call | solution.py:137
  23.7 0.1 shard_map.152.stats
  23.8 0.7 %shard_map.157 = (f32[32,2176]{1,0:T(8,128)S(1)}, bf16[32,2176]{1,0:T(8,128)(2,1)S(1)}) custom-call(bf16[32,384]{1,0:T(8,128)(2,1)S(1)} %get-tuple-element.39.home.in0, bf16[32,384]{1,0:T(8,128)(2,1)S(1)} %collective-permute-done.3.part1.in1, bf16[32,384]{1,0:T(8,128)(2,1)S(1)} %collective-permute-done.4.part2.in2, ...), custom_call_target="tpu_custom_call" | custom-call | flops 400000000 | bytes 3500000 | tf_op jit(solution)/shard_map/pallas_call | solution.py:137
  24.5 1.1 %collective-permute-done.6.blocks = bf16[64,384]{1,0:T(8,128)(2,1)S(1)} collective-permute-done((bf16[64,384]{1,0:T(8,128)(2,1)S(1)}, bf16[64,384]{1,0:T(8,128)(2,1)S(1)}, u32[]{:S(2)}, u32[]{:S(2)}) %collective-permute-start.6) | collective-permute-done | bytes 49184 | tf_op jit(solution)/shard_map/ppermute | solution.py:150
  25.6 0.7 %shard_map.155 = (f32[32,2176]{1,0:T(8,128)S(1)}, bf16[32,2176]{1,0:T(8,128)(2,1)S(1)}) custom-call(bf16[64,384]{1,0:T(8,128)(2,1)S(1)} %collective-permute-done.6.blocks, f32[1,384]{1,0:T(1,128)S(1)} %reshape.21.gain, bf16[768,1024]{1,0:T(8,128)(2,1)S(1)} %get-tuple-element.43.w_gate, bf16[768,1024]{1,0:T(8,128)(2,1)S(1)} %get-tuple-element.44.w_up), custom_call_target="tpu_custom_call" | custom-call | flops 400000000 | bytes 3500000 | tf_op jit(solution)/shard_map/pallas_call | solution.py:137
  26.3 0.1 collective-permute-start.7
  26.4 0.2 shard_map.158
  26.5 1.0 %collective-permute-start.10 = (bf16[16,2176]{1,0:T(8,128)(2,1)S(1)}, bf16[16,2176]{1,0:T(8,128)(2,1)S(1)}, u32[]{:S(2)}, u32[]{:S(2)}) collective-permute-start(bf16[16,2176]{1,0:T(8,128)(2,1)S(1)} %get-tuple-element.53), channel_id=1, source_target_pairs={{0,2},{1,3},{2,0},{3,1},{4,6},{5,7},{6,4},{7,5},{8,10},{9,11},{10,... | collective-permute-start | bytes 208904 | tf_op jit(solution)/shard_map/ppermute | solution.py:150
  27.5 0.2 collective-permute-done.7.part
  27.7 0.2 shard_map.156
  27.9 1.0 %collective-permute-start.8 = (bf16[16,2176]{1,0:T(8,128)(2,1)S(1)}, bf16[16,2176]{1,0:T(8,128)(2,1)S(1)}, u32[]{:S(2)}, u32[]{:S(2)}) collective-permute-start(bf16[16,2176]{1,0:T(8,128)(2,1)S(1)} %get-tuple-element.48), channel_id=1, source_target_pairs={{0,2},{1,3},{2,0},{3,1},{4,6},{5,7},{6,4},{7,5},{8,10},{9,11},{10,... | collective-permute-start | bytes 208904 | tf_op jit(solution)/shard_map/ppermute | solution.py:150
  28.9 2.7 %collective-permute-done.10.refs_3_ = bf16[16,2176]{1,0:T(8,128)(2,1)S(1)} collective-permute-done((bf16[16,2176]{1,0:T(8,128)(2,1)S(1)}, bf16[16,2176]{1,0:T(8,128)(2,1)S(1)}, u32[]{:S(2)}, u32[]{:S(2)}) %collective-permute-start.10) | collective-permute-done | bytes 69664 | tf_op jit(solution)/shard_map/ppermute | solution.py:150
  31.5 1.1 %collective-permute-done.8.refs_1_ = bf16[16,2176]{1,0:T(8,128)(2,1)S(1)} collective-permute-done((bf16[16,2176]{1,0:T(8,128)(2,1)S(1)}, bf16[16,2176]{1,0:T(8,128)(2,1)S(1)}, u32[]{:S(2)}, u32[]{:S(2)}) %collective-permute-start.8) | collective-permute-done | bytes 69664 | tf_op jit(solution)/shard_map/ppermute | solution.py:150
  32.6 0.2 shard_map.159
  32.9 1.0 %collective-permute-start.12 = (bf16[32,1024]{1,0:T(8,128)(2,1)S(1)}, bf16[32,1024]{1,0:T(8,128)(2,1)S(1)}, u32[]{:S(2)}, u32[]{:S(2)}) collective-permute-start(bf16[32,1024]{1,0:T(8,128)(2,1)S(1)} %get-tuple-element.54.own), channel_id=1, source_target_pairs={{0,2},{1,3},{2,0},{3,1},{4,6},{5,7},{6,4},{7,5},{8,10},{9,11},{10,... | collective-permute-start | bytes 196616 | tf_op jit(solution)/shard_map/ppermute | solution.py:150
  33.9 3.3 %collective-permute-done.12.part2 = bf16[32,1024]{1,0:T(8,128)(2,1)S(1)} collective-permute-done((bf16[32,1024]{1,0:T(8,128)(2,1)S(1)}, bf16[32,1024]{1,0:T(8,128)(2,1)S(1)}, u32[]{:S(2)}, u32[]{:S(2)}) %collective-permute-start.12) | collective-permute-done | bytes 65568 | tf_op jit(solution)/shard_map/ppermute | solution.py:150
  37.2 1.2 %collective-permute-done.13.part3 = bf16[32,1024]{1,0:T(8,128)(2,1)S(1)} collective-permute-done((bf16[32,1024]{1,0:T(8,128)(2,1)S(1)}, bf16[32,1024]{1,0:T(8,128)(2,1)S(1)}, u32[]{:S(2)}, u32[]{:S(2)}) %collective-permute-start.13) | collective-permute-done | bytes 65568 | tf_op jit(solution)/shard_map/ppermute | solution.py:150
  38.4 0.5 shard_map.160
  38.9 9.7 %all_to_all.5 = bf16[8,16,384]{2,1,0:T(8,128)(2,1)S(1)} all-to-all(bf16[8,16,384]{2,1,0:T(8,128)(2,1)S(1)} %shard_map.160), channel_id=1, replica_groups=mesh['req'=8,'tp'=4] {'req'}, dimensions={0} | all-to-all | bytes 196608 | tf_op jit(solution)/shard_map/all_to_all | solution.py:643
  48.6 0.8 %shard_map.161 = bf16[32,384]{1,0:T(8,128)(2,1)} custom-call(bf16[128,384]{1,0:T(8,128)(2,1)S(1)} %bitcast.7, bf16[32,128]{1,0:T(8,128)(2,1)S(1)} %get-tuple-element.55.pick0, bf16[32,128]{1,0:T(8,128)(2,1)S(1)} %get-tuple-element.56.pick1, f32[32,128]{1,0:T(8,128)S(1)} %get-tuple-element.57.first_weight, bf16[32,384]{1,0:T(8,128)(2,1)S(1)} %get-tuple-element.36.attended), custom_call_target="tpu_custom_call" | custom-call | flops 100000 | bytes 100000 | tf_op jit(solution)/shard_map/pallas_call | solution.py:137
  (21 shorter events, 0.1 us)
Async XLA Ops:
  0.6 7.8 %copy-start.3 = (s32[32,2]{0,1:T(2,128)S(1)}, s32[32,2]{0,1:T(2,128)}, u32[]{:S(2)}) copy-start(s32[32,2]{0,1:T(2,128)} %param.24) | copy-start | bytes 772
  0.6 7.8 %copy-start.2 = (f32[384,16]{0,1:T(8,128)S(1)}, f32[384,16]{0,1:T(8,128)}, u32[]{:S(2)}) copy-start(f32[384,16]{0,1:T(8,128)} %param.23) | copy-start | bytes 73732
  0.7 7.8 %copy-start.1 = (bf16[32,384]{1,0:T(8,128)(2,1)S(1)}, bf16[32,384]{1,0:T(8,128)(2,1)}, u32[]{:S(2)}) copy-start(bf16[32,384]{1,0:T(8,128)(2,1)} %resid.1) | copy-start | bytes 73732
  5.3 5.3 %collective-permute-start = (bf16[32,384]{1,0:T(8,128)(2,1)S(1)}, bf16[32,384]{1,0:T(8,128)(2,1)S(1)}, u32[]{:S(2)}, u32[]{:S(2)}) collective-permute-start(bf16[32,384]{1,0:T(8,128)(2,1)S(1)} %get-tuple-element.32), channel_id=1, source_target_pairs={{0,2},{1,3},{2,0},{3,1},{4,6},{5,7},{6,4},{7,5},{8,10},{9,11},{10,... | collective-permute-start | bytes 73736 | tf_op jit(solution)/shard_map/ppermute | solution.py:150
  8.3 3.3 %collective-permute-start.1 = (bf16[32,384]{1,0:T(8,128)(2,1)S(1)}, bf16[32,384]{1,0:T(8,128)(2,1)S(1)}, u32[]{:S(2)}, u32[]{:S(2)}) collective-permute-start(bf16[32,384]{1,0:T(8,128)(2,1)S(1)} %get-tuple-element.33), channel_id=1, source_target_pairs={{0,3},{1,2},{2,1},{3,0},{4,7},{5,6},{6,5},{7,4},{8,11},{9,10},{10,... | collective-permute-start | bytes 73736 | tf_op jit(solution)/shard_map/ppermute | solution.py:150
  8.3 3.3 %collective-permute-start.2 = (bf16[32,384]{1,0:T(8,128)(2,1)S(1)}, bf16[32,384]{1,0:T(8,128)(2,1)S(1)}, u32[]{:S(2)}, u32[]{:S(2)}) collective-permute-start(bf16[32,384]{1,0:T(8,128)(2,1)S(1)} %get-tuple-element.34), channel_id=1, source_target_pairs={{0,1},{1,0},{2,3},{3,2},{4,5},{5,4},{6,7},{7,6},{8,9},{9,8},{10,11... | collective-permute-start | bytes 73736 | tf_op jit(solution)/shard_map/ppermute | solution.py:150
  8.5 14.6 %copy-start.4 = (f32[384]{0:T(512)S(1)}, f32[384]{0:T(512)}, u32[]{:S(2)}) copy-start(f32[384]{0:T(512)} %param.22) | copy-start | bytes 4612
  11.7 4.5 %collective-permute-start.3 = (bf16[32,384]{1,0:T(8,128)(2,1)S(1)}, bf16[32,384]{1,0:T(8,128)(2,1)S(1)}, u32[]{:S(2)}, u32[]{:S(2)}) collective-permute-start(bf16[32,384]{1,0:T(8,128)(2,1)S(1)} %get-tuple-element.40), channel_id=1, source_target_pairs={{0,8},{4,12},{8,0},{12,4},{16,24},{20,28},{24,16},{28,20},{1,9},{5... | collective-permute-start | bytes 73736 | tf_op jit(solution)/shard_map/ppermute | solution.py:150
  13.3 4.9 %collective-permute-start.4 = (bf16[32,384]{1,0:T(8,128)(2,1)S(1)}, bf16[32,384]{1,0:T(8,128)(2,1)S(1)}, u32[]{:S(2)}, u32[]{:S(2)}) collective-permute-start(bf16[32,384]{1,0:T(8,128)(2,1)S(1)} %get-tuple-element.41), channel_id=1, source_target_pairs={{0,16},{4,20},{8,24},{12,28},{16,0},{20,4},{24,8},{28,12},{1,17},{... | collective-permute-start | bytes 73736 | tf_op jit(solution)/shard_map/ppermute | solution.py:150
  15.9 5.6 %collective-permute-start.5 = (bf16[32,384]{1,0:T(8,128)(2,1)S(1)}, bf16[32,384]{1,0:T(8,128)(2,1)S(1)}, u32[]{:S(2)}, u32[]{:S(2)}) collective-permute-start(bf16[32,384]{1,0:T(8,128)(2,1)S(1)} %get-tuple-element.42), channel_id=1, source_target_pairs={{0,24},{4,28},{8,16},{12,20},{16,8},{20,12},{24,0},{28,4},{1,25},{... | collective-permute-start | bytes 73736 | tf_op jit(solution)/shard_map/ppermute | solution.py:150
  21.5 4.1 %collective-permute-start.6 = (bf16[64,384]{1,0:T(8,128)(2,1)S(1)}, bf16[64,384]{1,0:T(8,128)(2,1)S(1)}, u32[]{:S(2)}, u32[]{:S(2)}) collective-permute-start(bf16[64,384]{1,0:T(8,128)(2,1)S(1)} %shard_map.154), channel_id=1, source_target_pairs={{0,4},{4,0},{8,12},{12,8},{16,20},{20,16},{24,28},{28,24},{1,5},{5... | collective-permute-start | bytes 147464 | tf_op jit(solution)/shard_map/ppermute | solution.py:150
  24.5 14.0 %copy-start = (bf16[2,1024,384]{2,1,0:T(8,128)(2,1)S(1)}, bf16[2,1024,384]{2,1,0:T(8,128)(2,1)}, u32[]{:S(2)}) copy-start(bf16[2,1024,384]{2,1,0:T(8,128)(2,1)} %param.27) | copy-start | bytes 4718596
  24.5 1.9 %collective-permute-start.9 = (bf16[32,2176]{1,0:T(8,128)(2,1)S(1)}, bf16[32,2176]{1,0:T(8,128)(2,1)S(1)}, u32[]{:S(2)}, u32[]{:S(2)}) collective-permute-start(bf16[32,2176]{1,0:T(8,128)(2,1)S(1)} %get-tuple-element.51), channel_id=1, source_target_pairs={{0,1},{1,0},{2,3},{3,2},{4,5},{5,4},{6,7},{7,6},{8,9},{9,8},{10,11... | collective-permute-start | bytes 417800 | tf_op jit(solution)/shard_map/ppermute | solution.py:150
  26.3 1.4 %collective-permute-start.7 = (bf16[32,2176]{1,0:T(8,128)(2,1)S(1)}, bf16[32,2176]{1,0:T(8,128)(2,1)S(1)}, u32[]{:S(2)}, u32[]{:S(2)}) collective-permute-start(bf16[32,2176]{1,0:T(8,128)(2,1)S(1)} %get-tuple-element.46), channel_id=1, source_target_pairs={{0,1},{1,0},{2,3},{3,2},{4,5},{5,4},{6,7},{7,6},{8,9},{9,8},{10,11... | collective-permute-start | bytes 417800 | tf_op jit(solution)/shard_map/ppermute | solution.py:150
  26.5 5.0 %collective-permute-start.10 = (bf16[16,2176]{1,0:T(8,128)(2,1)S(1)}, bf16[16,2176]{1,0:T(8,128)(2,1)S(1)}, u32[]{:S(2)}, u32[]{:S(2)}) collective-permute-start(bf16[16,2176]{1,0:T(8,128)(2,1)S(1)} %get-tuple-element.53), channel_id=1, source_target_pairs={{0,2},{1,3},{2,0},{3,1},{4,6},{5,7},{6,4},{7,5},{8,10},{9,11},{10,... | collective-permute-start | bytes 208904 | tf_op jit(solution)/shard_map/ppermute | solution.py:150
  27.9 4.7 %collective-permute-start.8 = (bf16[16,2176]{1,0:T(8,128)(2,1)S(1)}, bf16[16,2176]{1,0:T(8,128)(2,1)S(1)}, u32[]{:S(2)}, u32[]{:S(2)}) collective-permute-start(bf16[16,2176]{1,0:T(8,128)(2,1)S(1)} %get-tuple-element.48), channel_id=1, source_target_pairs={{0,2},{1,3},{2,0},{3,1},{4,6},{5,7},{6,4},{7,5},{8,10},{9,11},{10,... | collective-permute-start | bytes 208904 | tf_op jit(solution)/shard_map/ppermute | solution.py:150
  32.9 4.3 %collective-permute-start.12 = (bf16[32,1024]{1,0:T(8,128)(2,1)S(1)}, bf16[32,1024]{1,0:T(8,128)(2,1)S(1)}, u32[]{:S(2)}, u32[]{:S(2)}) collective-permute-start(bf16[32,1024]{1,0:T(8,128)(2,1)S(1)} %get-tuple-element.54.own), channel_id=1, source_target_pairs={{0,2},{1,3},{2,0},{3,1},{4,6},{5,7},{6,4},{7,5},{8,10},{9,11},{10,... | collective-permute-start | bytes 196616 | tf_op jit(solution)/shard_map/ppermute | solution.py:150
  33.9 3.3 %collective-permute-start.11 = (bf16[32,1024]{1,0:T(8,128)(2,1)S(1)}, bf16[32,1024]{1,0:T(8,128)(2,1)S(1)}, u32[]{:S(2)}, u32[]{:S(2)}) collective-permute-start(bf16[32,1024]{1,0:T(8,128)(2,1)S(1)} %get-tuple-element.54.own), channel_id=1, source_target_pairs={{0,1},{1,0},{2,3},{3,2},{4,5},{5,4},{6,7},{7,6},{8,9},{9,8},{10,11... | collective-permute-start | bytes 196616 | tf_op jit(solution)/shard_map/ppermute | solution.py:150
  37.2 1.3 %collective-permute-start.13 = (bf16[32,1024]{1,0:T(8,128)(2,1)S(1)}, bf16[32,1024]{1,0:T(8,128)(2,1)S(1)}, u32[]{:S(2)}, u32[]{:S(2)}) collective-permute-start(bf16[32,1024]{1,0:T(8,128)(2,1)S(1)} %collective-permute-done.12.part2), channel_id=1, source_target_pairs={{0,1},{1,0},{2,3},{3,2},{4,5},{5,4},{6,7},{7,6},{8,9},{9,8},{10,11... | collective-permute-start | bytes 196616 | tf_op jit(solution)/shard_map/ppermute | solution.py:150

commit v9 on v7

--- a/solution.py
+++ b/solution.py
@@ -126,7 +126,7 @@
     return (attended, layer_out)
 
 
-TP_ORDER = (0, 2, 3, 1)
+FAR_FIRST = (0, 2, 3, 1)
 
 
 def spec(space=pltpu.VMEM):
@@ -257,7 +257,7 @@
         copy.wait()
     place_tp = lax.axis_index("tp")
     product_s[...] = jnp.dot(attention, w_buf[...], preferred_element_type=jnp.float32)
-    for shift, out in zip(TP_ORDER, (own, sent1, sent2, sent3)):
+    for shift, out in zip(FAR_FIRST, (own, sent1, sent2, sent3)):
         columns = pl.ds(pl.multiple_of((place_tp ^ shift) * width, width), width)
         out[...] = product_s[:, columns].astype(out.dtype)
 
@@ -317,7 +317,7 @@
     attended[...] = rows
     packed = jnp.dot(pick_rows[...], rows, preferred_element_type=jnp.float32)
     size = home.shape[0]
-    for distance, out in enumerate((home, sent1, sent2, sent3)):
+    for distance, out in zip(FAR_FIRST, (home, sent1, sent2, sent3)):
         out[...] = packed[distance * size : (distance + 1) * size].astype(out.dtype)
 
 
@@ -335,7 +335,7 @@
 
 def turn_kernel(home, part1, part2, part3, along):
     half = home.shape[0] // 2
-    for index, part in enumerate((home, part1, part2, part3)):
+    for index, part in zip(FAR_FIRST, (home, part1, part2, part3)):
         along[index * half : (index + 1) * half, :] = part[half:, :]
 
 
@@ -384,10 +384,11 @@
 
 
 def early_kernel(
-    slot_dev, in0, in1, in2, in3, gain, stats, w_gate, w_up, kept, sent, blocks, lhs
+    slot_dev, in0, in1, in2, in3, gain, stats, w_gate, w_up, turned, kept, sent, blocks, lhs
 ):
+    del turned
     half = kept.shape[0] // 2
-    for index, part in enumerate((in0, in1, in2, in3)):
+    for index, part in zip(FAR_FIRST, (in0, in1, in2, in3)):
         blocks[index * half : (index + 1) * half, :] = part[:half, :]
     gate_terms(slot_dev, blocks, gain, stats, w_gate, w_up, kept, sent, lhs)
 
@@ -397,22 +398,26 @@
 
 
 def chip_kernel(kept, part, own, sent):
-    size, width = own.shape
-    own[...] = kept[:size, :] + part[:size, :].astype(jnp.float32)
-    total = kept[size:, :] + part[size:, :].astype(jnp.float32)
+    size, width = own.shape[0] // 2, own.shape[1]
+    total = kept[...] + part[...].astype(jnp.float32)
+    own[...] = total
     extra = total[:, width - 128 :]
     lane = lax.broadcasted_iota(jnp.int32, extra.shape, 1)
     high, low = split_high(extra + pltpu.roll(extra, 127, 1))
-    sent[:, : width - 128] = total[:, : width - 128].astype(sent.dtype)
-    sent[:, width - 128 :] = jnp.where(
-        lax.rem(lane, 2) == 0, high, pltpu.roll(low, 1, 1)
-    ).astype(sent.dtype)
+    extra = jnp.where(lax.rem(lane, 2) == 0, high, pltpu.roll(low, 1, 1))
+    for target, source in ((0, size), (size, 0)):
+        sent[target : target + size, : width - 128] = total[
+            source : source + size, : width - 128
+        ].astype(sent.dtype)
+        sent[target : target + size, width - 128 :] = extra[source : source + size].astype(
+            sent.dtype
+        )
 
 
 def hidden_kernel(*refs):
     late, early, (hidden, first_weight) = refs[:2], refs[2:4], refs[4:]
     width = hidden.shape[1]
-    half = hidden.shape[0] // 2
+    half = hidden.shape[0] // 4
 
     def total(parts, columns):
         result = parts[0][:, columns]
@@ -429,9 +434,11 @@
         row_inv = inverse_rms(extra, 0)
         gate = total(parts, slice(0, width)) * row_inv
         up = total(parts, slice(width, 2 * width)) * row_inv
-        hidden[index * half : (index + 1) * half, :] = (
-            gate / (1.0 + jnp.exp(-gate)) * up
-        ).astype(jnp.bfloat16)
+        rows = (gate / (1.0 + jnp.exp(-gate)) * up).astype(jnp.bfloat16)
+        for block in range(2):
+            start = (2 * block + index) * half
+            hidden[start : start + half, :] = rows[block * half : (block + 1) * half]
+    extra = extra[:half]
     for index in range(first_weight.shape[0] // half):
         place = 2 + 4 * index
         logit = extra[:, place + 2 : place + 3] + extra[:, place + 3 : place + 4]
@@ -439,14 +446,15 @@
         first_weight[index * half : (index + 1) * half, :] = jnp.broadcast_to(weight, (half, 128))
 
 
-def down_kernel(slot_dev, own, part1, part2, part3, w_down, computed, lhs):
-    quarter, width = own.shape
+def down_kernel(slot_dev, own, part, w_down, computed, lhs):
+    quarter, width = own.shape[0] // 2, own.shape[1]
     block = computed.shape[1]
     place_tp = lax.axis_index("tp")
     place_req = lax.axis_index("req")
     masks = slot_masks(quarter, slot_dev)
-    for shift, part in enumerate((own, part1, part2, part3)):
-        rows = part[...].astype(jnp.float32)
+    for shift in range(4):
+        first = shift // 2 * quarter
+        rows = (own, part)[shift % 2][first : first + quarter, :].astype(jnp.float32)
         place = pl.ds(pl.multiple_of((place_tp ^ shift) * quarter, quarter), quarter)
         for index, mask in enumerate(masks):
             lhs[place, index * width : (index + 1) * width] = jnp.where(mask, rows, 0.0).astype(
@@ -532,7 +540,7 @@
         moved=3_400_000,
     )
     def sum_exchange(sents):
-        return [partner_permute(block, "tp", k) for k, block in zip(TP_ORDER[1:], sents)]
+        return [partner_permute(block, "tp", k) for k, block in zip(FAR_FIRST[1:], sents)]
 
     parts = sum_exchange(sents)
     weight = (slot_dev * width, hidden)
@@ -571,33 +579,35 @@
     )
     (result,) = call(result_kernel, [((row_count, width), bf16)], [spec()], (attended,))
     stats, result = lax.optimization_barrier((stats, result))
-    parts = [partner_permute(block, "req", 2 * k) for k, block in enumerate(sents, 1)]
-    (along,) = call(
+    parts = [
+        partner_permute(block, "req", 2 * k) for k, block in zip(FAR_FIRST[1:], sents)
+    ]
+    (turned,) = call(
         turn_kernel, [((2 * quarter, width), bf16)], [spec()] * 4, (home, *parts)
     )
-    along = partner_permute(along, "req", 1)
-    half = quarter // 2
-    message = (half, 2 * hidden + 128)
+    along = partner_permute(turned, "req", 1)
     lhs = pltpu.VMEM((packed_count // 2, slot_dev * width), bf16)
 
+    pair = (quarter, 2 * hidden + 128)
+
     def chip_sums(kept, sent):
-        own, sent = call(
-            chip_kernel, [(message, f32), (message, bf16)], [spec()] * 2,
+        return call(
+            chip_kernel, [(pair, f32), (pair, bf16)], [spec()] * 2,
             (kept, partner_permute(sent, "tp", 1)),
         )
-        return own, partner_permute(sent, "tp", 2)
-
-    pair = (quarter, message[1])
-    early = call(
+
+    kept, sent = call(
         functools.partial(early_kernel, slot_dev),
         [(pair, f32), (pair, bf16)],
-        [spec()] * 8,
-        (home, *parts, gain, stats, *weights),
+        [spec()] * 9,
+        (home, *parts, gain, stats, *weights, turned),
         scratch=[pltpu.VMEM((2 * quarter, width), bf16), lhs],
         flops=400_000_000,
         moved=3_500_000,
     )
-    late = call(
+    early, sent = chip_sums(kept, sent)
+    early = (early, partner_permute(sent, "tp", 2))
+    kept, sent = call(
         functools.partial(late_kernel, slot_dev),
         [(pair, f32), (pair, bf16)],
         [spec()] * 4,
@@ -606,21 +616,19 @@
         flops=400_000_000,
         moved=3_500_000,
     )
-    early = chip_sums(*early)
-    late = chip_sums(*late)
+    late, sent = chip_sums(kept, sent)
+    late = (late, partner_permute(sent, "tp", 2))
     own, first_weight = call(
         hidden_kernel,
-        [((quarter, hidden), bf16), ((row_count, 128), f32)],
+        [((2 * quarter, hidden), bf16), ((row_count, 128), f32)],
         [spec()] * 4,
         (*late, *early),
     )
-    across = partner_permute(own, "tp", 2)
-    parts = [partner_permute(own, "tp", 1), across, partner_permute(across, "tp", 1)]
     (computed,) = call(
         functools.partial(down_kernel, slot_dev),
         [((8, packed_count // 8, width), bf16)],
-        [spec()] * 5,
-        (own, *parts, w_down.reshape(slot_dev * hidden, width)),
+        [spec()] * 3,
+        (own, partner_permute(own, "tp", 1), w_down.reshape(slot_dev * hidden, width)),
         scratch=[pltpu.VMEM((packed_count, slot_dev * hidden), bf16)],
         flops=200_000_000,
         moved=2_000_000,

time: 48.9 us -> 47.7 us (0.975)
  waiting for transfers between devices: 16 us -> 14.4 us
  blocking collectives: 9.72 us -> 11.1 us
  starting transfers between devices: 12.3 us -> 11.2 us
    ppermute x14 -> x12, waiting for transfers between devices: 16 us -> 14.4 us  [partner_permute(): return lax.ppermute(block, axis, [(i, i ^ distance) for i in range(count)])]
    all_to_all x1, blocking collectives: 9.72 us -> 11.1 us  [shards(): lax.all_to_all(computed, 'req', split_axis=0, concat_axis=0, tiled=True)]
    ppermute x14 -> x12, starting transfers between devices: 12.3 us -> 11.2 us  [partner_permute(): return lax.ppermute(block, axis, [(i, i ^ distance) for i in range(count)])]
  transfers between devices with their start and end apart: 14 -> 12, of which waited for: 9 -> 8; matrix products, arithmetic and copies ran while one was open for 0% -> 0% of each run, Pallas kernels for 9% -> 9%
where the time goes in v9:
time: 47.7 us; the launch traced here: 47.5 us
  waiting for transfers between devices  14.4 us (30%)
  starting transfers between devices  11.2 us (23%)
  blocking collectives  11.1 us (23%)
  Pallas kernels  10 us (21%)
  between operations  0.77 us (2%)
    ppermute x12, waiting for transfers between devices, partner_permute(): return lax.ppermute(block, axis, [(i, i ^ distance) for i in range(count)])  14.4 us
    ppermute x12, starting transfers between devices, partner_permute(): return lax.ppermute(block, axis, [(i, i ^ distance) for i in range(count)])  11.2 us
    all_to_all x1, blocking collectives, shards(): lax.all_to_all(computed, 'req', split_axis=0, concat_axis=0, tiled=True)  11.1 us
    pallas_call x13, Pallas kernels, call(): pl.pallas_call(kernel, out_shape=[jax.ShapeDtypeStruct(shape, dtype) for...  10 us
  transfers between devices with their start and end apart: 12, of which 8 were waited for; matrix products, arithmetic and copies ran while one was open for 0% of the time, Pallas kernels for 9%

profile of v9, /device:TPU:0, one launch (start us, length us, event | category | flops | bytes accessed | tf_op | source)
XLA Modules:
  0.0 47.5 jit_solution(668710021675559911)
XLA Ops:
  0.7 4.0 %shard_map.149 = (f32[32,384]{1,0:T(8,128)S(1)}, bf16[32,384]{1,0:T(8,128)(2,1)S(1)}, bf16[32,384]{1,0:T(8,128)(2,1)S(1)}, bf16[32,384]{1,0:T(8,128)(2,1)S(1)}) custom-call(s32[32]{0:T(128)} %lengths_hbm.1, bf16[32,384]{1,0:T(8,128)(2,1)} %queries_hbm.1, bf16[32,128]{1,0:T(8,128)(2,1)} %keys_hbm.1, bf16[32,128]{1,0:T(8,128)(2,1)} %values_hbm.1, ...), custom_call_target="tpu_custom_call" | custom-call | flops 200000000 | bytes 3400000 | tf_op jit(solution)/shard_map/pallas_call | solution.py:137
  4.6 3.0 %collective-permute-start = (bf16[32,384]{1,0:T(8,128)(2,1)S(1)}, bf16[32,384]{1,0:T(8,128)(2,1)S(1)}, u32[]{:S(2)}, u32[]{:S(2)}) collective-permute-start(bf16[32,384]{1,0:T(8,128)(2,1)S(1)} %get-tuple-element.32), channel_id=1, source_target_pairs={{0,2},{1,3},{2,0},{3,1},{4,6},{5,7},{6,4},{7,5},{8,10},{9,11},{10,... | collective-permute-start | bytes 73736 | tf_op jit(solution)/shard_map/ppermute | solution.py:150
  7.6 0.2 collective-permute-start.2
  7.8 2.0 %shard_map.150 = (f32[32,384]{1,0:T(8,128)S(1)}, bf16[128,32]{1,0:T(8,128)(2,1)S(1)}, bf16[32,128]{1,0:T(8,128)(2,1)S(1)}, bf16[32,128]{1,0:T(8,128)(2,1)S(1)}, ...) custom-call(f32[32,384]{1,0:T(8,128)S(1)} %get-tuple-element.30.own, ...), custom_call_target="tpu_custom_call" | custom-call | flops 100000 | bytes 3300000 | tf_op jit(solution)/shard_map/pallas_call | solution.py:137
  9.9 1.0 %collective-permute-done.1.part2 = bf16[32,384]{1,0:T(8,128)(2,1)S(1)} collective-permute-done((bf16[32,384]{1,0:T(8,128)(2,1)S(1)}, bf16[32,384]{1,0:T(8,128)(2,1)S(1)}, u32[]{:S(2)}, u32[]{:S(2)}) %collective-permute-start.1) | collective-permute-done | bytes 24608 | tf_op jit(solution)/shard_map/ppermute | solution.py:150
  10.9 0.2 shard_map.151
  11.1 2.7 %collective-permute-start.3 = (bf16[32,384]{1,0:T(8,128)(2,1)S(1)}, bf16[32,384]{1,0:T(8,128)(2,1)S(1)}, u32[]{:S(2)}, u32[]{:S(2)}) collective-permute-start(bf16[32,384]{1,0:T(8,128)(2,1)S(1)} %get-tuple-element.40), channel_id=1, source_target_pairs={{0,16},{4,20},{8,24},{12,28},{16,0},{20,4},{24,8},{28,12},{1,17},{... | collective-permute-start | bytes 73736 | tf_op jit(solution)/shard_map/ppermute | solution.py:150
  13.7 1.3 %collective-permute-start.4 = (bf16[32,384]{1,0:T(8,128)(2,1)S(1)}, bf16[32,384]{1,0:T(8,128)(2,1)S(1)}, u32[]{:S(2)}, u32[]{:S(2)}) collective-permute-start(bf16[32,384]{1,0:T(8,128)(2,1)S(1)} %get-tuple-element.41), channel_id=1, source_target_pairs={{0,24},{4,28},{8,16},{12,20},{16,8},{20,12},{24,0},{28,4},{1,25},{... | collective-permute-start | bytes 73736 | tf_op jit(solution)/shard_map/ppermute | solution.py:150
  15.1 0.2 collective-permute-start.5
  15.3 0.6 %collective-permute-done.3.part1.in1 = bf16[32,384]{1,0:T(8,128)(2,1)S(1)} collective-permute-done((bf16[32,384]{1,0:T(8,128)(2,1)S(1)}, bf16[32,384]{1,0:T(8,128)(2,1)S(1)}, u32[]{:S(2)}, u32[]{:S(2)}) %collective-permute-start.3) | collective-permute-done | bytes 24608 | tf_op jit(solution)/shard_map/ppermute | solution.py:150
  15.8 3.5 %collective-permute-done.4.part2.in2 = bf16[32,384]{1,0:T(8,128)(2,1)S(1)} collective-permute-done((bf16[32,384]{1,0:T(8,128)(2,1)S(1)}, bf16[32,384]{1,0:T(8,128)(2,1)S(1)}, u32[]{:S(2)}, u32[]{:S(2)}) %collective-permute-start.4) | collective-permute-done | bytes 24608 | tf_op jit(solution)/shard_map/ppermute | solution.py:150
  19.3 1.6 %collective-permute-start.6 = (bf16[64,384]{1,0:T(8,128)(2,1)S(1)}, bf16[64,384]{1,0:T(8,128)(2,1)S(1)}, u32[]{:S(2)}, u32[]{:S(2)}) collective-permute-start(bf16[64,384]{1,0:T(8,128)(2,1)S(1)} %shard_map.154.turned), channel_id=1, source_target_pairs={{0,4},{4,0},{8,12},{12,8},{16,20},{20,16},{24,28},{28,24},{1,5},{5... | collective-permute-start | bytes 147464 | tf_op jit(solution)/shard_map/ppermute | solution.py:150
  20.9 0.6 %shard_map.153 = bf16[32,384]{1,0:T(8,128)(2,1)} custom-call(bf16[32,384]{1,0:T(8,128)(2,1)S(1)} %get-tuple-element.36.attended), custom_call_target="tpu_custom_call" | custom-call | flops 100000 | bytes 100000 | tf_op jit(solution)/shard_map/pallas_call | solution.py:137
  21.5 0.1 shard_map.152.stats
  21.6 0.7 %shard_map.157 = (f32[32,2176]{1,0:T(8,128)S(1)}, bf16[32,2176]{1,0:T(8,128)(2,1)S(1)}) custom-call(bf16[32,384]{1,0:T(8,128)(2,1)S(1)} %get-tuple-element.39.home.in0, bf16[32,384]{1,0:T(8,128)(2,1)S(1)} %collective-permute-done.3.part1.in1, bf16[32,384]{1,0:T(8,128)(2,1)S(1)} %collective-permute-done.4.part2.in2, ...), custom_call_target="tpu_custom_call" | custom-call | flops 400000000 | bytes 3500000 | tf_op jit(solution)/shard_map/pallas_call | solution.py:137
  22.3 0.1 collective-permute-start.9
  22.4 1.1 %collective-permute-done.6.blocks = bf16[64,384]{1,0:T(8,128)(2,1)S(1)} collective-permute-done((bf16[64,384]{1,0:T(8,128)(2,1)S(1)}, bf16[64,384]{1,0:T(8,128)(2,1)S(1)}, u32[]{:S(2)}, u32[]{:S(2)}) %collective-permute-start.6) | collective-permute-done | bytes 49184 | tf_op jit(solution)/shard_map/ppermute | solution.py:150
  23.5 0.7 %shard_map.155 = (f32[32,2176]{1,0:T(8,128)S(1)}, bf16[32,2176]{1,0:T(8,128)(2,1)S(1)}) custom-call(bf16[64,384]{1,0:T(8,128)(2,1)S(1)} %collective-permute-done.6.blocks, f32[1,384]{1,0:T(1,128)S(1)} %reshape.21.gain, bf16[768,1024]{1,0:T(8,128)(2,1)S(1)} %get-tuple-element.43.w_gate, bf16[768,1024]{1,0:T(8,128)(2,1)S(1)} %get-tuple-element.44.w_up), custom_call_target="tpu_custom_call" | custom-call | flops 400000000 | bytes 3500000 | tf_op jit(solution)/shard_map/pallas_call | solution.py:137
  24.2 0.1 collective-permute-start.7
  24.3 0.2 shard_map.158
  24.4 1.0 %collective-permute-start.10 = (bf16[32,2176]{1,0:T(8,128)(2,1)S(1)}, bf16[32,2176]{1,0:T(8,128)(2,1)S(1)}, u32[]{:S(2)}, u32[]{:S(2)}) collective-permute-start(bf16[32,2176]{1,0:T(8,128)(2,1)S(1)} %get-tuple-element.53), channel_id=1, source_target_pairs={{0,2},{1,3},{2,0},{3,1},{4,6},{5,7},{6,4},{7,5},{8,10},{9,11},{10,... | collective-permute-start | bytes 417800 | tf_op jit(solution)/shard_map/ppermute | solution.py:150
  25.4 0.2 collective-permute-done.7.part
  25.6 0.2 shard_map.156
  25.8 1.0 %collective-permute-start.8 = (bf16[32,2176]{1,0:T(8,128)(2,1)S(1)}, bf16[32,2176]{1,0:T(8,128)(2,1)S(1)}, u32[]{:S(2)}, u32[]{:S(2)}) collective-permute-start(bf16[32,2176]{1,0:T(8,128)(2,1)S(1)} %get-tuple-element.48), channel_id=1, source_target_pairs={{0,2},{1,3},{2,0},{3,1},{4,6},{5,7},{6,4},{7,5},{8,10},{9,11},{10,... | collective-permute-start | bytes 417800 | tf_op jit(solution)/shard_map/ppermute | solution.py:150
  26.8 4.2 %collective-permute-done.10.refs_3_ = bf16[32,2176]{1,0:T(8,128)(2,1)S(1)} collective-permute-done((bf16[32,2176]{1,0:T(8,128)(2,1)S(1)}, bf16[32,2176]{1,0:T(8,128)(2,1)S(1)}, u32[]{:S(2)}, u32[]{:S(2)}) %collective-permute-start.10) | collective-permute-done | bytes 139296 | tf_op jit(solution)/shard_map/ppermute | solution.py:150
  30.9 2.6 %collective-permute-done.8.refs_1_ = bf16[32,2176]{1,0:T(8,128)(2,1)S(1)} collective-permute-done((bf16[32,2176]{1,0:T(8,128)(2,1)S(1)}, bf16[32,2176]{1,0:T(8,128)(2,1)S(1)}, u32[]{:S(2)}, u32[]{:S(2)}) %collective-permute-start.8) | collective-permute-done | bytes 139296 | tf_op jit(solution)/shard_map/ppermute | solution.py:150
  33.5 0.3 shard_map.159
  33.8 0.1 collective-permute-start.11
  33.8 1.3 %collective-permute-done.11.part = bf16[64,1024]{1,0:T(8,128)(2,1)S(1)} collective-permute-done((bf16[64,1024]{1,0:T(8,128)(2,1)S(1)}, bf16[64,1024]{1,0:T(8,128)(2,1)S(1)}, u32[]{:S(2)}, u32[]{:S(2)}) %collective-permute-start.11) | collective-permute-done | bytes 131104 | tf_op jit(solution)/shard_map/ppermute | solution.py:150
  35.2 0.5 shard_map.160
  35.6 11.1 %all_to_all.5 = bf16[8,16,384]{2,1,0:T(8,128)(2,1)S(1)} all-to-all(bf16[8,16,384]{2,1,0:T(8,128)(2,1)S(1)} %shard_map.160), channel_id=1, replica_groups=mesh['req'=8,'tp'=4] {'req'}, dimensions={0} | all-to-all | bytes 196608 | tf_op jit(solution)/shard_map/all_to_all | solution.py:636
  46.8 0.8 %shard_map.161 = bf16[32,384]{1,0:T(8,128)(2,1)} custom-call(bf16[128,384]{1,0:T(8,128)(2,1)S(1)} %bitcast.7, bf16[32,128]{1,0:T(8,128)(2,1)S(1)} %get-tuple-element.55.pick0, bf16[32,128]{1,0:T(8,128)(2,1)S(1)} %get-tuple-element.56.pick1, f32[32,128]{1,0:T(8,128)S(1)} %get-tuple-element.57.first_weight, bf16[32,384]{1,0:T(8,128)(2,1)S(1)} %get-tuple-element.36.attended), custom_call_target="tpu_custom_call" | custom-call | flops 100000 | bytes 100000 | tf_op jit(solution)/shard_map/pallas_call | solution.py:137
  (17 shorter events, 0.0 us)
Async XLA Ops:
  0.6 7.2 %copy-start.3 = (s32[32,2]{0,1:T(2,128)S(1)}, s32[32,2]{0,1:T(2,128)}, u32[]{:S(2)}) copy-start(s32[32,2]{0,1:T(2,128)} %param.24) | copy-start | bytes 772
  0.6 7.2 %copy-start.2 = (f32[384,16]{0,1:T(8,128)S(1)}, f32[384,16]{0,1:T(8,128)}, u32[]{:S(2)}) copy-start(f32[384,16]{0,1:T(8,128)} %param.23) | copy-start | bytes 73732
  0.7 7.2 %copy-start.1 = (bf16[32,384]{1,0:T(8,128)(2,1)S(1)}, bf16[32,384]{1,0:T(8,128)(2,1)}, u32[]{:S(2)}) copy-start(bf16[32,384]{1,0:T(8,128)(2,1)} %resid.1) | copy-start | bytes 73732
  4.6 5.3 %collective-permute-start = (bf16[32,384]{1,0:T(8,128)(2,1)S(1)}, bf16[32,384]{1,0:T(8,128)(2,1)S(1)}, u32[]{:S(2)}, u32[]{:S(2)}) collective-permute-start(bf16[32,384]{1,0:T(8,128)(2,1)S(1)} %get-tuple-element.32), channel_id=1, source_target_pairs={{0,2},{1,3},{2,0},{3,1},{4,6},{5,7},{6,4},{7,5},{8,10},{9,11},{10,... | collective-permute-start | bytes 73736 | tf_op jit(solution)/shard_map/ppermute | solution.py:150
  7.6 3.3 %collective-permute-start.1 = (bf16[32,384]{1,0:T(8,128)(2,1)S(1)}, bf16[32,384]{1,0:T(8,128)(2,1)S(1)}, u32[]{:S(2)}, u32[]{:S(2)}) collective-permute-start(bf16[32,384]{1,0:T(8,128)(2,1)S(1)} %get-tuple-element.33), channel_id=1, source_target_pairs={{0,3},{1,2},{2,1},{3,0},{4,7},{5,6},{6,5},{7,4},{8,11},{9,10},{10,... | collective-permute-start | bytes 73736 | tf_op jit(solution)/shard_map/ppermute | solution.py:150
  7.6 3.3 %collective-permute-start.2 = (bf16[32,384]{1,0:T(8,128)(2,1)S(1)}, bf16[32,384]{1,0:T(8,128)(2,1)S(1)}, u32[]{:S(2)}, u32[]{:S(2)}) collective-permute-start(bf16[32,384]{1,0:T(8,128)(2,1)S(1)} %get-tuple-element.34), channel_id=1, source_target_pairs={{0,1},{1,0},{2,3},{3,2},{4,5},{5,4},{6,7},{7,6},{8,9},{9,8},{10,11... | collective-permute-start | bytes 73736 | tf_op jit(solution)/shard_map/ppermute | solution.py:150
  7.8 13.1 %copy-start.4 = (f32[384]{0:T(512)S(1)}, f32[384]{0:T(512)}, u32[]{:S(2)}) copy-start(f32[384]{0:T(512)} %param.22) | copy-start | bytes 4612
  11.1 4.8 %collective-permute-start.3 = (bf16[32,384]{1,0:T(8,128)(2,1)S(1)}, bf16[32,384]{1,0:T(8,128)(2,1)S(1)}, u32[]{:S(2)}, u32[]{:S(2)}) collective-permute-start(bf16[32,384]{1,0:T(8,128)(2,1)S(1)} %get-tuple-element.40), channel_id=1, source_target_pairs={{0,16},{4,20},{8,24},{12,28},{16,0},{20,4},{24,8},{28,12},{1,17},{... | collective-permute-start | bytes 73736 | tf_op jit(solution)/shard_map/ppermute | solution.py:150
  13.7 5.6 %collective-permute-start.4 = (bf16[32,384]{1,0:T(8,128)(2,1)S(1)}, bf16[32,384]{1,0:T(8,128)(2,1)S(1)}, u32[]{:S(2)}, u32[]{:S(2)}) collective-permute-start(bf16[32,384]{1,0:T(8,128)(2,1)S(1)} %get-tuple-element.41), channel_id=1, source_target_pairs={{0,24},{4,28},{8,16},{12,20},{16,8},{20,12},{24,0},{28,4},{1,25},{... | collective-permute-start | bytes 73736 | tf_op jit(solution)/shard_map/ppermute | solution.py:150
  15.1 4.3 %collective-permute-start.5 = (bf16[32,384]{1,0:T(8,128)(2,1)S(1)}, bf16[32,384]{1,0:T(8,128)(2,1)S(1)}, u32[]{:S(2)}, u32[]{:S(2)}) collective-permute-start(bf16[32,384]{1,0:T(8,128)(2,1)S(1)} %get-tuple-element.42), channel_id=1, source_target_pairs={{0,8},{4,12},{8,0},{12,4},{16,24},{20,28},{24,16},{28,20},{1,9},{5... | collective-permute-start | bytes 73736 | tf_op jit(solution)/shard_map/ppermute | solution.py:150
  19.3 4.2 %collective-permute-start.6 = (bf16[64,384]{1,0:T(8,128)(2,1)S(1)}, bf16[64,384]{1,0:T(8,128)(2,1)S(1)}, u32[]{:S(2)}, u32[]{:S(2)}) collective-permute-start(bf16[64,384]{1,0:T(8,128)(2,1)S(1)} %shard_map.154.turned), channel_id=1, source_target_pairs={{0,4},{4,0},{8,12},{12,8},{16,20},{20,16},{24,28},{28,24},{1,5},{5... | collective-permute-start | bytes 147464 | tf_op jit(solution)/shard_map/ppermute | solution.py:150
  22.3 1.9 %collective-permute-start.9 = (bf16[32,2176]{1,0:T(8,128)(2,1)S(1)}, bf16[32,2176]{1,0:T(8,128)(2,1)S(1)}, u32[]{:S(2)}, u32[]{:S(2)}) collective-permute-start(bf16[32,2176]{1,0:T(8,128)(2,1)S(1)} %get-tuple-element.51), channel_id=1, source_target_pairs={{0,1},{1,0},{2,3},{3,2},{4,5},{5,4},{6,7},{7,6},{8,9},{9,8},{10,11... | collective-permute-start | bytes 417800 | tf_op jit(solution)/shard_map/ppermute | solution.py:150
  24.2 11.0 %copy-start = (bf16[2,1024,384]{2,1,0:T(8,128)(2,1)S(1)}, bf16[2,1024,384]{2,1,0:T(8,128)(2,1)}, u32[]{:S(2)}) copy-start(bf16[2,1024,384]{2,1,0:T(8,128)(2,1)} %param.27) | copy-start | bytes 4718596
  24.2 1.4 %collective-permute-start.7 = (bf16[32,2176]{1,0:T(8,128)(2,1)S(1)}, bf16[32,2176]{1,0:T(8,128)(2,1)S(1)}, u32[]{:S(2)}, u32[]{:S(2)}) collective-permute-start(bf16[32,2176]{1,0:T(8,128)(2,1)S(1)} %get-tuple-element.46), channel_id=1, source_target_pairs={{0,1},{1,0},{2,3},{3,2},{4,5},{5,4},{6,7},{7,6},{8,9},{9,8},{10,11... | collective-permute-start | bytes 417800 | tf_op jit(solution)/shard_map/ppermute | solution.py:150
  24.4 6.5 %collective-permute-start.10 = (bf16[32,2176]{1,0:T(8,128)(2,1)S(1)}, bf16[32,2176]{1,0:T(8,128)(2,1)S(1)}, u32[]{:S(2)}, u32[]{:S(2)}) collective-permute-start(bf16[32,2176]{1,0:T(8,128)(2,1)S(1)} %get-tuple-element.53), channel_id=1, source_target_pairs={{0,2},{1,3},{2,0},{3,1},{4,6},{5,7},{6,4},{7,5},{8,10},{9,11},{10,... | collective-permute-start | bytes 417800 | tf_op jit(solution)/shard_map/ppermute | solution.py:150
  25.8 7.7 %collective-permute-start.8 = (bf16[32,2176]{1,0:T(8,128)(2,1)S(1)}, bf16[32,2176]{1,0:T(8,128)(2,1)S(1)}, u32[]{:S(2)}, u32[]{:S(2)}) collective-permute-start(bf16[32,2176]{1,0:T(8,128)(2,1)S(1)} %get-tuple-element.48), channel_id=1, source_target_pairs={{0,2},{1,3},{2,0},{3,1},{4,6},{5,7},{6,4},{7,5},{8,10},{9,11},{10,... | collective-permute-start | bytes 417800 | tf_op jit(solution)/shard_map/ppermute | solution.py:150
  33.8 1.4 %collective-permute-start.11 = (bf16[64,1024]{1,0:T(8,128)(2,1)S(1)}, bf16[64,1024]{1,0:T(8,128)(2,1)S(1)}, u32[]{:S(2)}, u32[]{:S(2)}) collective-permute-start(bf16[64,1024]{1,0:T(8,128)(2,1)S(1)} %get-tuple-element.54.own), channel_id=1, source_target_pairs={{0,1},{1,0},{2,3},{3,2},{4,5},{5,4},{6,7},{7,6},{8,9},{9,8},{10,11... | collective-permute-start | bytes 393224 | tf_op jit(solution)/shard_map/ppermute | solution.py:150

commit v10 on v9

--- a/solution.py
+++ b/solution.py
@@ -159,7 +159,7 @@
     width = own.shape[1]
     lanes = 2 * HEAD_DIM
     cache_len = k_hbm.shape[1]
-    chunks = 4
+    chunks = 2
     small = [
         pltpu.make_async_copy(source, target, small_sems.at[index])
         for index, (source, target) in enumerate(
@@ -181,7 +181,6 @@
             )
     for copy in small + copies:
         copy.start()
-    per_chunk = row_count // chunks
 
     for copy in small:
         copy.wait()
@@ -210,9 +209,9 @@
 
     upper = lax.broadcasted_iota(jnp.int32, (16, lanes), 0) < 8
     position = lax.broadcasted_iota(jnp.int32, (16, cache_len), 1)
+    for copy in copies[:chunks]:
+        copy.wait()
     for pair in range(row_count // 2):
-        if pair % (per_chunk // 2) == 0:
-            copies[pair // (per_chunk // 2)].wait()
         pair_rows = slice(16 * pair, 16 * pair + 16)
         keys = k_buf[2 * pair : 2 * pair + 2].reshape(2 * cache_len, lanes)
         raw = lax.dot_general(
@@ -234,9 +233,9 @@
     weight_s[...] = (terms * inverse).astype(jnp.bfloat16)
     own_weight = (own_term * inverse).astype(jnp.bfloat16).astype(jnp.float32)
     self_s[...] = own_weight * values_new
+    for copy in copies[chunks : 2 * chunks]:
+        copy.wait()
     for pair in range(row_count // 2):
-        if pair % (per_chunk // 2) == 0:
-            copies[chunks + pair // (per_chunk // 2)].wait()
         pair_rows = slice(16 * pair, 16 * pair + 16)
         values = jnp.concatenate([v_buf[2 * pair], v_buf[2 * pair + 1]], axis=1)
         mixed = jnp.dot(weight_s[pair_rows, :], values, preferred_element_type=jnp.float32)
@@ -533,7 +532,7 @@
             pltpu.VMEM((8 * row_count, cache_len), bf16),
             pltpu.VMEM((row_count, w_out.shape[1]), f32),
             pltpu.SemaphoreType.DMA((4,)),
-            pltpu.SemaphoreType.DMA((12,)),
+            pltpu.SemaphoreType.DMA((6,)),
         ],
         mebibytes=16,
         flops=200_000_000,

time: 47.7 us -> 46.8 us (0.981)
  Pallas kernels: 10 us -> 9.1 us
    pallas_call x13, Pallas kernels: 10 us -> 9.1 us  [call(): pl.pallas_call(kernel, out_shape=[jax.ShapeDtypeStruct(shape, dtype) for...]
  transfers between devices with their start and end apart: 12 -> 12, of which waited for: 8 -> 8; matrix products, arithmetic and copies ran while one was open for 0% -> 0% of each run, Pallas kernels for 9% -> 10%
where the time goes in v10:
time: 46.8 us; the launch traced here: 46.6 us
  waiting for transfers between devices  14.4 us (31%)
  starting transfers between devices  11.2 us (24%)
  blocking collectives  11.1 us (24%)
  Pallas kernels  9.1 us (19%)
  between operations  0.77 us (2%)
    ppermute x12, waiting for transfers between devices, partner_permute(): return lax.ppermute(block, axis, [(i, i ^ distance) for i in range(count)])  14.4 us
    ppermute x12, starting transfers between devices, partner_permute(): return lax.ppermute(block, axis, [(i, i ^ distance) for i in range(count)])  11.2 us
    all_to_all x1, blocking collectives, shards(): lax.all_to_all(computed, 'req', split_axis=0, concat_axis=0, tiled=True)  11.1 us
    pallas_call x13, Pallas kernels, call(): pl.pallas_call(kernel, out_shape=[jax.ShapeDtypeStruct(shape, dtype) for...  9.1 us
  transfers between devices with their start and end apart: 12, of which 8 were waited for; matrix products, arithmetic and copies ran while one was open for 0% of the time, Pallas kernels for 10%

profile of v10, /device:TPU:0, one launch (start us, length us, event | category | flops | bytes accessed | tf_op | source)
XLA Modules:
  0.0 46.6 jit_solution(12023289672354249010)
XLA Ops:
  0.7 3.0 %shard_map.149 = (f32[32,384]{1,0:T(8,128)S(1)}, bf16[32,384]{1,0:T(8,128)(2,1)S(1)}, bf16[32,384]{1,0:T(8,128)(2,1)S(1)}, bf16[32,384]{1,0:T(8,128)(2,1)S(1)}) custom-call(s32[32]{0:T(128)} %lengths_hbm.1, bf16[32,384]{1,0:T(8,128)(2,1)} %queries_hbm.1, bf16[32,128]{1,0:T(8,128)(2,1)} %keys_hbm.1, bf16[32,128]{1,0:T(8,128)(2,1)} %values_hbm.1, ...), custom_call_target="tpu_custom_call" | custom-call | flops 200000000 | bytes 3400000 | tf_op jit(solution)/shard_map/pallas_call | solution.py:137
  3.7 3.0 %collective-permute-start = (bf16[32,384]{1,0:T(8,128)(2,1)S(1)}, bf16[32,384]{1,0:T(8,128)(2,1)S(1)}, u32[]{:S(2)}, u32[]{:S(2)}) collective-permute-start(bf16[32,384]{1,0:T(8,128)(2,1)S(1)} %get-tuple-element.32), channel_id=1, source_target_pairs={{0,2},{1,3},{2,0},{3,1},{4,6},{5,7},{6,4},{7,5},{8,10},{9,11},{10,... | collective-permute-start | bytes 73736 | tf_op jit(solution)/shard_map/ppermute | solution.py:150
  6.7 0.2 collective-permute-start.2
  6.9 2.0 %shard_map.150 = (f32[32,384]{1,0:T(8,128)S(1)}, bf16[128,32]{1,0:T(8,128)(2,1)S(1)}, bf16[32,128]{1,0:T(8,128)(2,1)S(1)}, bf16[32,128]{1,0:T(8,128)(2,1)S(1)}, ...) custom-call(f32[32,384]{1,0:T(8,128)S(1)} %get-tuple-element.30.own, ...), custom_call_target="tpu_custom_call" | custom-call | flops 100000 | bytes 3300000 | tf_op jit(solution)/shard_map/pallas_call | solution.py:137
  8.9 1.0 %collective-permute-done.1.part2 = bf16[32,384]{1,0:T(8,128)(2,1)S(1)} collective-permute-done((bf16[32,384]{1,0:T(8,128)(2,1)S(1)}, bf16[32,384]{1,0:T(8,128)(2,1)S(1)}, u32[]{:S(2)}, u32[]{:S(2)}) %collective-permute-start.1) | collective-permute-done | bytes 24608 | tf_op jit(solution)/shard_map/ppermute | solution.py:150
  10.0 0.2 shard_map.151
  10.1 2.6 %collective-permute-start.3 = (bf16[32,384]{1,0:T(8,128)(2,1)S(1)}, bf16[32,384]{1,0:T(8,128)(2,1)S(1)}, u32[]{:S(2)}, u32[]{:S(2)}) collective-permute-start(bf16[32,384]{1,0:T(8,128)(2,1)S(1)} %get-tuple-element.40), channel_id=1, source_target_pairs={{0,16},{4,20},{8,24},{12,28},{16,0},{20,4},{24,8},{28,12},{1,17},{... | collective-permute-start | bytes 73736 | tf_op jit(solution)/shard_map/ppermute | solution.py:150
  12.8 1.3 %collective-permute-start.4 = (bf16[32,384]{1,0:T(8,128)(2,1)S(1)}, bf16[32,384]{1,0:T(8,128)(2,1)S(1)}, u32[]{:S(2)}, u32[]{:S(2)}) collective-permute-start(bf16[32,384]{1,0:T(8,128)(2,1)S(1)} %get-tuple-element.41), channel_id=1, source_target_pairs={{0,24},{4,28},{8,16},{12,20},{16,8},{20,12},{24,0},{28,4},{1,25},{... | collective-permute-start | bytes 73736 | tf_op jit(solution)/shard_map/ppermute | solution.py:150
  14.1 0.2 collective-permute-start.5
  14.3 0.6 %collective-permute-done.3.part1.in1 = bf16[32,384]{1,0:T(8,128)(2,1)S(1)} collective-permute-done((bf16[32,384]{1,0:T(8,128)(2,1)S(1)}, bf16[32,384]{1,0:T(8,128)(2,1)S(1)}, u32[]{:S(2)}, u32[]{:S(2)}) %collective-permute-start.3) | collective-permute-done | bytes 24608 | tf_op jit(solution)/shard_map/ppermute | solution.py:150
  14.9 3.5 %collective-permute-done.4.part2.in2 = bf16[32,384]{1,0:T(8,128)(2,1)S(1)} collective-permute-done((bf16[32,384]{1,0:T(8,128)(2,1)S(1)}, bf16[32,384]{1,0:T(8,128)(2,1)S(1)}, u32[]{:S(2)}, u32[]{:S(2)}) %collective-permute-start.4) | collective-permute-done | bytes 24608 | tf_op jit(solution)/shard_map/ppermute | solution.py:150
  18.4 1.6 %collective-permute-start.6 = (bf16[64,384]{1,0:T(8,128)(2,1)S(1)}, bf16[64,384]{1,0:T(8,128)(2,1)S(1)}, u32[]{:S(2)}, u32[]{:S(2)}) collective-permute-start(bf16[64,384]{1,0:T(8,128)(2,1)S(1)} %shard_map.154.turned), channel_id=1, source_target_pairs={{0,4},{4,0},{8,12},{12,8},{16,20},{20,16},{24,28},{28,24},{1,5},{5... | collective-permute-start | bytes 147464 | tf_op jit(solution)/shard_map/ppermute | solution.py:150
  20.0 0.6 %shard_map.153 = bf16[32,384]{1,0:T(8,128)(2,1)} custom-call(bf16[32,384]{1,0:T(8,128)(2,1)S(1)} %get-tuple-element.36.attended), custom_call_target="tpu_custom_call" | custom-call | flops 100000 | bytes 100000 | tf_op jit(solution)/shard_map/pallas_call | solution.py:137
  20.6 0.1 shard_map.152.stats
  20.7 0.7 %shard_map.157 = (f32[32,2176]{1,0:T(8,128)S(1)}, bf16[32,2176]{1,0:T(8,128)(2,1)S(1)}) custom-call(bf16[32,384]{1,0:T(8,128)(2,1)S(1)} %get-tuple-element.39.home.in0, bf16[32,384]{1,0:T(8,128)(2,1)S(1)} %collective-permute-done.3.part1.in1, bf16[32,384]{1,0:T(8,128)(2,1)S(1)} %collective-permute-done.4.part2.in2, ...), custom_call_target="tpu_custom_call" | custom-call | flops 400000000 | bytes 3500000 | tf_op jit(solution)/shard_map/pallas_call | solution.py:137
  21.4 0.1 collective-permute-start.9
  21.5 1.1 %collective-permute-done.6.blocks = bf16[64,384]{1,0:T(8,128)(2,1)S(1)} collective-permute-done((bf16[64,384]{1,0:T(8,128)(2,1)S(1)}, bf16[64,384]{1,0:T(8,128)(2,1)S(1)}, u32[]{:S(2)}, u32[]{:S(2)}) %collective-permute-start.6) | collective-permute-done | bytes 49184 | tf_op jit(solution)/shard_map/ppermute | solution.py:150
  22.6 0.7 %shard_map.155 = (f32[32,2176]{1,0:T(8,128)S(1)}, bf16[32,2176]{1,0:T(8,128)(2,1)S(1)}) custom-call(bf16[64,384]{1,0:T(8,128)(2,1)S(1)} %collective-permute-done.6.blocks, f32[1,384]{1,0:T(1,128)S(1)} %reshape.21.gain, bf16[768,1024]{1,0:T(8,128)(2,1)S(1)} %get-tuple-element.43.w_gate, bf16[768,1024]{1,0:T(8,128)(2,1)S(1)} %get-tuple-element.44.w_up), custom_call_target="tpu_custom_call" | custom-call | flops 400000000 | bytes 3500000 | tf_op jit(solution)/shard_map/pallas_call | solution.py:137
  23.2 0.1 collective-permute-start.7
  23.3 0.2 shard_map.158
  23.5 1.0 %collective-permute-start.10 = (bf16[32,2176]{1,0:T(8,128)(2,1)S(1)}, bf16[32,2176]{1,0:T(8,128)(2,1)S(1)}, u32[]{:S(2)}, u32[]{:S(2)}) collective-permute-start(bf16[32,2176]{1,0:T(8,128)(2,1)S(1)} %get-tuple-element.53), channel_id=1, source_target_pairs={{0,2},{1,3},{2,0},{3,1},{4,6},{5,7},{6,4},{7,5},{8,10},{9,11},{10,... | collective-permute-start | bytes 417800 | tf_op jit(solution)/shard_map/ppermute | solution.py:150
  24.5 0.2 collective-permute-done.7.part
  24.7 0.2 shard_map.156
  24.8 1.0 %collective-permute-start.8 = (bf16[32,2176]{1,0:T(8,128)(2,1)S(1)}, bf16[32,2176]{1,0:T(8,128)(2,1)S(1)}, u32[]{:S(2)}, u32[]{:S(2)}) collective-permute-start(bf16[32,2176]{1,0:T(8,128)(2,1)S(1)} %get-tuple-element.48), channel_id=1, source_target_pairs={{0,2},{1,3},{2,0},{3,1},{4,6},{5,7},{6,4},{7,5},{8,10},{9,11},{10,... | collective-permute-start | bytes 417800 | tf_op jit(solution)/shard_map/ppermute | solution.py:150
  25.8 4.2 %collective-permute-done.10.refs_3_ = bf16[32,2176]{1,0:T(8,128)(2,1)S(1)} collective-permute-done((bf16[32,2176]{1,0:T(8,128)(2,1)S(1)}, bf16[32,2176]{1,0:T(8,128)(2,1)S(1)}, u32[]{:S(2)}, u32[]{:S(2)}) %collective-permute-start.10) | collective-permute-done | bytes 139296 | tf_op jit(solution)/shard_map/ppermute | solution.py:150
  30.0 2.6 %collective-permute-done.8.refs_1_ = bf16[32,2176]{1,0:T(8,128)(2,1)S(1)} collective-permute-done((bf16[32,2176]{1,0:T(8,128)(2,1)S(1)}, bf16[32,2176]{1,0:T(8,128)(2,1)S(1)}, u32[]{:S(2)}, u32[]{:S(2)}) %collective-permute-start.8) | collective-permute-done | bytes 139296 | tf_op jit(solution)/shard_map/ppermute | solution.py:150
  32.6 0.3 shard_map.159
  32.8 0.1 collective-permute-start.11
  32.9 1.3 %collective-permute-done.11.part = bf16[64,1024]{1,0:T(8,128)(2,1)S(1)} collective-permute-done((bf16[64,1024]{1,0:T(8,128)(2,1)S(1)}, bf16[64,1024]{1,0:T(8,128)(2,1)S(1)}, u32[]{:S(2)}, u32[]{:S(2)}) %collective-permute-start.11) | collective-permute-done | bytes 131104 | tf_op jit(solution)/shard_map/ppermute | solution.py:150
  34.2 0.5 shard_map.160
  34.7 11.1 %all_to_all.5 = bf16[8,16,384]{2,1,0:T(8,128)(2,1)S(1)} all-to-all(bf16[8,16,384]{2,1,0:T(8,128)(2,1)S(1)} %shard_map.160), channel_id=1, replica_groups=mesh['req'=8,'tp'=4] {'req'}, dimensions={0} | all-to-all | bytes 196608 | tf_op jit(solution)/shard_map/all_to_all | solution.py:635
  45.8 0.8 %shard_map.161 = bf16[32,384]{1,0:T(8,128)(2,1)} custom-call(bf16[128,384]{1,0:T(8,128)(2,1)S(1)} %bitcast.7, bf16[32,128]{1,0:T(8,128)(2,1)S(1)} %get-tuple-element.55.pick0, bf16[32,128]{1,0:T(8,128)(2,1)S(1)} %get-tuple-element.56.pick1, f32[32,128]{1,0:T(8,128)S(1)} %get-tuple-element.57.first_weight, bf16[32,384]{1,0:T(8,128)(2,1)S(1)} %get-tuple-element.36.attended), custom_call_target="tpu_custom_call" | custom-call | flops 100000 | bytes 100000 | tf_op jit(solution)/shard_map/pallas_call | solution.py:137
  (17 shorter events, 0.0 us)
Async XLA Ops:
  0.6 6.3 %copy-start.3 = (s32[32,2]{0,1:T(2,128)S(1)}, s32[32,2]{0,1:T(2,128)}, u32[]{:S(2)}) copy-start(s32[32,2]{0,1:T(2,128)} %param.24) | copy-start | bytes 772
  0.6 6.3 %copy-start.2 = (f32[384,16]{0,1:T(8,128)S(1)}, f32[384,16]{0,1:T(8,128)}, u32[]{:S(2)}) copy-start(f32[384,16]{0,1:T(8,128)} %param.23) | copy-start | bytes 73732
  0.7 6.2 %copy-start.1 = (bf16[32,384]{1,0:T(8,128)(2,1)S(1)}, bf16[32,384]{1,0:T(8,128)(2,1)}, u32[]{:S(2)}) copy-start(bf16[32,384]{1,0:T(8,128)(2,1)} %resid.1) | copy-start | bytes 73732
  3.7 5.3 %collective-permute-start = (bf16[32,384]{1,0:T(8,128)(2,1)S(1)}, bf16[32,384]{1,0:T(8,128)(2,1)S(1)}, u32[]{:S(2)}, u32[]{:S(2)}) collective-permute-start(bf16[32,384]{1,0:T(8,128)(2,1)S(1)} %get-tuple-element.32), channel_id=1, source_target_pairs={{0,2},{1,3},{2,0},{3,1},{4,6},{5,7},{6,4},{7,5},{8,10},{9,11},{10,... | collective-permute-start | bytes 73736 | tf_op jit(solution)/shard_map/ppermute | solution.py:150
  6.7 3.3 %collective-permute-start.1 = (bf16[32,384]{1,0:T(8,128)(2,1)S(1)}, bf16[32,384]{1,0:T(8,128)(2,1)S(1)}, u32[]{:S(2)}, u32[]{:S(2)}) collective-permute-start(bf16[32,384]{1,0:T(8,128)(2,1)S(1)} %get-tuple-element.33), channel_id=1, source_target_pairs={{0,3},{1,2},{2,1},{3,0},{4,7},{5,6},{6,5},{7,4},{8,11},{9,10},{10,... | collective-permute-start | bytes 73736 | tf_op jit(solution)/shard_map/ppermute | solution.py:150
  6.7 3.3 %collective-permute-start.2 = (bf16[32,384]{1,0:T(8,128)(2,1)S(1)}, bf16[32,384]{1,0:T(8,128)(2,1)S(1)}, u32[]{:S(2)}, u32[]{:S(2)}) collective-permute-start(bf16[32,384]{1,0:T(8,128)(2,1)S(1)} %get-tuple-element.34), channel_id=1, source_target_pairs={{0,1},{1,0},{2,3},{3,2},{4,5},{5,4},{6,7},{7,6},{8,9},{9,8},{10,11... | collective-permute-start | bytes 73736 | tf_op jit(solution)/shard_map/ppermute | solution.py:150
  6.9 13.1 %copy-start.4 = (f32[384]{0:T(512)S(1)}, f32[384]{0:T(512)}, u32[]{:S(2)}) copy-start(f32[384]{0:T(512)} %param.22) | copy-start | bytes 4612
  10.1 4.8 %collective-permute-start.3 = (bf16[32,384]{1,0:T(8,128)(2,1)S(1)}, bf16[32,384]{1,0:T(8,128)(2,1)S(1)}, u32[]{:S(2)}, u32[]{:S(2)}) collective-permute-start(bf16[32,384]{1,0:T(8,128)(2,1)S(1)} %get-tuple-element.40), channel_id=1, source_target_pairs={{0,16},{4,20},{8,24},{12,28},{16,0},{20,4},{24,8},{28,12},{1,17},{... | collective-permute-start | bytes 73736 | tf_op jit(solution)/shard_map/ppermute | solution.py:150
  12.8 5.6 %collective-permute-start.4 = (bf16[32,384]{1,0:T(8,128)(2,1)S(1)}, bf16[32,384]{1,0:T(8,128)(2,1)S(1)}, u32[]{:S(2)}, u32[]{:S(2)}) collective-permute-start(bf16[32,384]{1,0:T(8,128)(2,1)S(1)} %get-tuple-element.41), channel_id=1, source_target_pairs={{0,24},{4,28},{8,16},{12,20},{16,8},{20,12},{24,0},{28,4},{1,25},{... | collective-permute-start | bytes 73736 | tf_op jit(solution)/shard_map/ppermute | solution.py:150
  14.1 4.3 %collective-permute-start.5 = (bf16[32,384]{1,0:T(8,128)(2,1)S(1)}, bf16[32,384]{1,0:T(8,128)(2,1)S(1)}, u32[]{:S(2)}, u32[]{:S(2)}) collective-permute-start(bf16[32,384]{1,0:T(8,128)(2,1)S(1)} %get-tuple-element.42), channel_id=1, source_target_pairs={{0,8},{4,12},{8,0},{12,4},{16,24},{20,28},{24,16},{28,20},{1,9},{5... | collective-permute-start | bytes 73736 | tf_op jit(solution)/shard_map/ppermute | solution.py:150
  18.4 4.2 %collective-permute-start.6 = (bf16[64,384]{1,0:T(8,128)(2,1)S(1)}, bf16[64,384]{1,0:T(8,128)(2,1)S(1)}, u32[]{:S(2)}, u32[]{:S(2)}) collective-permute-start(bf16[64,384]{1,0:T(8,128)(2,1)S(1)} %shard_map.154.turned), channel_id=1, source_target_pairs={{0,4},{4,0},{8,12},{12,8},{16,20},{20,16},{24,28},{28,24},{1,5},{5... | collective-permute-start | bytes 147464 | tf_op jit(solution)/shard_map/ppermute | solution.py:150
  21.4 1.9 %collective-permute-start.9 = (bf16[32,2176]{1,0:T(8,128)(2,1)S(1)}, bf16[32,2176]{1,0:T(8,128)(2,1)S(1)}, u32[]{:S(2)}, u32[]{:S(2)}) collective-permute-start(bf16[32,2176]{1,0:T(8,128)(2,1)S(1)} %get-tuple-element.51), channel_id=1, source_target_pairs={{0,1},{1,0},{2,3},{3,2},{4,5},{5,4},{6,7},{7,6},{8,9},{9,8},{10,11... | collective-permute-start | bytes 417800 | tf_op jit(solution)/shard_map/ppermute | solution.py:150
  23.2 11.0 %copy-start = (bf16[2,1024,384]{2,1,0:T(8,128)(2,1)S(1)}, bf16[2,1024,384]{2,1,0:T(8,128)(2,1)}, u32[]{:S(2)}) copy-start(bf16[2,1024,384]{2,1,0:T(8,128)(2,1)} %param.27) | copy-start | bytes 4718596
  23.2 1.4 %collective-permute-start.7 = (bf16[32,2176]{1,0:T(8,128)(2,1)S(1)}, bf16[32,2176]{1,0:T(8,128)(2,1)S(1)}, u32[]{:S(2)}, u32[]{:S(2)}) collective-permute-start(bf16[32,2176]{1,0:T(8,128)(2,1)S(1)} %get-tuple-element.46), channel_id=1, source_target_pairs={{0,1},{1,0},{2,3},{3,2},{4,5},{5,4},{6,7},{7,6},{8,9},{9,8},{10,11... | collective-permute-start | bytes 417800 | tf_op jit(solution)/shard_map/ppermute | solution.py:150
  23.5 6.5 %collective-permute-start.10 = (bf16[32,2176]{1,0:T(8,128)(2,1)S(1)}, bf16[32,2176]{1,0:T(8,128)(2,1)S(1)}, u32[]{:S(2)}, u32[]{:S(2)}) collective-permute-start(bf16[32,2176]{1,0:T(8,128)(2,1)S(1)} %get-tuple-element.53), channel_id=1, source_target_pairs={{0,2},{1,3},{2,0},{3,1},{4,6},{5,7},{6,4},{7,5},{8,10},{9,11},{10,... | collective-permute-start | bytes 417800 | tf_op jit(solution)/shard_map/ppermute | solution.py:150
  24.8 7.7 %collective-permute-start.8 = (bf16[32,2176]{1,0:T(8,128)(2,1)S(1)}, bf16[32,2176]{1,0:T(8,128)(2,1)S(1)}, u32[]{:S(2)}, u32[]{:S(2)}) collective-permute-start(bf16[32,2176]{1,0:T(8,128)(2,1)S(1)} %get-tuple-element.48), channel_id=1, source_target_pairs={{0,2},{1,3},{2,0},{3,1},{4,6},{5,7},{6,4},{7,5},{8,10},{9,11},{10,... | collective-permute-start | bytes 417800 | tf_op jit(solution)/shard_map/ppermute | solution.py:150
  32.8 1.4 %collective-permute-start.11 = (bf16[64,1024]{1,0:T(8,128)(2,1)S(1)}, bf16[64,1024]{1,0:T(8,128)(2,1)S(1)}, u32[]{:S(2)}, u32[]{:S(2)}) collective-permute-start(bf16[64,1024]{1,0:T(8,128)(2,1)S(1)} %get-tuple-element.54.own), channel_id=1, source_target_pairs={{0,1},{1,0},{2,3},{3,2},{4,5},{5,4},{6,7},{7,6},{8,9},{9,8},{10,11... | collective-permute-start | bytes 393224 | tf_op jit(solution)/shard_map/ppermute | solution.py:150

commit v11 on v10

--- a/solution.py
+++ b/solution.py
@@ -153,7 +153,7 @@
 def attend_kernel(
     lengths_hbm, queries_hbm, keys_hbm, values_hbm, k_hbm, v_hbm, w_hbm, own, sent1, sent2, sent3,
     lengths, queries, new_keys, new_values, k_buf, v_buf, w_buf,
-    query_s, self_s, score_s, weight_s, product_s, small_sems, sems,
+    query_s, score_s, product_s, small_sems, sems,
 ):
     row_count = queries.shape[0]
     width = own.shape[1]
@@ -225,23 +225,26 @@
             -1e30,
         )
 
-    scores = score_s[...]
-    peak = jnp.maximum(jnp.max(scores, axis=1, keepdims=True), own_score)
-    terms = jnp.exp(scores - peak)
-    own_term = jnp.exp(own_score - peak)
-    inverse = 1.0 / (jnp.sum(terms, axis=1, keepdims=True) + own_term)
-    weight_s[...] = (terms * inverse).astype(jnp.bfloat16)
-    own_weight = (own_term * inverse).astype(jnp.bfloat16).astype(jnp.float32)
-    self_s[...] = own_weight * values_new
     for copy in copies[chunks : 2 * chunks]:
         copy.wait()
-    for pair in range(row_count // 2):
-        pair_rows = slice(16 * pair, 16 * pair + 16)
-        values = jnp.concatenate([v_buf[2 * pair], v_buf[2 * pair + 1]], axis=1)
-        mixed = jnp.dot(weight_s[pair_rows, :], values, preferred_element_type=jnp.float32)
-        query_s[pair_rows, :] = (
-            jnp.where(upper, mixed[:, :lanes], mixed[:, lanes:]) + self_s[pair_rows, :]
-        )
+    for first in range(0, row_count, 8):
+        chunk_rows = slice(8 * first, 8 * first + 64)
+        scores = score_s[chunk_rows, :]
+        own_rows = own_score[chunk_rows]
+        peak = jnp.maximum(jnp.max(scores, axis=1, keepdims=True), own_rows)
+        terms = jnp.exp(scores - peak)
+        own_term = jnp.exp(own_rows - peak)
+        inverse = 1.0 / (jnp.sum(terms, axis=1, keepdims=True) + own_term)
+        weights = (terms * inverse).astype(jnp.bfloat16)
+        own_weight = (own_term * inverse).astype(jnp.bfloat16).astype(jnp.float32)
+        own_part = own_weight * values_new[chunk_rows]
+        for index in range(0, 8, 2):
+            values = jnp.concatenate([v_buf[first + index], v_buf[first + index + 1]], axis=1)
+            rows = slice(8 * index, 8 * index + 16)
+            mixed = jnp.dot(weights[rows], values, preferred_element_type=jnp.float32)
+            query_s[8 * (first + index) : 8 * (first + index) + 16, :] = (
+                jnp.where(upper, mixed[:, :lanes], mixed[:, lanes:]) + own_part[rows]
+            )
 
     mixed = [query_s[pl.ds(head, row_count, stride=8), :] for head in range(6)]
     attention = jnp.concatenate(
@@ -527,9 +530,7 @@
             pltpu.VMEM(v_cache.shape, bf16),
             pltpu.VMEM(w_out.shape, bf16),
             pltpu.VMEM((8 * row_count, lanes), f32),
-            pltpu.VMEM((8 * row_count, lanes), f32),
             pltpu.VMEM((8 * row_count, cache_len), f32),
-            pltpu.VMEM((8 * row_count, cache_len), bf16),
             pltpu.VMEM((row_count, w_out.shape[1]), f32),
             pltpu.SemaphoreType.DMA((4,)),
             pltpu.SemaphoreType.DMA((6,)),

time: 46.8 us -> 46.8 us (level)
  no operation moved by 1% of the time
where the time goes in v11:
time: 46.8 us; the launch traced here: 46.6 us
  waiting for transfers between devices  14.4 us (31%)
  starting transfers between devices  11.2 us (24%)
  blocking collectives  11.1 us (24%)
  Pallas kernels  9.16 us (20%)
  between operations  0.77 us (2%)
    ppermute x12, waiting for transfers between devices, partner_permute(): return lax.ppermute(block, axis, [(i, i ^ distance) for i in range(count)])  14.4 us
    ppermute x12, starting transfers between devices, partner_permute(): return lax.ppermute(block, axis, [(i, i ^ distance) for i in range(count)])  11.2 us
    all_to_all x1, blocking collectives, shards(): lax.all_to_all(computed, 'req', split_axis=0, concat_axis=0, tiled=True)  11.1 us
    pallas_call x13, Pallas kernels, call(): pl.pallas_call(kernel, out_shape=[jax.ShapeDtypeStruct(shape, dtype) for...  9.16 us
  transfers between devices with their start and end apart: 12, of which 8 were waited for; matrix products, arithmetic and copies ran while one was open for 0% of the time, Pallas kernels for 10%

profile of v11, /device:TPU:0, one launch (start us, length us, event | category | flops | bytes accessed | tf_op | source)
XLA Modules:
  0.0 46.6 jit_solution(2777070277263521921)
XLA Ops:
  0.7 3.1 %shard_map.149 = (f32[32,384]{1,0:T(8,128)S(1)}, bf16[32,384]{1,0:T(8,128)(2,1)S(1)}, bf16[32,384]{1,0:T(8,128)(2,1)S(1)}, bf16[32,384]{1,0:T(8,128)(2,1)S(1)}) custom-call(s32[32]{0:T(128)} %lengths_hbm.1, bf16[32,384]{1,0:T(8,128)(2,1)} %queries_hbm.1, bf16[32,128]{1,0:T(8,128)(2,1)} %keys_hbm.1, bf16[32,128]{1,0:T(8,128)(2,1)} %values_hbm.1, ...), custom_call_target="tpu_custom_call" | custom-call | flops 200000000 | bytes 3400000 | tf_op jit(solution)/shard_map/pallas_call | solution.py:137
  3.7 3.0 %collective-permute-start = (bf16[32,384]{1,0:T(8,128)(2,1)S(1)}, bf16[32,384]{1,0:T(8,128)(2,1)S(1)}, u32[]{:S(2)}, u32[]{:S(2)}) collective-permute-start(bf16[32,384]{1,0:T(8,128)(2,1)S(1)} %get-tuple-element.32), channel_id=1, source_target_pairs={{0,2},{1,3},{2,0},{3,1},{4,6},{5,7},{6,4},{7,5},{8,10},{9,11},{10,... | collective-permute-start | bytes 73736 | tf_op jit(solution)/shard_map/ppermute | solution.py:150
  6.7 0.2 collective-permute-start.2
  7.0 2.0 %shard_map.150 = (f32[32,384]{1,0:T(8,128)S(1)}, bf16[128,32]{1,0:T(8,128)(2,1)S(1)}, bf16[32,128]{1,0:T(8,128)(2,1)S(1)}, bf16[32,128]{1,0:T(8,128)(2,1)S(1)}, ...) custom-call(f32[32,384]{1,0:T(8,128)S(1)} %get-tuple-element.30.own, ...), custom_call_target="tpu_custom_call" | custom-call | flops 100000 | bytes 3300000 | tf_op jit(solution)/shard_map/pallas_call | solution.py:137
  9.0 1.0 %collective-permute-done.1.part2 = bf16[32,384]{1,0:T(8,128)(2,1)S(1)} collective-permute-done((bf16[32,384]{1,0:T(8,128)(2,1)S(1)}, bf16[32,384]{1,0:T(8,128)(2,1)S(1)}, u32[]{:S(2)}, u32[]{:S(2)}) %collective-permute-start.1) | collective-permute-done | bytes 24608 | tf_op jit(solution)/shard_map/ppermute | solution.py:150
  10.0 0.2 shard_map.151
  10.2 2.6 %collective-permute-start.3 = (bf16[32,384]{1,0:T(8,128)(2,1)S(1)}, bf16[32,384]{1,0:T(8,128)(2,1)S(1)}, u32[]{:S(2)}, u32[]{:S(2)}) collective-permute-start(bf16[32,384]{1,0:T(8,128)(2,1)S(1)} %get-tuple-element.40), channel_id=1, source_target_pairs={{0,16},{4,20},{8,24},{12,28},{16,0},{20,4},{24,8},{28,12},{1,17},{... | collective-permute-start | bytes 73736 | tf_op jit(solution)/shard_map/ppermute | solution.py:150
  12.8 1.4 %collective-permute-start.4 = (bf16[32,384]{1,0:T(8,128)(2,1)S(1)}, bf16[32,384]{1,0:T(8,128)(2,1)S(1)}, u32[]{:S(2)}, u32[]{:S(2)}) collective-permute-start(bf16[32,384]{1,0:T(8,128)(2,1)S(1)} %get-tuple-element.41), channel_id=1, source_target_pairs={{0,24},{4,28},{8,16},{12,20},{16,8},{20,12},{24,0},{28,4},{1,25},{... | collective-permute-start | bytes 73736 | tf_op jit(solution)/shard_map/ppermute | solution.py:150
  14.2 0.2 collective-permute-start.5
  14.4 0.6 %collective-permute-done.3.part1.in1 = bf16[32,384]{1,0:T(8,128)(2,1)S(1)} collective-permute-done((bf16[32,384]{1,0:T(8,128)(2,1)S(1)}, bf16[32,384]{1,0:T(8,128)(2,1)S(1)}, u32[]{:S(2)}, u32[]{:S(2)}) %collective-permute-start.3) | collective-permute-done | bytes 24608 | tf_op jit(solution)/shard_map/ppermute | solution.py:150
  15.0 3.5 %collective-permute-done.4.part2.in2 = bf16[32,384]{1,0:T(8,128)(2,1)S(1)} collective-permute-done((bf16[32,384]{1,0:T(8,128)(2,1)S(1)}, bf16[32,384]{1,0:T(8,128)(2,1)S(1)}, u32[]{:S(2)}, u32[]{:S(2)}) %collective-permute-start.4) | collective-permute-done | bytes 24608 | tf_op jit(solution)/shard_map/ppermute | solution.py:150
  18.5 1.6 %collective-permute-start.6 = (bf16[64,384]{1,0:T(8,128)(2,1)S(1)}, bf16[64,384]{1,0:T(8,128)(2,1)S(1)}, u32[]{:S(2)}, u32[]{:S(2)}) collective-permute-start(bf16[64,384]{1,0:T(8,128)(2,1)S(1)} %shard_map.154.turned), channel_id=1, source_target_pairs={{0,4},{4,0},{8,12},{12,8},{16,20},{20,16},{24,28},{28,24},{1,5},{5... | collective-permute-start | bytes 147464 | tf_op jit(solution)/shard_map/ppermute | solution.py:150
  20.1 0.6 %shard_map.153 = bf16[32,384]{1,0:T(8,128)(2,1)} custom-call(bf16[32,384]{1,0:T(8,128)(2,1)S(1)} %get-tuple-element.36.attended), custom_call_target="tpu_custom_call" | custom-call | flops 100000 | bytes 100000 | tf_op jit(solution)/shard_map/pallas_call | solution.py:137
  20.7 0.1 shard_map.152.stats
  20.7 0.7 %shard_map.157 = (f32[32,2176]{1,0:T(8,128)S(1)}, bf16[32,2176]{1,0:T(8,128)(2,1)S(1)}) custom-call(bf16[32,384]{1,0:T(8,128)(2,1)S(1)} %get-tuple-element.39.home.in0, bf16[32,384]{1,0:T(8,128)(2,1)S(1)} %collective-permute-done.3.part1.in1, bf16[32,384]{1,0:T(8,128)(2,1)S(1)} %collective-permute-done.4.part2.in2, ...), custom_call_target="tpu_custom_call" | custom-call | flops 400000000 | bytes 3500000 | tf_op jit(solution)/shard_map/pallas_call | solution.py:137
  21.4 0.1 collective-permute-start.9
  21.5 1.1 %collective-permute-done.6.blocks = bf16[64,384]{1,0:T(8,128)(2,1)S(1)} collective-permute-done((bf16[64,384]{1,0:T(8,128)(2,1)S(1)}, bf16[64,384]{1,0:T(8,128)(2,1)S(1)}, u32[]{:S(2)}, u32[]{:S(2)}) %collective-permute-start.6) | collective-permute-done | bytes 49184 | tf_op jit(solution)/shard_map/ppermute | solution.py:150
  22.6 0.7 %shard_map.155 = (f32[32,2176]{1,0:T(8,128)S(1)}, bf16[32,2176]{1,0:T(8,128)(2,1)S(1)}) custom-call(bf16[64,384]{1,0:T(8,128)(2,1)S(1)} %collective-permute-done.6.blocks, f32[1,384]{1,0:T(1,128)S(1)} %reshape.21.gain, bf16[768,1024]{1,0:T(8,128)(2,1)S(1)} %get-tuple-element.43.w_gate, bf16[768,1024]{1,0:T(8,128)(2,1)S(1)} %get-tuple-element.44.w_up), custom_call_target="tpu_custom_call" | custom-call | flops 400000000 | bytes 3500000 | tf_op jit(solution)/shard_map/pallas_call | solution.py:137
  23.3 0.1 collective-permute-start.7
  23.4 0.2 shard_map.158
  23.6 1.0 %collective-permute-start.10 = (bf16[32,2176]{1,0:T(8,128)(2,1)S(1)}, bf16[32,2176]{1,0:T(8,128)(2,1)S(1)}, u32[]{:S(2)}, u32[]{:S(2)}) collective-permute-start(bf16[32,2176]{1,0:T(8,128)(2,1)S(1)} %get-tuple-element.53), channel_id=1, source_target_pairs={{0,2},{1,3},{2,0},{3,1},{4,6},{5,7},{6,4},{7,5},{8,10},{9,11},{10,... | collective-permute-start | bytes 417800 | tf_op jit(solution)/shard_map/ppermute | solution.py:150
  24.5 0.2 collective-permute-done.7.part
  24.7 0.2 shard_map.156
  24.9 1.0 %collective-permute-start.8 = (bf16[32,2176]{1,0:T(8,128)(2,1)S(1)}, bf16[32,2176]{1,0:T(8,128)(2,1)S(1)}, u32[]{:S(2)}, u32[]{:S(2)}) collective-permute-start(bf16[32,2176]{1,0:T(8,128)(2,1)S(1)} %get-tuple-element.48), channel_id=1, source_target_pairs={{0,2},{1,3},{2,0},{3,1},{4,6},{5,7},{6,4},{7,5},{8,10},{9,11},{10,... | collective-permute-start | bytes 417800 | tf_op jit(solution)/shard_map/ppermute | solution.py:150
  25.9 4.2 %collective-permute-done.10.refs_3_ = bf16[32,2176]{1,0:T(8,128)(2,1)S(1)} collective-permute-done((bf16[32,2176]{1,0:T(8,128)(2,1)S(1)}, bf16[32,2176]{1,0:T(8,128)(2,1)S(1)}, u32[]{:S(2)}, u32[]{:S(2)}) %collective-permute-start.10) | collective-permute-done | bytes 139296 | tf_op jit(solution)/shard_map/ppermute | solution.py:150
  30.0 2.6 %collective-permute-done.8.refs_1_ = bf16[32,2176]{1,0:T(8,128)(2,1)S(1)} collective-permute-done((bf16[32,2176]{1,0:T(8,128)(2,1)S(1)}, bf16[32,2176]{1,0:T(8,128)(2,1)S(1)}, u32[]{:S(2)}, u32[]{:S(2)}) %collective-permute-start.8) | collective-permute-done | bytes 139296 | tf_op jit(solution)/shard_map/ppermute | solution.py:150
  32.6 0.3 shard_map.159
  32.9 0.1 collective-permute-start.11
  33.0 1.3 %collective-permute-done.11.part = bf16[64,1024]{1,0:T(8,128)(2,1)S(1)} collective-permute-done((bf16[64,1024]{1,0:T(8,128)(2,1)S(1)}, bf16[64,1024]{1,0:T(8,128)(2,1)S(1)}, u32[]{:S(2)}, u32[]{:S(2)}) %collective-permute-start.11) | collective-permute-done | bytes 131104 | tf_op jit(solution)/shard_map/ppermute | solution.py:150
  34.3 0.5 shard_map.160
  34.8 11.1 %all_to_all.5 = bf16[8,16,384]{2,1,0:T(8,128)(2,1)S(1)} all-to-all(bf16[8,16,384]{2,1,0:T(8,128)(2,1)S(1)} %shard_map.160), channel_id=1, replica_groups=mesh['req'=8,'tp'=4] {'req'}, dimensions={0} | all-to-all | bytes 196608 | tf_op jit(solution)/shard_map/all_to_all | solution.py:636
  45.9 0.8 %shard_map.161 = bf16[32,384]{1,0:T(8,128)(2,1)} custom-call(bf16[128,384]{1,0:T(8,128)(2,1)S(1)} %bitcast.7, bf16[32,128]{1,0:T(8,128)(2,1)S(1)} %get-tuple-element.55.pick0, bf16[32,128]{1,0:T(8,128)(2,1)S(1)} %get-tuple-element.56.pick1, f32[32,128]{1,0:T(8,128)S(1)} %get-tuple-element.57.first_weight, bf16[32,384]{1,0:T(8,128)(2,1)S(1)} %get-tuple-element.36.attended), custom_call_target="tpu_custom_call" | custom-call | flops 100000 | bytes 100000 | tf_op jit(solution)/shard_map/pallas_call | solution.py:137
  (17 shorter events, 0.0 us)
Async XLA Ops:
  0.6 6.3 %copy-start.3 = (s32[32,2]{0,1:T(2,128)S(1)}, s32[32,2]{0,1:T(2,128)}, u32[]{:S(2)}) copy-start(s32[32,2]{0,1:T(2,128)} %param.24) | copy-start | bytes 772
  0.6 6.3 %copy-start.2 = (f32[384,16]{0,1:T(8,128)S(1)}, f32[384,16]{0,1:T(8,128)}, u32[]{:S(2)}) copy-start(f32[384,16]{0,1:T(8,128)} %param.23) | copy-start | bytes 73732
  0.7 6.3 %copy-start.1 = (bf16[32,384]{1,0:T(8,128)(2,1)S(1)}, bf16[32,384]{1,0:T(8,128)(2,1)}, u32[]{:S(2)}) copy-start(bf16[32,384]{1,0:T(8,128)(2,1)} %resid.1) | copy-start | bytes 73732
  3.7 5.3 %collective-permute-start = (bf16[32,384]{1,0:T(8,128)(2,1)S(1)}, bf16[32,384]{1,0:T(8,128)(2,1)S(1)}, u32[]{:S(2)}, u32[]{:S(2)}) collective-permute-start(bf16[32,384]{1,0:T(8,128)(2,1)S(1)} %get-tuple-element.32), channel_id=1, source_target_pairs={{0,2},{1,3},{2,0},{3,1},{4,6},{5,7},{6,4},{7,5},{8,10},{9,11},{10,... | collective-permute-start | bytes 73736 | tf_op jit(solution)/shard_map/ppermute | solution.py:150
  6.7 3.3 %collective-permute-start.1 = (bf16[32,384]{1,0:T(8,128)(2,1)S(1)}, bf16[32,384]{1,0:T(8,128)(2,1)S(1)}, u32[]{:S(2)}, u32[]{:S(2)}) collective-permute-start(bf16[32,384]{1,0:T(8,128)(2,1)S(1)} %get-tuple-element.33), channel_id=1, source_target_pairs={{0,3},{1,2},{2,1},{3,0},{4,7},{5,6},{6,5},{7,4},{8,11},{9,10},{10,... | collective-permute-start | bytes 73736 | tf_op jit(solution)/shard_map/ppermute | solution.py:150
  6.7 3.3 %collective-permute-start.2 = (bf16[32,384]{1,0:T(8,128)(2,1)S(1)}, bf16[32,384]{1,0:T(8,128)(2,1)S(1)}, u32[]{:S(2)}, u32[]{:S(2)}) collective-permute-start(bf16[32,384]{1,0:T(8,128)(2,1)S(1)} %get-tuple-element.34), channel_id=1, source_target_pairs={{0,1},{1,0},{2,3},{3,2},{4,5},{5,4},{6,7},{7,6},{8,9},{9,8},{10,11... | collective-permute-start | bytes 73736 | tf_op jit(solution)/shard_map/ppermute | solution.py:150
  6.9 13.1 %copy-start.4 = (f32[384]{0:T(512)S(1)}, f32[384]{0:T(512)}, u32[]{:S(2)}) copy-start(f32[384]{0:T(512)} %param.22) | copy-start | bytes 4612
  10.2 4.8 %collective-permute-start.3 = (bf16[32,384]{1,0:T(8,128)(2,1)S(1)}, bf16[32,384]{1,0:T(8,128)(2,1)S(1)}, u32[]{:S(2)}, u32[]{:S(2)}) collective-permute-start(bf16[32,384]{1,0:T(8,128)(2,1)S(1)} %get-tuple-element.40), channel_id=1, source_target_pairs={{0,16},{4,20},{8,24},{12,28},{16,0},{20,4},{24,8},{28,12},{1,17},{... | collective-permute-start | bytes 73736 | tf_op jit(solution)/shard_map/ppermute | solution.py:150
  12.8 5.6 %collective-permute-start.4 = (bf16[32,384]{1,0:T(8,128)(2,1)S(1)}, bf16[32,384]{1,0:T(8,128)(2,1)S(1)}, u32[]{:S(2)}, u32[]{:S(2)}) collective-permute-start(bf16[32,384]{1,0:T(8,128)(2,1)S(1)} %get-tuple-element.41), channel_id=1, source_target_pairs={{0,24},{4,28},{8,16},{12,20},{16,8},{20,12},{24,0},{28,4},{1,25},{... | collective-permute-start | bytes 73736 | tf_op jit(solution)/shard_map/ppermute | solution.py:150
  14.2 4.3 %collective-permute-start.5 = (bf16[32,384]{1,0:T(8,128)(2,1)S(1)}, bf16[32,384]{1,0:T(8,128)(2,1)S(1)}, u32[]{:S(2)}, u32[]{:S(2)}) collective-permute-start(bf16[32,384]{1,0:T(8,128)(2,1)S(1)} %get-tuple-element.42), channel_id=1, source_target_pairs={{0,8},{4,12},{8,0},{12,4},{16,24},{20,28},{24,16},{28,20},{1,9},{5... | collective-permute-start | bytes 73736 | tf_op jit(solution)/shard_map/ppermute | solution.py:150
  18.5 4.2 %collective-permute-start.6 = (bf16[64,384]{1,0:T(8,128)(2,1)S(1)}, bf16[64,384]{1,0:T(8,128)(2,1)S(1)}, u32[]{:S(2)}, u32[]{:S(2)}) collective-permute-start(bf16[64,384]{1,0:T(8,128)(2,1)S(1)} %shard_map.154.turned), channel_id=1, source_target_pairs={{0,4},{4,0},{8,12},{12,8},{16,20},{20,16},{24,28},{28,24},{1,5},{5... | collective-permute-start | bytes 147464 | tf_op jit(solution)/shard_map/ppermute | solution.py:150
  21.4 1.9 %collective-permute-start.9 = (bf16[32,2176]{1,0:T(8,128)(2,1)S(1)}, bf16[32,2176]{1,0:T(8,128)(2,1)S(1)}, u32[]{:S(2)}, u32[]{:S(2)}) collective-permute-start(bf16[32,2176]{1,0:T(8,128)(2,1)S(1)} %get-tuple-element.51), channel_id=1, source_target_pairs={{0,1},{1,0},{2,3},{3,2},{4,5},{5,4},{6,7},{7,6},{8,9},{9,8},{10,11... | collective-permute-start | bytes 417800 | tf_op jit(solution)/shard_map/ppermute | solution.py:150
  23.3 11.0 %copy-start = (bf16[2,1024,384]{2,1,0:T(8,128)(2,1)S(1)}, bf16[2,1024,384]{2,1,0:T(8,128)(2,1)}, u32[]{:S(2)}) copy-start(bf16[2,1024,384]{2,1,0:T(8,128)(2,1)} %param.27) | copy-start | bytes 4718596
  23.3 1.4 %collective-permute-start.7 = (bf16[32,2176]{1,0:T(8,128)(2,1)S(1)}, bf16[32,2176]{1,0:T(8,128)(2,1)S(1)}, u32[]{:S(2)}, u32[]{:S(2)}) collective-permute-start(bf16[32,2176]{1,0:T(8,128)(2,1)S(1)} %get-tuple-element.46), channel_id=1, source_target_pairs={{0,1},{1,0},{2,3},{3,2},{4,5},{5,4},{6,7},{7,6},{8,9},{9,8},{10,11... | collective-permute-start | bytes 417800 | tf_op jit(solution)/shard_map/ppermute | solution.py:150
  23.6 6.5 %collective-permute-start.10 = (bf16[32,2176]{1,0:T(8,128)(2,1)S(1)}, bf16[32,2176]{1,0:T(8,128)(2,1)S(1)}, u32[]{:S(2)}, u32[]{:S(2)}) collective-permute-start(bf16[32,2176]{1,0:T(8,128)(2,1)S(1)} %get-tuple-element.53), channel_id=1, source_target_pairs={{0,2},{1,3},{2,0},{3,1},{4,6},{5,7},{6,4},{7,5},{8,10},{9,11},{10,... | collective-permute-start | bytes 417800 | tf_op jit(solution)/shard_map/ppermute | solution.py:150
  24.9 7.7 %collective-permute-start.8 = (bf16[32,2176]{1,0:T(8,128)(2,1)S(1)}, bf16[32,2176]{1,0:T(8,128)(2,1)S(1)}, u32[]{:S(2)}, u32[]{:S(2)}) collective-permute-start(bf16[32,2176]{1,0:T(8,128)(2,1)S(1)} %get-tuple-element.48), channel_id=1, source_target_pairs={{0,2},{1,3},{2,0},{3,1},{4,6},{5,7},{6,4},{7,5},{8,10},{9,11},{10,... | collective-permute-start | bytes 417800 | tf_op jit(solution)/shard_map/ppermute | solution.py:150
  32.9 1.4 %collective-permute-start.11 = (bf16[64,1024]{1,0:T(8,128)(2,1)S(1)}, bf16[64,1024]{1,0:T(8,128)(2,1)S(1)}, u32[]{:S(2)}, u32[]{:S(2)}) collective-permute-start(bf16[64,1024]{1,0:T(8,128)(2,1)S(1)} %get-tuple-element.54.own), channel_id=1, source_target_pairs={{0,1},{1,0},{2,3},{3,2},{4,5},{5,4},{6,7},{7,6},{8,9},{9,8},{10,11... | collective-permute-start | bytes 393224 | tf_op jit(solution)/shard_map/ppermute | solution.py:150

commit v12 on v10

--- a/solution.py
+++ b/solution.py
@@ -290,15 +290,15 @@
     )
     place_req = lax.axis_index("req")
 
-    def pick(route, named, mine):
+    def pick(route, named):
         rank = jnp.sum(named * before, axis=0, keepdims=True).astype(jnp.int32)
-        block = ((route // slot_dev) ^ mine) * slot_dev + lax.rem(route, slot_dev)
+        block = ((route // slot_dev) ^ place_req) * slot_dev + lax.rem(route, slot_dev)
         return jnp.where(place == block * CAP + rank, 1.0, 0.0)
 
-    sent_rows = pick(route0, named0, place_req) + pick(route1, named1, place_req)
-    pick_rows[...] = sent_rows.astype(jnp.bfloat16)
-    pick0[...] = jnp.transpose(pick(route0, named0, 0)).astype(jnp.bfloat16)
-    pick1[...] = jnp.transpose(pick(route1, named1, 0)).astype(jnp.bfloat16)
+    first, second = pick(route0, named0), pick(route1, named1)
+    pick_rows[...] = (first + second).astype(jnp.bfloat16)
+    pick0[...] = jnp.transpose(first).astype(jnp.bfloat16)
+    pick1[...] = jnp.transpose(second).astype(jnp.bfloat16)
     signed = jnp.transpose(named0 - named1)
     router_rows[...] = jnp.dot(
         signed[:, :EXPERTS], w_router[...],
@@ -445,28 +445,65 @@
         first_weight[index * half : (index + 1) * half, :] = jnp.broadcast_to(weight, (half, 128))
 
 
-def down_kernel(slot_dev, own, part, w_down, computed, lhs):
-    quarter, width = own.shape[0] // 2, own.shape[1]
-    block = computed.shape[1]
-    place_tp = lax.axis_index("tp")
-    place_req = lax.axis_index("req")
-    masks = slot_masks(quarter, slot_dev)
-    for shift in range(4):
-        first = shift // 2 * quarter
-        rows = (own, part)[shift % 2][first : first + quarter, :].astype(jnp.float32)
-        place = pl.ds(pl.multiple_of((place_tp ^ shift) * quarter, quarter), quarter)
-        for index, mask in enumerate(masks):
-            lhs[place, index * width : (index + 1) * width] = jnp.where(mask, rows, 0.0).astype(
-                jnp.bfloat16
-            )
-    product = jnp.dot(lhs[...], w_down[...], preferred_element_type=jnp.float32)
-    for index in range(computed.shape[0]):
-        computed[place_req ^ index] = product[index * block : (index + 1) * block].astype(
-            computed.dtype
-        )
-
-
-def combine_kernel(returned, pick0, pick1, first_weight, attended, layer_out):
+BACK = ((0, 2, 3, 1), (0, 3, 1, 2))
+
+
+def down_rows(slot_dev, hidden, w_down, lhs, product):
+    count, width = hidden.shape
+    rows = hidden[...].astype(jnp.float32)
+    for index, mask in enumerate(slot_masks(count, slot_dev)):
+        lhs[:, index * width : (index + 1) * width] = jnp.where(mask, rows, 0.0).astype(
+            jnp.bfloat16
+        )
+    product[...] = jnp.dot(lhs[...], w_down[...], preferred_element_type=jnp.float32)
+    half = count // 2
+    upper = lax.axis_index("tp") // 2
+    near = pl.ds(pl.multiple_of(upper * half, half), half)
+    far = pl.ds(pl.multiple_of((1 - upper) * half, half), half)
+    return product[near, :], product[far, :]
+
+
+def own_down_kernel(slot_dev, hidden, w_down, near, far, lhs, product):
+    results = down_rows(slot_dev, hidden, w_down, lhs, product)
+    for out, rows in zip((near, far), results):
+        out[...] = rows.astype(out.dtype)
+
+
+def other_down_kernel(slot_dev, hidden, w_down, own_near, home, second, third, lhs, product):
+    near, far = down_rows(slot_dev, hidden, w_down, lhs, product)
+    own = own_near[...].astype(jnp.float32)
+    first_core = lax.rem(lax.axis_index("tp"), 2) == 0
+    home[...] = jnp.where(first_core, own, near).astype(home.dtype)
+    second[...] = jnp.where(first_core, far, own).astype(second.dtype)
+    third[...] = jnp.where(first_core, near, far).astype(third.dtype)
+
+
+def back_permute(block, order):
+    reqs, tps = lax.axis_size("req"), lax.axis_size("tp")
+    pairs = [
+        (req * tps + tp, (req ^ (2 * BACK[tp % 2][order])) * tps + tp)
+        for req in range(reqs)
+        for tp in range(tps)
+    ]
+    return lax.ppermute(block, ("req", "tp"), pairs)
+
+
+def back_turn_kernel(home, part1, part2, part3, along):
+    half = home.shape[0] // 2
+    for index, part in enumerate((home, part1, part2, part3)):
+        along[index * half : (index + 1) * half, :] = part[half:, :]
+
+
+def combine_kernel(
+    home, part1, part2, part3, along, pick0, pick1, first_weight, attended, layer_out, returned
+):
+    half = home.shape[0] // 2
+    core = lax.rem(lax.axis_index("tp"), 2)
+    for index, part in enumerate((home, part1, part2, part3)):
+        distance = jnp.where(core == 0, BACK[0][index], BACK[1][index])
+        start = pl.multiple_of(distance * 2 * half, 2 * half)
+        returned[pl.ds(start, half), :] = part[:half, :]
+        returned[pl.ds(start + half, half), :] = along[index * half : (index + 1) * half, :]
     rows = returned[...]
     out0 = jnp.dot(pick0[...], rows, preferred_element_type=jnp.float32)
     out1 = jnp.dot(pick1[...], rows, preferred_element_type=jnp.float32)
@@ -623,21 +660,33 @@
         [spec()] * 4,
         (*late, *early),
     )
-    (computed,) = call(
-        functools.partial(down_kernel, slot_dev),
-        [((8, packed_count // 8, width), bf16)],
-        [spec()] * 3,
-        (own, partner_permute(own, "tp", 1), w_down.reshape(slot_dev * hidden, width)),
-        scratch=[pltpu.VMEM((packed_count, slot_dev * hidden), bf16)],
-        flops=200_000_000,
-        moved=2_000_000,
-    )
-    returned = lax.all_to_all(computed, "req", split_axis=0, concat_axis=0, tiled=True)
+    w_down = w_down.reshape(slot_dev * hidden, width)
+    block = ((quarter, width), bf16)
+    down_scratch = [
+        pltpu.VMEM((2 * quarter, slot_dev * hidden), bf16),
+        pltpu.VMEM((2 * quarter, width), f32),
+    ]
+    near, far = call(
+        functools.partial(own_down_kernel, slot_dev), [block] * 2, [spec()] * 2, (own, w_down),
+        scratch=down_scratch, flops=100_000_000, moved=2_000_000,
+    )
+    home, second, third = call(
+        functools.partial(other_down_kernel, slot_dev), [block] * 3, [spec()] * 3,
+        (partner_permute(own, "tp", 1), w_down, near),
+        scratch=down_scratch, flops=100_000_000, moved=2_000_000,
+    )
+    parts = [back_permute(rows, order) for order, rows in enumerate((far, second, third), 1)]
+    (along,) = call(
+        back_turn_kernel, [((2 * quarter, width), bf16)], [spec()] * 4, (home, *parts)
+    )
     (layer_out,) = call(
         combine_kernel,
         [((row_count, width), bf16)],
-        [spec()] * 5,
-        (returned.reshape(packed_count, width), pick0, pick1, first_weight, attended),
+        [spec()] * 9,
+        (
+            home, *parts, partner_permute(along, "req", 1), pick0, pick1, first_weight, attended,
+        ),
+        scratch=[pltpu.VMEM((packed_count, width), bf16)],
     )
     return (result, layer_out)
 

time: 46.8 us -> 45.8 us (0.979)
  blocking collectives: 11.1 us -> 0 us
  starting transfers between devices: 11.2 us -> 16.4 us
  waiting for transfers between devices: 14.4 us -> 19.1 us
    all_to_all x1 -> x0, blocking collectives: 11.1 us -> none  [shards(): lax.all_to_all(computed, 'req', split_axis=0, concat_axis=0, tiled=True)]
    ppermute x0 -> x3, starting transfers between devices: none -> 3.62 us  [back_permute(): return lax.ppermute(block, ('req', 'tp'), pairs)]
    ppermute x0 -> x3, waiting for transfers between devices: none -> 3.42 us  [back_permute(): return lax.ppermute(block, ('req', 'tp'), pairs)]
    ppermute x12 -> x13, starting transfers between devices: 11.2 us -> 12.7 us  [partner_permute(): return lax.ppermute(block, axis, [(i, i ^ distance) for i in range(count)])]
    ppermute x12 -> x13, waiting for transfers between devices: 14.4 us -> 15.7 us  [partner_permute(): return lax.ppermute(block, axis, [(i, i ^ distance) for i in range(count)])]
    pallas_call x13 -> x15, Pallas kernels: 9.1 us -> 9.44 us  [call(): pl.pallas_call(kernel, out_shape=[jax.ShapeDtypeStruct(shape, dtype) for...]
  transfers between devices with their start and end apart: 12 -> 16, of which waited for: 8 -> 10; matrix products, arithmetic and copies ran while one was open for 0% -> 0% of each run, Pallas kernels for 10% -> 11%
where the time goes in v12:
time: 45.8 us; the launch traced here: 45.7 us
  waiting for transfers between devices  19.1 us (42%)
  starting transfers between devices  16.4 us (36%)
  Pallas kernels  9.44 us (21%)
  between operations  0.79 us (2%)
    ppermute x13, waiting for transfers between devices, partner_permute(): return lax.ppermute(block, axis, [(i, i ^ distance) for i in range(count)])  15.7 us
    ppermute x13, starting transfers between devices, partner_permute(): return lax.ppermute(block, axis, [(i, i ^ distance) for i in range(count)])  12.7 us
    pallas_call x15, Pallas kernels, call(): pl.pallas_call(kernel, out_shape=[jax.ShapeDtypeStruct(shape, dtype) for...  9.44 us
    ppermute x3, starting transfers between devices, back_permute(): return lax.ppermute(block, ('req', 'tp'), pairs)  3.62 us
    ppermute x3, waiting for transfers between devices, back_permute(): return lax.ppermute(block, ('req', 'tp'), pairs)  3.42 us
  transfers between devices with their start and end apart: 16, of which 10 were waited for; matrix products, arithmetic and copies ran while one was open for 0% of the time, Pallas kernels for 11%

profile of v12, /device:TPU:0, one launch (start us, length us, event | category | flops | bytes accessed | tf_op | source)
XLA Modules:
  0.0 45.7 jit_solution(13071860951006539675)
XLA Ops:
  0.7 3.0 %shard_map.149 = (f32[32,384]{1,0:T(8,128)S(1)}, bf16[32,384]{1,0:T(8,128)(2,1)S(1)}, bf16[32,384]{1,0:T(8,128)(2,1)S(1)}, bf16[32,384]{1,0:T(8,128)(2,1)S(1)}) custom-call(s32[32]{0:T(128)} %lengths_hbm.1, bf16[32,384]{1,0:T(8,128)(2,1)} %queries_hbm.1, bf16[32,128]{1,0:T(8,128)(2,1)} %keys_hbm.1, bf16[32,128]{1,0:T(8,128)(2,1)} %values_hbm.1, ...), custom_call_target="tpu_custom_call" | custom-call | flops 200000000 | bytes 3400000 | tf_op jit(solution)/shard_map/pallas_call | solution.py:137
  3.7 3.0 %collective-permute-start = (bf16[32,384]{1,0:T(8,128)(2,1)S(1)}, bf16[32,384]{1,0:T(8,128)(2,1)S(1)}, u32[]{:S(2)}, u32[]{:S(2)}) collective-permute-start(bf16[32,384]{1,0:T(8,128)(2,1)S(1)} %get-tuple-element.37), channel_id=1, source_target_pairs={{0,2},{1,3},{2,0},{3,1},{4,6},{5,7},{6,4},{7,5},{8,10},{9,11},{10,... | collective-permute-start | bytes 73736 | tf_op jit(solution)/shard_map/ppermute | solution.py:150
  6.7 0.2 collective-permute-start.2
  6.9 2.0 %shard_map.150 = (f32[32,384]{1,0:T(8,128)S(1)}, bf16[128,32]{1,0:T(8,128)(2,1)S(1)}, bf16[32,128]{1,0:T(8,128)(2,1)S(1)}, bf16[32,128]{1,0:T(8,128)(2,1)S(1)}, ...) custom-call(f32[32,384]{1,0:T(8,128)S(1)} %get-tuple-element.35.own, ...), custom_call_target="tpu_custom_call" | custom-call | flops 100000 | bytes 3300000 | tf_op jit(solution)/shard_map/pallas_call | solution.py:137
  8.9 1.0 %collective-permute-done.1.part2 = bf16[32,384]{1,0:T(8,128)(2,1)S(1)} collective-permute-done((bf16[32,384]{1,0:T(8,128)(2,1)S(1)}, bf16[32,384]{1,0:T(8,128)(2,1)S(1)}, u32[]{:S(2)}, u32[]{:S(2)}) %collective-permute-start.1) | collective-permute-done | bytes 24608 | tf_op jit(solution)/shard_map/ppermute | solution.py:150
  10.1 2.6 %collective-permute-start.3 = (bf16[32,384]{1,0:T(8,128)(2,1)S(1)}, bf16[32,384]{1,0:T(8,128)(2,1)S(1)}, u32[]{:S(2)}, u32[]{:S(2)}) collective-permute-start(bf16[32,384]{1,0:T(8,128)(2,1)S(1)} %get-tuple-element.45), channel_id=1, source_target_pairs={{0,16},{4,20},{8,24},{12,28},{16,0},{20,4},{24,8},{28,12},{1,17},{... | collective-permute-start | bytes 73736 | tf_op jit(solution)/shard_map/ppermute | solution.py:150
  12.8 1.3 %collective-permute-start.4 = (bf16[32,384]{1,0:T(8,128)(2,1)S(1)}, bf16[32,384]{1,0:T(8,128)(2,1)S(1)}, u32[]{:S(2)}, u32[]{:S(2)}) collective-permute-start(bf16[32,384]{1,0:T(8,128)(2,1)S(1)} %get-tuple-element.46), channel_id=1, source_target_pairs={{0,24},{4,28},{8,16},{12,20},{16,8},{20,12},{24,0},{28,4},{1,25},{... | collective-permute-start | bytes 73736 | tf_op jit(solution)/shard_map/ppermute | solution.py:150
  14.1 0.2 collective-permute-start.5
  14.3 0.6 %collective-permute-done.3.part1.in1 = bf16[32,384]{1,0:T(8,128)(2,1)S(1)} collective-permute-done((bf16[32,384]{1,0:T(8,128)(2,1)S(1)}, bf16[32,384]{1,0:T(8,128)(2,1)S(1)}, u32[]{:S(2)}, u32[]{:S(2)}) %collective-permute-start.3) | collective-permute-done | bytes 24608 | tf_op jit(solution)/shard_map/ppermute | solution.py:150
  14.9 3.5 %collective-permute-done.4.part2.in2 = bf16[32,384]{1,0:T(8,128)(2,1)S(1)} collective-permute-done((bf16[32,384]{1,0:T(8,128)(2,1)S(1)}, bf16[32,384]{1,0:T(8,128)(2,1)S(1)}, u32[]{:S(2)}, u32[]{:S(2)}) %collective-permute-start.4) | collective-permute-done | bytes 24608 | tf_op jit(solution)/shard_map/ppermute | solution.py:150
  18.4 1.6 %collective-permute-start.6 = (bf16[64,384]{1,0:T(8,128)(2,1)S(1)}, bf16[64,384]{1,0:T(8,128)(2,1)S(1)}, u32[]{:S(2)}, u32[]{:S(2)}) collective-permute-start(bf16[64,384]{1,0:T(8,128)(2,1)S(1)} %shard_map.154.turned), channel_id=1, source_target_pairs={{0,4},{4,0},{8,12},{12,8},{16,20},{20,16},{24,28},{28,24},{1,5},{5... | collective-permute-start | bytes 147464 | tf_op jit(solution)/shard_map/ppermute | solution.py:150
  20.0 0.6 %shard_map.153 = bf16[32,384]{1,0:T(8,128)(2,1)} custom-call(bf16[32,384]{1,0:T(8,128)(2,1)S(1)} %get-tuple-element.41.attended), custom_call_target="tpu_custom_call" | custom-call | flops 100000 | bytes 100000 | tf_op jit(solution)/shard_map/pallas_call | solution.py:137
  20.7 0.7 %shard_map.157 = (f32[32,2176]{1,0:T(8,128)S(1)}, bf16[32,2176]{1,0:T(8,128)(2,1)S(1)}) custom-call(bf16[32,384]{1,0:T(8,128)(2,1)S(1)} %get-tuple-element.44.home.in0, bf16[32,384]{1,0:T(8,128)(2,1)S(1)} %collective-permute-done.3.part1.in1, bf16[32,384]{1,0:T(8,128)(2,1)S(1)} %collective-permute-done.4.part2.in2, ...), custom_call_target="tpu_custom_call" | custom-call | flops 400000000 | bytes 3500000 | tf_op jit(solution)/shard_map/pallas_call | solution.py:137
  21.5 1.1 %collective-permute-done.6.blocks = bf16[64,384]{1,0:T(8,128)(2,1)S(1)} collective-permute-done((bf16[64,384]{1,0:T(8,128)(2,1)S(1)}, bf16[64,384]{1,0:T(8,128)(2,1)S(1)}, u32[]{:S(2)}, u32[]{:S(2)}) %collective-permute-start.6) | collective-permute-done | bytes 49184 | tf_op jit(solution)/shard_map/ppermute | solution.py:150
  22.6 0.7 %shard_map.155 = (f32[32,2176]{1,0:T(8,128)S(1)}, bf16[32,2176]{1,0:T(8,128)(2,1)S(1)}) custom-call(bf16[64,384]{1,0:T(8,128)(2,1)S(1)} %collective-permute-done.6.blocks, f32[1,384]{1,0:T(1,128)S(1)} %reshape.18.gain, bf16[768,1024]{1,0:T(8,128)(2,1)S(1)} %get-tuple-element.48.w_gate, bf16[768,1024]{1,0:T(8,128)(2,1)S(1)} %get-tuple-element.49.w_up), custom_call_target="tpu_custom_call" | custom-call | flops 400000000 | bytes 3500000 | tf_op jit(solution)/shard_map/pallas_call | solution.py:137
  23.3 0.2 shard_map.158
  23.5 1.0 %collective-permute-start.10 = (bf16[32,2176]{1,0:T(8,128)(2,1)S(1)}, bf16[32,2176]{1,0:T(8,128)(2,1)S(1)}, u32[]{:S(2)}, u32[]{:S(2)}) collective-permute-start(bf16[32,2176]{1,0:T(8,128)(2,1)S(1)} %get-tuple-element.58), channel_id=1, source_target_pairs={{0,2},{1,3},{2,0},{3,1},{4,6},{5,7},{6,4},{7,5},{8,10},{9,11},{10,... | collective-permute-start | bytes 417800 | tf_op jit(solution)/shard_map/ppermute | solution.py:150
  24.5 0.2 collective-permute-done.7.part
  24.8 1.0 %collective-permute-start.8 = (bf16[32,2176]{1,0:T(8,128)(2,1)S(1)}, bf16[32,2176]{1,0:T(8,128)(2,1)S(1)}, u32[]{:S(2)}, u32[]{:S(2)}) collective-permute-start(bf16[32,2176]{1,0:T(8,128)(2,1)S(1)} %get-tuple-element.53), channel_id=1, source_target_pairs={{0,2},{1,3},{2,0},{3,1},{4,6},{5,7},{6,4},{7,5},{8,10},{9,11},{10,... | collective-permute-start | bytes 417800 | tf_op jit(solution)/shard_map/ppermute | solution.py:150
  25.8 4.2 %collective-permute-done.10.refs_3_ = bf16[32,2176]{1,0:T(8,128)(2,1)S(1)} collective-permute-done((bf16[32,2176]{1,0:T(8,128)(2,1)S(1)}, bf16[32,2176]{1,0:T(8,128)(2,1)S(1)}, u32[]{:S(2)}, u32[]{:S(2)}) %collective-permute-start.10) | collective-permute-done | bytes 139296 | tf_op jit(solution)/shard_map/ppermute | solution.py:150
  30.0 2.6 %collective-permute-done.8.refs_1_ = bf16[32,2176]{1,0:T(8,128)(2,1)S(1)} collective-permute-done((bf16[32,2176]{1,0:T(8,128)(2,1)S(1)}, bf16[32,2176]{1,0:T(8,128)(2,1)S(1)}, u32[]{:S(2)}, u32[]{:S(2)}) %collective-permute-start.8) | collective-permute-done | bytes 139296 | tf_op jit(solution)/shard_map/ppermute | solution.py:150
  32.6 0.3 shard_map.159
  32.9 0.4 shard_map.160
  33.3 1.2 %collective-permute-start.12 = (bf16[32,384]{1,0:T(8,128)(2,1)S(1)}, bf16[32,384]{1,0:T(8,128)(2,1)S(1)}, u32[]{:S(2)}, u32[]{:S(2)}) collective-permute-start(bf16[32,384]{1,0:T(8,128)(2,1)S(1)} %get-tuple-element.62), channel_id=1, source_target_pairs={{0,16},{1,25},{2,18},{3,27},{4,20},{5,29},{6,22},{7,31},{8,24},{9,... | collective-permute-start | bytes 73736 | tf_op jit(solution)/shard_map/ppermute | solution.py:488
  34.5 0.4 shard_map.161
  34.9 1.7 %collective-permute-start.13 = (bf16[32,384]{1,0:T(8,128)(2,1)S(1)}, bf16[32,384]{1,0:T(8,128)(2,1)S(1)}, u32[]{:S(2)}, u32[]{:S(2)}) collective-permute-start(bf16[32,384]{1,0:T(8,128)(2,1)S(1)} %get-tuple-element.63), channel_id=1, source_target_pairs={{0,24},{1,9},{2,26},{3,11},{4,28},{5,13},{6,30},{7,15},{8,16},{9,1... | collective-permute-start | bytes 73736 | tf_op jit(solution)/shard_map/ppermute | solution.py:488
  36.6 0.7 %collective-permute-start.14 = (bf16[32,384]{1,0:T(8,128)(2,1)S(1)}, bf16[32,384]{1,0:T(8,128)(2,1)S(1)}, u32[]{:S(2)}, u32[]{:S(2)}) collective-permute-start(bf16[32,384]{1,0:T(8,128)(2,1)S(1)} %get-tuple-element.64), channel_id=1, source_target_pairs={{0,8},{1,17},{2,10},{3,19},{4,12},{5,21},{6,14},{7,23},{8,0},{9,25... | collective-permute-start | bytes 73736 | tf_op jit(solution)/shard_map/ppermute | solution.py:488
  37.3 0.8 %collective-permute-done.12.part1 = bf16[32,384]{1,0:T(8,128)(2,1)S(1)} collective-permute-done((bf16[32,384]{1,0:T(8,128)(2,1)S(1)}, bf16[32,384]{1,0:T(8,128)(2,1)S(1)}, u32[]{:S(2)}, u32[]{:S(2)}) %collective-permute-start.12) | collective-permute-done | bytes 24608 | tf_op jit(solution)/shard_map/ppermute | solution.py:488
  38.1 2.6 %collective-permute-done.13.part2 = bf16[32,384]{1,0:T(8,128)(2,1)S(1)} collective-permute-done((bf16[32,384]{1,0:T(8,128)(2,1)S(1)}, bf16[32,384]{1,0:T(8,128)(2,1)S(1)}, u32[]{:S(2)}, u32[]{:S(2)}) %collective-permute-start.13) | collective-permute-done | bytes 24608 | tf_op jit(solution)/shard_map/ppermute | solution.py:488
  40.8 1.6 %collective-permute-start.15 = (bf16[64,384]{1,0:T(8,128)(2,1)S(1)}, bf16[64,384]{1,0:T(8,128)(2,1)S(1)}, u32[]{:S(2)}, u32[]{:S(2)}) collective-permute-start(bf16[64,384]{1,0:T(8,128)(2,1)S(1)} %shard_map.162), channel_id=1, source_target_pairs={{0,4},{4,0},{8,12},{12,8},{16,20},{20,16},{24,28},{28,24},{1,5},{5... | collective-permute-start | bytes 147464 | tf_op jit(solution)/shard_map/ppermute | solution.py:150
  42.3 2.6 %collective-permute-done.15.along = bf16[64,384]{1,0:T(8,128)(2,1)S(1)} collective-permute-done((bf16[64,384]{1,0:T(8,128)(2,1)S(1)}, bf16[64,384]{1,0:T(8,128)(2,1)S(1)}, u32[]{:S(2)}, u32[]{:S(2)}) %collective-permute-start.15) | collective-permute-done | bytes 49184 | tf_op jit(solution)/shard_map/ppermute | solution.py:150
  44.9 0.8 %shard_map.163 = bf16[32,384]{1,0:T(8,128)(2,1)} custom-call(bf16[32,384]{1,0:T(8,128)(2,1)S(1)} %get-tuple-element.61.home, bf16[32,384]{1,0:T(8,128)(2,1)S(1)} %collective-permute-done.12.part1, bf16[32,384]{1,0:T(8,128)(2,1)S(1)} %collective-permute-done.13.part2, bf16[32,384]{1,0:T(8,128)(2,1)S(1)} %collective-permute-done.14.part3, ...), custom_call_target="tpu_custom_call" | custom-call | flops 100000 | bytes 100000 | tf_op jit(solution)/shard_map/pallas_call | solution.py:137
  (26 shorter events, 0.7 us)
Async XLA Ops:
  0.6 6.3 %copy-start.3 = (s32[32,2]{0,1:T(2,128)S(1)}, s32[32,2]{0,1:T(2,128)}, u32[]{:S(2)}) copy-start(s32[32,2]{0,1:T(2,128)} %param.24) | copy-start | bytes 772
  0.6 6.3 %copy-start.2 = (f32[384,16]{0,1:T(8,128)S(1)}, f32[384,16]{0,1:T(8,128)}, u32[]{:S(2)}) copy-start(f32[384,16]{0,1:T(8,128)} %param.23) | copy-start | bytes 73732
  0.7 6.2 %copy-start.1 = (bf16[32,384]{1,0:T(8,128)(2,1)S(1)}, bf16[32,384]{1,0:T(8,128)(2,1)}, u32[]{:S(2)}) copy-start(bf16[32,384]{1,0:T(8,128)(2,1)} %resid.1) | copy-start | bytes 73732
  3.7 5.3 %collective-permute-start = (bf16[32,384]{1,0:T(8,128)(2,1)S(1)}, bf16[32,384]{1,0:T(8,128)(2,1)S(1)}, u32[]{:S(2)}, u32[]{:S(2)}) collective-permute-start(bf16[32,384]{1,0:T(8,128)(2,1)S(1)} %get-tuple-element.37), channel_id=1, source_target_pairs={{0,2},{1,3},{2,0},{3,1},{4,6},{5,7},{6,4},{7,5},{8,10},{9,11},{10,... | collective-permute-start | bytes 73736 | tf_op jit(solution)/shard_map/ppermute | solution.py:150
  6.7 3.3 %collective-permute-start.1 = (bf16[32,384]{1,0:T(8,128)(2,1)S(1)}, bf16[32,384]{1,0:T(8,128)(2,1)S(1)}, u32[]{:S(2)}, u32[]{:S(2)}) collective-permute-start(bf16[32,384]{1,0:T(8,128)(2,1)S(1)} %get-tuple-element.38), channel_id=1, source_target_pairs={{0,3},{1,2},{2,1},{3,0},{4,7},{5,6},{6,5},{7,4},{8,11},{9,10},{10,... | collective-permute-start | bytes 73736 | tf_op jit(solution)/shard_map/ppermute | solution.py:150
  6.7 3.3 %collective-permute-start.2 = (bf16[32,384]{1,0:T(8,128)(2,1)S(1)}, bf16[32,384]{1,0:T(8,128)(2,1)S(1)}, u32[]{:S(2)}, u32[]{:S(2)}) collective-permute-start(bf16[32,384]{1,0:T(8,128)(2,1)S(1)} %get-tuple-element.39), channel_id=1, source_target_pairs={{0,1},{1,0},{2,3},{3,2},{4,5},{5,4},{6,7},{7,6},{8,9},{9,8},{10,11... | collective-permute-start | bytes 73736 | tf_op jit(solution)/shard_map/ppermute | solution.py:150
  6.9 13.1 %copy-start.4 = (f32[384]{0:T(512)S(1)}, f32[384]{0:T(512)}, u32[]{:S(2)}) copy-start(f32[384]{0:T(512)} %param.22) | copy-start | bytes 4612
  10.1 4.8 %collective-permute-start.3 = (bf16[32,384]{1,0:T(8,128)(2,1)S(1)}, bf16[32,384]{1,0:T(8,128)(2,1)S(1)}, u32[]{:S(2)}, u32[]{:S(2)}) collective-permute-start(bf16[32,384]{1,0:T(8,128)(2,1)S(1)} %get-tuple-element.45), channel_id=1, source_target_pairs={{0,16},{4,20},{8,24},{12,28},{16,0},{20,4},{24,8},{28,12},{1,17},{... | collective-permute-start | bytes 73736 | tf_op jit(solution)/shard_map/ppermute | solution.py:150
  12.8 5.6 %collective-permute-start.4 = (bf16[32,384]{1,0:T(8,128)(2,1)S(1)}, bf16[32,384]{1,0:T(8,128)(2,1)S(1)}, u32[]{:S(2)}, u32[]{:S(2)}) collective-permute-start(bf16[32,384]{1,0:T(8,128)(2,1)S(1)} %get-tuple-element.46), channel_id=1, source_target_pairs={{0,24},{4,28},{8,16},{12,20},{16,8},{20,12},{24,0},{28,4},{1,25},{... | collective-permute-start | bytes 73736 | tf_op jit(solution)/shard_map/ppermute | solution.py:150
  14.1 4.3 %collective-permute-start.5 = (bf16[32,384]{1,0:T(8,128)(2,1)S(1)}, bf16[32,384]{1,0:T(8,128)(2,1)S(1)}, u32[]{:S(2)}, u32[]{:S(2)}) collective-permute-start(bf16[32,384]{1,0:T(8,128)(2,1)S(1)} %get-tuple-element.47), channel_id=1, source_target_pairs={{0,8},{4,12},{8,0},{12,4},{16,24},{20,28},{24,16},{28,20},{1,9},{5... | collective-permute-start | bytes 73736 | tf_op jit(solution)/shard_map/ppermute | solution.py:150
  18.4 4.2 %collective-permute-start.6 = (bf16[64,384]{1,0:T(8,128)(2,1)S(1)}, bf16[64,384]{1,0:T(8,128)(2,1)S(1)}, u32[]{:S(2)}, u32[]{:S(2)}) collective-permute-start(bf16[64,384]{1,0:T(8,128)(2,1)S(1)} %shard_map.154.turned), channel_id=1, source_target_pairs={{0,4},{4,0},{8,12},{12,8},{16,20},{20,16},{24,28},{28,24},{1,5},{5... | collective-permute-start | bytes 147464 | tf_op jit(solution)/shard_map/ppermute | solution.py:150
  21.4 1.9 %collective-permute-start.9 = (bf16[32,2176]{1,0:T(8,128)(2,1)S(1)}, bf16[32,2176]{1,0:T(8,128)(2,1)S(1)}, u32[]{:S(2)}, u32[]{:S(2)}) collective-permute-start(bf16[32,2176]{1,0:T(8,128)(2,1)S(1)} %get-tuple-element.56), channel_id=1, source_target_pairs={{0,1},{1,0},{2,3},{3,2},{4,5},{5,4},{6,7},{7,6},{8,9},{9,8},{10,11... | collective-permute-start | bytes 417800 | tf_op jit(solution)/shard_map/ppermute | solution.py:150
  23.2 9.7 %copy-start = (bf16[2,1024,384]{2,1,0:T(8,128)(2,1)S(1)}, bf16[2,1024,384]{2,1,0:T(8,128)(2,1)}, u32[]{:S(2)}) copy-start(bf16[2,1024,384]{2,1,0:T(8,128)(2,1)} %param.27) | copy-start | bytes 4718596
  23.2 1.4 %collective-permute-start.7 = (bf16[32,2176]{1,0:T(8,128)(2,1)S(1)}, bf16[32,2176]{1,0:T(8,128)(2,1)S(1)}, u32[]{:S(2)}, u32[]{:S(2)}) collective-permute-start(bf16[32,2176]{1,0:T(8,128)(2,1)S(1)} %get-tuple-element.51), channel_id=1, source_target_pairs={{0,1},{1,0},{2,3},{3,2},{4,5},{5,4},{6,7},{7,6},{8,9},{9,8},{10,11... | collective-permute-start | bytes 417800 | tf_op jit(solution)/shard_map/ppermute | solution.py:150
  23.5 6.5 %collective-permute-start.10 = (bf16[32,2176]{1,0:T(8,128)(2,1)S(1)}, bf16[32,2176]{1,0:T(8,128)(2,1)S(1)}, u32[]{:S(2)}, u32[]{:S(2)}) collective-permute-start(bf16[32,2176]{1,0:T(8,128)(2,1)S(1)} %get-tuple-element.58), channel_id=1, source_target_pairs={{0,2},{1,3},{2,0},{3,1},{4,6},{5,7},{6,4},{7,5},{8,10},{9,11},{10,... | collective-permute-start | bytes 417800 | tf_op jit(solution)/shard_map/ppermute | solution.py:150
  24.8 7.7 %collective-permute-start.8 = (bf16[32,2176]{1,0:T(8,128)(2,1)S(1)}, bf16[32,2176]{1,0:T(8,128)(2,1)S(1)}, u32[]{:S(2)}, u32[]{:S(2)}) collective-permute-start(bf16[32,2176]{1,0:T(8,128)(2,1)S(1)} %get-tuple-element.53), channel_id=1, source_target_pairs={{0,2},{1,3},{2,0},{3,1},{4,6},{5,7},{6,4},{7,5},{8,10},{9,11},{10,... | collective-permute-start | bytes 417800 | tf_op jit(solution)/shard_map/ppermute | solution.py:150
  32.8 1.7 %collective-permute-start.11 = (bf16[64,1024]{1,0:T(8,128)(2,1)S(1)}, bf16[64,1024]{1,0:T(8,128)(2,1)S(1)}, u32[]{:S(2)}, u32[]{:S(2)}) collective-permute-start(bf16[64,1024]{1,0:T(8,128)(2,1)S(1)} %get-tuple-element.59.hidden), channel_id=1, source_target_pairs={{0,1},{1,0},{2,3},{3,2},{4,5},{5,4},{6,7},{7,6},{8,9},{9,8},{10,11... | collective-permute-start | bytes 393224 | tf_op jit(solution)/shard_map/ppermute | solution.py:150
  33.3 4.8 %collective-permute-start.12 = (bf16[32,384]{1,0:T(8,128)(2,1)S(1)}, bf16[32,384]{1,0:T(8,128)(2,1)S(1)}, u32[]{:S(2)}, u32[]{:S(2)}) collective-permute-start(bf16[32,384]{1,0:T(8,128)(2,1)S(1)} %get-tuple-element.62), channel_id=1, source_target_pairs={{0,16},{1,25},{2,18},{3,27},{4,20},{5,29},{6,22},{7,31},{8,24},{9,... | collective-permute-start | bytes 73736 | tf_op jit(solution)/shard_map/ppermute | solution.py:488
  34.9 5.8 %collective-permute-start.13 = (bf16[32,384]{1,0:T(8,128)(2,1)S(1)}, bf16[32,384]{1,0:T(8,128)(2,1)S(1)}, u32[]{:S(2)}, u32[]{:S(2)}) collective-permute-start(bf16[32,384]{1,0:T(8,128)(2,1)S(1)} %get-tuple-element.63), channel_id=1, source_target_pairs={{0,24},{1,9},{2,26},{3,11},{4,28},{5,13},{6,30},{7,15},{8,16},{9,1... | collective-permute-start | bytes 73736 | tf_op jit(solution)/shard_map/ppermute | solution.py:488
  36.6 4.1 %collective-permute-start.14 = (bf16[32,384]{1,0:T(8,128)(2,1)S(1)}, bf16[32,384]{1,0:T(8,128)(2,1)S(1)}, u32[]{:S(2)}, u32[]{:S(2)}) collective-permute-start(bf16[32,384]{1,0:T(8,128)(2,1)S(1)} %get-tuple-element.64), channel_id=1, source_target_pairs={{0,8},{1,17},{2,10},{3,19},{4,12},{5,21},{6,14},{7,23},{8,0},{9,25... | collective-permute-start | bytes 73736 | tf_op jit(solution)/shard_map/ppermute | solution.py:488
  40.8 4.2 %collective-permute-start.15 = (bf16[64,384]{1,0:T(8,128)(2,1)S(1)}, bf16[64,384]{1,0:T(8,128)(2,1)S(1)}, u32[]{:S(2)}, u32[]{:S(2)}) collective-permute-start(bf16[64,384]{1,0:T(8,128)(2,1)S(1)} %shard_map.162), channel_id=1, source_target_pairs={{0,4},{4,0},{8,12},{12,8},{16,20},{20,16},{24,28},{28,24},{1,5},{5... | collective-permute-start | bytes 147464 | tf_op jit(solution)/shard_map/ppermute | solution.py:150

commit v13 on v12

--- a/solution.py
+++ b/solution.py
@@ -159,7 +159,7 @@
     width = own.shape[1]
     lanes = 2 * HEAD_DIM
     cache_len = k_hbm.shape[1]
-    chunks = 2
+    chunks = 1
     small = [
         pltpu.make_async_copy(source, target, small_sems.at[index])
         for index, (source, target) in enumerate(
@@ -225,6 +225,8 @@
             -1e30,
         )
 
+    for copy in copies[chunks:]:
+        copy.wait()
     scores = score_s[...]
     peak = jnp.maximum(jnp.max(scores, axis=1, keepdims=True), own_score)
     terms = jnp.exp(scores - peak)
@@ -233,8 +235,6 @@
     weight_s[...] = (terms * inverse).astype(jnp.bfloat16)
     own_weight = (own_term * inverse).astype(jnp.bfloat16).astype(jnp.float32)
     self_s[...] = own_weight * values_new
-    for copy in copies[chunks : 2 * chunks]:
-        copy.wait()
     for pair in range(row_count // 2):
         pair_rows = slice(16 * pair, 16 * pair + 16)
         values = jnp.concatenate([v_buf[2 * pair], v_buf[2 * pair + 1]], axis=1)
@@ -252,8 +252,6 @@
         ],
         axis=1,
     ).astype(jnp.bfloat16)
-    for copy in copies[2 * chunks :]:
-        copy.wait()
     place_tp = lax.axis_index("tp")
     product_s[...] = jnp.dot(attention, w_buf[...], preferred_element_type=jnp.float32)
     for shift, out in zip(FAR_FIRST, (own, sent1, sent2, sent3)):
@@ -569,7 +567,7 @@
             pltpu.VMEM((8 * row_count, cache_len), bf16),
             pltpu.VMEM((row_count, w_out.shape[1]), f32),
             pltpu.SemaphoreType.DMA((4,)),
-            pltpu.SemaphoreType.DMA((6,)),
+            pltpu.SemaphoreType.DMA((3,)),
         ],
         mebibytes=16,
         flops=200_000_000,

time: 45.8 us -> 45.7 us (level)
  no operation moved by 1% of the time
where the time goes in v13:
time: 45.7 us; the launch traced here: 45.6 us
  waiting for transfers between devices  19.1 us (42%)
  starting transfers between devices  16.4 us (36%)
  Pallas kernels  9.31 us (20%)
  between operations  0.79 us (2%)
    ppermute x13, waiting for transfers between devices, partner_permute(): return lax.ppermute(block, axis, [(i, i ^ distance) for i in range(count)])  15.7 us
    ppermute x13, starting transfers between devices, partner_permute(): return lax.ppermute(block, axis, [(i, i ^ distance) for i in range(count)])  12.7 us
    pallas_call x15, Pallas kernels, call(): pl.pallas_call(kernel, out_shape=[jax.ShapeDtypeStruct(shape, dtype) for...  9.31 us
    ppermute x3, starting transfers between devices, back_permute(): return lax.ppermute(block, ('req', 'tp'), pairs)  3.62 us
    ppermute x3, waiting for transfers between devices, back_permute(): return lax.ppermute(block, ('req', 'tp'), pairs)  3.42 us
  transfers between devices with their start and end apart: 16, of which 10 were waited for; matrix products, arithmetic and copies ran while one was open for 0% of the time, Pallas kernels for 11%

profile of v13, /device:TPU:0, one launch (start us, length us, event | category | flops | bytes accessed | tf_op | source)
XLA Modules:
  0.0 45.6 jit_solution(11128146133645886517)
XLA Ops:
  0.7 2.9 %shard_map.149 = (f32[32,384]{1,0:T(8,128)S(1)}, bf16[32,384]{1,0:T(8,128)(2,1)S(1)}, bf16[32,384]{1,0:T(8,128)(2,1)S(1)}, bf16[32,384]{1,0:T(8,128)(2,1)S(1)}) custom-call(s32[32]{0:T(128)} %lengths_hbm.1, bf16[32,384]{1,0:T(8,128)(2,1)} %queries_hbm.1, bf16[32,128]{1,0:T(8,128)(2,1)} %keys_hbm.1, bf16[32,128]{1,0:T(8,128)(2,1)} %values_hbm.1, ...), custom_call_target="tpu_custom_call" | custom-call | flops 200000000 | bytes 3400000 | tf_op jit(solution)/shard_map/pallas_call | solution.py:137
  3.6 3.0 %collective-permute-start = (bf16[32,384]{1,0:T(8,128)(2,1)S(1)}, bf16[32,384]{1,0:T(8,128)(2,1)S(1)}, u32[]{:S(2)}, u32[]{:S(2)}) collective-permute-start(bf16[32,384]{1,0:T(8,128)(2,1)S(1)} %get-tuple-element.37), channel_id=1, source_target_pairs={{0,2},{1,3},{2,0},{3,1},{4,6},{5,7},{6,4},{7,5},{8,10},{9,11},{10,... | collective-permute-start | bytes 73736 | tf_op jit(solution)/shard_map/ppermute | solution.py:150
  6.6 0.2 collective-permute-start.2
  6.8 2.0 %shard_map.150 = (f32[32,384]{1,0:T(8,128)S(1)}, bf16[128,32]{1,0:T(8,128)(2,1)S(1)}, bf16[32,128]{1,0:T(8,128)(2,1)S(1)}, bf16[32,128]{1,0:T(8,128)(2,1)S(1)}, ...) custom-call(f32[32,384]{1,0:T(8,128)S(1)} %get-tuple-element.35.own, ...), custom_call_target="tpu_custom_call" | custom-call | flops 100000 | bytes 3300000 | tf_op jit(solution)/shard_map/pallas_call | solution.py:137
  8.8 1.0 %collective-permute-done.1.part2 = bf16[32,384]{1,0:T(8,128)(2,1)S(1)} collective-permute-done((bf16[32,384]{1,0:T(8,128)(2,1)S(1)}, bf16[32,384]{1,0:T(8,128)(2,1)S(1)}, u32[]{:S(2)}, u32[]{:S(2)}) %collective-permute-start.1) | collective-permute-done | bytes 24608 | tf_op jit(solution)/shard_map/ppermute | solution.py:150
  10.0 2.6 %collective-permute-start.3 = (bf16[32,384]{1,0:T(8,128)(2,1)S(1)}, bf16[32,384]{1,0:T(8,128)(2,1)S(1)}, u32[]{:S(2)}, u32[]{:S(2)}) collective-permute-start(bf16[32,384]{1,0:T(8,128)(2,1)S(1)} %get-tuple-element.45), channel_id=1, source_target_pairs={{0,16},{4,20},{8,24},{12,28},{16,0},{20,4},{24,8},{28,12},{1,17},{... | collective-permute-start | bytes 73736 | tf_op jit(solution)/shard_map/ppermute | solution.py:150
  12.6 1.3 %collective-permute-start.4 = (bf16[32,384]{1,0:T(8,128)(2,1)S(1)}, bf16[32,384]{1,0:T(8,128)(2,1)S(1)}, u32[]{:S(2)}, u32[]{:S(2)}) collective-permute-start(bf16[32,384]{1,0:T(8,128)(2,1)S(1)} %get-tuple-element.46), channel_id=1, source_target_pairs={{0,24},{4,28},{8,16},{12,20},{16,8},{20,12},{24,0},{28,4},{1,25},{... | collective-permute-start | bytes 73736 | tf_op jit(solution)/shard_map/ppermute | solution.py:150
  14.0 0.2 collective-permute-start.5
  14.2 0.6 %collective-permute-done.3.part1.in1 = bf16[32,384]{1,0:T(8,128)(2,1)S(1)} collective-permute-done((bf16[32,384]{1,0:T(8,128)(2,1)S(1)}, bf16[32,384]{1,0:T(8,128)(2,1)S(1)}, u32[]{:S(2)}, u32[]{:S(2)}) %collective-permute-start.3) | collective-permute-done | bytes 24608 | tf_op jit(solution)/shard_map/ppermute | solution.py:150
  14.8 3.5 %collective-permute-done.4.part2.in2 = bf16[32,384]{1,0:T(8,128)(2,1)S(1)} collective-permute-done((bf16[32,384]{1,0:T(8,128)(2,1)S(1)}, bf16[32,384]{1,0:T(8,128)(2,1)S(1)}, u32[]{:S(2)}, u32[]{:S(2)}) %collective-permute-start.4) | collective-permute-done | bytes 24608 | tf_op jit(solution)/shard_map/ppermute | solution.py:150
  18.3 1.6 %collective-permute-start.6 = (bf16[64,384]{1,0:T(8,128)(2,1)S(1)}, bf16[64,384]{1,0:T(8,128)(2,1)S(1)}, u32[]{:S(2)}, u32[]{:S(2)}) collective-permute-start(bf16[64,384]{1,0:T(8,128)(2,1)S(1)} %shard_map.154.turned), channel_id=1, source_target_pairs={{0,4},{4,0},{8,12},{12,8},{16,20},{20,16},{24,28},{28,24},{1,5},{5... | collective-permute-start | bytes 147464 | tf_op jit(solution)/shard_map/ppermute | solution.py:150
  19.9 0.6 %shard_map.153 = bf16[32,384]{1,0:T(8,128)(2,1)} custom-call(bf16[32,384]{1,0:T(8,128)(2,1)S(1)} %get-tuple-element.41.attended), custom_call_target="tpu_custom_call" | custom-call | flops 100000 | bytes 100000 | tf_op jit(solution)/shard_map/pallas_call | solution.py:137
  20.6 0.7 %shard_map.157 = (f32[32,2176]{1,0:T(8,128)S(1)}, bf16[32,2176]{1,0:T(8,128)(2,1)S(1)}) custom-call(bf16[32,384]{1,0:T(8,128)(2,1)S(1)} %get-tuple-element.44.home.in0, bf16[32,384]{1,0:T(8,128)(2,1)S(1)} %collective-permute-done.3.part1.in1, bf16[32,384]{1,0:T(8,128)(2,1)S(1)} %collective-permute-done.4.part2.in2, ...), custom_call_target="tpu_custom_call" | custom-call | flops 400000000 | bytes 3500000 | tf_op jit(solution)/shard_map/pallas_call | solution.py:137
  21.3 1.1 %collective-permute-done.6.blocks = bf16[64,384]{1,0:T(8,128)(2,1)S(1)} collective-permute-done((bf16[64,384]{1,0:T(8,128)(2,1)S(1)}, bf16[64,384]{1,0:T(8,128)(2,1)S(1)}, u32[]{:S(2)}, u32[]{:S(2)}) %collective-permute-start.6) | collective-permute-done | bytes 49184 | tf_op jit(solution)/shard_map/ppermute | solution.py:150
  22.4 0.7 %shard_map.155 = (f32[32,2176]{1,0:T(8,128)S(1)}, bf16[32,2176]{1,0:T(8,128)(2,1)S(1)}) custom-call(bf16[64,384]{1,0:T(8,128)(2,1)S(1)} %collective-permute-done.6.blocks, f32[1,384]{1,0:T(1,128)S(1)} %reshape.18.gain, bf16[768,1024]{1,0:T(8,128)(2,1)S(1)} %get-tuple-element.48.w_gate, bf16[768,1024]{1,0:T(8,128)(2,1)S(1)} %get-tuple-element.49.w_up), custom_call_target="tpu_custom_call" | custom-call | flops 400000000 | bytes 3500000 | tf_op jit(solution)/shard_map/pallas_call | solution.py:137
  23.2 0.2 shard_map.158
  23.4 1.0 %collective-permute-start.10 = (bf16[32,2176]{1,0:T(8,128)(2,1)S(1)}, bf16[32,2176]{1,0:T(8,128)(2,1)S(1)}, u32[]{:S(2)}, u32[]{:S(2)}) collective-permute-start(bf16[32,2176]{1,0:T(8,128)(2,1)S(1)} %get-tuple-element.58), channel_id=1, source_target_pairs={{0,2},{1,3},{2,0},{3,1},{4,6},{5,7},{6,4},{7,5},{8,10},{9,11},{10,... | collective-permute-start | bytes 417800 | tf_op jit(solution)/shard_map/ppermute | solution.py:150
  24.3 0.2 collective-permute-done.7.part
  24.7 1.0 %collective-permute-start.8 = (bf16[32,2176]{1,0:T(8,128)(2,1)S(1)}, bf16[32,2176]{1,0:T(8,128)(2,1)S(1)}, u32[]{:S(2)}, u32[]{:S(2)}) collective-permute-start(bf16[32,2176]{1,0:T(8,128)(2,1)S(1)} %get-tuple-element.53), channel_id=1, source_target_pairs={{0,2},{1,3},{2,0},{3,1},{4,6},{5,7},{6,4},{7,5},{8,10},{9,11},{10,... | collective-permute-start | bytes 417800 | tf_op jit(solution)/shard_map/ppermute | solution.py:150
  25.7 4.2 %collective-permute-done.10.refs_3_ = bf16[32,2176]{1,0:T(8,128)(2,1)S(1)} collective-permute-done((bf16[32,2176]{1,0:T(8,128)(2,1)S(1)}, bf16[32,2176]{1,0:T(8,128)(2,1)S(1)}, u32[]{:S(2)}, u32[]{:S(2)}) %collective-permute-start.10) | collective-permute-done | bytes 139296 | tf_op jit(solution)/shard_map/ppermute | solution.py:150
  29.8 2.6 %collective-permute-done.8.refs_1_ = bf16[32,2176]{1,0:T(8,128)(2,1)S(1)} collective-permute-done((bf16[32,2176]{1,0:T(8,128)(2,1)S(1)}, bf16[32,2176]{1,0:T(8,128)(2,1)S(1)}, u32[]{:S(2)}, u32[]{:S(2)}) %collective-permute-start.8) | collective-permute-done | bytes 139296 | tf_op jit(solution)/shard_map/ppermute | solution.py:150
  32.4 0.3 shard_map.159
  32.8 0.4 shard_map.160
  33.2 1.2 %collective-permute-start.12 = (bf16[32,384]{1,0:T(8,128)(2,1)S(1)}, bf16[32,384]{1,0:T(8,128)(2,1)S(1)}, u32[]{:S(2)}, u32[]{:S(2)}) collective-permute-start(bf16[32,384]{1,0:T(8,128)(2,1)S(1)} %get-tuple-element.62), channel_id=1, source_target_pairs={{0,16},{1,25},{2,18},{3,27},{4,20},{5,29},{6,22},{7,31},{8,24},{9,... | collective-permute-start | bytes 73736 | tf_op jit(solution)/shard_map/ppermute | solution.py:486
  34.4 0.4 shard_map.161
  34.8 1.7 %collective-permute-start.13 = (bf16[32,384]{1,0:T(8,128)(2,1)S(1)}, bf16[32,384]{1,0:T(8,128)(2,1)S(1)}, u32[]{:S(2)}, u32[]{:S(2)}) collective-permute-start(bf16[32,384]{1,0:T(8,128)(2,1)S(1)} %get-tuple-element.63), channel_id=1, source_target_pairs={{0,24},{1,9},{2,26},{3,11},{4,28},{5,13},{6,30},{7,15},{8,16},{9,1... | collective-permute-start | bytes 73736 | tf_op jit(solution)/shard_map/ppermute | solution.py:486
  36.5 0.7 %collective-permute-start.14 = (bf16[32,384]{1,0:T(8,128)(2,1)S(1)}, bf16[32,384]{1,0:T(8,128)(2,1)S(1)}, u32[]{:S(2)}, u32[]{:S(2)}) collective-permute-start(bf16[32,384]{1,0:T(8,128)(2,1)S(1)} %get-tuple-element.64), channel_id=1, source_target_pairs={{0,8},{1,17},{2,10},{3,19},{4,12},{5,21},{6,14},{7,23},{8,0},{9,25... | collective-permute-start | bytes 73736 | tf_op jit(solution)/shard_map/ppermute | solution.py:486
  37.2 0.8 %collective-permute-done.12.part1 = bf16[32,384]{1,0:T(8,128)(2,1)S(1)} collective-permute-done((bf16[32,384]{1,0:T(8,128)(2,1)S(1)}, bf16[32,384]{1,0:T(8,128)(2,1)S(1)}, u32[]{:S(2)}, u32[]{:S(2)}) %collective-permute-start.12) | collective-permute-done | bytes 24608 | tf_op jit(solution)/shard_map/ppermute | solution.py:486
  38.0 2.6 %collective-permute-done.13.part2 = bf16[32,384]{1,0:T(8,128)(2,1)S(1)} collective-permute-done((bf16[32,384]{1,0:T(8,128)(2,1)S(1)}, bf16[32,384]{1,0:T(8,128)(2,1)S(1)}, u32[]{:S(2)}, u32[]{:S(2)}) %collective-permute-start.13) | collective-permute-done | bytes 24608 | tf_op jit(solution)/shard_map/ppermute | solution.py:486
  40.6 1.6 %collective-permute-start.15 = (bf16[64,384]{1,0:T(8,128)(2,1)S(1)}, bf16[64,384]{1,0:T(8,128)(2,1)S(1)}, u32[]{:S(2)}, u32[]{:S(2)}) collective-permute-start(bf16[64,384]{1,0:T(8,128)(2,1)S(1)} %shard_map.162), channel_id=1, source_target_pairs={{0,4},{4,0},{8,12},{12,8},{16,20},{20,16},{24,28},{28,24},{1,5},{5... | collective-permute-start | bytes 147464 | tf_op jit(solution)/shard_map/ppermute | solution.py:150
  42.2 2.6 %collective-permute-done.15.along = bf16[64,384]{1,0:T(8,128)(2,1)S(1)} collective-permute-done((bf16[64,384]{1,0:T(8,128)(2,1)S(1)}, bf16[64,384]{1,0:T(8,128)(2,1)S(1)}, u32[]{:S(2)}, u32[]{:S(2)}) %collective-permute-start.15) | collective-permute-done | bytes 49184 | tf_op jit(solution)/shard_map/ppermute | solution.py:150
  44.8 0.8 %shard_map.163 = bf16[32,384]{1,0:T(8,128)(2,1)} custom-call(bf16[32,384]{1,0:T(8,128)(2,1)S(1)} %get-tuple-element.61.home, bf16[32,384]{1,0:T(8,128)(2,1)S(1)} %collective-permute-done.12.part1, bf16[32,384]{1,0:T(8,128)(2,1)S(1)} %collective-permute-done.13.part2, bf16[32,384]{1,0:T(8,128)(2,1)S(1)} %collective-permute-done.14.part3, ...), custom_call_target="tpu_custom_call" | custom-call | flops 100000 | bytes 100000 | tf_op jit(solution)/shard_map/pallas_call | solution.py:137
  (26 shorter events, 0.7 us)
Async XLA Ops:
  0.6 6.1 %copy-start.3 = (s32[32,2]{0,1:T(2,128)S(1)}, s32[32,2]{0,1:T(2,128)}, u32[]{:S(2)}) copy-start(s32[32,2]{0,1:T(2,128)} %param.24) | copy-start | bytes 772
  0.6 6.1 %copy-start.2 = (f32[384,16]{0,1:T(8,128)S(1)}, f32[384,16]{0,1:T(8,128)}, u32[]{:S(2)}) copy-start(f32[384,16]{0,1:T(8,128)} %param.23) | copy-start | bytes 73732
  0.7 6.1 %copy-start.1 = (bf16[32,384]{1,0:T(8,128)(2,1)S(1)}, bf16[32,384]{1,0:T(8,128)(2,1)}, u32[]{:S(2)}) copy-start(bf16[32,384]{1,0:T(8,128)(2,1)} %resid.1) | copy-start | bytes 73732
  3.6 5.3 %collective-permute-start = (bf16[32,384]{1,0:T(8,128)(2,1)S(1)}, bf16[32,384]{1,0:T(8,128)(2,1)S(1)}, u32[]{:S(2)}, u32[]{:S(2)}) collective-permute-start(bf16[32,384]{1,0:T(8,128)(2,1)S(1)} %get-tuple-element.37), channel_id=1, source_target_pairs={{0,2},{1,3},{2,0},{3,1},{4,6},{5,7},{6,4},{7,5},{8,10},{9,11},{10,... | collective-permute-start | bytes 73736 | tf_op jit(solution)/shard_map/ppermute | solution.py:150
  6.6 3.3 %collective-permute-start.1 = (bf16[32,384]{1,0:T(8,128)(2,1)S(1)}, bf16[32,384]{1,0:T(8,128)(2,1)S(1)}, u32[]{:S(2)}, u32[]{:S(2)}) collective-permute-start(bf16[32,384]{1,0:T(8,128)(2,1)S(1)} %get-tuple-element.38), channel_id=1, source_target_pairs={{0,3},{1,2},{2,1},{3,0},{4,7},{5,6},{6,5},{7,4},{8,11},{9,10},{10,... | collective-permute-start | bytes 73736 | tf_op jit(solution)/shard_map/ppermute | solution.py:150
  6.6 3.3 %collective-permute-start.2 = (bf16[32,384]{1,0:T(8,128)(2,1)S(1)}, bf16[32,384]{1,0:T(8,128)(2,1)S(1)}, u32[]{:S(2)}, u32[]{:S(2)}) collective-permute-start(bf16[32,384]{1,0:T(8,128)(2,1)S(1)} %get-tuple-element.39), channel_id=1, source_target_pairs={{0,1},{1,0},{2,3},{3,2},{4,5},{5,4},{6,7},{7,6},{8,9},{9,8},{10,11... | collective-permute-start | bytes 73736 | tf_op jit(solution)/shard_map/ppermute | solution.py:150
  6.8 13.1 %copy-start.4 = (f32[384]{0:T(512)S(1)}, f32[384]{0:T(512)}, u32[]{:S(2)}) copy-start(f32[384]{0:T(512)} %param.22) | copy-start | bytes 4612
  10.0 4.8 %collective-permute-start.3 = (bf16[32,384]{1,0:T(8,128)(2,1)S(1)}, bf16[32,384]{1,0:T(8,128)(2,1)S(1)}, u32[]{:S(2)}, u32[]{:S(2)}) collective-permute-start(bf16[32,384]{1,0:T(8,128)(2,1)S(1)} %get-tuple-element.45), channel_id=1, source_target_pairs={{0,16},{4,20},{8,24},{12,28},{16,0},{20,4},{24,8},{28,12},{1,17},{... | collective-permute-start | bytes 73736 | tf_op jit(solution)/shard_map/ppermute | solution.py:150
  12.6 5.6 %collective-permute-start.4 = (bf16[32,384]{1,0:T(8,128)(2,1)S(1)}, bf16[32,384]{1,0:T(8,128)(2,1)S(1)}, u32[]{:S(2)}, u32[]{:S(2)}) collective-permute-start(bf16[32,384]{1,0:T(8,128)(2,1)S(1)} %get-tuple-element.46), channel_id=1, source_target_pairs={{0,24},{4,28},{8,16},{12,20},{16,8},{20,12},{24,0},{28,4},{1,25},{... | collective-permute-start | bytes 73736 | tf_op jit(solution)/shard_map/ppermute | solution.py:150
  14.0 4.3 %collective-permute-start.5 = (bf16[32,384]{1,0:T(8,128)(2,1)S(1)}, bf16[32,384]{1,0:T(8,128)(2,1)S(1)}, u32[]{:S(2)}, u32[]{:S(2)}) collective-permute-start(bf16[32,384]{1,0:T(8,128)(2,1)S(1)} %get-tuple-element.47), channel_id=1, source_target_pairs={{0,8},{4,12},{8,0},{12,4},{16,24},{20,28},{24,16},{28,20},{1,9},{5... | collective-permute-start | bytes 73736 | tf_op jit(solution)/shard_map/ppermute | solution.py:150
  18.3 4.2 %collective-permute-start.6 = (bf16[64,384]{1,0:T(8,128)(2,1)S(1)}, bf16[64,384]{1,0:T(8,128)(2,1)S(1)}, u32[]{:S(2)}, u32[]{:S(2)}) collective-permute-start(bf16[64,384]{1,0:T(8,128)(2,1)S(1)} %shard_map.154.turned), channel_id=1, source_target_pairs={{0,4},{4,0},{8,12},{12,8},{16,20},{20,16},{24,28},{28,24},{1,5},{5... | collective-permute-start | bytes 147464 | tf_op jit(solution)/shard_map/ppermute | solution.py:150
  21.3 1.9 %collective-permute-start.9 = (bf16[32,2176]{1,0:T(8,128)(2,1)S(1)}, bf16[32,2176]{1,0:T(8,128)(2,1)S(1)}, u32[]{:S(2)}, u32[]{:S(2)}) collective-permute-start(bf16[32,2176]{1,0:T(8,128)(2,1)S(1)} %get-tuple-element.56), channel_id=1, source_target_pairs={{0,1},{1,0},{2,3},{3,2},{4,5},{5,4},{6,7},{7,6},{8,9},{9,8},{10,11... | collective-permute-start | bytes 417800 | tf_op jit(solution)/shard_map/ppermute | solution.py:150
  23.1 9.7 %copy-start = (bf16[2,1024,384]{2,1,0:T(8,128)(2,1)S(1)}, bf16[2,1024,384]{2,1,0:T(8,128)(2,1)}, u32[]{:S(2)}) copy-start(bf16[2,1024,384]{2,1,0:T(8,128)(2,1)} %param.27) | copy-start | bytes 4718596
  23.1 1.4 %collective-permute-start.7 = (bf16[32,2176]{1,0:T(8,128)(2,1)S(1)}, bf16[32,2176]{1,0:T(8,128)(2,1)S(1)}, u32[]{:S(2)}, u32[]{:S(2)}) collective-permute-start(bf16[32,2176]{1,0:T(8,128)(2,1)S(1)} %get-tuple-element.51), channel_id=1, source_target_pairs={{0,1},{1,0},{2,3},{3,2},{4,5},{5,4},{6,7},{7,6},{8,9},{9,8},{10,11... | collective-permute-start | bytes 417800 | tf_op jit(solution)/shard_map/ppermute | solution.py:150
  23.4 6.5 %collective-permute-start.10 = (bf16[32,2176]{1,0:T(8,128)(2,1)S(1)}, bf16[32,2176]{1,0:T(8,128)(2,1)S(1)}, u32[]{:S(2)}, u32[]{:S(2)}) collective-permute-start(bf16[32,2176]{1,0:T(8,128)(2,1)S(1)} %get-tuple-element.58), channel_id=1, source_target_pairs={{0,2},{1,3},{2,0},{3,1},{4,6},{5,7},{6,4},{7,5},{8,10},{9,11},{10,... | collective-permute-start | bytes 417800 | tf_op jit(solution)/shard_map/ppermute | solution.py:150
  24.7 7.7 %collective-permute-start.8 = (bf16[32,2176]{1,0:T(8,128)(2,1)S(1)}, bf16[32,2176]{1,0:T(8,128)(2,1)S(1)}, u32[]{:S(2)}, u32[]{:S(2)}) collective-permute-start(bf16[32,2176]{1,0:T(8,128)(2,1)S(1)} %get-tuple-element.53), channel_id=1, source_target_pairs={{0,2},{1,3},{2,0},{3,1},{4,6},{5,7},{6,4},{7,5},{8,10},{9,11},{10,... | collective-permute-start | bytes 417800 | tf_op jit(solution)/shard_map/ppermute | solution.py:150
  32.7 1.7 %collective-permute-start.11 = (bf16[64,1024]{1,0:T(8,128)(2,1)S(1)}, bf16[64,1024]{1,0:T(8,128)(2,1)S(1)}, u32[]{:S(2)}, u32[]{:S(2)}) collective-permute-start(bf16[64,1024]{1,0:T(8,128)(2,1)S(1)} %get-tuple-element.59.hidden), channel_id=1, source_target_pairs={{0,1},{1,0},{2,3},{3,2},{4,5},{5,4},{6,7},{7,6},{8,9},{9,8},{10,11... | collective-permute-start | bytes 393224 | tf_op jit(solution)/shard_map/ppermute | solution.py:150
  33.2 4.8 %collective-permute-start.12 = (bf16[32,384]{1,0:T(8,128)(2,1)S(1)}, bf16[32,384]{1,0:T(8,128)(2,1)S(1)}, u32[]{:S(2)}, u32[]{:S(2)}) collective-permute-start(bf16[32,384]{1,0:T(8,128)(2,1)S(1)} %get-tuple-element.62), channel_id=1, source_target_pairs={{0,16},{1,25},{2,18},{3,27},{4,20},{5,29},{6,22},{7,31},{8,24},{9,... | collective-permute-start | bytes 73736 | tf_op jit(solution)/shard_map/ppermute | solution.py:486
  34.8 5.8 %collective-permute-start.13 = (bf16[32,384]{1,0:T(8,128)(2,1)S(1)}, bf16[32,384]{1,0:T(8,128)(2,1)S(1)}, u32[]{:S(2)}, u32[]{:S(2)}) collective-permute-start(bf16[32,384]{1,0:T(8,128)(2,1)S(1)} %get-tuple-element.63), channel_id=1, source_target_pairs={{0,24},{1,9},{2,26},{3,11},{4,28},{5,13},{6,30},{7,15},{8,16},{9,1... | collective-permute-start | bytes 73736 | tf_op jit(solution)/shard_map/ppermute | solution.py:486
  36.5 4.1 %collective-permute-start.14 = (bf16[32,384]{1,0:T(8,128)(2,1)S(1)}, bf16[32,384]{1,0:T(8,128)(2,1)S(1)}, u32[]{:S(2)}, u32[]{:S(2)}) collective-permute-start(bf16[32,384]{1,0:T(8,128)(2,1)S(1)} %get-tuple-element.64), channel_id=1, source_target_pairs={{0,8},{1,17},{2,10},{3,19},{4,12},{5,21},{6,14},{7,23},{8,0},{9,25... | collective-permute-start | bytes 73736 | tf_op jit(solution)/shard_map/ppermute | solution.py:486
  40.6 4.2 %collective-permute-start.15 = (bf16[64,384]{1,0:T(8,128)(2,1)S(1)}, bf16[64,384]{1,0:T(8,128)(2,1)S(1)}, u32[]{:S(2)}, u32[]{:S(2)}) collective-permute-start(bf16[64,384]{1,0:T(8,128)(2,1)S(1)} %shard_map.162), channel_id=1, source_target_pairs={{0,4},{4,0},{8,12},{12,8},{16,20},{20,16},{24,28},{28,24},{1,5},{5... | collective-permute-start | bytes 147464 | tf_op jit(solution)/shard_map/ppermute | solution.py:150

commit v14 on v13

--- a/solution.py
+++ b/solution.py
@@ -225,8 +225,6 @@
             -1e30,
         )
 
-    for copy in copies[chunks:]:
-        copy.wait()
     scores = score_s[...]
     peak = jnp.maximum(jnp.max(scores, axis=1, keepdims=True), own_score)
     terms = jnp.exp(scores - peak)
@@ -235,6 +233,8 @@
     weight_s[...] = (terms * inverse).astype(jnp.bfloat16)
     own_weight = (own_term * inverse).astype(jnp.bfloat16).astype(jnp.float32)
     self_s[...] = own_weight * values_new
+    for copy in copies[chunks:]:
+        copy.wait()
     for pair in range(row_count // 2):
         pair_rows = slice(16 * pair, 16 * pair + 16)
         values = jnp.concatenate([v_buf[2 * pair], v_buf[2 * pair + 1]], axis=1)

time: 45.7 us -> 45.5 us (level)
  transfers between devices with their start and end apart: 16 -> 16, of which waited for: 10 -> 10; matrix products, arithmetic and copies ran while one was open for 0% -> 0% of each run, Pallas kernels for 11% -> 12%
where the time goes in v14:
time: 45.5 us; the launch traced here: 45.3 us
  waiting for transfers between devices  19.1 us (42%)
  starting transfers between devices  16.4 us (36%)
  Pallas kernels  9.08 us (20%)
  between operations  0.79 us (2%)
    ppermute x13, waiting for transfers between devices, partner_permute(): return lax.ppermute(block, axis, [(i, i ^ distance) for i in range(count)])  15.7 us
    ppermute x13, starting transfers between devices, partner_permute(): return lax.ppermute(block, axis, [(i, i ^ distance) for i in range(count)])  12.7 us
    pallas_call x15, Pallas kernels, call(): pl.pallas_call(kernel, out_shape=[jax.ShapeDtypeStruct(shape, dtype) for...  9.08 us
    ppermute x3, starting transfers between devices, back_permute(): return lax.ppermute(block, ('req', 'tp'), pairs)  3.62 us
    ppermute x3, waiting for transfers between devices, back_permute(): return lax.ppermute(block, ('req', 'tp'), pairs)  3.42 us
  transfers between devices with their start and end apart: 16, of which 10 were waited for; matrix products, arithmetic and copies ran while one was open for 0% of the time, Pallas kernels for 12%

profile of v14, /device:TPU:0, one launch (start us, length us, event | category | flops | bytes accessed | tf_op | source)
XLA Modules:
  0.0 45.3 jit_solution(18339968857224745149)
XLA Ops:
  0.7 2.7 %shard_map.149 = (f32[32,384]{1,0:T(8,128)S(1)}, bf16[32,384]{1,0:T(8,128)(2,1)S(1)}, bf16[32,384]{1,0:T(8,128)(2,1)S(1)}, bf16[32,384]{1,0:T(8,128)(2,1)S(1)}) custom-call(s32[32]{0:T(128)} %lengths_hbm.1, bf16[32,384]{1,0:T(8,128)(2,1)} %queries_hbm.1, bf16[32,128]{1,0:T(8,128)(2,1)} %keys_hbm.1, bf16[32,128]{1,0:T(8,128)(2,1)} %values_hbm.1, ...), custom_call_target="tpu_custom_call" | custom-call | flops 200000000 | bytes 3400000 | tf_op jit(solution)/shard_map/pallas_call | solution.py:137
  3.3 3.0 %collective-permute-start = (bf16[32,384]{1,0:T(8,128)(2,1)S(1)}, bf16[32,384]{1,0:T(8,128)(2,1)S(1)}, u32[]{:S(2)}, u32[]{:S(2)}) collective-permute-start(bf16[32,384]{1,0:T(8,128)(2,1)S(1)} %get-tuple-element.37), channel_id=1, source_target_pairs={{0,2},{1,3},{2,0},{3,1},{4,6},{5,7},{6,4},{7,5},{8,10},{9,11},{10,... | collective-permute-start | bytes 73736 | tf_op jit(solution)/shard_map/ppermute | solution.py:150
  6.3 0.2 collective-permute-start.2
  6.5 2.0 %shard_map.150 = (f32[32,384]{1,0:T(8,128)S(1)}, bf16[128,32]{1,0:T(8,128)(2,1)S(1)}, bf16[32,128]{1,0:T(8,128)(2,1)S(1)}, bf16[32,128]{1,0:T(8,128)(2,1)S(1)}, ...) custom-call(f32[32,384]{1,0:T(8,128)S(1)} %get-tuple-element.35.own, ...), custom_call_target="tpu_custom_call" | custom-call | flops 100000 | bytes 3300000 | tf_op jit(solution)/shard_map/pallas_call | solution.py:137
  8.6 1.0 %collective-permute-done.1.part2 = bf16[32,384]{1,0:T(8,128)(2,1)S(1)} collective-permute-done((bf16[32,384]{1,0:T(8,128)(2,1)S(1)}, bf16[32,384]{1,0:T(8,128)(2,1)S(1)}, u32[]{:S(2)}, u32[]{:S(2)}) %collective-permute-start.1) | collective-permute-done | bytes 24608 | tf_op jit(solution)/shard_map/ppermute | solution.py:150
  9.7 2.7 %collective-permute-start.3 = (bf16[32,384]{1,0:T(8,128)(2,1)S(1)}, bf16[32,384]{1,0:T(8,128)(2,1)S(1)}, u32[]{:S(2)}, u32[]{:S(2)}) collective-permute-start(bf16[32,384]{1,0:T(8,128)(2,1)S(1)} %get-tuple-element.45), channel_id=1, source_target_pairs={{0,16},{4,20},{8,24},{12,28},{16,0},{20,4},{24,8},{28,12},{1,17},{... | collective-permute-start | bytes 73736 | tf_op jit(solution)/shard_map/ppermute | solution.py:150
  12.4 1.3 %collective-permute-start.4 = (bf16[32,384]{1,0:T(8,128)(2,1)S(1)}, bf16[32,384]{1,0:T(8,128)(2,1)S(1)}, u32[]{:S(2)}, u32[]{:S(2)}) collective-permute-start(bf16[32,384]{1,0:T(8,128)(2,1)S(1)} %get-tuple-element.46), channel_id=1, source_target_pairs={{0,24},{4,28},{8,16},{12,20},{16,8},{20,12},{24,0},{28,4},{1,25},{... | collective-permute-start | bytes 73736 | tf_op jit(solution)/shard_map/ppermute | solution.py:150
  13.8 0.2 collective-permute-start.5
  14.0 0.6 %collective-permute-done.3.part1.in1 = bf16[32,384]{1,0:T(8,128)(2,1)S(1)} collective-permute-done((bf16[32,384]{1,0:T(8,128)(2,1)S(1)}, bf16[32,384]{1,0:T(8,128)(2,1)S(1)}, u32[]{:S(2)}, u32[]{:S(2)}) %collective-permute-start.3) | collective-permute-done | bytes 24608 | tf_op jit(solution)/shard_map/ppermute | solution.py:150
  14.5 3.5 %collective-permute-done.4.part2.in2 = bf16[32,384]{1,0:T(8,128)(2,1)S(1)} collective-permute-done((bf16[32,384]{1,0:T(8,128)(2,1)S(1)}, bf16[32,384]{1,0:T(8,128)(2,1)S(1)}, u32[]{:S(2)}, u32[]{:S(2)}) %collective-permute-start.4) | collective-permute-done | bytes 24608 | tf_op jit(solution)/shard_map/ppermute | solution.py:150
  18.0 1.6 %collective-permute-start.6 = (bf16[64,384]{1,0:T(8,128)(2,1)S(1)}, bf16[64,384]{1,0:T(8,128)(2,1)S(1)}, u32[]{:S(2)}, u32[]{:S(2)}) collective-permute-start(bf16[64,384]{1,0:T(8,128)(2,1)S(1)} %shard_map.154.turned), channel_id=1, source_target_pairs={{0,4},{4,0},{8,12},{12,8},{16,20},{20,16},{24,28},{28,24},{1,5},{5... | collective-permute-start | bytes 147464 | tf_op jit(solution)/shard_map/ppermute | solution.py:150
  19.6 0.6 %shard_map.153 = bf16[32,384]{1,0:T(8,128)(2,1)} custom-call(bf16[32,384]{1,0:T(8,128)(2,1)S(1)} %get-tuple-element.41.attended), custom_call_target="tpu_custom_call" | custom-call | flops 100000 | bytes 100000 | tf_op jit(solution)/shard_map/pallas_call | solution.py:137
  20.3 0.7 %shard_map.157 = (f32[32,2176]{1,0:T(8,128)S(1)}, bf16[32,2176]{1,0:T(8,128)(2,1)S(1)}) custom-call(bf16[32,384]{1,0:T(8,128)(2,1)S(1)} %get-tuple-element.44.home.in0, bf16[32,384]{1,0:T(8,128)(2,1)S(1)} %collective-permute-done.3.part1.in1, bf16[32,384]{1,0:T(8,128)(2,1)S(1)} %collective-permute-done.4.part2.in2, ...), custom_call_target="tpu_custom_call" | custom-call | flops 400000000 | bytes 3500000 | tf_op jit(solution)/shard_map/pallas_call | solution.py:137
  21.1 1.1 %collective-permute-done.6.blocks = bf16[64,384]{1,0:T(8,128)(2,1)S(1)} collective-permute-done((bf16[64,384]{1,0:T(8,128)(2,1)S(1)}, bf16[64,384]{1,0:T(8,128)(2,1)S(1)}, u32[]{:S(2)}, u32[]{:S(2)}) %collective-permute-start.6) | collective-permute-done | bytes 49184 | tf_op jit(solution)/shard_map/ppermute | solution.py:150
  22.2 0.7 %shard_map.155 = (f32[32,2176]{1,0:T(8,128)S(1)}, bf16[32,2176]{1,0:T(8,128)(2,1)S(1)}) custom-call(bf16[64,384]{1,0:T(8,128)(2,1)S(1)} %collective-permute-done.6.blocks, f32[1,384]{1,0:T(1,128)S(1)} %reshape.18.gain, bf16[768,1024]{1,0:T(8,128)(2,1)S(1)} %get-tuple-element.48.w_gate, bf16[768,1024]{1,0:T(8,128)(2,1)S(1)} %get-tuple-element.49.w_up), custom_call_target="tpu_custom_call" | custom-call | flops 400000000 | bytes 3500000 | tf_op jit(solution)/shard_map/pallas_call | solution.py:137
  23.0 0.2 shard_map.158
  23.1 1.0 %collective-permute-start.10 = (bf16[32,2176]{1,0:T(8,128)(2,1)S(1)}, bf16[32,2176]{1,0:T(8,128)(2,1)S(1)}, u32[]{:S(2)}, u32[]{:S(2)}) collective-permute-start(bf16[32,2176]{1,0:T(8,128)(2,1)S(1)} %get-tuple-element.58), channel_id=1, source_target_pairs={{0,2},{1,3},{2,0},{3,1},{4,6},{5,7},{6,4},{7,5},{8,10},{9,11},{10,... | collective-permute-start | bytes 417800 | tf_op jit(solution)/shard_map/ppermute | solution.py:150
  24.1 0.2 collective-permute-done.7.part
  24.5 1.0 %collective-permute-start.8 = (bf16[32,2176]{1,0:T(8,128)(2,1)S(1)}, bf16[32,2176]{1,0:T(8,128)(2,1)S(1)}, u32[]{:S(2)}, u32[]{:S(2)}) collective-permute-start(bf16[32,2176]{1,0:T(8,128)(2,1)S(1)} %get-tuple-element.53), channel_id=1, source_target_pairs={{0,2},{1,3},{2,0},{3,1},{4,6},{5,7},{6,4},{7,5},{8,10},{9,11},{10,... | collective-permute-start | bytes 417800 | tf_op jit(solution)/shard_map/ppermute | solution.py:150
  25.4 4.2 %collective-permute-done.10.refs_3_ = bf16[32,2176]{1,0:T(8,128)(2,1)S(1)} collective-permute-done((bf16[32,2176]{1,0:T(8,128)(2,1)S(1)}, bf16[32,2176]{1,0:T(8,128)(2,1)S(1)}, u32[]{:S(2)}, u32[]{:S(2)}) %collective-permute-start.10) | collective-permute-done | bytes 139296 | tf_op jit(solution)/shard_map/ppermute | solution.py:150
  29.6 2.6 %collective-permute-done.8.refs_1_ = bf16[32,2176]{1,0:T(8,128)(2,1)S(1)} collective-permute-done((bf16[32,2176]{1,0:T(8,128)(2,1)S(1)}, bf16[32,2176]{1,0:T(8,128)(2,1)S(1)}, u32[]{:S(2)}, u32[]{:S(2)}) %collective-permute-start.8) | collective-permute-done | bytes 139296 | tf_op jit(solution)/shard_map/ppermute | solution.py:150
  32.2 0.3 shard_map.159
  32.5 0.4 shard_map.160
  32.9 1.2 %collective-permute-start.12 = (bf16[32,384]{1,0:T(8,128)(2,1)S(1)}, bf16[32,384]{1,0:T(8,128)(2,1)S(1)}, u32[]{:S(2)}, u32[]{:S(2)}) collective-permute-start(bf16[32,384]{1,0:T(8,128)(2,1)S(1)} %get-tuple-element.62), channel_id=1, source_target_pairs={{0,16},{1,25},{2,18},{3,27},{4,20},{5,29},{6,22},{7,31},{8,24},{9,... | collective-permute-start | bytes 73736 | tf_op jit(solution)/shard_map/ppermute | solution.py:486
  34.2 0.4 shard_map.161
  34.6 1.7 %collective-permute-start.13 = (bf16[32,384]{1,0:T(8,128)(2,1)S(1)}, bf16[32,384]{1,0:T(8,128)(2,1)S(1)}, u32[]{:S(2)}, u32[]{:S(2)}) collective-permute-start(bf16[32,384]{1,0:T(8,128)(2,1)S(1)} %get-tuple-element.63), channel_id=1, source_target_pairs={{0,24},{1,9},{2,26},{3,11},{4,28},{5,13},{6,30},{7,15},{8,16},{9,1... | collective-permute-start | bytes 73736 | tf_op jit(solution)/shard_map/ppermute | solution.py:486
  36.3 0.7 %collective-permute-start.14 = (bf16[32,384]{1,0:T(8,128)(2,1)S(1)}, bf16[32,384]{1,0:T(8,128)(2,1)S(1)}, u32[]{:S(2)}, u32[]{:S(2)}) collective-permute-start(bf16[32,384]{1,0:T(8,128)(2,1)S(1)} %get-tuple-element.64), channel_id=1, source_target_pairs={{0,8},{1,17},{2,10},{3,19},{4,12},{5,21},{6,14},{7,23},{8,0},{9,25... | collective-permute-start | bytes 73736 | tf_op jit(solution)/shard_map/ppermute | solution.py:486
  37.0 0.8 %collective-permute-done.12.part1 = bf16[32,384]{1,0:T(8,128)(2,1)S(1)} collective-permute-done((bf16[32,384]{1,0:T(8,128)(2,1)S(1)}, bf16[32,384]{1,0:T(8,128)(2,1)S(1)}, u32[]{:S(2)}, u32[]{:S(2)}) %collective-permute-start.12) | collective-permute-done | bytes 24608 | tf_op jit(solution)/shard_map/ppermute | solution.py:486
  37.7 2.6 %collective-permute-done.13.part2 = bf16[32,384]{1,0:T(8,128)(2,1)S(1)} collective-permute-done((bf16[32,384]{1,0:T(8,128)(2,1)S(1)}, bf16[32,384]{1,0:T(8,128)(2,1)S(1)}, u32[]{:S(2)}, u32[]{:S(2)}) %collective-permute-start.13) | collective-permute-done | bytes 24608 | tf_op jit(solution)/shard_map/ppermute | solution.py:486
  40.4 1.6 %collective-permute-start.15 = (bf16[64,384]{1,0:T(8,128)(2,1)S(1)}, bf16[64,384]{1,0:T(8,128)(2,1)S(1)}, u32[]{:S(2)}, u32[]{:S(2)}) collective-permute-start(bf16[64,384]{1,0:T(8,128)(2,1)S(1)} %shard_map.162), channel_id=1, source_target_pairs={{0,4},{4,0},{8,12},{12,8},{16,20},{20,16},{24,28},{28,24},{1,5},{5... | collective-permute-start | bytes 147464 | tf_op jit(solution)/shard_map/ppermute | solution.py:150
  42.0 2.6 %collective-permute-done.15.along = bf16[64,384]{1,0:T(8,128)(2,1)S(1)} collective-permute-done((bf16[64,384]{1,0:T(8,128)(2,1)S(1)}, bf16[64,384]{1,0:T(8,128)(2,1)S(1)}, u32[]{:S(2)}, u32[]{:S(2)}) %collective-permute-start.15) | collective-permute-done | bytes 49184 | tf_op jit(solution)/shard_map/ppermute | solution.py:150
  44.5 0.8 %shard_map.163 = bf16[32,384]{1,0:T(8,128)(2,1)} custom-call(bf16[32,384]{1,0:T(8,128)(2,1)S(1)} %get-tuple-element.61.home, bf16[32,384]{1,0:T(8,128)(2,1)S(1)} %collective-permute-done.12.part1, bf16[32,384]{1,0:T(8,128)(2,1)S(1)} %collective-permute-done.13.part2, bf16[32,384]{1,0:T(8,128)(2,1)S(1)} %collective-permute-done.14.part3, ...), custom_call_target="tpu_custom_call" | custom-call | flops 100000 | bytes 100000 | tf_op jit(solution)/shard_map/pallas_call | solution.py:137
  (26 shorter events, 0.7 us)
Async XLA Ops:
  0.6 5.9 %copy-start.3 = (s32[32,2]{0,1:T(2,128)S(1)}, s32[32,2]{0,1:T(2,128)}, u32[]{:S(2)}) copy-start(s32[32,2]{0,1:T(2,128)} %param.24) | copy-start | bytes 772
  0.6 5.9 %copy-start.2 = (f32[384,16]{0,1:T(8,128)S(1)}, f32[384,16]{0,1:T(8,128)}, u32[]{:S(2)}) copy-start(f32[384,16]{0,1:T(8,128)} %param.23) | copy-start | bytes 73732
  0.7 5.9 %copy-start.1 = (bf16[32,384]{1,0:T(8,128)(2,1)S(1)}, bf16[32,384]{1,0:T(8,128)(2,1)}, u32[]{:S(2)}) copy-start(bf16[32,384]{1,0:T(8,128)(2,1)} %resid.1) | copy-start | bytes 73732
  3.3 5.3 %collective-permute-start = (bf16[32,384]{1,0:T(8,128)(2,1)S(1)}, bf16[32,384]{1,0:T(8,128)(2,1)S(1)}, u32[]{:S(2)}, u32[]{:S(2)}) collective-permute-start(bf16[32,384]{1,0:T(8,128)(2,1)S(1)} %get-tuple-element.37), channel_id=1, source_target_pairs={{0,2},{1,3},{2,0},{3,1},{4,6},{5,7},{6,4},{7,5},{8,10},{9,11},{10,... | collective-permute-start | bytes 73736 | tf_op jit(solution)/shard_map/ppermute | solution.py:150
  6.3 3.3 %collective-permute-start.1 = (bf16[32,384]{1,0:T(8,128)(2,1)S(1)}, bf16[32,384]{1,0:T(8,128)(2,1)S(1)}, u32[]{:S(2)}, u32[]{:S(2)}) collective-permute-start(bf16[32,384]{1,0:T(8,128)(2,1)S(1)} %get-tuple-element.38), channel_id=1, source_target_pairs={{0,3},{1,2},{2,1},{3,0},{4,7},{5,6},{6,5},{7,4},{8,11},{9,10},{10,... | collective-permute-start | bytes 73736 | tf_op jit(solution)/shard_map/ppermute | solution.py:150
  6.3 3.3 %collective-permute-start.2 = (bf16[32,384]{1,0:T(8,128)(2,1)S(1)}, bf16[32,384]{1,0:T(8,128)(2,1)S(1)}, u32[]{:S(2)}, u32[]{:S(2)}) collective-permute-start(bf16[32,384]{1,0:T(8,128)(2,1)S(1)} %get-tuple-element.39), channel_id=1, source_target_pairs={{0,1},{1,0},{2,3},{3,2},{4,5},{5,4},{6,7},{7,6},{8,9},{9,8},{10,11... | collective-permute-start | bytes 73736 | tf_op jit(solution)/shard_map/ppermute | solution.py:150
  6.5 13.1 %copy-start.4 = (f32[384]{0:T(512)S(1)}, f32[384]{0:T(512)}, u32[]{:S(2)}) copy-start(f32[384]{0:T(512)} %param.22) | copy-start | bytes 4612
  9.7 4.8 %collective-permute-start.3 = (bf16[32,384]{1,0:T(8,128)(2,1)S(1)}, bf16[32,384]{1,0:T(8,128)(2,1)S(1)}, u32[]{:S(2)}, u32[]{:S(2)}) collective-permute-start(bf16[32,384]{1,0:T(8,128)(2,1)S(1)} %get-tuple-element.45), channel_id=1, source_target_pairs={{0,16},{4,20},{8,24},{12,28},{16,0},{20,4},{24,8},{28,12},{1,17},{... | collective-permute-start | bytes 73736 | tf_op jit(solution)/shard_map/ppermute | solution.py:150
  12.4 5.6 %collective-permute-start.4 = (bf16[32,384]{1,0:T(8,128)(2,1)S(1)}, bf16[32,384]{1,0:T(8,128)(2,1)S(1)}, u32[]{:S(2)}, u32[]{:S(2)}) collective-permute-start(bf16[32,384]{1,0:T(8,128)(2,1)S(1)} %get-tuple-element.46), channel_id=1, source_target_pairs={{0,24},{4,28},{8,16},{12,20},{16,8},{20,12},{24,0},{28,4},{1,25},{... | collective-permute-start | bytes 73736 | tf_op jit(solution)/shard_map/ppermute | solution.py:150
  13.8 4.3 %collective-permute-start.5 = (bf16[32,384]{1,0:T(8,128)(2,1)S(1)}, bf16[32,384]{1,0:T(8,128)(2,1)S(1)}, u32[]{:S(2)}, u32[]{:S(2)}) collective-permute-start(bf16[32,384]{1,0:T(8,128)(2,1)S(1)} %get-tuple-element.47), channel_id=1, source_target_pairs={{0,8},{4,12},{8,0},{12,4},{16,24},{20,28},{24,16},{28,20},{1,9},{5... | collective-permute-start | bytes 73736 | tf_op jit(solution)/shard_map/ppermute | solution.py:150
  18.0 4.2 %collective-permute-start.6 = (bf16[64,384]{1,0:T(8,128)(2,1)S(1)}, bf16[64,384]{1,0:T(8,128)(2,1)S(1)}, u32[]{:S(2)}, u32[]{:S(2)}) collective-permute-start(bf16[64,384]{1,0:T(8,128)(2,1)S(1)} %shard_map.154.turned), channel_id=1, source_target_pairs={{0,4},{4,0},{8,12},{12,8},{16,20},{20,16},{24,28},{28,24},{1,5},{5... | collective-permute-start | bytes 147464 | tf_op jit(solution)/shard_map/ppermute | solution.py:150
  21.0 1.9 %collective-permute-start.9 = (bf16[32,2176]{1,0:T(8,128)(2,1)S(1)}, bf16[32,2176]{1,0:T(8,128)(2,1)S(1)}, u32[]{:S(2)}, u32[]{:S(2)}) collective-permute-start(bf16[32,2176]{1,0:T(8,128)(2,1)S(1)} %get-tuple-element.56), channel_id=1, source_target_pairs={{0,1},{1,0},{2,3},{3,2},{4,5},{5,4},{6,7},{7,6},{8,9},{9,8},{10,11... | collective-permute-start | bytes 417800 | tf_op jit(solution)/shard_map/ppermute | solution.py:150
  22.9 9.7 %copy-start = (bf16[2,1024,384]{2,1,0:T(8,128)(2,1)S(1)}, bf16[2,1024,384]{2,1,0:T(8,128)(2,1)}, u32[]{:S(2)}) copy-start(bf16[2,1024,384]{2,1,0:T(8,128)(2,1)} %param.27) | copy-start | bytes 4718596
  22.9 1.4 %collective-permute-start.7 = (bf16[32,2176]{1,0:T(8,128)(2,1)S(1)}, bf16[32,2176]{1,0:T(8,128)(2,1)S(1)}, u32[]{:S(2)}, u32[]{:S(2)}) collective-permute-start(bf16[32,2176]{1,0:T(8,128)(2,1)S(1)} %get-tuple-element.51), channel_id=1, source_target_pairs={{0,1},{1,0},{2,3},{3,2},{4,5},{5,4},{6,7},{7,6},{8,9},{9,8},{10,11... | collective-permute-start | bytes 417800 | tf_op jit(solution)/shard_map/ppermute | solution.py:150
  23.1 6.5 %collective-permute-start.10 = (bf16[32,2176]{1,0:T(8,128)(2,1)S(1)}, bf16[32,2176]{1,0:T(8,128)(2,1)S(1)}, u32[]{:S(2)}, u32[]{:S(2)}) collective-permute-start(bf16[32,2176]{1,0:T(8,128)(2,1)S(1)} %get-tuple-element.58), channel_id=1, source_target_pairs={{0,2},{1,3},{2,0},{3,1},{4,6},{5,7},{6,4},{7,5},{8,10},{9,11},{10,... | collective-permute-start | bytes 417800 | tf_op jit(solution)/shard_map/ppermute | solution.py:150
  24.5 7.7 %collective-permute-start.8 = (bf16[32,2176]{1,0:T(8,128)(2,1)S(1)}, bf16[32,2176]{1,0:T(8,128)(2,1)S(1)}, u32[]{:S(2)}, u32[]{:S(2)}) collective-permute-start(bf16[32,2176]{1,0:T(8,128)(2,1)S(1)} %get-tuple-element.53), channel_id=1, source_target_pairs={{0,2},{1,3},{2,0},{3,1},{4,6},{5,7},{6,4},{7,5},{8,10},{9,11},{10,... | collective-permute-start | bytes 417800 | tf_op jit(solution)/shard_map/ppermute | solution.py:150
  32.5 1.7 %collective-permute-start.11 = (bf16[64,1024]{1,0:T(8,128)(2,1)S(1)}, bf16[64,1024]{1,0:T(8,128)(2,1)S(1)}, u32[]{:S(2)}, u32[]{:S(2)}) collective-permute-start(bf16[64,1024]{1,0:T(8,128)(2,1)S(1)} %get-tuple-element.59.hidden), channel_id=1, source_target_pairs={{0,1},{1,0},{2,3},{3,2},{4,5},{5,4},{6,7},{7,6},{8,9},{9,8},{10,11... | collective-permute-start | bytes 393224 | tf_op jit(solution)/shard_map/ppermute | solution.py:150
  32.9 4.8 %collective-permute-start.12 = (bf16[32,384]{1,0:T(8,128)(2,1)S(1)}, bf16[32,384]{1,0:T(8,128)(2,1)S(1)}, u32[]{:S(2)}, u32[]{:S(2)}) collective-permute-start(bf16[32,384]{1,0:T(8,128)(2,1)S(1)} %get-tuple-element.62), channel_id=1, source_target_pairs={{0,16},{1,25},{2,18},{3,27},{4,20},{5,29},{6,22},{7,31},{8,24},{9,... | collective-permute-start | bytes 73736 | tf_op jit(solution)/shard_map/ppermute | solution.py:486
  34.6 5.8 %collective-permute-start.13 = (bf16[32,384]{1,0:T(8,128)(2,1)S(1)}, bf16[32,384]{1,0:T(8,128)(2,1)S(1)}, u32[]{:S(2)}, u32[]{:S(2)}) collective-permute-start(bf16[32,384]{1,0:T(8,128)(2,1)S(1)} %get-tuple-element.63), channel_id=1, source_target_pairs={{0,24},{1,9},{2,26},{3,11},{4,28},{5,13},{6,30},{7,15},{8,16},{9,1... | collective-permute-start | bytes 73736 | tf_op jit(solution)/shard_map/ppermute | solution.py:486
  36.3 4.1 %collective-permute-start.14 = (bf16[32,384]{1,0:T(8,128)(2,1)S(1)}, bf16[32,384]{1,0:T(8,128)(2,1)S(1)}, u32[]{:S(2)}, u32[]{:S(2)}) collective-permute-start(bf16[32,384]{1,0:T(8,128)(2,1)S(1)} %get-tuple-element.64), channel_id=1, source_target_pairs={{0,8},{1,17},{2,10},{3,19},{4,12},{5,21},{6,14},{7,23},{8,0},{9,25... | collective-permute-start | bytes 73736 | tf_op jit(solution)/shard_map/ppermute | solution.py:486
  40.4 4.2 %collective-permute-start.15 = (bf16[64,384]{1,0:T(8,128)(2,1)S(1)}, bf16[64,384]{1,0:T(8,128)(2,1)S(1)}, u32[]{:S(2)}, u32[]{:S(2)}) collective-permute-start(bf16[64,384]{1,0:T(8,128)(2,1)S(1)} %shard_map.162), channel_id=1, source_target_pairs={{0,4},{4,0},{8,12},{12,8},{16,20},{20,16},{24,28},{28,24},{1,5},{5... | collective-permute-start | bytes 147464 | tf_op jit(solution)/shard_map/ppermute | solution.py:150

commit v15 on v14

--- a/solution.py
+++ b/solution.py
@@ -179,7 +179,7 @@
             copies.append(
                 pltpu.make_async_copy(source.at[part], target.at[part], sems.at[len(copies)])
             )
-    for copy in small + copies:
+    for copy in copies[:chunks] + small + copies[chunks:]:
         copy.start()
 
     for copy in small:

time: 45.5 us -> 45.5 us (level)
  no operation moved by 1% of the time
where the time goes in v15:
time: 45.5 us; the launch traced here: 45.3 us
  waiting for transfers between devices  19.1 us (42%)
  starting transfers between devices  16.4 us (36%)
  Pallas kernels  9.08 us (20%)
  between operations  0.79 us (2%)
    ppermute x13, waiting for transfers between devices, partner_permute(): return lax.ppermute(block, axis, [(i, i ^ distance) for i in range(count)])  15.7 us
    ppermute x13, starting transfers between devices, partner_permute(): return lax.ppermute(block, axis, [(i, i ^ distance) for i in range(count)])  12.7 us
    pallas_call x15, Pallas kernels, call(): pl.pallas_call(kernel, out_shape=[jax.ShapeDtypeStruct(shape, dtype) for...  9.08 us
    ppermute x3, starting transfers between devices, back_permute(): return lax.ppermute(block, ('req', 'tp'), pairs)  3.62 us
    ppermute x3, waiting for transfers between devices, back_permute(): return lax.ppermute(block, ('req', 'tp'), pairs)  3.42 us
  transfers between devices with their start and end apart: 16, of which 10 were waited for; matrix products, arithmetic and copies ran while one was open for 0% of the time, Pallas kernels for 12%

profile of v15, /device:TPU:0, one launch (start us, length us, event | category | flops | bytes accessed | tf_op | source)
XLA Modules:
  0.0 45.3 jit_solution(14531348812394866036)
XLA Ops:
  0.7 2.7 %shard_map.149 = (f32[32,384]{1,0:T(8,128)S(1)}, bf16[32,384]{1,0:T(8,128)(2,1)S(1)}, bf16[32,384]{1,0:T(8,128)(2,1)S(1)}, bf16[32,384]{1,0:T(8,128)(2,1)S(1)}) custom-call(s32[32]{0:T(128)} %lengths_hbm.1, bf16[32,384]{1,0:T(8,128)(2,1)} %queries_hbm.1, bf16[32,128]{1,0:T(8,128)(2,1)} %keys_hbm.1, bf16[32,128]{1,0:T(8,128)(2,1)} %values_hbm.1, ...), custom_call_target="tpu_custom_call" | custom-call | flops 200000000 | bytes 3400000 | tf_op jit(solution)/shard_map/pallas_call | solution.py:137
  3.3 3.0 %collective-permute-start = (bf16[32,384]{1,0:T(8,128)(2,1)S(1)}, bf16[32,384]{1,0:T(8,128)(2,1)S(1)}, u32[]{:S(2)}, u32[]{:S(2)}) collective-permute-start(bf16[32,384]{1,0:T(8,128)(2,1)S(1)} %get-tuple-element.37), channel_id=1, source_target_pairs={{0,2},{1,3},{2,0},{3,1},{4,6},{5,7},{6,4},{7,5},{8,10},{9,11},{10,... | collective-permute-start | bytes 73736 | tf_op jit(solution)/shard_map/ppermute | solution.py:150
  6.3 0.2 collective-permute-start.2
  6.5 2.0 %shard_map.150 = (f32[32,384]{1,0:T(8,128)S(1)}, bf16[128,32]{1,0:T(8,128)(2,1)S(1)}, bf16[32,128]{1,0:T(8,128)(2,1)S(1)}, bf16[32,128]{1,0:T(8,128)(2,1)S(1)}, ...) custom-call(f32[32,384]{1,0:T(8,128)S(1)} %get-tuple-element.35.own, ...), custom_call_target="tpu_custom_call" | custom-call | flops 100000 | bytes 3300000 | tf_op jit(solution)/shard_map/pallas_call | solution.py:137
  8.6 1.0 %collective-permute-done.1.part2 = bf16[32,384]{1,0:T(8,128)(2,1)S(1)} collective-permute-done((bf16[32,384]{1,0:T(8,128)(2,1)S(1)}, bf16[32,384]{1,0:T(8,128)(2,1)S(1)}, u32[]{:S(2)}, u32[]{:S(2)}) %collective-permute-start.1) | collective-permute-done | bytes 24608 | tf_op jit(solution)/shard_map/ppermute | solution.py:150
  9.7 2.7 %collective-permute-start.3 = (bf16[32,384]{1,0:T(8,128)(2,1)S(1)}, bf16[32,384]{1,0:T(8,128)(2,1)S(1)}, u32[]{:S(2)}, u32[]{:S(2)}) collective-permute-start(bf16[32,384]{1,0:T(8,128)(2,1)S(1)} %get-tuple-element.45), channel_id=1, source_target_pairs={{0,16},{4,20},{8,24},{12,28},{16,0},{20,4},{24,8},{28,12},{1,17},{... | collective-permute-start | bytes 73736 | tf_op jit(solution)/shard_map/ppermute | solution.py:150
  12.4 1.3 %collective-permute-start.4 = (bf16[32,384]{1,0:T(8,128)(2,1)S(1)}, bf16[32,384]{1,0:T(8,128)(2,1)S(1)}, u32[]{:S(2)}, u32[]{:S(2)}) collective-permute-start(bf16[32,384]{1,0:T(8,128)(2,1)S(1)} %get-tuple-element.46), channel_id=1, source_target_pairs={{0,24},{4,28},{8,16},{12,20},{16,8},{20,12},{24,0},{28,4},{1,25},{... | collective-permute-start | bytes 73736 | tf_op jit(solution)/shard_map/ppermute | solution.py:150
  13.8 0.2 collective-permute-start.5
  14.0 0.6 %collective-permute-done.3.part1.in1 = bf16[32,384]{1,0:T(8,128)(2,1)S(1)} collective-permute-done((bf16[32,384]{1,0:T(8,128)(2,1)S(1)}, bf16[32,384]{1,0:T(8,128)(2,1)S(1)}, u32[]{:S(2)}, u32[]{:S(2)}) %collective-permute-start.3) | collective-permute-done | bytes 24608 | tf_op jit(solution)/shard_map/ppermute | solution.py:150
  14.5 3.5 %collective-permute-done.4.part2.in2 = bf16[32,384]{1,0:T(8,128)(2,1)S(1)} collective-permute-done((bf16[32,384]{1,0:T(8,128)(2,1)S(1)}, bf16[32,384]{1,0:T(8,128)(2,1)S(1)}, u32[]{:S(2)}, u32[]{:S(2)}) %collective-permute-start.4) | collective-permute-done | bytes 24608 | tf_op jit(solution)/shard_map/ppermute | solution.py:150
  18.0 1.6 %collective-permute-start.6 = (bf16[64,384]{1,0:T(8,128)(2,1)S(1)}, bf16[64,384]{1,0:T(8,128)(2,1)S(1)}, u32[]{:S(2)}, u32[]{:S(2)}) collective-permute-start(bf16[64,384]{1,0:T(8,128)(2,1)S(1)} %shard_map.154.turned), channel_id=1, source_target_pairs={{0,4},{4,0},{8,12},{12,8},{16,20},{20,16},{24,28},{28,24},{1,5},{5... | collective-permute-start | bytes 147464 | tf_op jit(solution)/shard_map/ppermute | solution.py:150
  19.6 0.6 %shard_map.153 = bf16[32,384]{1,0:T(8,128)(2,1)} custom-call(bf16[32,384]{1,0:T(8,128)(2,1)S(1)} %get-tuple-element.41.attended), custom_call_target="tpu_custom_call" | custom-call | flops 100000 | bytes 100000 | tf_op jit(solution)/shard_map/pallas_call | solution.py:137
  20.3 0.7 %shard_map.157 = (f32[32,2176]{1,0:T(8,128)S(1)}, bf16[32,2176]{1,0:T(8,128)(2,1)S(1)}) custom-call(bf16[32,384]{1,0:T(8,128)(2,1)S(1)} %get-tuple-element.44.home.in0, bf16[32,384]{1,0:T(8,128)(2,1)S(1)} %collective-permute-done.3.part1.in1, bf16[32,384]{1,0:T(8,128)(2,1)S(1)} %collective-permute-done.4.part2.in2, ...), custom_call_target="tpu_custom_call" | custom-call | flops 400000000 | bytes 3500000 | tf_op jit(solution)/shard_map/pallas_call | solution.py:137
  21.1 1.1 %collective-permute-done.6.blocks = bf16[64,384]{1,0:T(8,128)(2,1)S(1)} collective-permute-done((bf16[64,384]{1,0:T(8,128)(2,1)S(1)}, bf16[64,384]{1,0:T(8,128)(2,1)S(1)}, u32[]{:S(2)}, u32[]{:S(2)}) %collective-permute-start.6) | collective-permute-done | bytes 49184 | tf_op jit(solution)/shard_map/ppermute | solution.py:150
  22.2 0.7 %shard_map.155 = (f32[32,2176]{1,0:T(8,128)S(1)}, bf16[32,2176]{1,0:T(8,128)(2,1)S(1)}) custom-call(bf16[64,384]{1,0:T(8,128)(2,1)S(1)} %collective-permute-done.6.blocks, f32[1,384]{1,0:T(1,128)S(1)} %reshape.18.gain, bf16[768,1024]{1,0:T(8,128)(2,1)S(1)} %get-tuple-element.48.w_gate, bf16[768,1024]{1,0:T(8,128)(2,1)S(1)} %get-tuple-element.49.w_up), custom_call_target="tpu_custom_call" | custom-call | flops 400000000 | bytes 3500000 | tf_op jit(solution)/shard_map/pallas_call | solution.py:137
  23.0 0.2 shard_map.158
  23.1 1.0 %collective-permute-start.10 = (bf16[32,2176]{1,0:T(8,128)(2,1)S(1)}, bf16[32,2176]{1,0:T(8,128)(2,1)S(1)}, u32[]{:S(2)}, u32[]{:S(2)}) collective-permute-start(bf16[32,2176]{1,0:T(8,128)(2,1)S(1)} %get-tuple-element.58), channel_id=1, source_target_pairs={{0,2},{1,3},{2,0},{3,1},{4,6},{5,7},{6,4},{7,5},{8,10},{9,11},{10,... | collective-permute-start | bytes 417800 | tf_op jit(solution)/shard_map/ppermute | solution.py:150
  24.1 0.2 collective-permute-done.7.part
  24.5 1.0 %collective-permute-start.8 = (bf16[32,2176]{1,0:T(8,128)(2,1)S(1)}, bf16[32,2176]{1,0:T(8,128)(2,1)S(1)}, u32[]{:S(2)}, u32[]{:S(2)}) collective-permute-start(bf16[32,2176]{1,0:T(8,128)(2,1)S(1)} %get-tuple-element.53), channel_id=1, source_target_pairs={{0,2},{1,3},{2,0},{3,1},{4,6},{5,7},{6,4},{7,5},{8,10},{9,11},{10,... | collective-permute-start | bytes 417800 | tf_op jit(solution)/shard_map/ppermute | solution.py:150
  25.4 4.2 %collective-permute-done.10.refs_3_ = bf16[32,2176]{1,0:T(8,128)(2,1)S(1)} collective-permute-done((bf16[32,2176]{1,0:T(8,128)(2,1)S(1)}, bf16[32,2176]{1,0:T(8,128)(2,1)S(1)}, u32[]{:S(2)}, u32[]{:S(2)}) %collective-permute-start.10) | collective-permute-done | bytes 139296 | tf_op jit(solution)/shard_map/ppermute | solution.py:150
  29.6 2.6 %collective-permute-done.8.refs_1_ = bf16[32,2176]{1,0:T(8,128)(2,1)S(1)} collective-permute-done((bf16[32,2176]{1,0:T(8,128)(2,1)S(1)}, bf16[32,2176]{1,0:T(8,128)(2,1)S(1)}, u32[]{:S(2)}, u32[]{:S(2)}) %collective-permute-start.8) | collective-permute-done | bytes 139296 | tf_op jit(solution)/shard_map/ppermute | solution.py:150
  32.2 0.3 shard_map.159
  32.5 0.4 shard_map.160
  32.9 1.2 %collective-permute-start.12 = (bf16[32,384]{1,0:T(8,128)(2,1)S(1)}, bf16[32,384]{1,0:T(8,128)(2,1)S(1)}, u32[]{:S(2)}, u32[]{:S(2)}) collective-permute-start(bf16[32,384]{1,0:T(8,128)(2,1)S(1)} %get-tuple-element.62), channel_id=1, source_target_pairs={{0,16},{1,25},{2,18},{3,27},{4,20},{5,29},{6,22},{7,31},{8,24},{9,... | collective-permute-start | bytes 73736 | tf_op jit(solution)/shard_map/ppermute | solution.py:486
  34.2 0.4 shard_map.161
  34.6 1.7 %collective-permute-start.13 = (bf16[32,384]{1,0:T(8,128)(2,1)S(1)}, bf16[32,384]{1,0:T(8,128)(2,1)S(1)}, u32[]{:S(2)}, u32[]{:S(2)}) collective-permute-start(bf16[32,384]{1,0:T(8,128)(2,1)S(1)} %get-tuple-element.63), channel_id=1, source_target_pairs={{0,24},{1,9},{2,26},{3,11},{4,28},{5,13},{6,30},{7,15},{8,16},{9,1... | collective-permute-start | bytes 73736 | tf_op jit(solution)/shard_map/ppermute | solution.py:486
  36.3 0.7 %collective-permute-start.14 = (bf16[32,384]{1,0:T(8,128)(2,1)S(1)}, bf16[32,384]{1,0:T(8,128)(2,1)S(1)}, u32[]{:S(2)}, u32[]{:S(2)}) collective-permute-start(bf16[32,384]{1,0:T(8,128)(2,1)S(1)} %get-tuple-element.64), channel_id=1, source_target_pairs={{0,8},{1,17},{2,10},{3,19},{4,12},{5,21},{6,14},{7,23},{8,0},{9,25... | collective-permute-start | bytes 73736 | tf_op jit(solution)/shard_map/ppermute | solution.py:486
  37.0 0.8 %collective-permute-done.12.part1 = bf16[32,384]{1,0:T(8,128)(2,1)S(1)} collective-permute-done((bf16[32,384]{1,0:T(8,128)(2,1)S(1)}, bf16[32,384]{1,0:T(8,128)(2,1)S(1)}, u32[]{:S(2)}, u32[]{:S(2)}) %collective-permute-start.12) | collective-permute-done | bytes 24608 | tf_op jit(solution)/shard_map/ppermute | solution.py:486
  37.7 2.6 %collective-permute-done.13.part2 = bf16[32,384]{1,0:T(8,128)(2,1)S(1)} collective-permute-done((bf16[32,384]{1,0:T(8,128)(2,1)S(1)}, bf16[32,384]{1,0:T(8,128)(2,1)S(1)}, u32[]{:S(2)}, u32[]{:S(2)}) %collective-permute-start.13) | collective-permute-done | bytes 24608 | tf_op jit(solution)/shard_map/ppermute | solution.py:486
  40.4 1.6 %collective-permute-start.15 = (bf16[64,384]{1,0:T(8,128)(2,1)S(1)}, bf16[64,384]{1,0:T(8,128)(2,1)S(1)}, u32[]{:S(2)}, u32[]{:S(2)}) collective-permute-start(bf16[64,384]{1,0:T(8,128)(2,1)S(1)} %shard_map.162), channel_id=1, source_target_pairs={{0,4},{4,0},{8,12},{12,8},{16,20},{20,16},{24,28},{28,24},{1,5},{5... | collective-permute-start | bytes 147464 | tf_op jit(solution)/shard_map/ppermute | solution.py:150
  42.0 2.6 %collective-permute-done.15.along = bf16[64,384]{1,0:T(8,128)(2,1)S(1)} collective-permute-done((bf16[64,384]{1,0:T(8,128)(2,1)S(1)}, bf16[64,384]{1,0:T(8,128)(2,1)S(1)}, u32[]{:S(2)}, u32[]{:S(2)}) %collective-permute-start.15) | collective-permute-done | bytes 49184 | tf_op jit(solution)/shard_map/ppermute | solution.py:150
  44.5 0.8 %shard_map.163 = bf16[32,384]{1,0:T(8,128)(2,1)} custom-call(bf16[32,384]{1,0:T(8,128)(2,1)S(1)} %get-tuple-element.61.home, bf16[32,384]{1,0:T(8,128)(2,1)S(1)} %collective-permute-done.12.part1, bf16[32,384]{1,0:T(8,128)(2,1)S(1)} %collective-permute-done.13.part2, bf16[32,384]{1,0:T(8,128)(2,1)S(1)} %collective-permute-done.14.part3, ...), custom_call_target="tpu_custom_call" | custom-call | flops 100000 | bytes 100000 | tf_op jit(solution)/shard_map/pallas_call | solution.py:137
  (26 shorter events, 0.7 us)
Async XLA Ops:
  0.6 5.9 %copy-start.3 = (s32[32,2]{0,1:T(2,128)S(1)}, s32[32,2]{0,1:T(2,128)}, u32[]{:S(2)}) copy-start(s32[32,2]{0,1:T(2,128)} %param.24) | copy-start | bytes 772
  0.6 5.9 %copy-start.2 = (f32[384,16]{0,1:T(8,128)S(1)}, f32[384,16]{0,1:T(8,128)}, u32[]{:S(2)}) copy-start(f32[384,16]{0,1:T(8,128)} %param.23) | copy-start | bytes 73732
  0.7 5.9 %copy-start.1 = (bf16[32,384]{1,0:T(8,128)(2,1)S(1)}, bf16[32,384]{1,0:T(8,128)(2,1)}, u32[]{:S(2)}) copy-start(bf16[32,384]{1,0:T(8,128)(2,1)} %resid.1) | copy-start | bytes 73732
  3.3 5.3 %collective-permute-start = (bf16[32,384]{1,0:T(8,128)(2,1)S(1)}, bf16[32,384]{1,0:T(8,128)(2,1)S(1)}, u32[]{:S(2)}, u32[]{:S(2)}) collective-permute-start(bf16[32,384]{1,0:T(8,128)(2,1)S(1)} %get-tuple-element.37), channel_id=1, source_target_pairs={{0,2},{1,3},{2,0},{3,1},{4,6},{5,7},{6,4},{7,5},{8,10},{9,11},{10,... | collective-permute-start | bytes 73736 | tf_op jit(solution)/shard_map/ppermute | solution.py:150
  6.3 3.3 %collective-permute-start.1 = (bf16[32,384]{1,0:T(8,128)(2,1)S(1)}, bf16[32,384]{1,0:T(8,128)(2,1)S(1)}, u32[]{:S(2)}, u32[]{:S(2)}) collective-permute-start(bf16[32,384]{1,0:T(8,128)(2,1)S(1)} %get-tuple-element.38), channel_id=1, source_target_pairs={{0,3},{1,2},{2,1},{3,0},{4,7},{5,6},{6,5},{7,4},{8,11},{9,10},{10,... | collective-permute-start | bytes 73736 | tf_op jit(solution)/shard_map/ppermute | solution.py:150
  6.3 3.3 %collective-permute-start.2 = (bf16[32,384]{1,0:T(8,128)(2,1)S(1)}, bf16[32,384]{1,0:T(8,128)(2,1)S(1)}, u32[]{:S(2)}, u32[]{:S(2)}) collective-permute-start(bf16[32,384]{1,0:T(8,128)(2,1)S(1)} %get-tuple-element.39), channel_id=1, source_target_pairs={{0,1},{1,0},{2,3},{3,2},{4,5},{5,4},{6,7},{7,6},{8,9},{9,8},{10,11... | collective-permute-start | bytes 73736 | tf_op jit(solution)/shard_map/ppermute | solution.py:150
  6.5 13.1 %copy-start.4 = (f32[384]{0:T(512)S(1)}, f32[384]{0:T(512)}, u32[]{:S(2)}) copy-start(f32[384]{0:T(512)} %param.22) | copy-start | bytes 4612
  9.7 4.8 %collective-permute-start.3 = (bf16[32,384]{1,0:T(8,128)(2,1)S(1)}, bf16[32,384]{1,0:T(8,128)(2,1)S(1)}, u32[]{:S(2)}, u32[]{:S(2)}) collective-permute-start(bf16[32,384]{1,0:T(8,128)(2,1)S(1)} %get-tuple-element.45), channel_id=1, source_target_pairs={{0,16},{4,20},{8,24},{12,28},{16,0},{20,4},{24,8},{28,12},{1,17},{... | collective-permute-start | bytes 73736 | tf_op jit(solution)/shard_map/ppermute | solution.py:150
  12.4 5.6 %collective-permute-start.4 = (bf16[32,384]{1,0:T(8,128)(2,1)S(1)}, bf16[32,384]{1,0:T(8,128)(2,1)S(1)}, u32[]{:S(2)}, u32[]{:S(2)}) collective-permute-start(bf16[32,384]{1,0:T(8,128)(2,1)S(1)} %get-tuple-element.46), channel_id=1, source_target_pairs={{0,24},{4,28},{8,16},{12,20},{16,8},{20,12},{24,0},{28,4},{1,25},{... | collective-permute-start | bytes 73736 | tf_op jit(solution)/shard_map/ppermute | solution.py:150
  13.8 4.3 %collective-permute-start.5 = (bf16[32,384]{1,0:T(8,128)(2,1)S(1)}, bf16[32,384]{1,0:T(8,128)(2,1)S(1)}, u32[]{:S(2)}, u32[]{:S(2)}) collective-permute-start(bf16[32,384]{1,0:T(8,128)(2,1)S(1)} %get-tuple-element.47), channel_id=1, source_target_pairs={{0,8},{4,12},{8,0},{12,4},{16,24},{20,28},{24,16},{28,20},{1,9},{5... | collective-permute-start | bytes 73736 | tf_op jit(solution)/shard_map/ppermute | solution.py:150
  18.0 4.2 %collective-permute-start.6 = (bf16[64,384]{1,0:T(8,128)(2,1)S(1)}, bf16[64,384]{1,0:T(8,128)(2,1)S(1)}, u32[]{:S(2)}, u32[]{:S(2)}) collective-permute-start(bf16[64,384]{1,0:T(8,128)(2,1)S(1)} %shard_map.154.turned), channel_id=1, source_target_pairs={{0,4},{4,0},{8,12},{12,8},{16,20},{20,16},{24,28},{28,24},{1,5},{5... | collective-permute-start | bytes 147464 | tf_op jit(solution)/shard_map/ppermute | solution.py:150
  21.0 1.9 %collective-permute-start.9 = (bf16[32,2176]{1,0:T(8,128)(2,1)S(1)}, bf16[32,2176]{1,0:T(8,128)(2,1)S(1)}, u32[]{:S(2)}, u32[]{:S(2)}) collective-permute-start(bf16[32,2176]{1,0:T(8,128)(2,1)S(1)} %get-tuple-element.56), channel_id=1, source_target_pairs={{0,1},{1,0},{2,3},{3,2},{4,5},{5,4},{6,7},{7,6},{8,9},{9,8},{10,11... | collective-permute-start | bytes 417800 | tf_op jit(solution)/shard_map/ppermute | solution.py:150
  22.9 9.7 %copy-start = (bf16[2,1024,384]{2,1,0:T(8,128)(2,1)S(1)}, bf16[2,1024,384]{2,1,0:T(8,128)(2,1)}, u32[]{:S(2)}) copy-start(bf16[2,1024,384]{2,1,0:T(8,128)(2,1)} %param.27) | copy-start | bytes 4718596
  22.9 1.4 %collective-permute-start.7 = (bf16[32,2176]{1,0:T(8,128)(2,1)S(1)}, bf16[32,2176]{1,0:T(8,128)(2,1)S(1)}, u32[]{:S(2)}, u32[]{:S(2)}) collective-permute-start(bf16[32,2176]{1,0:T(8,128)(2,1)S(1)} %get-tuple-element.51), channel_id=1, source_target_pairs={{0,1},{1,0},{2,3},{3,2},{4,5},{5,4},{6,7},{7,6},{8,9},{9,8},{10,11... | collective-permute-start | bytes 417800 | tf_op jit(solution)/shard_map/ppermute | solution.py:150
  23.1 6.5 %collective-permute-start.10 = (bf16[32,2176]{1,0:T(8,128)(2,1)S(1)}, bf16[32,2176]{1,0:T(8,128)(2,1)S(1)}, u32[]{:S(2)}, u32[]{:S(2)}) collective-permute-start(bf16[32,2176]{1,0:T(8,128)(2,1)S(1)} %get-tuple-element.58), channel_id=1, source_target_pairs={{0,2},{1,3},{2,0},{3,1},{4,6},{5,7},{6,4},{7,5},{8,10},{9,11},{10,... | collective-permute-start | bytes 417800 | tf_op jit(solution)/shard_map/ppermute | solution.py:150
  24.5 7.7 %collective-permute-start.8 = (bf16[32,2176]{1,0:T(8,128)(2,1)S(1)}, bf16[32,2176]{1,0:T(8,128)(2,1)S(1)}, u32[]{:S(2)}, u32[]{:S(2)}) collective-permute-start(bf16[32,2176]{1,0:T(8,128)(2,1)S(1)} %get-tuple-element.53), channel_id=1, source_target_pairs={{0,2},{1,3},{2,0},{3,1},{4,6},{5,7},{6,4},{7,5},{8,10},{9,11},{10,... | collective-permute-start | bytes 417800 | tf_op jit(solution)/shard_map/ppermute | solution.py:150
  32.5 1.7 %collective-permute-start.11 = (bf16[64,1024]{1,0:T(8,128)(2,1)S(1)}, bf16[64,1024]{1,0:T(8,128)(2,1)S(1)}, u32[]{:S(2)}, u32[]{:S(2)}) collective-permute-start(bf16[64,1024]{1,0:T(8,128)(2,1)S(1)} %get-tuple-element.59.hidden), channel_id=1, source_target_pairs={{0,1},{1,0},{2,3},{3,2},{4,5},{5,4},{6,7},{7,6},{8,9},{9,8},{10,11... | collective-permute-start | bytes 393224 | tf_op jit(solution)/shard_map/ppermute | solution.py:150
  32.9 4.8 %collective-permute-start.12 = (bf16[32,384]{1,0:T(8,128)(2,1)S(1)}, bf16[32,384]{1,0:T(8,128)(2,1)S(1)}, u32[]{:S(2)}, u32[]{:S(2)}) collective-permute-start(bf16[32,384]{1,0:T(8,128)(2,1)S(1)} %get-tuple-element.62), channel_id=1, source_target_pairs={{0,16},{1,25},{2,18},{3,27},{4,20},{5,29},{6,22},{7,31},{8,24},{9,... | collective-permute-start | bytes 73736 | tf_op jit(solution)/shard_map/ppermute | solution.py:486
  34.6 5.8 %collective-permute-start.13 = (bf16[32,384]{1,0:T(8,128)(2,1)S(1)}, bf16[32,384]{1,0:T(8,128)(2,1)S(1)}, u32[]{:S(2)}, u32[]{:S(2)}) collective-permute-start(bf16[32,384]{1,0:T(8,128)(2,1)S(1)} %get-tuple-element.63), channel_id=1, source_target_pairs={{0,24},{1,9},{2,26},{3,11},{4,28},{5,13},{6,30},{7,15},{8,16},{9,1... | collective-permute-start | bytes 73736 | tf_op jit(solution)/shard_map/ppermute | solution.py:486
  36.3 4.1 %collective-permute-start.14 = (bf16[32,384]{1,0:T(8,128)(2,1)S(1)}, bf16[32,384]{1,0:T(8,128)(2,1)S(1)}, u32[]{:S(2)}, u32[]{:S(2)}) collective-permute-start(bf16[32,384]{1,0:T(8,128)(2,1)S(1)} %get-tuple-element.64), channel_id=1, source_target_pairs={{0,8},{1,17},{2,10},{3,19},{4,12},{5,21},{6,14},{7,23},{8,0},{9,25... | collective-permute-start | bytes 73736 | tf_op jit(solution)/shard_map/ppermute | solution.py:486
  40.4 4.1 %collective-permute-start.15 = (bf16[64,384]{1,0:T(8,128)(2,1)S(1)}, bf16[64,384]{1,0:T(8,128)(2,1)S(1)}, u32[]{:S(2)}, u32[]{:S(2)}) collective-permute-start(bf16[64,384]{1,0:T(8,128)(2,1)S(1)} %shard_map.162), channel_id=1, source_target_pairs={{0,4},{4,0},{8,12},{12,8},{16,20},{20,16},{24,28},{28,24},{1,5},{5... | collective-permute-start | bytes 147464 | tf_op jit(solution)/shard_map/ppermute | solution.py:150
